TPU v7x, 32 devices: a whole 2x2x4 slice. The times are simulated.
32 devices in a mesh: rng: 4 (over y, x), az: 8 (over z, core).
Axes of the slice: x: 2, y: 2, z: 4, core: 2. Of those that a mesh axis runs over, the one named last changes fastest.
Arguments:
- raw_echo: float32 [2, 16384, 4096], P(None, 'az', 'rng'), may hold values from -6 to 6
- chirp_spectrum: float32 [2, 4096], replicated, may hold values from -6 to 6
- azimuth_rate: float32 [4096], P(('rng', 'az')), may hold values from 100 to 400
- shift_table: int32 [16, 4096], P(None, ('rng', 'az')), may hold values from -28 to 29
- filter_index: int32 [16, 4096], P(None, ('rng', 'az')), may hold values from 0 to 15
- tap_table: float32 [16, 8], replicated, may hold values from -3 to 3
Outputs:
- image_out: float32 [2, 4096, 16384], P(None, ('rng', 'az'))
All inputs are finite; a program needn't handle non-finite values.
Results may differ from a plain program's by a relative error of at most 0.0003.
Values sent between devices are 32-bit elements; how exact they have to be, the bound alone decides.
No kernel may reach another device: no remote copies, remote signals or barrier semaphores. Data moves between devices by JAX's collectives and lax.ppermute only.
A program may use at most 128 MiB of HBM per device.

v0:
```python
import jax
import jax.numpy as jnp
from jax import lax
from jax.sharding import PartitionSpec as P

NRG = 4096
RG1 = 32
NAZ = 16384
AZ1 = 128
GROUPS = 16
NFILT = 16
TAPS = 8
HALO = 32


HIGHEST = lax.Precision.HIGHEST


def extended_2(shard, sides, width):
    for axis, dim in sides:
        count, length = (lax.axis_size(axis), shard.shape[dim])
        up = [(i, (i + 1) % count) for i in range(count - 1)]
        down = [(j, i) for i, j in up]
        last = lax.slice_in_dim(shard, length - width, length, axis=dim)
        first = lax.slice_in_dim(shard, 0, width, axis=dim)
        before = lax.ppermute(last, axis, up)
        after = lax.ppermute(first, axis, down)
        shard = jnp.concatenate([before, shard, after], axis=dim)
    return shard


def dft_table(length, conj_sign):
    indices = jnp.arange(length, dtype=jnp.int32)
    angles = indices[:, None] * indices[None, :] % length
    radians = angles.astype(jnp.float32) * (2.0 * jnp.pi / length)
    return (jnp.cos(radians), conj_sign * jnp.sin(radians))


def twiddles(outer_len, inner_len, conj_sign):
    outer_ids = jnp.arange(outer_len, dtype=jnp.int32)
    inner_ids = jnp.arange(inner_len, dtype=jnp.int32)
    angles = outer_ids[:, None] * inner_ids[None, :] % (outer_len * inner_len)
    radians = angles.astype(jnp.float32) * (2.0 * jnp.pi / (outer_len * inner_len))
    return (jnp.cos(radians), conj_sign * jnp.sin(radians))


def complex_mix(joined, matrix, values):
    block_matrix = jnp.stack(
        [jnp.stack([matrix[0], -matrix[1]]), jnp.stack([matrix[1], matrix[0]])]
    )
    return jnp.einsum(joined, block_matrix, values, precision=HIGHEST)


def complex_scale(values, factor):
    real_part = values[0] * factor[0] - values[1] * factor[1]
    imag_part = values[0] * factor[1] + values[1] * factor[0]
    return jnp.stack([real_part, imag_part])


def forward_dft(values, outer_len, inner_len):
    batch = values.shape[1]
    blocks = values.reshape(2, batch, outer_len, inner_len)
    blocks = complex_mix("prkn,rjnm->pjkm", dft_table(outer_len, -1.0), blocks)
    blocks = complex_scale(blocks, twiddles(outer_len, inner_len, -1.0))
    return complex_mix("prkn,rjmn->pjmk", dft_table(inner_len, -1.0), blocks)


def inverse_dft(blocks, outer_len, inner_len, joined):
    blocks = complex_mix("prmk,rjnk->pjnm", dft_table(inner_len, 1.0), blocks)
    blocks = complex_scale(blocks, twiddles(outer_len, inner_len, 1.0))
    result = complex_mix(joined, dft_table(outer_len, 1.0), blocks)
    return result * (1.0 / (outer_len * inner_len))


def local(raw_echo, chirp_spectrum, azimuth_rate, shift_table, filter_index, tap_table):
    range_rows = lax.all_to_all(raw_echo, "rng", split_axis=1, concat_axis=2, tiled=True)
    line_count = range_rows.shape[1]
    inner_range = NRG // RG1
    spectrum = forward_dft(range_rows, RG1, inner_range)
    chirp_ref = chirp_spectrum.reshape(2, inner_range, RG1).transpose(0, 2, 1)
    spectrum = complex_scale(spectrum, (chirp_ref[0], chirp_ref[1]))
    compressed = inverse_dft(spectrum, RG1, inner_range, "prnk,rjkm->pnmj").reshape(
        2, NRG, line_count
    )
    turned = lax.all_to_all(
        lax.all_to_all(compressed, "rng", split_axis=1, concat_axis=2, tiled=True),
        "az",
        split_axis=1,
        concat_axis=2,
        tiled=True,
    )
    bin_count = turned.shape[1]
    inner_az = NAZ // AZ1
    doppler = forward_dft(turned, AZ1, inner_az)
    extended = extended_2(doppler, ((("rng", "az"), 1),), HALO)
    ext_len = bin_count + 2 * HALO
    onehot = (filter_index[:, :, None] == jnp.arange(NFILT, dtype=jnp.int32)[None, None, :]).astype(
        jnp.float32
    )
    tap_weights = jnp.einsum("gbf,ft->gbt", onehot, tap_table, precision=HIGHEST)
    targets = (
        jnp.arange(bin_count, dtype=jnp.int32)[None, :, None]
        + shift_table[:, :, None]
        + (jnp.arange(TAPS, dtype=jnp.int32)[None, None, :] + (HALO - 4))
    )
    hits = (targets[..., None] == jnp.arange(ext_len, dtype=jnp.int32)).astype(jnp.float32)
    migrate_mat = jnp.einsum("gbt,gbtj->gjb", tap_weights, hits, precision=HIGHEST)
    per_band = inner_az // GROUPS
    banded = extended.reshape(2, ext_len, AZ1, GROUPS, per_band)
    migrated = jnp.einsum("gjb,cjkgm->cbkgm", migrate_mat, banded, precision=HIGHEST).reshape(
        2, bin_count, AZ1, inner_az
    )
    low_ids = jnp.arange(AZ1, dtype=jnp.int32)[:, None]
    high_ids = jnp.arange(inner_az, dtype=jnp.int32)[None, :]
    freq_ids = low_ids + AZ1 * high_ids
    centred = ((freq_ids + NAZ // 2) % NAZ - NAZ // 2).astype(jnp.float32) / NAZ
    phase_map = (jnp.pi * azimuth_rate)[:, None, None] * (centred * centred)[None]
    focused = complex_scale(migrated, (jnp.cos(phase_map), -jnp.sin(phase_map)))
    image_out = inverse_dft(focused, AZ1, inner_az, "prnk,rjkm->pjnm")
    return image_out.reshape(2, bin_count, NAZ)


def solution(mesh):
    return jax.shard_map(
        local,
        mesh=mesh,
        in_specs=(
            P(None, "az", "rng"),
            P(),
            P(("rng", "az")),
            P(None, ("rng", "az")),
            P(None, ("rng", "az")),
            P(),
        ),
        out_specs=P(None, ("rng", "az"), None),
        check_vma=False,
    )
```

profile of v0, /device:TPU:4, one launch (start us, length us, event | category | flops | bytes accessed | tf_op | source)
XLA Modules:
  0.0 1435.7 jit_solution(5656424492286186623)
XLA Ops:
  0.0 28.6 %copy.104 = f32[2,2048,1024]{2,0,1:T(2,128)} copy(f32[2,2048,1024]{2,1,0:T(8,128)} %param.6) | data formatting | bytes 33554432 | tf_op args[0]
  37.4 180.6 %all-to-all-done = f32[2,2048,1024]{2,0,1:T(2,128)} async-done(((f32[2,2048,1024]{2,0,1:T(2,128)}), f32[2,2048,1024]{2,0,1:T(2,128)}, u32[]{:S(2)}, u32[]{:S(2)}) %all-to-all-start) | async-done | bytes 16777248 | tf_op jit(solution)/shard_map/all_to_all | solution.py:76
  218.0 20.9 %copy.180 = f32[2,4,512,1024]{3,1,0,2:T(4,128)} copy(f32[2,4,512,1024]{3,0,2,1:T(2,128)} %bitcast.4) | data formatting | bytes 33554432 | tf_op jit(solution)/shard_map/all_to_all | solution.py:76
  238.9 19.9 %reshape.427 = f32[2,512,32,128,1]{3,2,0,1,4:T(8,128)} reshape(f32[2,512,4,1024]{3,2,0,1:T(4,128)} %bitcast.148) | data formatting | bytes 33554432 | tf_op jit(solution)/shard_map/reshape | solution.py:62
  258.8 22.6 %convolution_bitcast_fusion.1 = f32[2,512,32,128]{3,2,1,0:T(8,128)} fusion(f32[2,512,32,128,1]{3,2,0,1,4:T(8,128)} %reshape.427, f32[1,2,32,32]{3,2,1,0:T(8,128)S(1)} %get-tuple-element.29, f32[1,2,32,32]{3,2,1,0:T(8,128)S(1)} %get-tuple-element.30), kind=kOutput, calls=%fused_computation.56 | convolution fusion | flops 3221229568 | bytes 33570816 | tf_op jit(solution)/shard_map/prkn,rjnm->pjkm/dot_general | solution.py:51
  294.9 29.1 %fusion.23 = f32[2,512,32,128]{3,1,0,2:T(8,128)S(1)} fusion(f32[2,512,32,128,1]{3,2,1,0,4:T(8,128)} %maximum_bitcast_fusion.1, f32[1,2,128,128]{3,2,1,0:T(8,128)S(1)} %get-tuple-element.25, f32[1,2,128,128]{3,2,1,0:T(8,128)S(1)} %get-tuple-element.26), kind=kOutput, calls=%fused_computation.35 | convolution fusion | flops 12884967424 | bytes 33816576 | tf_op jit(solution)/shard_map/prkn,rjmn->pjmk/dot_general | solution.py:51
  337.9 26.9 %fusion.36 = f32[2,512,32,128]{3,2,1,0:T(8,128)S(1)} fusion(f32[2,512,32,128,1]{3,1,0,2,4:T(8,128)S(1)} %maximum_bitcast_fusion.2, f32[1,2,128,128]{3,2,1,0:T(8,128)S(1)} %get-tuple-element.24, f32[1,2,128,128]{3,2,1,0:T(8,128)S(1)} %get-tuple-element.23), kind=kOutput, calls=%fused_computation.55 | convolution fusion | flops 12884967424 | bytes 33816576 | tf_op jit(solution)/shard_map/prmk,rjnk->pjnm/dot_general | solution.py:51
  371.8 19.9 %fusion.12 = f32[2,32,128,512]{2,1,0,3:T(8,128)} fusion(f32[1,2,32,32]{3,2,1,0:T(8,128)S(1)} %get-tuple-element.28, f32[1,2,32,32]{3,2,1,0:T(8,128)S(1)} %get-tuple-element.27, f32[1,512,32,128]{3,2,1,0:T(8,128)} %get-tuple-element.12, f32[1,512,32,128]{3,2,1,0:T(8,128)} %get-tuple-element.11), kind=kOutput, calls=%fused_computation.21 | convolution fusion | flops 3229618176 | bytes 33570816 | tf_op jit(solution)/shard_map/prnk,rjkm->pnmj/dot_general | solution.py:51
  391.7 19.6 %copy.156 = f32[2,32,128,512]{3,0,2,1:T(2,128)} copy(f32[2,32,128,512]{2,1,0,3:T(8,128)} %fusion.12) | data formatting | bytes 33554432 | tf_op jit(solution)/shard_map/reshape | solution.py:82
  411.3 186.6 %all_to_all.48 = f32[2,4096,512]{2,0,1:T(2,128)S(1)} all-to-all(f32[2,4096,512]{2,0,1:T(2,128)} %bitcast.149), channel_id=1, replica_groups=mesh['rng'=4,'az'=8] {'rng'}, dimensions={1} | all-to-all | bytes 33554432 | tf_op jit(solution)/shard_map/all_to_all | solution.py:86
  597.8 8.9 copy.112
  606.7 16.5 %copy.113 = f32[2,1024,4,512]{1,3,2,0:T(8,128)} copy(f32[2,1024,4,512]{3,1,2,0:T(8,128)} %bitcast.150) | data formatting | bytes 33554432 | tf_op jit(solution)/shard_map/all_to_all | solution.py:86
  623.2 25.3 %copy.114 = f32[2,1024,2048]{2,0,1:T(2,128)} copy(f32[2,1024,2048]{1,2,0:T(8,128)} %bitcast.151) | data formatting | bytes 33554432 | tf_op jit(solution)/shard_map/all_to_all | solution.py:86
  654.9 363.4 %all-to-all-done.2 = f32[2,1024,2048]{2,0,1:T(2,128)} async-done(((f32[2,1024,2048]{2,0,1:T(2,128)}), f32[2,1024,2048]{2,0,1:T(2,128)}, u32[]{:S(2)}, u32[]{:S(2)}) %all-to-all-start.2) | async-done | bytes 16777248 | tf_op jit(solution)/shard_map/all_to_all | solution.py:85
  1018.3 17.7 %copy.115 = f32[2,1024,2048]{2,1,0:T(8,128)} copy(f32[2,1024,2048]{2,0,1:T(2,128)} %all-to-all-done.2) | data formatting | bytes 33554432 | tf_op jit(solution)/shard_map/all_to_all | solution.py:85
  1036.0 17.2 %copy.116 = f32[2,128,8,2048]{1,3,2,0:T(8,128)} copy(f32[2,128,8,2048]{3,1,2,0:T(8,128)} %bitcast.152) | data formatting | bytes 33554432 | tf_op jit(solution)/shard_map/all_to_all | solution.py:85
  1053.3 18.1 %copy.137 = f32[2,128,128,128,1]{2,3,0,4,1:T(8,128)} copy(f32[2,128,128,128,1]{1,3,2,0,4:T(8,128)} %bitcast.153) | data formatting | bytes 33554432 | tf_op jit(solution)/shard_map/reshape | solution.py:62
  1071.4 16.1 %convolution_bitcast_fusion = f32[2,128,128,128]{2,3,0,1:T(8,128)S(1)} fusion(f32[2,128,128,128,1]{2,3,0,4,1:T(8,128)} %copy.137, f32[1,2,128,128]{3,2,1,0:T(8,128)S(1)} %get-tuple-element.25, f32[1,2,128,128]{3,2,1,0:T(8,128)S(1)} %get-tuple-element.26), kind=kOutput, calls=%fused_computation.39 | convolution fusion | flops 12884967424 | bytes 33816576 | tf_op jit(solution)/shard_map/prkn,rjnm->pjkm/dot_general | solution.py:51
  1087.5 7.2 multiply_subtract_fusion.1
  1094.8 18.3 %fusion.27 = f32[2,128,128,128]{2,3,0,1:T(8,128)S(1)} fusion(f32[1,128,128,128]{2,3,0,1:T(8,128)} %get-tuple-element.8, f32[1,128,128,128]{2,3,0,1:T(8,128)} %get-tuple-element.7, f32[1,2,128,128]{3,2,1,0:T(8,128)S(1)} %get-tuple-element.25, f32[1,2,128,128]{3,2,1,0:T(8,128)S(1)} %get-tuple-element.26), kind=kOutput, calls=%fused_computation.37 | convolution fusion | flops 12889161728 | bytes 33816576 | tf_op jit(solution)/shard_map/prkn,rjmn->pjmk/dot_general | solution.py:51
  1123.7 7.2 collective-permute-start.1
  1133.8 86.0 %collective-permute-done = f32[2,32,128,128]{2,3,0,1:T(8,128)} collective-permute-done((f32[2,32,128,128]{2,3,0,1:T(8,128)}, f32[2,32,128,128]{2,3,0,1:T(8,128)}, u32[]{:S(2)}, u32[]{:S(2)}) %collective-permute-start) | collective-permute-done | bytes 4194336 | tf_op jit(solution)/shard_map/ppermute | solution.py:26
  1219.8 10.3 maximum_bitcast_fusion
  1230.1 62.4 %fusion.28 = f32[2,128,128,16,8]{1,2,4,0,3:T(8,128)} fusion(f32[2,192,128,16,8]{2,4,3,0,1:T(8,128)S(1)} %maximum_bitcast_fusion, f32[16,128,192]{1,2,0:T(8,128)S(1)} %select_reduce_fusion), kind=kOutput, calls=%fused_computation.38 | convolution fusion | flops 9663676416 | bytes 43515904 | tf_op jit(solution)/shard_map/gjb,cjkgm->cbkgm/dot_general | solution.py:110
  1292.5 10.9 fusion.107
  1303.4 9.3 copy.121
  1312.7 9.3 copy.122
  1322.0 34.5 %fusion.31 = (f32[1,128,128,128]{3,2,0,1:T(8,128)S(1)}, f32[1,128,128,128]{3,2,0,1:T(8,128)}) fusion(f32[1,128,128,128]{3,2,0,1:T(8,128)} %copy.121, f32[1,128,128,128]{3,2,0,1:T(8,128)} %copy.122, f32[128,128]{1,0:T(8,128)S(1)} %copy.120, f32[128]{0:T(128)S(1)} %broadcast_multiply_fusion.4), kind=kLoop, calls=%fused_computation.40 | loop fusion | flops 16777216 | bytes 33620480 | tf_op jit(solution)/shard_map/sub | solution.py:55
  1356.5 17.7 %fusion.26 = f32[2,128,128,128]{2,3,0,1:T(8,128)S(1)} fusion(f32[1,128,128,128]{3,2,0,1:T(8,128)} %get-tuple-element.10, f32[1,128,128,128]{3,2,0,1:T(8,128)S(1)} %get-tuple-element.9, f32[1,2,128,128]{3,2,1,0:T(8,128)S(1)} %copy-done.5, f32[1,2,128,128]{3,2,1,0:T(8,128)S(1)} %copy-done.3), kind=kOutput, calls=%fused_computation.36 | convolution fusion | flops 12889161728 | bytes 33816576 | tf_op jit(solution)/shard_map/prmk,rjnk->pjnm/dot_general | solution.py:51
  1381.2 18.7 %fusion.11 = f32[2,128,128,128]{2,3,0,1:T(8,128)} fusion(f32[1,128,128,128]{2,3,0,1:T(8,128)} %get-tuple-element.6, f32[1,128,128,128]{2,3,0,1:T(8,128)} %get-tuple-element.5, f32[1,2,128,128]{3,2,1,0:T(8,128)S(1)} %copy-done.5, f32[1,2,128,128]{3,2,1,0:T(8,128)S(1)} %copy-done.3), kind=kOutput, calls=%fused_computation.19 | convolution fusion | flops 12893356032 | bytes 33816576 | tf_op jit(solution)/shard_map/prnk,rjkm->pjnm/dot_general | solution.py:51
  1399.9 18.1 %copy.126 = f32[2,128,128,128]{1,3,2,0:T(8,128)} copy(f32[2,128,128,128]{2,3,0,1:T(8,128)} %fusion.11) | data formatting | bytes 33554432 | tf_op jit(solution)/shard_map/mul | solution.py:72
  1418.0 17.5 %copy.127 = f32[2,128,16384]{2,1,0:T(8,128)} copy(f32[2,128,16384]{1,2,0:T(8,128)} %bitcast.154) | data formatting | bytes 33554432 | tf_op jit(solution)/shard_map/reshape | solution.py:120
  (56 shorter events, 70.0 us)
Async XLA Ops:
  0.0 1131.6 %copy-start = (f32[16,8]{0,1:T(8,128)S(1)}, f32[16,8]{0,1:T(8,128)}, u32[]{:S(2)}) copy-start(f32[16,8]{0,1:T(8,128)} %param.11) | copy-start | bytes 1540
  28.6 7.2 copy-start.6
  28.6 189.4 %all-to-all-start = ((f32[2,2048,1024]{2,0,1:T(2,128)}), f32[2,2048,1024]{2,0,1:T(2,128)}, u32[]{:S(2)}, u32[]{:S(2)}) async-start(f32[2,2048,1024]{2,0,1:T(2,128)} %copy.104), calls=%async_computation | async-start | bytes 33554432 | tf_op jit(solution)/shard_map/all_to_all | solution.py:76
  37.4 300.5 %copy-start.2 = (f32[1,2,128,128]{3,2,1,0:T(8,128)}, f32[1,2,128,128]{3,2,1,0:T(8,128)S(1)}, u32[]{:S(2)}) copy-start(f32[1,2,128,128]{3,2,1,0:T(8,128)S(1)} %get-tuple-element.23) | copy-start | bytes 393220
  37.4 300.5 %copy-start.4 = (f32[1,2,128,128]{3,2,1,0:T(8,128)}, f32[1,2,128,128]{3,2,1,0:T(8,128)S(1)}, u32[]{:S(2)}) copy-start(f32[1,2,128,128]{3,2,1,0:T(8,128)S(1)} %get-tuple-element.24) | copy-start | bytes 393220
  648.5 369.8 %all-to-all-start.2 = ((f32[2,1024,2048]{2,0,1:T(2,128)}), f32[2,1024,2048]{2,0,1:T(2,128)}, u32[]{:S(2)}, u32[]{:S(2)}) async-start(f32[2,1024,2048]{2,0,1:T(2,128)} %copy.114), calls=%async_computation.2 | async-start | bytes 33554432 | tf_op jit(solution)/shard_map/all_to_all | solution.py:85
  1113.1 8.7 copy-start.1
  1113.1 18.4 %copy-start.9 = (f32[128]{0:T(128)S(1)}, f32[128]{0:T(128)}, u32[]{:S(2)}) copy-start(f32[128]{0:T(128)} %param.8) | copy-start | bytes 1540
  1113.1 18.4 %copy-start.8 = (s32[16,128]{1,0:T(8,128)S(1)}, s32[16,128]{1,0:T(8,128)}, u32[]{:S(2)}) copy-start(s32[16,128]{1,0:T(8,128)} %param.9) | copy-start | bytes 24580
  1113.1 18.5 %copy-start.7 = (s32[16,128]{1,0:T(8,128)S(1)}, s32[16,128]{1,0:T(8,128)}, u32[]{:S(2)}) copy-start(s32[16,128]{1,0:T(8,128)} %param.10) | copy-start | bytes 24580
  1121.8 97.9 %collective-permute-start = (f32[2,32,128,128]{2,3,0,1:T(8,128)}, f32[2,32,128,128]{2,3,0,1:T(8,128)}, u32[]{:S(2)}, u32[]{:S(2)}) collective-permute-start(f32[2,32,128,128]{2,3,0,1:T(8,128)} %get-tuple-element.19), channel_id=1, source_target_pairs={{0,1},{1,2},{2,3},{3,4},{4,5},{5,6},{6,7},{7,8},{8,9},{9,10},{10,1... | collective-permute-start | bytes 12582920 | tf_op jit(solution)/shard_map/ppermute | solution.py:26
  1123.7 96.0 %collective-permute-start.1 = (f32[2,32,128,128]{2,3,0,1:T(8,128)}, f32[2,32,128,128]{2,3,0,1:T(8,128)}, u32[]{:S(2)}, u32[]{:S(2)}) collective-permute-start(f32[2,32,128,128]{2,3,0,1:T(8,128)} %get-tuple-element.20), channel_id=1, source_target_pairs={{1,0},{2,1},{3,2},{4,3},{5,4},{6,5},{7,6},{8,7},{9,8},{10,9},{11,1... | collective-permute-start | bytes 12582920 | tf_op jit(solution)/shard_map/ppermute | solution.py:27
  1322.0 34.5 %copy-start.3 = (f32[1,2,128,128]{3,2,1,0:T(8,128)S(1)}, f32[1,2,128,128]{3,2,1,0:T(8,128)}, u32[]{:S(2)}) copy-start(f32[1,2,128,128]{3,2,1,0:T(8,128)} %copy-done.2) | copy-start | bytes 393220
  1322.0 34.5 %copy-start.5 = (f32[1,2,128,128]{3,2,1,0:T(8,128)S(1)}, f32[1,2,128,128]{3,2,1,0:T(8,128)}, u32[]{:S(2)}) copy-start(f32[1,2,128,128]{3,2,1,0:T(8,128)} %copy-done.4) | copy-start | bytes 393220
where the time goes:
time: 1440 us
  waiting for transfers between devices  630 us (44%)
  local copies, waits for them, and re-layouts  267 us (19%)
  matrix products  232 us (16%)
  blocking collectives  187 us (13%)
  other arithmetic  97.5 us (7%)
  starting transfers between devices  22.5 us (2%)
    all_to_all x1, waiting for transfers between devices, local(): lax.all_to_all(lax.all_to_all(compressed, 'rng', split_axis=1, concat_axi...  363 us
    all_to_all x1, blocking collectives, local(): lax.all_to_all(compressed, 'rng', split_axis=1, concat_axis=2, tiled=True)  187 us
    all_to_all x1, waiting for transfers between devices, local(): lax.all_to_all(raw_echo, 'rng', split_axis=1, concat_axis=2, tiled=True)  181 us
    dot_general x8, matrix products, complex_mix(): return jnp.einsum(joined, block_matrix, values, precision=HIGHEST)  169 us
    ppermute x1, waiting for transfers between devices, extended_2(): before = lax.ppermute(last, axis, up)  86 us
    sub x6, other arithmetic, complex_scale(): real_part = values[0] * factor[0] - values[1] * factor[1]  70 us
    dot_general x1, matrix products, local(): jnp.einsum('gjb,cjkgm->cbkgm', migrate_mat, banded, precision=HIGHEST)  62.4 us
    all_to_all x3, local copies, waits for them, and re-layouts, local(): lax.all_to_all(compressed, 'rng', split_axis=1, concat_axis=2, tiled=True)  50.6 us
  transfers between devices with their start and end apart: 4, of which 3 were waited for; matrix products, arithmetic and copies ran while one was open for 0% of the time, Pallas kernels for 0%

commit v1 on v0

v1 whole, which is shorter than its diff:
```python
import functools

import jax
import jax.numpy as jnp
import ml_dtypes
import numpy as np
from jax import lax
from jax.experimental import pallas as pl
from jax.experimental.pallas import tpu as pltpu
from jax.sharding import PartitionSpec as P

NRG = 4096
NAZ = 16384
GROUPS = 16
NFILT = 16
TAPS = 8
HALO = 32
LANES = 128
RG1 = NRG // LANES
CHUNKS = 8
PER_CHUNK = LANES // CHUNKS
BF16 = jnp.bfloat16
F32 = jnp.float32


def split_np(table):
    table = np.asarray(table, np.float32)
    high = table.astype(ml_dtypes.bfloat16)
    low = (table - high.astype(np.float32)).astype(ml_dtypes.bfloat16)
    return high, low


def unit(angle_num, period, sign):
    angles = (np.asarray(angle_num, np.int64) % period) * (2.0 * np.pi / period)
    return np.cos(angles), sign * np.sin(angles)


def dft_matrix(sign):
    ids = np.arange(LANES)
    return unit(ids[:, None] * ids[None, :], LANES, sign)


def right_tables(sign, scale=1.0):
    c, s = dft_matrix(sign)
    return split_np(np.block([[c, s], [-s, c]]) * scale)


def left_table(sign, scale=1.0):
    c, s = dft_matrix(sign)
    high, low = split_np(np.block([[c, -s], [s, c]]) * scale)
    return np.concatenate([high, high, low], axis=1)


def split(x):
    high = x.astype(BF16)
    low = (x - high.astype(F32)).astype(BF16)
    return high, low


def dot(a, b):
    return jnp.dot(a, b, preferred_element_type=F32)


def scale_by(value, re, im):
    a, b = value
    eps = 1e-12
    if abs(im) < eps:
        if abs(re - 1.0) < eps:
            return value
        if abs(re + 1.0) < eps:
            return -a, -b
    if abs(re) < eps:
        if abs(im - 1.0) < eps:
            return -b, a
        if abs(im + 1.0) < eps:
            return b, -a
    if abs(abs(re) - abs(im)) < eps:
        sr, si = (1.0 if re > 0 else -1.0), (1.0 if im > 0 else -1.0)
        h = abs(re)
        total, diff = (a + b) * h, (a - b) * h
        if si == sr:
            return (diff, total) if sr > 0 else (-diff, -total)
        return (total, -diff) if sr > 0 else (-total, diff)
    re, im = float(re), float(im)
    return a * re - b * im, a * im + b * re


def dft_list(values, sign):
    count = len(values)
    if count == 1:
        return values
    even, odd = dft_list(values[0::2], sign), dft_list(values[1::2], sign)
    first, second = [], []
    for k in range(count // 2):
        re, im = unit(k, count, sign)
        a, b = even[k], scale_by(odd[k], float(re), float(im))
        first.append((a[0] + b[0], a[1] + b[1]))
        second.append((a[0] - b[0], a[1] - b[1]))
    return first + second


def dft_two_step(load, mid_ref, finish, outer, inner, sign):
    for ib in range(inner):
        column = dft_list([load(ia * inner + ib) for ia in range(outer)], sign)
        for ka in range(outer):
            re, im = unit(ib * ka, outer * inner, sign)
            a, b = scale_by(column[ka], float(re), float(im))
            mid_ref[ka * inner + ib, 0] = a
            mid_ref[ka * inner + ib, 1] = b
    for ka in range(outer):
        row = [(mid_ref[ka * inner + ib, 0], mid_ref[ka * inner + ib, 1]) for ib in range(inner)]
        for kb, value in enumerate(dft_list(row, sign)):
            finish(ka + outer * kb, value)


def pack_kernel(chunks, parts, per_part, rows_in, rank_ref, x_ref, *out_refs):
    rank = rank_ref[0]
    for j in range(parts):
        part = jnp.bitwise_xor(rank, j)
        for at, c in enumerate(chunks):
            for m in range(per_part):
                start = CHUNKS * (part * per_part + m) + c
                for ri in range(2):
                    out_refs[at * parts + j][ri, 0, m * rows_in : (m + 1) * rows_in, :] = x_ref[
                        ri, pl.ds(start, rows_in, stride=LANES), :
                    ]


def pack(raw, rank, parts, chunks):
    lines, bins = raw.shape[1], raw.shape[2]
    rows_in, tiles, per_part = lines // LANES, bins // LANES, PER_CHUNK // parts
    rows = per_part * rows_in
    count = len(chunks) * parts
    shape = jax.ShapeDtypeStruct((2, tiles, rows, LANES), F32)
    spec = pl.BlockSpec((2, 1, rows, LANES), lambda i: (0, i, 0, 0))
    flat = pl.pallas_call(
        functools.partial(pack_kernel, chunks, parts, per_part, rows_in),
        grid=(tiles,),
        in_specs=[
            pl.BlockSpec(memory_space=pltpu.SMEM),
            pl.BlockSpec((2, lines, LANES), lambda i: (0, 0, i)),
        ],
        out_specs=[spec] * count,
        out_shape=[shape] * count,
        compiler_params=pltpu.CompilerParams(vmem_limit_bytes=32 << 20),
        cost_estimate=pl.CostEstimate(flops=0, bytes_accessed=16 * lines * bins, transcendentals=0),
        name="pack",
    )(rank, raw)
    return [flat[i * parts : (i + 1) * parts] for i in range(len(chunks))]


STEP = 16


def compress_kernel(parts, rows, rank_ref, *refs):
    x_refs = refs[:parts]
    chirp_ref, tw_ref, fwd_ref, fwd_low_ref, inv_ref, inv_low_ref = refs[parts : parts + 6]
    out_ref, buf_ref, lhs_ref, y_ref, mid_ref, sems = refs[parts + 6 :]
    tiles = buf_ref.shape[3]
    rank = rank_ref[0]
    step = pl.program_id(0)
    slot = lax.rem(step, 2)

    def copies(at, to):
        return [
            pltpu.make_async_copy(
                x_refs[j].at[:, :, pl.ds(pl.multiple_of(at * rows, rows), rows), :],
                buf_ref.at[to, jnp.bitwise_xor(rank, j)],
                sems.at[to, j],
            )
            for j in range(parts)
        ]

    @pl.when(step == 0)
    def _():
        for copy in copies(step, slot):
            copy.start()

    @pl.when(step + 1 < pl.num_programs(0))
    def _():
        for copy in copies(step + 1, 1 - slot):
            copy.start()

    for copy in copies(step, slot):
        copy.wait()

    def put(at, re, im):
        for half, part in enumerate((re, im)):
            high, low = split(part)
            lhs_ref[at, half * LANES : (half + 1) * LANES] = high
            lhs_ref[at, (2 + half) * LANES : (3 + half) * LANES] = low

    def forward(i, carry):
        at = pl.ds(pl.multiple_of(i * STEP, STEP), STEP)

        def load(p):
            source = buf_ref.at[slot, p // tiles]
            return source[0, p % tiles, at, :], source[1, p % tiles, at, :]

        def finish(k, value):
            wr, wi = tw_ref[0, k : k + 1, :], tw_ref[1, k : k + 1, :]
            a, b = value
            put(
                pl.ds(pl.multiple_of(k * rows + i * STEP, STEP), STEP),
                a * wr - b * wi,
                a * wi + b * wr,
            )

        dft_two_step(load, mid_ref, finish, 4, RG1 // 4, -1.0)
        return carry

    lax.fori_loop(0, rows // STEP, forward, 0)

    group = max(1, LANES // rows)

    def middle(i, carry):
        at = pl.ds(pl.multiple_of(i * group * rows, group * rows), group * rows)
        y = dot(lhs_ref[at, :], fwd_ref[...]) + dot(lhs_ref[at, 0 : 2 * LANES], fwd_low_ref[...])
        for s in range(group):
            k = i * group + s
            cr, ci = chirp_ref[0, pl.ds(k, 1), :], chirp_ref[1, pl.ds(k, 1), :]
            a = y[s * rows : (s + 1) * rows, 0:LANES]
            b = y[s * rows : (s + 1) * rows, LANES : 2 * LANES]
            put(pl.ds(pl.multiple_of(k * rows, rows), rows), a * cr - b * ci, a * ci + b * cr)
        z = dot(lhs_ref[at, :], inv_ref[...]) + dot(lhs_ref[at, 0 : 2 * LANES], inv_low_ref[...])
        for s in range(group):
            k = i * group + s
            wr, wi = tw_ref[0, pl.ds(k, 1), :], tw_ref[1, pl.ds(k, 1), :]
            a = z[s * rows : (s + 1) * rows, 0:LANES]
            b = z[s * rows : (s + 1) * rows, LANES : 2 * LANES]
            y_ref[k, 0] = a * wr + b * wi
            y_ref[k, 1] = b * wr - a * wi
        return carry

    lax.fori_loop(0, RG1 // group, middle, 0)

    def backward(i, carry):
        at = pl.ds(pl.multiple_of(i * STEP, STEP), STEP)

        def load(k):
            return y_ref[k, 0, at, :], y_ref[k, 1, at, :]

        def finish(p, value):
            out_ref[p, 0, at, :] = value[0]
            out_ref[p, 1, at, :] = value[1]

        dft_two_step(load, mid_ref, finish, 4, RG1 // 4, 1.0)
        return carry

    lax.fori_loop(0, rows // STEP, backward, 0)


def whole_spec(array):
    zeros = (0,) * array.ndim
    return pl.BlockSpec(array.shape, lambda *_: zeros)


def compress(pieces, rank, chirp):
    parts = len(pieces)
    _, tiles, rows, _ = pieces[0].shape
    block = min(rows, 32)
    ids = np.arange(RG1)[:, None] * np.arange(LANES)[None, :]
    tw = jnp.asarray(np.stack(unit(ids, NRG, -1.0)), F32)
    fwd, fwd_low = right_tables(-1.0)
    inv, inv_low = right_tables(1.0, 1.0 / NRG)
    consts = [
        chirp,
        tw,
        jnp.asarray(np.concatenate([fwd, fwd])),
        jnp.asarray(fwd_low),
        jnp.asarray(np.concatenate([inv, inv])),
        jnp.asarray(inv_low),
    ]
    points = rows * NRG
    return pl.pallas_call(
        functools.partial(compress_kernel, parts, block),
        grid=(rows // block,),
        in_specs=[pl.BlockSpec(memory_space=pltpu.SMEM)]
        + [pl.BlockSpec(memory_space=pl.ANY)] * parts
        + [whole_spec(a) for a in consts],
        out_specs=pl.BlockSpec((RG1, 2, block, LANES), lambda i: (0, 0, i, 0)),
        out_shape=jax.ShapeDtypeStruct((RG1, 2, rows, LANES), F32),
        scratch_shapes=[
            pltpu.VMEM((2, parts, 2, tiles, block, LANES), F32),
            pltpu.VMEM((RG1 * block, 4 * LANES), BF16),
            pltpu.VMEM((RG1, 2, block, LANES), F32),
            pltpu.VMEM((RG1, 2, STEP, LANES), F32),
            pltpu.SemaphoreType.DMA((2, parts)),
        ],
        compiler_params=pltpu.CompilerParams(vmem_limit_bytes=40 << 20),
        cost_estimate=pl.CostEstimate(
            flops=points * 8 * LANES * 6, bytes_accessed=16 * points, transcendentals=0
        ),
        name="compress",
    )(rank, *pieces, *consts)


def azimuth_kernel(chunk, x_ref, tw_ref, fwd_ref, fwd_low_ref, out_ref, up_ref, down_ref, t_ref, mid_ref):
    part = pl.program_id(0)
    pieces, per_part, bins = x_ref.shape[1], x_ref.shape[3], x_ref.shape[5]

    def stage(m, carry):
        sides = []
        for ri in range(2):
            column = jnp.concatenate([x_ref[0, a, ri, m] for a in range(pieces)], axis=0)
            sides.append(split(jnp.transpose(column)))
        high = jnp.concatenate([sides[0][0], sides[1][0]], axis=1)
        low = jnp.concatenate([sides[0][1], sides[1][1]], axis=1)
        y = dot(high, fwd_ref[...]) + dot(low, fwd_ref[...]) + dot(high, fwd_low_ref[...])
        index = part * per_part + m
        at = pl.ds(CHUNKS * index + chunk, 1)
        wr, wi = tw_ref[0, at, :], tw_ref[1, at, :]
        a, b = y[:, 0:LANES], y[:, LANES : 2 * LANES]
        t_ref[index, 0] = a * wr - b * wi
        t_ref[index, 1] = a * wi + b * wr
        return carry

    lax.fori_loop(0, per_part, stage, 0)

    @pl.when(part == pl.num_programs(0) - 1)
    def _():
        def rest(i, carry):
            at = pl.ds(pl.multiple_of(i * STEP, STEP), STEP)

            def load(m):
                return t_ref[m, 0, at, :], t_ref[m, 1, at, :]

            def finish(k, value):
                re, im = unit(chunk * k, LANES, -1.0)
                a, b = scale_by(value, float(re), float(im))
                out_ref[k, 0, at, :] = a
                out_ref[k, 1, at, :] = b

            dft_two_step(load, mid_ref, finish, 4, PER_CHUNK // 4, -1.0)
            return carry

        lax.fori_loop(0, bins // STEP, rest, 0)

        def edges(k, carry):
            for ri in range(2):
                up_ref[k, ri] = out_ref[k, ri, bins - HALO : bins, :]
                down_ref[k, ri] = out_ref[k, ri, 0:HALO, :]
            return carry

        lax.fori_loop(0, PER_CHUNK, edges, 0)


def azimuth(x, chunk):
    parts, pieces, _, per_part, rows_in, bins = x.shape
    ids = np.arange(LANES)
    tw = jnp.asarray(np.stack(unit(ids[:, None] * ids[None, :], NAZ, -1.0)), F32)
    fwd, fwd_low = right_tables(-1.0)
    consts = [tw, jnp.asarray(fwd), jnp.asarray(fwd_low)]
    points = PER_CHUNK * LANES * bins
    shape = (PER_CHUNK, 2, bins, LANES)
    edge = (PER_CHUNK, 2, HALO, LANES)
    return pl.pallas_call(
        functools.partial(azimuth_kernel, chunk),
        grid=(parts,),
        in_specs=[
            pl.BlockSpec(
                (1, pieces, 2, per_part, rows_in, bins), lambda i: (i, 0, 0, 0, 0, 0)
            )
        ]
        + [whole_spec(a) for a in consts],
        out_specs=[pl.BlockSpec(s, lambda i: (0, 0, 0, 0)) for s in (shape, edge, edge)],
        out_shape=[jax.ShapeDtypeStruct(s, F32) for s in (shape, edge, edge)],
        scratch_shapes=[pltpu.VMEM(shape, F32), pltpu.VMEM((PER_CHUNK, 2, STEP, LANES), F32)],
        compiler_params=pltpu.CompilerParams(vmem_limit_bytes=32 << 20),
        cost_estimate=pl.CostEstimate(
            flops=points * 8 * LANES * 3, bytes_accessed=16 * points, transcendentals=0
        ),
        name=f"azimuth{chunk}",
    )(x, *consts)


KB = 4
BB = 8
QUAD = 4


def fit(fn, even):
    nodes = np.cos((2 * np.arange(64) + 1) * np.pi / 128) * 0.25
    z2 = (nodes + 0.25) / 2
    z = np.sqrt(z2)
    goal = fn(np.pi * z) if even else fn(np.pi * z) / z
    return [float(v) for v in np.polynomial.polynomial.polyfit(z2, goal, 4)]


SIN_FIT, COS_FIT = fit(np.sin, False), fit(np.cos, True)


def horner(coefficients, x):
    total = coefficients[-1]
    for c in reversed(coefficients[:-1]):
        total = total * x + c
    return total


def turn(t):
    z = t - jnp.round(t)
    z2 = z * z
    s = horner(SIN_FIT, z2) * z
    c = horner(COS_FIT, z2)
    twice = s + s
    return 1.0 - twice * s, twice * c


def final_kernel(steps, wide, *refs):
    d_refs, refs = refs[:CHUNKS], refs[CHUNKS:]
    low_refs, high_refs = (), ()
    if wide:
        low_refs, high_refs, refs = refs[:CHUNKS], refs[CHUNKS : 2 * CHUNKS], refs[2 * CHUNKS :]
    g_ref, rate_ref, inv1_ref, inv2_ref, tw_ref = refs[:5]
    out_ref, zr_ref, zi_ref, x_ref, s_ref = refs[-5:]
    own = d_refs[0].shape[2]
    ext = x_ref.shape[1] // 3
    bins = rate_ref.shape[0]
    step = pl.program_id(0)

    @pl.when(step < steps)
    def _():
        def one(kk, buf):
            k = step * KB + kk

            def combine(sources, start, to):
                at = slice(start, start + STEP)
                values = [(ref[kk, 0, at, :], ref[kk, 1, at, :]) for ref in sources]
                for q, (a, b) in enumerate(dft_list(values, -1.0)):
                    for half, part in enumerate((a, b)):
                        hi, lo = split(part)
                        cols = slice(half * LANES, (half + 1) * LANES)
                        x_ref[buf * CHUNKS + q, to : to + STEP, cols] = hi
                        x_ref[buf * CHUNKS + q, ext + to : ext + to + STEP, cols] = lo
                        x_ref[buf * CHUNKS + q, 2 * ext + to : 2 * ext + to + STEP, cols] = hi

            for start in range(0, own, STEP):
                combine(d_refs, start, start)
            if wide:
                for start in range(0, HALO, STEP):
                    combine(low_refs, start, own + start)
                    combine(high_refs, start, own + HALO + start)
            for q in range(CHUNKS):
                k2 = k + PER_CHUNK * q
                moved = dot(g_ref[lax.div(k2, LANES // GROUPS)], x_ref[buf * CHUNKS + q])
                f = k2 * LANES + lax.broadcasted_iota(jnp.int32, (1, LANES), 1)
                centred = jnp.where(f >= NAZ // 2, f - NAZ, f).astype(F32) * (1.0 / NAZ)
                square = centred * centred
                block = min(bins, 32)
                for start in range(0, bins, block):
                    at = slice(start, start + block)
                    c, s = turn(rate_ref[at, :] * square)
                    a, b = moved[at, 0:LANES], moved[at, LANES : 2 * LANES]
                    to = pl.ds(pl.multiple_of(k2 * bins + start, block), block)
                    zr_ref[to, :] = a * c + b * s
                    zi_ref[to, :] = b * c - a * s

        def first(i, carry):
            one(2 * i, 0)
            one(2 * i + 1, 1)
            return carry

        lax.fori_loop(0, KB // 2, first, 0)

    @pl.when(step >= steps)
    def _():
        base = (step - steps) * BB

        def some(j, carry):
            cols = []
            for t in range(QUAD):
                at = pl.ds(base + QUAD * j + t, LANES, stride=bins)
                cols.append(jnp.concatenate([zr_ref[at, :], zi_ref[at, :]], axis=0))
            hi, lo = split(jnp.concatenate(cols, axis=1))
            w = dot(inv1_ref[...], jnp.concatenate([hi, lo, hi], axis=0))
            rows = []
            for t in range(QUAD):
                a = w[0:LANES, t * LANES : (t + 1) * LANES]
                b = w[LANES : 2 * LANES, t * LANES : (t + 1) * LANES]
                wr, wi = tw_ref[0], tw_ref[1]
                rows.append(jnp.concatenate([a * wr - b * wi, a * wi + b * wr], axis=1))
            hi, lo = split(jnp.concatenate(rows, axis=0))
            image = lax.dot_general(
                inv2_ref[...],
                jnp.concatenate([hi, lo, hi], axis=1),
                (((1,), (1,)), ((), ())),
                preferred_element_type=F32,
            )
            for t in range(QUAD):
                for ri in range(2):
                    s_ref[ri, pl.ds(QUAD * j + t, LANES, stride=BB), :] = image[
                        ri * LANES : (ri + 1) * LANES, t * LANES : (t + 1) * LANES
                    ]
            return carry

        lax.fori_loop(0, BB // QUAD, some, 0)
        for ri in range(2):
            for n in range(LANES):
                out_ref[ri, :, n * LANES : (n + 1) * LANES] = s_ref[ri, n * BB : (n + 1) * BB, :]


def final(bins, mains, lows, highs, mover, rate, places, image=None):
    own, rows = mains[0].shape[2], rate.shape[0]
    wide = len(lows) > 0
    ext = own + (2 * HALO if wide else 0)
    steps = PER_CHUNK // KB
    ids = np.arange(LANES)
    tw = jnp.asarray(np.stack(unit(ids[:, None] * ids[None, :], NAZ, 1.0)), F32)
    consts = [
        mover,
        rate,
        jnp.asarray(left_table(1.0)),
        jnp.asarray(left_table(1.0, 1.0 / NAZ)),
        tw,
    ]
    start, gap_at = places[0], len(places)
    for i, place in enumerate(places):
        if place != start + i:
            gap_at = i
            break
    gap = places[-1] - start - len(places) + 1

    def early(i):
        return (jnp.minimum(i, steps - 1), 0, 0, 0)

    def late(i):
        at = jnp.maximum(i - steps, 0)
        return (0, start + at + jnp.where(at >= gap_at, gap, 0), 0)

    points = NAZ * rows
    given = [*mains, *lows, *highs, *consts]
    specs = [pl.BlockSpec((KB, 2, own, LANES), early)] * CHUNKS
    specs += [pl.BlockSpec((KB, 2, HALO, LANES), early)] * (2 * CHUNKS if wide else 0)
    specs += [whole_spec(a) for a in consts]
    aliases = {}
    if image is not None:
        aliases = {len(given): 0}
        given.append(image)
        specs.append(pl.BlockSpec(memory_space=pl.ANY))
    return pl.pallas_call(
        functools.partial(final_kernel, steps, wide),
        grid=(steps + len(places),),
        in_specs=specs,
        out_specs=pl.BlockSpec((2, BB, NAZ), late),
        out_shape=jax.ShapeDtypeStruct((2, bins, NAZ), F32),
        scratch_shapes=[
            pltpu.VMEM((LANES * rows, LANES), F32),
            pltpu.VMEM((LANES * rows, LANES), F32),
            pltpu.VMEM((2 * CHUNKS, 3 * ext, 2 * LANES), BF16),
            pltpu.VMEM((2, LANES * BB, LANES), F32),
        ],
        input_output_aliases=aliases,
        compiler_params=pltpu.CompilerParams(vmem_limit_bytes=56 << 20),
        cost_estimate=pl.CostEstimate(
            flops=points * 8 * LANES * 9, bytes_accessed=28 * points, transcendentals=0
        ),
        name="final_wide" if wide else "final_inner",
    )(*given)


def mover_table(bins, rows, wide, shift_table, filter_index, tap_table):
    ext = bins + (2 * HALO if wide else 0)
    shift_table, filter_index = shift_table[:, rows], filter_index[:, rows]
    onehot = (filter_index[:, :, None] == jnp.arange(NFILT, dtype=jnp.int32)).astype(F32)
    weights = jnp.einsum("gbf,ft->gbt", onehot, tap_table, precision=lax.Precision.HIGHEST)
    first = rows[None, :].astype(np.int32) + shift_table + (HALO - 4)
    column = np.arange(3 * ext) % ext
    natural = np.where(
        column < bins, column + HALO, np.where(column < bins + HALO, column - bins, column)
    ).astype(np.int32)
    offset = natural[None, None, :] - first[:, :, None]
    table = jnp.zeros(offset.shape, F32)
    for t in range(TAPS):
        table = table + jnp.where(offset == t, weights[:, :, t : t + 1], 0.0)
    high = lax.reduce_precision(table, 8, 7)
    return jnp.where(np.arange(3 * ext) < 2 * ext, high, table - high).astype(BF16)


def neighbours(axes, size, step):
    return [(i, i + step) for i in range(size) if 0 <= i + step < size]


def local(nrng, naz, raw_echo, chirp_spectrum, azimuth_rate, shift_table, filter_index, tap_table):
    axes = ("rng", "az")
    devices = nrng * naz
    bins = NRG // devices
    rows_in = raw_echo.shape[1] // LANES
    per_part = PER_CHUNK // nrng
    rows = per_part * rows_in
    chirp = chirp_spectrum.reshape(2, LANES, RG1).transpose(0, 2, 1)
    rate = jnp.broadcast_to((azimuth_rate * 0.5)[:, None], (bins, LANES))
    rank = lax.axis_index("rng").astype(jnp.int32).reshape(1)
    packed = pack(raw_echo, rank, nrng, [0]) + pack(raw_echo, rank, nrng, list(range(1, CHUNKS)))
    mains, lows, highs = [], [], []

    def finish(lines, c):
        if bins < LANES:
            cut = lines.reshape(RG1, 2, rows, LANES // bins, bins)
            lines = cut.transpose(0, 3, 1, 2, 4).reshape(devices, 2, rows, bins)
        turned = lax.all_to_all(lines, axes, split_axis=0, concat_axis=0, tiled=True)
        turned = turned.reshape(nrng, naz, 2, per_part, rows_in, bins)
        main, up, down = azimuth(turned, c)
        mains.append(main)
        lows.append(lax.ppermute(up, axes, neighbours(axes, devices, 1)))
        highs.append(lax.ppermute(down, axes, neighbours(axes, devices, -1)))

    arrived = None
    for c in range(CHUNKS):
        sent = packed[c]
        if arrived is not None:
            sent, arrived = lax.optimization_barrier((sent, arrived))
            lines = compress(arrived, rank, chirp)
            if c >= 3:
                lines, mains[c - 3] = lax.optimization_barrier((lines, mains[c - 3]))
            finish(lines, c - 1)
        arrived = [sent[0]] + [
            lax.ppermute(sent[j], "rng", [(i, i ^ j) for i in range(nrng)]) for j in range(1, nrng)
        ]
    finish(compress(arrived, rank, chirp), CHUNKS - 1)
    tables = (shift_table, filter_index, tap_table)
    blocks = np.arange(bins // BB)
    inner = (blocks >= HALO // BB) & (blocks < (bins - HALO) // BB)
    image = None
    for chosen, wide in ((inner, False), (~inner, True)):
        places = blocks[chosen].tolist()
        if not places:
            continue
        ids = np.concatenate([np.arange(BB) + BB * place for place in places])
        mover = mover_table(bins, ids, wide, *tables)
        halos = (lows, highs) if wide else ([], [])
        image = final(bins, mains, *halos, mover, rate[ids], places, image)
    return image
def solution(mesh):
    return jax.shard_map(
        functools.partial(local, mesh.shape["rng"], mesh.shape["az"]),
        mesh=mesh,
        in_specs=(
            P(None, "az", "rng"),
            P(),
            P(("rng", "az")),
            P(None, ("rng", "az")),
            P(None, ("rng", "az")),
            P(),
        ),
        out_specs=P(None, ("rng", "az"), None),
        check_vma=False,
    )
```

time: 1440 us -> 819 us (0.57)
  waiting for transfers between devices: 630 us -> 325 us
  matrix products: 232 us -> 0.36 us
  Pallas kernels: 0 us -> 227 us
  blocking collectives: 187 us -> 0 us
  local copies, waits for them, and re-layouts: 267 us -> 112 us
  starting transfers between devices: 22.5 us -> 141 us
  other arithmetic: 97.5 us -> 6.35 us
    all_to_all x2 -> x8, waiting for transfers between devices: 544 us -> 122 us  [finish(): lax.all_to_all(lines, axes, split_axis=0, concat_axis=0, tiled=True)]
    dot_general x10 -> x2, matrix products: 232 us -> 0.36 us  [mover_table(): jnp.einsum('gbf,ft->gbt', onehot, tap_table, precision=lax.Precision.HIGH...]
    pallas_call x0 -> x20, Pallas kernels: none -> 227 us  [the longest x2 80.2 us: final(): pl.pallas_call(functools.partial(final_kernel, steps, wide), grid=(steps...]
    all_to_all x1 -> x0, blocking collectives: 187 us -> none  [local(): lax.all_to_all(compressed, 'rng', split_axis=1, concat_axis=2, tiled=True)]
    ppermute x2 -> x40, waiting for transfers between devices: 86 us -> 203 us  [the longest x24 178 us: local(): lax.ppermute(sent[j], 'rng', [(i, i ^ j) for i in range(nrng)])]
    all_to_all x6 -> x0, local copies, waits for them, and re-layouts: 107 us -> none  [the longest x3 50.6 us: local(): lax.all_to_all(compressed, 'rng', split_axis=1, concat_axis=2, tiled=True)]
    ppermute x2 -> x40, starting transfers between devices: 9.15 us -> 97.1 us  [the longest x8 37.3 us: finish(): lows.append(lax.ppermute(up, axes, neighbours(axes, devices, 1)))]
    reshape x5 -> x2, local copies, waits for them, and re-layouts: 75.2 us -> 1.72 us  [local(): chirp = chirp_spectrum.reshape(2, LANES, RG1).transpose(0, 2, 1)]
  transfers between devices with their start and end apart: 4 -> 48, of which waited for: 3 -> 26; matrix products, arithmetic and copies ran while one was open for 0% -> 2% of each run, Pallas kernels for 0% -> 21%
where the time goes in v1:
time: 819 us; the launch traced here: 814 us
  waiting for transfers between devices  325 us (40%)
  Pallas kernels  227 us (28%)
  starting transfers between devices  141 us (17%)
  local copies, waits for them, and re-layouts  112 us (14%)
    ppermute x24, waiting for transfers between devices, local(): lax.ppermute(sent[j], 'rng', [(i, i ^ j) for i in range(nrng)])  178 us
    all_to_all x8, waiting for transfers between devices, finish(): lax.all_to_all(lines, axes, split_axis=0, concat_axis=0, tiled=True)  122 us
    unnamed x304, local copies, waits for them, and re-layouts  105 us
    pallas_call x2, Pallas kernels, final(): pl.pallas_call(functools.partial(final_kernel, steps, wide), grid=(steps...  80.2 us
    pallas_call x8, Pallas kernels, compress(): pl.pallas_call(functools.partial(compress_kernel, parts, block), grid=(ro...  79.2 us
    pallas_call x8, Pallas kernels, azimuth(): pl.pallas_call(functools.partial(azimuth_kernel, chunk), grid=(parts,), i...  49.9 us
    all_to_all x8, starting transfers between devices, finish(): lax.all_to_all(lines, axes, split_axis=0, concat_axis=0, tiled=True)  44.3 us
    ppermute x8, starting transfers between devices, finish(): lows.append(lax.ppermute(up, axes, neighbours(axes, devices, 1)))  37.3 us
  transfers between devices with their start and end apart: 48, of which 26 were waited for; matrix products, arithmetic and copies ran while one was open for 2% of the time, Pallas kernels for 21%

profile of v1, /device:TPU:4, one launch (start us, length us, event | category | flops | bytes accessed | tf_op | source)
XLA Modules:
  0.0 814.1 jit_solution(5829223641913058687)
XLA Ops:
  14.5 12.9 %pack.2 = (f32[2,8,64,128]{3,2,1,0:T(8,128)S(1)}, f32[2,8,64,128]{3,2,1,0:T(8,128)S(1)}, f32[2,8,64,128]{3,2,1,0:T(8,128)S(1)}, f32[2,8,64,128]{3,2,1,0:T(8,128)...) custom-call(s32[1]{0:T(128)} %bitcast.rank_ref, ...), custom_call_target="tpu_custom_call" | custom-call | bytes 33554432 | tf_op jit(solution)/shard_map/pack/pallas_call | solution.py:136
  53.0 10.6 %compress.9 = f32[32,2,64,128]{3,2,1,0:T(8,128)S(1)} custom-call(s32[1]{0:T(128)} %bitcast.rank_ref, f32[2,8,64,128]{3,2,1,0:T(8,128)S(1)} %get-tuple-element.155.refs_0_, f32[2,8,64,128]{3,2,1,0:T(8,128)S(1)} %collective-permute-done.refs_1_, f32[2,8,64,128]{3,2,1,0:T(8,128)S(1)} %collective-permute-done.1.refs_2_, ...), custom_call_target="tpu_custom_call" | custom-call | flops 1610612736 | bytes 4194304 | tf_op jit(solution)/shard_map/compress/pallas_call | solution.py:275
  74.6 27.5 %collective-permute-done.3.refs_1_ = f32[2,8,64,128]{3,2,1,0:T(8,128)S(1)} collective-permute-done((f32[2,8,64,128]{3,2,1,0:T(8,128)}, f32[2,8,64,128]{3,2,1,0:T(8,128)S(1)}, u32[]{:S(2)}, u32[]{:S(2)}) %collective-permute-start.3) | collective-permute-done | bytes 524320 | tf_op jit(solution)/shard_map/ppermute | solution.py:617
  103.0 14.8 %collective-permute-done.5.refs_3_ = f32[2,8,64,128]{3,2,1,0:T(8,128)S(1)} collective-permute-done((f32[2,8,64,128]{3,2,1,0:T(8,128)}, f32[2,8,64,128]{3,2,1,0:T(8,128)S(1)}, u32[]{:S(2)}, u32[]{:S(2)}) %collective-permute-start.5) | collective-permute-done | bytes 524320 | tf_op jit(solution)/shard_map/ppermute | solution.py:617
  121.6 9.8 %compress.11 = f32[32,2,64,128]{3,2,1,0:T(8,128)S(1)} custom-call(s32[1]{0:T(128)} %bitcast.rank_ref, f32[2,8,64,128]{3,2,1,0:T(8,128)S(1)} %copy-done.82, f32[2,8,64,128]{3,2,1,0:T(8,128)S(1)} %collective-permute-done.3.refs_1_, f32[2,8,64,128]{3,2,1,0:T(8,128)S(1)} %collective-permute-done.4.refs_2_, f32[2,8,64,128]{3,2,1,0:T(8,128)S(1)} %collective-permute-done.5.refs_3_, ...), custom_call_target="tpu_custom_call" | custom-call | flops 1610612736 | bytes 4194304 | tf_op jit(solution)/shard_map/compress/pallas_call | solution.py:275
  143.8 27.4 %collective-permute-done.6.refs_1_ = f32[2,8,64,128]{3,2,1,0:T(8,128)S(1)} collective-permute-done((f32[2,8,64,128]{3,2,1,0:T(8,128)}, f32[2,8,64,128]{3,2,1,0:T(8,128)S(1)}, u32[]{:S(2)}, u32[]{:S(2)}) %collective-permute-start.6) | collective-permute-done | bytes 524320 | tf_op jit(solution)/shard_map/ppermute | solution.py:617
  172.9 14.0 %collective-permute-done.8.refs_3_ = f32[2,8,64,128]{3,2,1,0:T(8,128)S(1)} collective-permute-done((f32[2,8,64,128]{3,2,1,0:T(8,128)}, f32[2,8,64,128]{3,2,1,0:T(8,128)S(1)}, u32[]{:S(2)}, u32[]{:S(2)}) %collective-permute-start.8) | collective-permute-done | bytes 524320 | tf_op jit(solution)/shard_map/ppermute | solution.py:617
  191.1 11.6 %collective-permute-done.9.refs_1_ = f32[2,8,64,128]{3,2,1,0:T(8,128)S(1)} collective-permute-done((f32[2,8,64,128]{3,2,1,0:T(8,128)}, f32[2,8,64,128]{3,2,1,0:T(8,128)S(1)}, u32[]{:S(2)}, u32[]{:S(2)}) %collective-permute-start.9) | collective-permute-done | bytes 524320 | tf_op jit(solution)/shard_map/ppermute | solution.py:617
  203.5 8.4 %collective-permute-done.10.refs_2_ = f32[2,8,64,128]{3,2,1,0:T(8,128)S(1)} collective-permute-done((f32[2,8,64,128]{3,2,1,0:T(8,128)}, f32[2,8,64,128]{3,2,1,0:T(8,128)S(1)}, u32[]{:S(2)}, u32[]{:S(2)}) %collective-permute-start.10) | collective-permute-done | bytes 524320 | tf_op jit(solution)/shard_map/ppermute | solution.py:617
  217.5 11.6 %collective-permute-done.12.refs_1_ = f32[2,8,64,128]{3,2,1,0:T(8,128)S(1)} collective-permute-done((f32[2,8,64,128]{3,2,1,0:T(8,128)}, f32[2,8,64,128]{3,2,1,0:T(8,128)S(1)}, u32[]{:S(2)}, u32[]{:S(2)}) %collective-permute-start.12) | collective-permute-done | bytes 524320 | tf_op jit(solution)/shard_map/ppermute | solution.py:617
  229.9 8.6 %collective-permute-done.13.refs_2_ = f32[2,8,64,128]{3,2,1,0:T(8,128)S(1)} collective-permute-done((f32[2,8,64,128]{3,2,1,0:T(8,128)}, f32[2,8,64,128]{3,2,1,0:T(8,128)S(1)}, u32[]{:S(2)}, u32[]{:S(2)}) %collective-permute-start.13) | collective-permute-done | bytes 524320 | tf_op jit(solution)/shard_map/ppermute | solution.py:617
  243.7 11.3 %collective-permute-done.15.refs_1_ = f32[2,8,64,128]{3,2,1,0:T(8,128)S(1)} collective-permute-done((f32[2,8,64,128]{3,2,1,0:T(8,128)}, f32[2,8,64,128]{3,2,1,0:T(8,128)S(1)}, u32[]{:S(2)}, u32[]{:S(2)}) %collective-permute-start.15) | collective-permute-done | bytes 524320 | tf_op jit(solution)/shard_map/ppermute | solution.py:617
  268.6 11.1 %collective-permute-done.18.refs_1_ = f32[2,8,64,128]{3,2,1,0:T(8,128)S(1)} collective-permute-done((f32[2,8,64,128]{3,2,1,0:T(8,128)}, f32[2,8,64,128]{3,2,1,0:T(8,128)S(1)}, u32[]{:S(2)}, u32[]{:S(2)}) %collective-permute-start.18) | collective-permute-done | bytes 524320 | tf_op jit(solution)/shard_map/ppermute | solution.py:617
  292.0 10.2 %collective-permute-done.21.refs_1_ = f32[2,8,64,128]{3,2,1,0:T(8,128)S(1)} collective-permute-done((f32[2,8,64,128]{3,2,1,0:T(8,128)}, f32[2,8,64,128]{3,2,1,0:T(8,128)S(1)}, u32[]{:S(2)}, u32[]{:S(2)}) %collective-permute-start.21) | collective-permute-done | bytes 524320 | tf_op jit(solution)/shard_map/ppermute | solution.py:617
  312.3 9.8 %compress.15 = f32[32,2,64,128]{3,2,1,0:T(8,128)S(1)} custom-call(s32[1]{0:T(128)} %bitcast.rank_ref, f32[2,8,64,128]{3,2,1,0:T(8,128)S(1)} %copy-done.32, f32[2,8,64,128]{3,2,1,0:T(8,128)S(1)} %collective-permute-done.21.refs_1_, f32[2,8,64,128]{3,2,1,0:T(8,128)S(1)} %collective-permute-done.22.refs_2_, ...), custom_call_target="tpu_custom_call" | custom-call | flops 1610612736 | bytes 4194304 | tf_op jit(solution)/shard_map/compress/pallas_call | solution.py:275
  323.5 10.1 %all-to-all-start.7 = ((f32[32,2,64,128]{3,2,1,0:T(8,128)}), f32[32,2,64,128]{3,2,1,0:T(8,128)}, u32[]{:S(2)}, u32[]{:S(2)}) async-start(f32[32,2,64,128]{3,2,1,0:T(8,128)} %copy-done.20), calls=%async_computation.7 | async-start | bytes 4194304 | tf_op jit(solution)/shard_map/all_to_all | solution.py:600
  340.6 9.8 %compress.8 = f32[32,2,64,128]{3,2,1,0:T(8,128)S(1)} custom-call(s32[1]{0:T(128)} %bitcast.rank_ref, f32[2,8,64,128]{3,2,1,0:T(8,128)S(1)} %copy-done.30, f32[2,8,64,128]{3,2,1,0:T(8,128)S(1)} %copy-done.43, f32[2,8,64,128]{3,2,1,0:T(8,128)S(1)} %copy-done.45, f32[2,8,64,128]{3,2,1,0:T(8,128)S(1)} %copy-done.49, f32[2,32,128]{2,1,0:T(8,128)S(1)} %bitcast.44, ...), custom_call_target="tpu_custom_call" | custom-call | flops 1610612736 | bytes 4194304 | tf_op jit(solution)/shard_map/compress/pallas_call | solution.py:275
  357.7 24.9 %all-to-all-done.7 = f32[32,2,64,128]{3,2,1,0:T(8,128)} async-done(((f32[32,2,64,128]{3,2,1,0:T(8,128)}), f32[32,2,64,128]{3,2,1,0:T(8,128)}, u32[]{:S(2)}, u32[]{:S(2)}) %all-to-all-start.7) | async-done | bytes 2097184 | tf_op jit(solution)/shard_map/all_to_all | solution.py:600
  393.4 9.8 %compress.10 = f32[32,2,64,128]{3,2,1,0:T(8,128)S(1)} custom-call(s32[1]{0:T(128)} %bitcast.rank_ref, f32[2,8,64,128]{3,2,1,0:T(8,128)S(1)} %copy-done.24, f32[2,8,64,128]{3,2,1,0:T(8,128)S(1)} %copy-done.47, f32[2,8,64,128]{3,2,1,0:T(8,128)S(1)} %copy-done.51, f32[2,8,64,128]{3,2,1,0:T(8,128)S(1)} %copy-done.56, f32[2,32,128]{2,1,0:T(8,128)S(1)} %bitcast.45, ...), custom_call_target="tpu_custom_call" | custom-call | flops 1610612736 | bytes 4194304 | tf_op jit(solution)/shard_map/compress/pallas_call | solution.py:275
  412.1 23.3 %all-to-all-done.2 = f32[32,2,64,128]{3,2,1,0:T(8,128)S(1)} async-done(((f32[32,2,64,128]{3,2,1,0:T(8,128)}), f32[32,2,64,128]{3,2,1,0:T(8,128)S(1)}, u32[]{:S(2)}, u32[]{:S(2)}) %all-to-all-start.2) | async-done | bytes 2097184 | tf_op jit(solution)/shard_map/all_to_all | solution.py:600
  446.9 9.8 %compress.12 = f32[32,2,64,128]{3,2,1,0:T(8,128)S(1)} custom-call(s32[1]{0:T(128)} %bitcast.rank_ref, f32[2,8,64,128]{3,2,1,0:T(8,128)S(1)} %copy-done.22, f32[2,8,64,128]{3,2,1,0:T(8,128)S(1)} %copy-done.53, f32[2,8,64,128]{3,2,1,0:T(8,128)S(1)} %copy-done.60, f32[2,8,64,128]{3,2,1,0:T(8,128)S(1)} %copy-done.67, f32[2,32,128]{2,1,0:T(8,128)S(1)} %bitcast.46, ...), custom_call_target="tpu_custom_call" | custom-call | flops 1610612736 | bytes 4194304 | tf_op jit(solution)/shard_map/compress/pallas_call | solution.py:275
  464.8 24.2 %all-to-all-done.3 = f32[32,2,64,128]{3,2,1,0:T(8,128)} async-done(((f32[32,2,64,128]{3,2,1,0:T(8,128)}), f32[32,2,64,128]{3,2,1,0:T(8,128)}, u32[]{:S(2)}, u32[]{:S(2)}) %all-to-all-start.3) | async-done | bytes 2097184 | tf_op jit(solution)/shard_map/all_to_all | solution.py:600
  498.7 9.8 %compress.13 = f32[32,2,64,128]{3,2,1,0:T(8,128)S(1)} custom-call(s32[1]{0:T(128)} %bitcast.rank_ref, f32[2,8,64,128]{3,2,1,0:T(8,128)S(1)} %get-tuple-element.202.refs_0_, f32[2,8,64,128]{3,2,1,0:T(8,128)S(1)} %copy-done.63, f32[2,8,64,128]{3,2,1,0:T(8,128)S(1)} %copy-done.70, f32[2,8,64,128]{3,2,1,0:T(8,128)S(1)} %copy-done.74, ...), custom_call_target="tpu_custom_call" | custom-call | flops 1610612736 | bytes 4194304 | tf_op jit(solution)/shard_map/compress/pallas_call | solution.py:275
  517.3 24.6 %all-to-all-done.4 = f32[32,2,64,128]{3,2,1,0:T(8,128)S(1)} async-done(((f32[32,2,64,128]{3,2,1,0:T(8,128)}), f32[32,2,64,128]{3,2,1,0:T(8,128)S(1)}, u32[]{:S(2)}, u32[]{:S(2)}) %all-to-all-start.4) | async-done | bytes 2097184 | tf_op jit(solution)/shard_map/all_to_all | solution.py:600
  552.9 9.8 %compress.14 = f32[32,2,64,128]{3,2,1,0:T(8,128)S(1)} custom-call(s32[1]{0:T(128)} %bitcast.rank_ref, f32[2,8,64,128]{3,2,1,0:T(8,128)S(1)} %get-tuple-element.217.refs_0_, f32[2,8,64,128]{3,2,1,0:T(8,128)S(1)} %copy-done.58, f32[2,8,64,128]{3,2,1,0:T(8,128)S(1)} %copy-done.65, f32[2,8,64,128]{3,2,1,0:T(8,128)S(1)} %copy-done.72, ...), custom_call_target="tpu_custom_call" | custom-call | flops 1610612736 | bytes 4194304 | tf_op jit(solution)/shard_map/compress/pallas_call | solution.py:275
  570.9 25.1 %all-to-all-done.5 = f32[32,2,64,128]{3,2,1,0:T(8,128)S(1)} async-done(((f32[32,2,64,128]{3,2,1,0:T(8,128)}), f32[32,2,64,128]{3,2,1,0:T(8,128)S(1)}, u32[]{:S(2)}, u32[]{:S(2)}) %all-to-all-start.5) | async-done | bytes 2097184 | tf_op jit(solution)/shard_map/all_to_all | solution.py:600
  635.3 15.3 %collective-permute-done.24.refs_8_ = f32[16,2,32,128]{3,2,1,0:T(8,128)S(1)} collective-permute-done((f32[16,2,32,128]{3,2,1,0:T(8,128)}, f32[16,2,32,128]{3,2,1,0:T(8,128)S(1)}, u32[]{:S(2)}, u32[]{:S(2)}) %collective-permute-start.24) | collective-permute-done | bytes 524320 | tf_op jit(solution)/shard_map/ppermute | solution.py:604
  675.0 9.8 %collective-permute-start.28 = (f32[16,2,32,128]{3,2,1,0:T(8,128)}, f32[16,2,32,128]{3,2,1,0:T(8,128)}, u32[]{:S(2)}, u32[]{:S(2)}) collective-permute-start(f32[16,2,32,128]{3,2,1,0:T(8,128)} %get-tuple-element.237), channel_id=1, source_target_pairs={{0,1},{1,2},{2,3},{3,4},{4,5},{5,6},{6,7},{7,8},{8,9},{9,10},{10,1... | collective-permute-start | bytes 1572872 | tf_op jit(solution)/shard_map/ppermute | solution.py:604
  710.2 8.0 collective-permute-start.29
  720.2 9.3 %collective-permute-start.30 = (f32[16,2,32,128]{3,2,1,0:T(8,128)S(1)}, f32[16,2,32,128]{3,2,1,0:T(8,128)S(1)}, u32[]{:S(2)}, u32[]{:S(2)}) collective-permute-start(f32[16,2,32,128]{3,2,1,0:T(8,128)S(1)} %get-tuple-element.239), channel_id=1, source_target_pairs={{0,1},{1,2},{2,3},{3,4},{4,5},{5,6},{6,7},{7,8},{8,9},{9,10},{10,1... | collective-permute-start | bytes 1572872 | tf_op jit(solution)/shard_map/ppermute | solution.py:604
  731.7 37.1 %final_inner.1.refs_29_ = f32[2,128,16384]{2,1,0:T(8,128)} custom-call(f32[16,2,128,128]{3,2,1,0:T(8,128)} %copy-done.3, f32[16,2,128,128]{3,2,1,0:T(8,128)} %copy-done.4, f32[16,2,128,128]{3,2,1,0:T(8,128)} %copy-done.5, f32[16,2,128,128]{3,2,1,0:T(8,128)} %copy-done.6, f32[16,2,128,128]{3,2,1,0:T(8,128)} %copy-done.7, f32[16,2,128,128]{3,2,1,0:T(8,128)} %copy-done.9, ...), custom_call_target="tpu_custom_call" | custom-call | flops 9663676416 | bytes 29360128 | tf_op jit(solution)/shard_map/final_inner/pallas_call | solution.py:540
  770.8 43.1 %final_wide.1 = f32[2,128,16384]{2,1,0:T(8,128)} custom-call(f32[16,2,128,128]{3,2,1,0:T(8,128)} %copy-done.3, f32[16,2,128,128]{3,2,1,0:T(8,128)} %copy-done.4, f32[16,2,128,128]{3,2,1,0:T(8,128)} %copy-done.5, f32[16,2,128,128]{3,2,1,0:T(8,128)} %copy-done.6, f32[16,2,128,128]{3,2,1,0:T(8,128)} %copy-done.7, ...), custom_call_target="tpu_custom_call", output_to_operand_aliasing={{}: (29, {})} | custom-call | flops 9663676416 | bytes 29360128 | tf_op jit(solution)/shard_map/final_wide/pallas_call | solution.py:540
  (412 shorter events, 309.6 us)
Async XLA Ops:
  11.0 39.2 %collective-permute-start = (f32[2,8,64,128]{3,2,1,0:T(8,128)}, f32[2,8,64,128]{3,2,1,0:T(8,128)S(1)}, u32[]{:S(2)}, u32[]{:S(2)}) collective-permute-start(f32[2,8,64,128]{3,2,1,0:T(8,128)} %get-tuple-element.140), channel_id=1, source_target_pairs={{0,8},{8,0},{16,24},{24,16},{1,9},{9,1},{17,25},{25,17},{2,10},{10... | collective-permute-start | bytes 1572872 | tf_op jit(solution)/shard_map/ppermute | solution.py:617
  12.5 37.7 %collective-permute-start.1 = (f32[2,8,64,128]{3,2,1,0:T(8,128)}, f32[2,8,64,128]{3,2,1,0:T(8,128)S(1)}, u32[]{:S(2)}, u32[]{:S(2)}) collective-permute-start(f32[2,8,64,128]{3,2,1,0:T(8,128)} %get-tuple-element.141), channel_id=1, source_target_pairs={{0,16},{8,24},{16,0},{24,8},{1,17},{9,25},{17,1},{25,9},{2,18},{10... | collective-permute-start | bytes 1572872 | tf_op jit(solution)/shard_map/ppermute | solution.py:617
  13.0 37.2 %collective-permute-start.2 = (f32[2,8,64,128]{3,2,1,0:T(8,128)S(1)}, f32[2,8,64,128]{3,2,1,0:T(8,128)}, u32[]{:S(2)}, u32[]{:S(2)}) collective-permute-start(f32[2,8,64,128]{3,2,1,0:T(8,128)S(1)} %get-tuple-element.142), channel_id=1, source_target_pairs={{0,24},{8,16},{16,8},{24,0},{1,25},{9,17},{17,9},{25,1},{2,26},{10... | collective-permute-start | bytes 1572872 | tf_op jit(solution)/shard_map/ppermute | solution.py:617
  65.0 67.8 %all-to-all-start = ((f32[32,2,64,128]{3,2,1,0:T(8,128)}), f32[32,2,64,128]{3,2,1,0:T(8,128)S(1)}, u32[]{:S(2)}, u32[]{:S(2)}) async-start(f32[32,2,64,128]{3,2,1,0:T(8,128)} %copy-done.15), calls=%async_computation | async-start | bytes 4194304 | tf_op jit(solution)/shard_map/all_to_all | solution.py:600
  71.1 31.0 %collective-permute-start.3 = (f32[2,8,64,128]{3,2,1,0:T(8,128)}, f32[2,8,64,128]{3,2,1,0:T(8,128)S(1)}, u32[]{:S(2)}, u32[]{:S(2)}) collective-permute-start(f32[2,8,64,128]{3,2,1,0:T(8,128)} %copy-done.89), channel_id=1, source_target_pairs={{0,8},{8,0},{16,24},{24,16},{1,9},{9,1},{17,25},{25,17},{2,10},{10... | collective-permute-start | bytes 1572872 | tf_op jit(solution)/shard_map/ppermute | solution.py:617
  72.6 30.4 %collective-permute-start.4 = (f32[2,8,64,128]{3,2,1,0:T(8,128)}, f32[2,8,64,128]{3,2,1,0:T(8,128)S(1)}, u32[]{:S(2)}, u32[]{:S(2)}) collective-permute-start(f32[2,8,64,128]{3,2,1,0:T(8,128)} %copy-done.86), channel_id=1, source_target_pairs={{0,16},{8,24},{16,0},{24,8},{1,17},{9,25},{17,1},{25,9},{2,18},{10... | collective-permute-start | bytes 1572872 | tf_op jit(solution)/shard_map/ppermute | solution.py:617
  73.2 44.6 %collective-permute-start.5 = (f32[2,8,64,128]{3,2,1,0:T(8,128)}, f32[2,8,64,128]{3,2,1,0:T(8,128)S(1)}, u32[]{:S(2)}, u32[]{:S(2)}) collective-permute-start(f32[2,8,64,128]{3,2,1,0:T(8,128)} %copy-done.83), channel_id=1, source_target_pairs={{0,24},{8,16},{16,8},{24,0},{1,25},{9,17},{17,9},{25,1},{2,26},{10... | collective-permute-start | bytes 1572872 | tf_op jit(solution)/shard_map/ppermute | solution.py:617
  132.7 190.8 %all-to-all-start.1 = ((f32[32,2,64,128]{3,2,1,0:T(8,128)}), f32[32,2,64,128]{3,2,1,0:T(8,128)}, u32[]{:S(2)}, u32[]{:S(2)}) async-start(f32[32,2,64,128]{3,2,1,0:T(8,128)} %copy-done.12), calls=%async_computation.1 | async-start | bytes 4194304 | tf_op jit(solution)/shard_map/all_to_all | solution.py:600
  140.2 31.0 %collective-permute-start.6 = (f32[2,8,64,128]{3,2,1,0:T(8,128)}, f32[2,8,64,128]{3,2,1,0:T(8,128)S(1)}, u32[]{:S(2)}, u32[]{:S(2)}) collective-permute-start(f32[2,8,64,128]{3,2,1,0:T(8,128)} %copy-done.80), channel_id=1, source_target_pairs={{0,8},{8,0},{16,24},{24,16},{1,9},{9,1},{17,25},{25,17},{2,10},{10... | collective-permute-start | bytes 1572872 | tf_op jit(solution)/shard_map/ppermute | solution.py:617
  141.7 30.4 %collective-permute-start.7 = (f32[2,8,64,128]{3,2,1,0:T(8,128)}, f32[2,8,64,128]{3,2,1,0:T(8,128)S(1)}, u32[]{:S(2)}, u32[]{:S(2)}) collective-permute-start(f32[2,8,64,128]{3,2,1,0:T(8,128)} %copy-done.79), channel_id=1, source_target_pairs={{0,16},{8,24},{16,0},{24,8},{1,17},{9,25},{17,1},{25,9},{2,18},{10... | collective-permute-start | bytes 1572872 | tf_op jit(solution)/shard_map/ppermute | solution.py:617
  142.3 44.5 %collective-permute-start.8 = (f32[2,8,64,128]{3,2,1,0:T(8,128)}, f32[2,8,64,128]{3,2,1,0:T(8,128)S(1)}, u32[]{:S(2)}, u32[]{:S(2)}) collective-permute-start(f32[2,8,64,128]{3,2,1,0:T(8,128)} %copy-done.78), channel_id=1, source_target_pairs={{0,24},{8,16},{16,8},{24,0},{1,25},{9,17},{17,9},{25,1},{2,26},{10... | collective-permute-start | bytes 1572872 | tf_op jit(solution)/shard_map/ppermute | solution.py:617
  323.5 59.1 %all-to-all-start.7 = ((f32[32,2,64,128]{3,2,1,0:T(8,128)}), f32[32,2,64,128]{3,2,1,0:T(8,128)}, u32[]{:S(2)}, u32[]{:S(2)}) async-start(f32[32,2,64,128]{3,2,1,0:T(8,128)} %copy-done.20), calls=%async_computation.7 | async-start | bytes 4194304 | tf_op jit(solution)/shard_map/all_to_all | solution.py:600
  382.6 52.8 %all-to-all-start.2 = ((f32[32,2,64,128]{3,2,1,0:T(8,128)}), f32[32,2,64,128]{3,2,1,0:T(8,128)S(1)}, u32[]{:S(2)}, u32[]{:S(2)}) async-start(f32[32,2,64,128]{3,2,1,0:T(8,128)} %copy-done.17), calls=%async_computation.2 | async-start | bytes 4194304 | tf_op jit(solution)/shard_map/all_to_all | solution.py:600
  435.4 53.6 %all-to-all-start.3 = ((f32[32,2,64,128]{3,2,1,0:T(8,128)}), f32[32,2,64,128]{3,2,1,0:T(8,128)}, u32[]{:S(2)}, u32[]{:S(2)}) async-start(f32[32,2,64,128]{3,2,1,0:T(8,128)} %copy-done.18), calls=%async_computation.3 | async-start | bytes 4194304 | tf_op jit(solution)/shard_map/all_to_all | solution.py:600
  489.0 52.8 %all-to-all-start.4 = ((f32[32,2,64,128]{3,2,1,0:T(8,128)}), f32[32,2,64,128]{3,2,1,0:T(8,128)S(1)}, u32[]{:S(2)}, u32[]{:S(2)}) async-start(f32[32,2,64,128]{3,2,1,0:T(8,128)} %copy-done.19), calls=%async_computation.4 | async-start | bytes 4194304 | tf_op jit(solution)/shard_map/all_to_all | solution.py:600
  543.2 52.8 %all-to-all-start.5 = ((f32[32,2,64,128]{3,2,1,0:T(8,128)}), f32[32,2,64,128]{3,2,1,0:T(8,128)S(1)}, u32[]{:S(2)}, u32[]{:S(2)}) async-start(f32[32,2,64,128]{3,2,1,0:T(8,128)} %copy-done.16), calls=%async_computation.5 | async-start | bytes 4194304 | tf_op jit(solution)/shard_map/all_to_all | solution.py:600
  596.0 99.5 %all-to-all-start.6 = ((f32[32,2,64,128]{3,2,1,0:T(8,128)}), f32[32,2,64,128]{3,2,1,0:T(8,128)}, u32[]{:S(2)}, u32[]{:S(2)}) async-start(f32[32,2,64,128]{3,2,1,0:T(8,128)} %copy-done.11), calls=%async_computation.6 | async-start | bytes 4194304 | tf_op jit(solution)/shard_map/all_to_all | solution.py:600
  606.3 44.2 %collective-permute-start.24 = (f32[16,2,32,128]{3,2,1,0:T(8,128)}, f32[16,2,32,128]{3,2,1,0:T(8,128)S(1)}, u32[]{:S(2)}, u32[]{:S(2)}) collective-permute-start(f32[16,2,32,128]{3,2,1,0:T(8,128)} %get-tuple-element.233), channel_id=1, source_target_pairs={{0,1},{1,2},{2,3},{3,4},{4,5},{5,6},{6,7},{7,8},{8,9},{9,10},{10,1... | collective-permute-start | bytes 1572872 | tf_op jit(solution)/shard_map/ppermute | solution.py:604
  608.6 47.4 %collective-permute-start.32 = (f32[16,2,32,128]{3,2,1,0:T(8,128)}, f32[16,2,32,128]{3,2,1,0:T(8,128)S(1)}, u32[]{:S(2)}, u32[]{:S(2)}) collective-permute-start(f32[16,2,32,128]{3,2,1,0:T(8,128)} %get-tuple-element.241), channel_id=1, source_target_pairs={{1,0},{2,1},{3,2},{4,3},{5,4},{6,5},{7,6},{8,7},{9,8},{10,9},{11,1... | collective-permute-start | bytes 1572872 | tf_op jit(solution)/shard_map/ppermute | solution.py:605
  615.7 46.1 %collective-permute-start.25 = (f32[16,2,32,128]{3,2,1,0:T(8,128)}, f32[16,2,32,128]{3,2,1,0:T(8,128)S(1)}, u32[]{:S(2)}, u32[]{:S(2)}) collective-permute-start(f32[16,2,32,128]{3,2,1,0:T(8,128)} %get-tuple-element.234), channel_id=1, source_target_pairs={{0,1},{1,2},{2,3},{3,4},{4,5},{5,6},{6,7},{7,8},{8,9},{9,10},{10,1... | collective-permute-start | bytes 1572872 | tf_op jit(solution)/shard_map/ppermute | solution.py:604
  617.6 47.6 %collective-permute-start.33 = (f32[16,2,32,128]{3,2,1,0:T(8,128)}, f32[16,2,32,128]{3,2,1,0:T(8,128)S(1)}, u32[]{:S(2)}, u32[]{:S(2)}) collective-permute-start(f32[16,2,32,128]{3,2,1,0:T(8,128)} %get-tuple-element.242), channel_id=1, source_target_pairs={{1,0},{2,1},{3,2},{4,3},{5,4},{6,5},{7,6},{8,7},{9,8},{10,9},{11,1... | collective-permute-start | bytes 1572872 | tf_op jit(solution)/shard_map/ppermute | solution.py:605
  633.3 39.7 %collective-permute-start.31 = (f32[16,2,32,128]{3,2,1,0:T(8,128)S(1)}, f32[16,2,32,128]{3,2,1,0:T(8,128)S(1)}, u32[]{:S(2)}, u32[]{:S(2)}) collective-permute-start(f32[16,2,32,128]{3,2,1,0:T(8,128)S(1)} %get-tuple-element.240), channel_id=1, source_target_pairs={{0,1},{1,2},{2,3},{3,4},{4,5},{5,6},{6,7},{7,8},{8,9},{9,10},{10,1... | collective-permute-start | bytes 1572872 | tf_op jit(solution)/shard_map/ppermute | solution.py:604
  656.0 48.0 %collective-permute-start.26 = (f32[16,2,32,128]{3,2,1,0:T(8,128)}, f32[16,2,32,128]{3,2,1,0:T(8,128)}, u32[]{:S(2)}, u32[]{:S(2)}) collective-permute-start(f32[16,2,32,128]{3,2,1,0:T(8,128)} %get-tuple-element.235), channel_id=1, source_target_pairs={{0,1},{1,2},{2,3},{3,4},{4,5},{5,6},{6,7},{7,8},{8,9},{9,10},{10,1... | collective-permute-start | bytes 1572872 | tf_op jit(solution)/shard_map/ppermute | solution.py:604
  661.8 48.4 %collective-permute-start.34 = (f32[16,2,32,128]{3,2,1,0:T(8,128)S(1)}, f32[16,2,32,128]{3,2,1,0:T(8,128)}, u32[]{:S(2)}, u32[]{:S(2)}) collective-permute-start(f32[16,2,32,128]{3,2,1,0:T(8,128)S(1)} %copy-done.26), channel_id=1, source_target_pairs={{1,0},{2,1},{3,2},{4,3},{5,4},{6,5},{7,6},{8,7},{9,8},{10,9},{11,1... | collective-permute-start | bytes 1572872 | tf_op jit(solution)/shard_map/ppermute | solution.py:605
  665.2 53.1 %collective-permute-start.27 = (f32[16,2,32,128]{3,2,1,0:T(8,128)}, f32[16,2,32,128]{3,2,1,0:T(8,128)}, u32[]{:S(2)}, u32[]{:S(2)}) collective-permute-start(f32[16,2,32,128]{3,2,1,0:T(8,128)} %get-tuple-element.236), channel_id=1, source_target_pairs={{0,1},{1,2},{2,3},{3,4},{4,5},{5,6},{6,7},{7,8},{8,9},{9,10},{10,1... | collective-permute-start | bytes 1572872 | tf_op jit(solution)/shard_map/ppermute | solution.py:604
  673.0 47.2 %collective-permute-start.35 = (f32[16,2,32,128]{3,2,1,0:T(8,128)S(1)}, f32[16,2,32,128]{3,2,1,0:T(8,128)}, u32[]{:S(2)}, u32[]{:S(2)}) collective-permute-start(f32[16,2,32,128]{3,2,1,0:T(8,128)S(1)} %get-tuple-element.244), channel_id=1, source_target_pairs={{1,0},{2,1},{3,2},{4,3},{5,4},{6,5},{7,6},{8,7},{9,8},{10,9},{11,1... | collective-permute-start | bytes 1572872 | tf_op jit(solution)/shard_map/ppermute | solution.py:605
  675.0 54.5 %collective-permute-start.28 = (f32[16,2,32,128]{3,2,1,0:T(8,128)}, f32[16,2,32,128]{3,2,1,0:T(8,128)}, u32[]{:S(2)}, u32[]{:S(2)}) collective-permute-start(f32[16,2,32,128]{3,2,1,0:T(8,128)} %get-tuple-element.237), channel_id=1, source_target_pairs={{0,1},{1,2},{2,3},{3,4},{4,5},{5,6},{6,7},{7,8},{8,9},{9,10},{10,1... | collective-permute-start | bytes 1572872 | tf_op jit(solution)/shard_map/ppermute | solution.py:604
  704.0 64.7 %collective-permute-start.36 = (f32[16,2,32,128]{3,2,1,0:T(8,128)S(1)}, f32[16,2,32,128]{3,2,1,0:T(8,128)S(1)}, u32[]{:S(2)}, u32[]{:S(2)}) collective-permute-start(f32[16,2,32,128]{3,2,1,0:T(8,128)S(1)} %copy-done.28), channel_id=1, source_target_pairs={{1,0},{2,1},{3,2},{4,3},{5,4},{6,5},{7,6},{8,7},{9,8},{10,9},{11,1... | collective-permute-start | bytes 1572872 | tf_op jit(solution)/shard_map/ppermute | solution.py:605
  710.2 58.5 %collective-permute-start.29 = (f32[16,2,32,128]{3,2,1,0:T(8,128)S(1)}, f32[16,2,32,128]{3,2,1,0:T(8,128)S(1)}, u32[]{:S(2)}, u32[]{:S(2)}) collective-permute-start(f32[16,2,32,128]{3,2,1,0:T(8,128)S(1)} %copy-done.88), channel_id=1, source_target_pairs={{0,1},{1,2},{2,3},{3,4},{4,5},{5,6},{6,7},{7,8},{8,9},{9,10},{10,1... | collective-permute-start | bytes 1572872 | tf_op jit(solution)/shard_map/ppermute | solution.py:604
  718.3 50.5 %collective-permute-start.37 = (f32[16,2,32,128]{3,2,1,0:T(8,128)S(1)}, f32[16,2,32,128]{3,2,1,0:T(8,128)S(1)}, u32[]{:S(2)}, u32[]{:S(2)}) collective-permute-start(f32[16,2,32,128]{3,2,1,0:T(8,128)S(1)} %copy-done.85), channel_id=1, source_target_pairs={{1,0},{2,1},{3,2},{4,3},{5,4},{6,5},{7,6},{8,7},{9,8},{10,9},{11,1... | collective-permute-start | bytes 1572872 | tf_op jit(solution)/shard_map/ppermute | solution.py:605
  720.2 48.5 %collective-permute-start.30 = (f32[16,2,32,128]{3,2,1,0:T(8,128)S(1)}, f32[16,2,32,128]{3,2,1,0:T(8,128)S(1)}, u32[]{:S(2)}, u32[]{:S(2)}) collective-permute-start(f32[16,2,32,128]{3,2,1,0:T(8,128)S(1)} %get-tuple-element.239), channel_id=1, source_target_pairs={{0,1},{1,2},{2,3},{3,4},{4,5},{5,6},{6,7},{7,8},{8,9},{9,10},{10,1... | collective-permute-start | bytes 1572872 | tf_op jit(solution)/shard_map/ppermute | solution.py:604
  729.5 39.3 %collective-permute-start.38 = (f32[16,2,32,128]{3,2,1,0:T(8,128)S(1)}, f32[16,2,32,128]{3,2,1,0:T(8,128)S(1)}, u32[]{:S(2)}, u32[]{:S(2)}) collective-permute-start(f32[16,2,32,128]{3,2,1,0:T(8,128)S(1)} %get-tuple-element.247), channel_id=1, source_target_pairs={{1,0},{2,1},{3,2},{4,3},{5,4},{6,5},{7,6},{8,7},{9,8},{10,9},{11,1... | collective-permute-start | bytes 1572872 | tf_op jit(solution)/shard_map/ppermute | solution.py:605
  (167 other events, 2027.1 us)

commit v2 on v1

--- a/solution.py
+++ b/solution.py
@@ -19,6 +19,7 @@
 RG1 = NRG // LANES
 CHUNKS = 8
 PER_CHUNK = LANES // CHUNKS
+VMEM_LIMIT = 60 << 20
 BF16 = jnp.bfloat16
 F32 = jnp.float32
 
@@ -142,7 +143,7 @@
         ],
         out_specs=[spec] * count,
         out_shape=[shape] * count,
-        compiler_params=pltpu.CompilerParams(vmem_limit_bytes=32 << 20),
+        compiler_params=pltpu.CompilerParams(vmem_limit_bytes=VMEM_LIMIT),
         cost_estimate=pl.CostEstimate(flops=0, bytes_accessed=16 * lines * bins, transcendentals=0),
         name="pack",
     )(rank, raw)
@@ -287,7 +288,7 @@
             pltpu.VMEM((RG1, 2, STEP, LANES), F32),
             pltpu.SemaphoreType.DMA((2, parts)),
         ],
-        compiler_params=pltpu.CompilerParams(vmem_limit_bytes=40 << 20),
+        compiler_params=pltpu.CompilerParams(vmem_limit_bytes=VMEM_LIMIT),
         cost_estimate=pl.CostEstimate(
             flops=points * 8 * LANES * 6, bytes_accessed=16 * points, transcendentals=0
         ),
@@ -366,7 +367,7 @@
         out_specs=[pl.BlockSpec(s, lambda i: (0, 0, 0, 0)) for s in (shape, edge, edge)],
         out_shape=[jax.ShapeDtypeStruct(s, F32) for s in (shape, edge, edge)],
         scratch_shapes=[pltpu.VMEM(shape, F32), pltpu.VMEM((PER_CHUNK, 2, STEP, LANES), F32)],
-        compiler_params=pltpu.CompilerParams(vmem_limit_bytes=32 << 20),
+        compiler_params=pltpu.CompilerParams(vmem_limit_bytes=VMEM_LIMIT),
         cost_estimate=pl.CostEstimate(
             flops=points * 8 * LANES * 3, bytes_accessed=16 * points, transcendentals=0
         ),
@@ -414,7 +415,7 @@
     g_ref, rate_ref, inv1_ref, inv2_ref, tw_ref = refs[:5]
     out_ref, zr_ref, zi_ref, x_ref, s_ref = refs[-5:]
     own = d_refs[0].shape[2]
-    ext = x_ref.shape[1] // 3
+    ext = x_ref.shape[1] // 2
     bins = rate_ref.shape[0]
     step = pl.program_id(0)
 
@@ -432,7 +433,6 @@
                         cols = slice(half * LANES, (half + 1) * LANES)
                         x_ref[buf * CHUNKS + q, to : to + STEP, cols] = hi
                         x_ref[buf * CHUNKS + q, ext + to : ext + to + STEP, cols] = lo
-                        x_ref[buf * CHUNKS + q, 2 * ext + to : 2 * ext + to + STEP, cols] = hi
 
             for start in range(0, own, STEP):
                 combine(d_refs, start, start)
@@ -450,7 +450,8 @@
                 for start in range(0, bins, block):
                     at = slice(start, start + block)
                     c, s = turn(rate_ref[at, :] * square)
-                    a, b = moved[at, 0:LANES], moved[at, LANES : 2 * LANES]
+                    both = moved[at, :] + moved[bins + start : bins + start + block, :]
+                    a, b = both[:, 0:LANES], both[:, LANES : 2 * LANES]
                     to = pl.ds(pl.multiple_of(k2 * bins + start, block), block)
                     zr_ref[to, :] = a * c + b * s
                     zi_ref[to, :] = b * c - a * s
@@ -546,11 +547,11 @@
         scratch_shapes=[
             pltpu.VMEM((LANES * rows, LANES), F32),
             pltpu.VMEM((LANES * rows, LANES), F32),
-            pltpu.VMEM((2 * CHUNKS, 3 * ext, 2 * LANES), BF16),
+            pltpu.VMEM((2 * CHUNKS, 2 * ext, 2 * LANES), BF16),
             pltpu.VMEM((2, LANES * BB, LANES), F32),
         ],
         input_output_aliases=aliases,
-        compiler_params=pltpu.CompilerParams(vmem_limit_bytes=56 << 20),
+        compiler_params=pltpu.CompilerParams(vmem_limit_bytes=VMEM_LIMIT),
         cost_estimate=pl.CostEstimate(
             flops=points * 8 * LANES * 9, bytes_accessed=28 * points, transcendentals=0
         ),
@@ -564,7 +565,7 @@
     onehot = (filter_index[:, :, None] == jnp.arange(NFILT, dtype=jnp.int32)).astype(F32)
     weights = jnp.einsum("gbf,ft->gbt", onehot, tap_table, precision=lax.Precision.HIGHEST)
     first = rows[None, :].astype(np.int32) + shift_table + (HALO - 4)
-    column = np.arange(3 * ext) % ext
+    column = np.arange(ext)
     natural = np.where(
         column < bins, column + HALO, np.where(column < bins + HALO, column - bins, column)
     ).astype(np.int32)
@@ -573,7 +574,10 @@
     for t in range(TAPS):
         table = table + jnp.where(offset == t, weights[:, :, t : t + 1], 0.0)
     high = lax.reduce_precision(table, 8, 7)
-    return jnp.where(np.arange(3 * ext) < 2 * ext, high, table - high).astype(BF16)
+    low = table - high
+    top = jnp.concatenate([high, high], axis=2)
+    bottom = jnp.concatenate([low, jnp.zeros_like(low)], axis=2)
+    return jnp.concatenate([top, bottom], axis=1).astype(BF16)
 
 
 def neighbours(axes, size, step):
@@ -592,31 +596,47 @@
     rank = lax.axis_index("rng").astype(jnp.int32).reshape(1)
     packed = pack(raw_echo, rank, nrng, [0]) + pack(raw_echo, rank, nrng, list(range(1, CHUNKS)))
     mains, lows, highs = [], [], []
-
-    def finish(lines, c):
+    turned = []
+
+    def gather(c):
+        return [packed[c][0]] + [
+            lax.ppermute(packed[c][j], "rng", [(i, i ^ j) for i in range(nrng)])
+            for j in range(1, nrng)
+        ]
+
+    def transform(c):
+        if c > 0:
+            turned[c], mains[c - 1] = lax.optimization_barrier((turned[c], mains[c - 1]))
+        main, up, down = azimuth(turned[c], c)
+        mains.append(main)
+        lows.append(lax.ppermute(up, axes, neighbours(axes, devices, 1)))
+        highs.append(lax.ppermute(down, axes, neighbours(axes, devices, -1)))
+
+    got = [gather(0)]
+    packed[1], got[0] = lax.optimization_barrier((packed[1], got[0]))
+    got.append(gather(1))
+    for c in range(CHUNKS):
+        lines = compress(got[c], rank, chirp)
+        if c + 2 < CHUNKS:
+            packed[c + 2], lines = lax.optimization_barrier((packed[c + 2], lines))
+            packed[c + 2], got[c + 1] = lax.optimization_barrier((packed[c + 2], got[c + 1]))
+            if c >= 1:
+                held = (packed[c + 2], turned[c - 1])
+                packed[c + 2], turned[c - 1] = lax.optimization_barrier(held)
+            got.append(gather(c + 2))
+        if c >= 2:
+            transform(c - 2)
+            lines, mains[c - 2] = lax.optimization_barrier((lines, mains[c - 2]))
+        if c >= 3:
+            held = (lines, lows[c - 3], highs[c - 3])
+            lines, lows[c - 3], highs[c - 3] = lax.optimization_barrier(held)
         if bins < LANES:
             cut = lines.reshape(RG1, 2, rows, LANES // bins, bins)
             lines = cut.transpose(0, 3, 1, 2, 4).reshape(devices, 2, rows, bins)
-        turned = lax.all_to_all(lines, axes, split_axis=0, concat_axis=0, tiled=True)
-        turned = turned.reshape(nrng, naz, 2, per_part, rows_in, bins)
-        main, up, down = azimuth(turned, c)
-        mains.append(main)
-        lows.append(lax.ppermute(up, axes, neighbours(axes, devices, 1)))
-        highs.append(lax.ppermute(down, axes, neighbours(axes, devices, -1)))
-
-    arrived = None
-    for c in range(CHUNKS):
-        sent = packed[c]
-        if arrived is not None:
-            sent, arrived = lax.optimization_barrier((sent, arrived))
-            lines = compress(arrived, rank, chirp)
-            if c >= 3:
-                lines, mains[c - 3] = lax.optimization_barrier((lines, mains[c - 3]))
-            finish(lines, c - 1)
-        arrived = [sent[0]] + [
-            lax.ppermute(sent[j], "rng", [(i, i ^ j) for i in range(nrng)]) for j in range(1, nrng)
-        ]
-    finish(compress(arrived, rank, chirp), CHUNKS - 1)
+        moved = lax.all_to_all(lines, axes, split_axis=0, concat_axis=0, tiled=True)
+        turned.append(moved.reshape(nrng, naz, 2, per_part, rows_in, bins))
+    transform(CHUNKS - 2)
+    transform(CHUNKS - 1)
     tables = (shift_table, filter_index, tap_table)
     blocks = np.arange(bins // BB)
     inner = (blocks >= HALO // BB) & (blocks < (bins - HALO) // BB)

time: 819 us -> 762 us (0.930)
  local copies, waits for them, and re-layouts: 112 us -> 22.4 us
  Pallas kernels: 227 us -> 269 us
  waiting for transfers between devices: 325 us -> 303 us
  starting transfers between devices: 141 us -> 158 us
    all_to_all x8, waiting for transfers between devices: 122 us -> 21 us  [local(): moved = lax.all_to_all(lines, axes, split_axis=0, concat_axis=0, tiled=True)]
    unnamed x304 -> x96, local copies, waits for them, and re-layouts: 105 us -> 16.4 us
    ppermute x40, waiting for transfers between devices: 203 us -> 282 us  [the longest x24 282 us: gather(): lax.ppermute(packed[c][j], 'rng', [(i, i ^ j) for i in range(nrng)])]
    pallas_call x8, Pallas kernels: 79.2 us -> 103 us  [compress(): pl.pallas_call(functools.partial(compress_kernel, parts, block), grid=(ro...]
    pallas_call x8, Pallas kernels: 49.9 us -> 63.4 us  [azimuth(): pl.pallas_call(functools.partial(azimuth_kernel, chunk), grid=(parts,), i...]
    all_to_all x8, starting transfers between devices: 44.3 us -> 56.1 us  [local(): moved = lax.all_to_all(lines, axes, split_axis=0, concat_axis=0, tiled=True)]
  transfers between devices with their start and end apart: 48 -> 48, of which waited for: 26 -> 23; matrix products, arithmetic and copies ran while one was open for 2% -> 2% of each run, Pallas kernels for 21% -> 27%
where the time goes in v2:
time: 762 us; the launch traced here: 760 us
  waiting for transfers between devices  303 us (40%)
  Pallas kernels  269 us (35%)
  starting transfers between devices  158 us (21%)
  local copies, waits for them, and re-layouts  22.4 us (3%)
    ppermute x24, waiting for transfers between devices, gather(): lax.ppermute(packed[c][j], 'rng', [(i, i ^ j) for i in range(nrng)])  282 us
    pallas_call x8, Pallas kernels, compress(): pl.pallas_call(functools.partial(compress_kernel, parts, block), grid=(ro...  103 us
    pallas_call x2, Pallas kernels, final(): pl.pallas_call(functools.partial(final_kernel, steps, wide), grid=(steps...  77.5 us
    pallas_call x8, Pallas kernels, azimuth(): pl.pallas_call(functools.partial(azimuth_kernel, chunk), grid=(parts,), i...  63.4 us
    ppermute x8, starting transfers between devices, transform(): highs.append(lax.ppermute(down, axes, neighbours(axes, devices, -1)))  57.9 us
    all_to_all x8, starting transfers between devices, local(): moved = lax.all_to_all(lines, axes, split_axis=0, concat_axis=0, tiled=True)  56.1 us
    ppermute x24, starting transfers between devices, gather(): lax.ppermute(packed[c][j], 'rng', [(i, i ^ j) for i in range(nrng)])  28.4 us
    pallas_call x2, Pallas kernels, pack(): pl.pallas_call(functools.partial(pack_kernel, chunks, parts, per_part, ro...  24.9 us
  transfers between devices with their start and end apart: 48, of which 23 were waited for; matrix products, arithmetic and copies ran while one was open for 2% of the time, Pallas kernels for 27%

profile of v2, /device:TPU:4, one launch (start us, length us, event | category | flops | bytes accessed | tf_op | source)
XLA Modules:
  0.0 759.7 jit_solution(10875286065925598534)
XLA Ops:
  0.0 9.3 %pack.3 = (f32[2,8,64,128]{3,2,1,0:T(8,128)}, f32[2,8,64,128]{3,2,1,0:T(8,128)}, f32[2,8,64,128]{3,2,1,0:T(8,128)}, f32[2,8,64,128]{3,2,1,0:T(8,128)}) custom-call(s32[1]{0:T(128)} %bitcast.rank_ref, f32[2,2048,1024]{2,1,0:T(8,128)} %x_ref.3), custom_call_target="tpu_custom_call" | custom-call | bytes 33554432 | tf_op jit(solution)/shard_map/pack/pallas_call | solution.py:137
  12.8 15.6 %pack.2 = (f32[2,8,64,128]{3,2,1,0:T(8,128)}, f32[2,8,64,128]{3,2,1,0:T(8,128)}, f32[2,8,64,128]{3,2,1,0:T(8,128)}, f32[2,8,64,128]{3,2,1,0:T(8,128)}, f32[2,8,6...) custom-call(s32[1]{0:T(128)} %bitcast.rank_ref, ...), custom_call_target="tpu_custom_call" | custom-call | bytes 33554432 | tf_op jit(solution)/shard_map/pack/pallas_call | solution.py:137
  36.6 12.8 %compress.8 = f32[32,2,64,128]{3,2,1,0:T(8,128)} custom-call(s32[1]{0:T(128)} %bitcast.rank_ref, f32[2,8,64,128]{3,2,1,0:T(8,128)} %get-tuple-element.233.refs_0_, f32[2,8,64,128]{3,2,1,0:T(8,128)} %copy-done.34, f32[2,8,64,128]{3,2,1,0:T(8,128)} %copy-done.35, f32[2,8,64,128]{3,2,1,0:T(8,128)} %copy-done.36, f32[2,32,128]{2,1,0:T(8,128)} %bitcast.61, ...), custom_call_target="tpu_custom_call" | custom-call | flops 1610612736 | bytes 4194304 | tf_op jit(solution)/shard_map/compress/pallas_call | solution.py:276
  58.2 27.5 %collective-permute-done.3.refs_1_ = f32[2,8,64,128]{3,2,1,0:T(8,128)S(1)} collective-permute-done((f32[2,8,64,128]{3,2,1,0:T(8,128)}, f32[2,8,64,128]{3,2,1,0:T(8,128)S(1)}, u32[]{:S(2)}, u32[]{:S(2)}) %collective-permute-start.3) | collective-permute-done | bytes 524320 | tf_op jit(solution)/shard_map/ppermute | solution.py:603
  87.4 14.1 %collective-permute-done.5.refs_3_ = f32[2,8,64,128]{3,2,1,0:T(8,128)} collective-permute-done((f32[2,8,64,128]{3,2,1,0:T(8,128)S(1)}, f32[2,8,64,128]{3,2,1,0:T(8,128)}, u32[]{:S(2)}, u32[]{:S(2)}) %collective-permute-start.5) | collective-permute-done | bytes 524320 | tf_op jit(solution)/shard_map/ppermute | solution.py:603
  101.5 12.9 %compress.9 = f32[32,2,64,128]{3,2,1,0:T(8,128)} custom-call(s32[1]{0:T(128)} %bitcast.rank_ref, f32[2,8,64,128]{3,2,1,0:T(8,128)} %get-tuple-element.245.refs_0_, f32[2,8,64,128]{3,2,1,0:T(8,128)} %copy-done.42, f32[2,8,64,128]{3,2,1,0:T(8,128)} %copy-done.44, f32[2,8,64,128]{3,2,1,0:T(8,128)} %collective-permute-done.5.refs_3_, f32[2,32,128]{2,1,0:T(8,128)} %bitcast.62, ...), custom_call_target="tpu_custom_call" | custom-call | flops 1610612736 | bytes 4194304 | tf_op jit(solution)/shard_map/compress/pallas_call | solution.py:276
  126.7 27.5 %collective-permute-done.6.refs_1_ = f32[2,8,64,128]{3,2,1,0:T(8,128)S(1)} collective-permute-done((f32[2,8,64,128]{3,2,1,0:T(8,128)}, f32[2,8,64,128]{3,2,1,0:T(8,128)S(1)}, u32[]{:S(2)}, u32[]{:S(2)}) %collective-permute-start.6) | collective-permute-done | bytes 524320 | tf_op jit(solution)/shard_map/ppermute | solution.py:603
  155.8 14.1 %collective-permute-done.8.refs_3_ = f32[2,8,64,128]{3,2,1,0:T(8,128)} collective-permute-done((f32[2,8,64,128]{3,2,1,0:T(8,128)S(1)}, f32[2,8,64,128]{3,2,1,0:T(8,128)}, u32[]{:S(2)}, u32[]{:S(2)}) %collective-permute-start.8) | collective-permute-done | bytes 524320 | tf_op jit(solution)/shard_map/ppermute | solution.py:603
  169.9 12.9 %compress.10 = f32[32,2,64,128]{3,2,1,0:T(8,128)} custom-call(s32[1]{0:T(128)} %bitcast.rank_ref, f32[2,8,64,128]{3,2,1,0:T(8,128)} %get-tuple-element.257.refs_0_, f32[2,8,64,128]{3,2,1,0:T(8,128)} %copy-done.43, f32[2,8,64,128]{3,2,1,0:T(8,128)} %copy-done.45, f32[2,8,64,128]{3,2,1,0:T(8,128)} %collective-permute-done.8.refs_3_, f32[2,32,128]{2,1,0:T(8,128)} %bitcast.63, ...), custom_call_target="tpu_custom_call" | custom-call | flops 1610612736 | bytes 4194304 | tf_op jit(solution)/shard_map/compress/pallas_call | solution.py:276
  212.0 18.3 %collective-permute-done.9.refs_1_ = f32[2,8,64,128]{3,2,1,0:T(8,128)S(1)} collective-permute-done((f32[2,8,64,128]{3,2,1,0:T(8,128)}, f32[2,8,64,128]{3,2,1,0:T(8,128)S(1)}, u32[]{:S(2)}, u32[]{:S(2)}) %collective-permute-start.9) | collective-permute-done | bytes 524320 | tf_op jit(solution)/shard_map/ppermute | solution.py:603
  231.3 20.5 %collective-permute-done.11.refs_3_ = f32[2,8,64,128]{3,2,1,0:T(8,128)} collective-permute-done((f32[2,8,64,128]{3,2,1,0:T(8,128)}, f32[2,8,64,128]{3,2,1,0:T(8,128)}, u32[]{:S(2)}, u32[]{:S(2)}) %collective-permute-start.11) | collective-permute-done | bytes 524320 | tf_op jit(solution)/shard_map/ppermute | solution.py:603
  251.9 12.9 %compress.11 = f32[32,2,64,128]{3,2,1,0:T(8,128)} custom-call(s32[1]{0:T(128)} %bitcast.rank_ref, f32[2,8,64,128]{3,2,1,0:T(8,128)} %get-tuple-element.289.refs_0_, f32[2,8,64,128]{3,2,1,0:T(8,128)} %copy-done.37, f32[2,8,64,128]{3,2,1,0:T(8,128)} %collective-permute-done.10.refs_2_, f32[2,8,64,128]{3,2,1,0:T(8,128)} %collective-permute-done.11.refs_3_, ...), custom_call_target="tpu_custom_call" | custom-call | flops 1610612736 | bytes 4194304 | tf_op jit(solution)/shard_map/compress/pallas_call | solution.py:276
  264.8 7.9 %azimuth1.1 = (f32[16,2,128,128]{3,2,1,0:T(8,128)}, f32[16,2,32,128]{3,2,1,0:T(8,128)}, f32[16,2,32,128]{3,2,1,0:T(8,128)}) custom-call(f32[4,8,2,4,16,128]{5,4,3,2,1,0:T(8,128)} %bitcast.40, f32[2,128,128]{2,1,0:T(8,128)} %constant.29.clone.tw_ref, bf16[256,256]{1,0:T(8,128)(2,1)} %constant.30.clone.fwd_ref, bf16[256,256]{1,0:T(8,128)(2,1)} %constant.26.clone.refs_7_.fwd_low_ref), custom_call_target="tpu_custom_call" | custom-call | flops 805306368 | bytes 4194304 | tf_op jit(solution)/shard_map/azimuth1/pallas_call | solution.py:358
  294.0 18.4 %collective-permute-done.12.refs_1_ = f32[2,8,64,128]{3,2,1,0:T(8,128)} collective-permute-done((f32[2,8,64,128]{3,2,1,0:T(8,128)}, f32[2,8,64,128]{3,2,1,0:T(8,128)}, u32[]{:S(2)}, u32[]{:S(2)}) %collective-permute-start.12) | collective-permute-done | bytes 524320 | tf_op jit(solution)/shard_map/ppermute | solution.py:603
  313.4 20.5 %collective-permute-done.14.refs_3_ = f32[2,8,64,128]{3,2,1,0:T(8,128)} collective-permute-done((f32[2,8,64,128]{3,2,1,0:T(8,128)}, f32[2,8,64,128]{3,2,1,0:T(8,128)}, u32[]{:S(2)}, u32[]{:S(2)}) %collective-permute-start.14) | collective-permute-done | bytes 524320 | tf_op jit(solution)/shard_map/ppermute | solution.py:603
  333.9 12.9 %compress.12 = f32[32,2,64,128]{3,2,1,0:T(8,128)} custom-call(s32[1]{0:T(128)} %bitcast.rank_ref, f32[2,8,64,128]{3,2,1,0:T(8,128)} %get-tuple-element.316.refs_0_, f32[2,8,64,128]{3,2,1,0:T(8,128)} %collective-permute-done.12.refs_1_, f32[2,8,64,128]{3,2,1,0:T(8,128)} %collective-permute-done.13.refs_2_, f32[2,8,64,128]{3,2,1,0:T(8,128)} %collective-permute-done.14.refs_3_, ...), custom_call_target="tpu_custom_call" | custom-call | flops 1610612736 | bytes 4194304 | tf_op jit(solution)/shard_map/compress/pallas_call | solution.py:276
  346.8 7.9 %azimuth2.1 = (f32[16,2,128,128]{3,2,1,0:T(8,128)}, f32[16,2,32,128]{3,2,1,0:T(8,128)}, f32[16,2,32,128]{3,2,1,0:T(8,128)}) custom-call(f32[4,8,2,4,16,128]{5,4,3,2,1,0:T(8,128)} %bitcast.39, f32[2,128,128]{2,1,0:T(8,128)} %constant.29.clone.tw_ref, bf16[256,256]{1,0:T(8,128)(2,1)} %constant.30.clone.fwd_ref, bf16[256,256]{1,0:T(8,128)(2,1)} %constant.26.clone.refs_7_.fwd_low_ref), custom_call_target="tpu_custom_call" | custom-call | flops 805306368 | bytes 4194304 | tf_op jit(solution)/shard_map/azimuth2/pallas_call | solution.py:358
  376.8 18.3 %collective-permute-done.15.refs_1_ = f32[2,8,64,128]{3,2,1,0:T(8,128)S(1)} collective-permute-done((f32[2,8,64,128]{3,2,1,0:T(8,128)}, f32[2,8,64,128]{3,2,1,0:T(8,128)S(1)}, u32[]{:S(2)}, u32[]{:S(2)}) %collective-permute-start.15) | collective-permute-done | bytes 524320 | tf_op jit(solution)/shard_map/ppermute | solution.py:603
  396.1 20.5 %collective-permute-done.17.refs_3_ = f32[2,8,64,128]{3,2,1,0:T(8,128)S(1)} collective-permute-done((f32[2,8,64,128]{3,2,1,0:T(8,128)}, f32[2,8,64,128]{3,2,1,0:T(8,128)S(1)}, u32[]{:S(2)}, u32[]{:S(2)}) %collective-permute-start.17) | collective-permute-done | bytes 524320 | tf_op jit(solution)/shard_map/ppermute | solution.py:603
  417.4 12.9 %compress.13 = f32[32,2,64,128]{3,2,1,0:T(8,128)} custom-call(s32[1]{0:T(128)} %bitcast.rank_ref, f32[2,8,64,128]{3,2,1,0:T(8,128)} %get-tuple-element.346.refs_0_, f32[2,8,64,128]{3,2,1,0:T(8,128)} %copy-done.38, f32[2,8,64,128]{3,2,1,0:T(8,128)} %copy-done.40, f32[2,8,64,128]{3,2,1,0:T(8,128)} %copy-done.41, f32[2,32,128]{2,1,0:T(8,128)} %bitcast.66, ...), custom_call_target="tpu_custom_call" | custom-call | flops 1610612736 | bytes 4194304 | tf_op jit(solution)/shard_map/compress/pallas_call | solution.py:276
  430.3 8.0 %azimuth3.1 = (f32[16,2,128,128]{3,2,1,0:T(8,128)}, f32[16,2,32,128]{3,2,1,0:T(8,128)}, f32[16,2,32,128]{3,2,1,0:T(8,128)}) custom-call(f32[4,8,2,4,16,128]{5,4,3,2,1,0:T(8,128)} %bitcast.38, f32[2,128,128]{2,1,0:T(8,128)} %constant.29.clone.tw_ref, bf16[256,256]{1,0:T(8,128)(2,1)} %constant.30.clone.fwd_ref, bf16[256,256]{1,0:T(8,128)(2,1)} %constant.26.clone.refs_7_.fwd_low_ref), custom_call_target="tpu_custom_call" | custom-call | flops 805306368 | bytes 4194304 | tf_op jit(solution)/shard_map/azimuth3/pallas_call | solution.py:358
  459.5 18.1 %collective-permute-done.20.refs_1_ = f32[2,8,64,128]{3,2,1,0:T(8,128)S(1)} collective-permute-done((f32[2,8,64,128]{3,2,1,0:T(8,128)}, f32[2,8,64,128]{3,2,1,0:T(8,128)S(1)}, u32[]{:S(2)}, u32[]{:S(2)}) %collective-permute-start.20) | collective-permute-done | bytes 524320 | tf_op jit(solution)/shard_map/ppermute | solution.py:603
  478.7 20.5 %collective-permute-done.22.refs_3_ = f32[2,8,64,128]{3,2,1,0:T(8,128)} collective-permute-done((f32[2,8,64,128]{3,2,1,0:T(8,128)}, f32[2,8,64,128]{3,2,1,0:T(8,128)}, u32[]{:S(2)}, u32[]{:S(2)}) %collective-permute-start.22) | collective-permute-done | bytes 524320 | tf_op jit(solution)/shard_map/ppermute | solution.py:603
  499.2 12.9 %compress.14 = f32[32,2,64,128]{3,2,1,0:T(8,128)} custom-call(s32[1]{0:T(128)} %bitcast.rank_ref, f32[2,8,64,128]{3,2,1,0:T(8,128)} %get-tuple-element.376.refs_0_, f32[2,8,64,128]{3,2,1,0:T(8,128)} %copy-done.39, f32[2,8,64,128]{3,2,1,0:T(8,128)} %collective-permute-done.21.refs_2_, f32[2,8,64,128]{3,2,1,0:T(8,128)} %collective-permute-done.22.refs_3_, ...), custom_call_target="tpu_custom_call" | custom-call | flops 1610612736 | bytes 4194304 | tf_op jit(solution)/shard_map/compress/pallas_call | solution.py:276
  541.3 8.1 %azimuth5.1 = (f32[16,2,128,128]{3,2,1,0:T(8,128)}, f32[16,2,32,128]{3,2,1,0:T(8,128)}, f32[16,2,32,128]{3,2,1,0:T(8,128)}) custom-call(f32[4,8,2,4,16,128]{5,4,3,2,1,0:T(8,128)} %bitcast.41, f32[2,128,128]{2,1,0:T(8,128)} %constant.29.clone.tw_ref, bf16[256,256]{1,0:T(8,128)(2,1)} %constant.30.clone.fwd_ref, bf16[256,256]{1,0:T(8,128)(2,1)} %constant.26.clone.refs_7_.fwd_low_ref), custom_call_target="tpu_custom_call" | custom-call | flops 805306368 | bytes 4194304 | tf_op jit(solution)/shard_map/azimuth5/pallas_call | solution.py:358
  549.4 10.4 %collective-permute-done.29.refs_1_ = f32[2,8,64,128]{3,2,1,0:T(8,128)} collective-permute-done((f32[2,8,64,128]{3,2,1,0:T(8,128)}, f32[2,8,64,128]{3,2,1,0:T(8,128)}, u32[]{:S(2)}, u32[]{:S(2)}) %collective-permute-start.29) | collective-permute-done | bytes 524320 | tf_op jit(solution)/shard_map/ppermute | solution.py:603
  560.7 20.5 %collective-permute-done.31.refs_3_ = f32[2,8,64,128]{3,2,1,0:T(8,128)} collective-permute-done((f32[2,8,64,128]{3,2,1,0:T(8,128)}, f32[2,8,64,128]{3,2,1,0:T(8,128)}, u32[]{:S(2)}, u32[]{:S(2)}) %collective-permute-start.31) | collective-permute-done | bytes 524320 | tf_op jit(solution)/shard_map/ppermute | solution.py:603
  581.2 12.9 %compress.15 = f32[32,2,64,128]{3,2,1,0:T(8,128)} custom-call(s32[1]{0:T(128)} %bitcast.rank_ref, f32[2,8,64,128]{3,2,1,0:T(8,128)} %get-tuple-element.388.refs_0_, f32[2,8,64,128]{3,2,1,0:T(8,128)} %collective-permute-done.29.refs_1_, f32[2,8,64,128]{3,2,1,0:T(8,128)} %collective-permute-done.30.refs_2_, f32[2,8,64,128]{3,2,1,0:T(8,128)} %collective-permute-done.31.refs_3_, ...), custom_call_target="tpu_custom_call" | custom-call | flops 1610612736 | bytes 4194304 | tf_op jit(solution)/shard_map/compress/pallas_call | solution.py:276
  641.8 21.0 %all-to-all-done.7 = f32[32,2,64,128]{3,2,1,0:T(8,128)} async-done(((f32[32,2,64,128]{3,2,1,0:T(8,128)}), f32[32,2,64,128]{3,2,1,0:T(8,128)}, u32[]{:S(2)}, u32[]{:S(2)}) %all-to-all-start.7) | async-done | bytes 2097184 | tf_op jit(solution)/shard_map/all_to_all | solution.py:636
  662.8 8.0 %azimuth7.1 = (f32[16,2,128,128]{3,2,1,0:T(8,128)}, f32[16,2,32,128]{3,2,1,0:T(8,128)}, f32[16,2,32,128]{3,2,1,0:T(8,128)}) custom-call(f32[4,8,2,4,16,128]{5,4,3,2,1,0:T(8,128)} %bitcast.9.x_ref, f32[2,128,128]{2,1,0:T(8,128)} %constant.29.clone.tw_ref, bf16[256,256]{1,0:T(8,128)(2,1)} %constant.30.clone.fwd_ref, ...), custom_call_target="tpu_custom_call" | custom-call | flops 805306368 | bytes 4194304 | tf_op jit(solution)/shard_map/azimuth7/pallas_call | solution.py:358
  679.9 36.1 %final_inner.1.refs_29_ = f32[2,128,16384]{2,1,0:T(8,128)} custom-call(f32[16,2,128,128]{3,2,1,0:T(8,128)} %get-tuple-element.284.refs_0_, f32[16,2,128,128]{3,2,1,0:T(8,128)} %get-tuple-element.311.refs_1_, f32[16,2,128,128]{3,2,1,0:T(8,128)} %get-tuple-element.341.refs_2_, f32[16,2,128,128]{3,2,1,0:T(8,128)} %get-tuple-element.371.refs_3_, ...), custom_call_target="tpu_custom_call" | custom-call | flops 9663676416 | bytes 29360128 | tf_op jit(solution)/shard_map/final_inner/pallas_call | solution.py:541
  718.2 41.4 %final_wide.1 = f32[2,128,16384]{2,1,0:T(8,128)} custom-call(f32[16,2,128,128]{3,2,1,0:T(8,128)} %get-tuple-element.284.refs_0_, f32[16,2,128,128]{3,2,1,0:T(8,128)} %get-tuple-element.311.refs_1_, f32[16,2,128,128]{3,2,1,0:T(8,128)} %get-tuple-element.341.refs_2_, f32[16,2,128,128]{3,2,1,0:T(8,128)} %get-tuple-element.371.refs_3_, ...), custom_call_target="tpu_custom_call", output_to_operand_aliasing={{}: (29, {})} | custom-call | flops 9663676416 | bytes 29360128 | tf_op jit(solution)/shard_map/final_wide/pallas_call | solution.py:541
  (206 shorter events, 223.4 us)
Async XLA Ops:
  49.5 64.9 %all-to-all-start = ((f32[32,2,64,128]{3,2,1,0:T(8,128)}), f32[32,2,64,128]{3,2,1,0:T(8,128)S(1)}, u32[]{:S(2)}, u32[]{:S(2)}) async-start(f32[32,2,64,128]{3,2,1,0:T(8,128)} %compress.8), calls=%async_computation | async-start | bytes 4194304 | tf_op jit(solution)/shard_map/all_to_all | solution.py:636
  56.8 44.7 %collective-permute-start.5 = (f32[2,8,64,128]{3,2,1,0:T(8,128)S(1)}, f32[2,8,64,128]{3,2,1,0:T(8,128)}, u32[]{:S(2)}, u32[]{:S(2)}) collective-permute-start(f32[2,8,64,128]{3,2,1,0:T(8,128)S(1)} %copy-done.32), channel_id=1, source_target_pairs={{0,24},{8,16},{16,8},{24,0},{1,25},{9,17},{17,9},{25,1},{2,26},{10... | collective-permute-start | bytes 1572872 | tf_op jit(solution)/shard_map/ppermute | solution.py:603
  115.7 74.8 %all-to-all-start.1 = ((f32[32,2,64,128]{3,2,1,0:T(8,128)}), f32[32,2,64,128]{3,2,1,0:T(8,128)S(1)}, u32[]{:S(2)}, u32[]{:S(2)}) async-start(f32[32,2,64,128]{3,2,1,0:T(8,128)} %compress.9), calls=%async_computation.1 | async-start | bytes 4194304 | tf_op jit(solution)/shard_map/all_to_all | solution.py:636
  125.2 44.7 %collective-permute-start.8 = (f32[2,8,64,128]{3,2,1,0:T(8,128)S(1)}, f32[2,8,64,128]{3,2,1,0:T(8,128)}, u32[]{:S(2)}, u32[]{:S(2)}) collective-permute-start(f32[2,8,64,128]{3,2,1,0:T(8,128)S(1)} %copy-done.30), channel_id=1, source_target_pairs={{0,24},{8,16},{16,8},{24,0},{1,25},{9,17},{17,9},{25,1},{2,26},{10... | collective-permute-start | bytes 1572872 | tf_op jit(solution)/shard_map/ppermute | solution.py:603
  191.8 80.9 %all-to-all-start.2 = ((f32[32,2,64,128]{3,2,1,0:T(8,128)}), f32[32,2,64,128]{3,2,1,0:T(8,128)S(1)}, u32[]{:S(2)}, u32[]{:S(2)}) async-start(f32[32,2,64,128]{3,2,1,0:T(8,128)} %compress.10), calls=%async_computation.2 | async-start | bytes 4194304 | tf_op jit(solution)/shard_map/all_to_all | solution.py:636
  201.3 50.5 %collective-permute-start.11 = (f32[2,8,64,128]{3,2,1,0:T(8,128)}, f32[2,8,64,128]{3,2,1,0:T(8,128)}, u32[]{:S(2)}, u32[]{:S(2)}) collective-permute-start(f32[2,8,64,128]{3,2,1,0:T(8,128)} %get-tuple-element.273), channel_id=1, source_target_pairs={{0,24},{8,16},{16,8},{24,0},{1,25},{9,17},{17,9},{25,1},{2,26},{10... | collective-permute-start | bytes 1572872 | tf_op jit(solution)/shard_map/ppermute | solution.py:603
  202.8 69.9 %collective-permute-start.18 = (f32[16,2,32,128]{3,2,1,0:T(8,128)}, f32[16,2,32,128]{3,2,1,0:T(8,128)S(1)}, u32[]{:S(2)}, u32[]{:S(2)}) collective-permute-start(f32[16,2,32,128]{3,2,1,0:T(8,128)} %get-tuple-element.333), channel_id=1, source_target_pairs={{0,1},{1,2},{2,3},{3,4},{4,5},{5,6},{6,7},{7,8},{8,9},{9,10},{10,1... | collective-permute-start | bytes 1572872 | tf_op jit(solution)/shard_map/ppermute | solution.py:612
  204.7 68.0 %collective-permute-start.19 = (f32[16,2,32,128]{3,2,1,0:T(8,128)}, f32[16,2,32,128]{3,2,1,0:T(8,128)S(1)}, u32[]{:S(2)}, u32[]{:S(2)}) collective-permute-start(f32[16,2,32,128]{3,2,1,0:T(8,128)} %get-tuple-element.334), channel_id=1, source_target_pairs={{1,0},{2,1},{3,2},{4,3},{5,4},{6,5},{7,6},{8,7},{9,8},{10,9},{11,1... | collective-permute-start | bytes 1572872 | tf_op jit(solution)/shard_map/ppermute | solution.py:613
  274.1 81.5 %all-to-all-start.3 = ((f32[32,2,64,128]{3,2,1,0:T(8,128)}), f32[32,2,64,128]{3,2,1,0:T(8,128)S(1)}, u32[]{:S(2)}, u32[]{:S(2)}) async-start(f32[32,2,64,128]{3,2,1,0:T(8,128)} %compress.11), calls=%async_computation.3 | async-start | bytes 4194304 | tf_op jit(solution)/shard_map/all_to_all | solution.py:636
  283.4 50.5 %collective-permute-start.14 = (f32[2,8,64,128]{3,2,1,0:T(8,128)}, f32[2,8,64,128]{3,2,1,0:T(8,128)}, u32[]{:S(2)}, u32[]{:S(2)}) collective-permute-start(f32[2,8,64,128]{3,2,1,0:T(8,128)} %get-tuple-element.300), channel_id=1, source_target_pairs={{0,24},{8,16},{16,8},{24,0},{1,25},{9,17},{17,9},{25,1},{2,26},{10... | collective-permute-start | bytes 1572872 | tf_op jit(solution)/shard_map/ppermute | solution.py:603
  284.8 69.9 %collective-permute-start.23 = (f32[16,2,32,128]{3,2,1,0:T(8,128)}, f32[16,2,32,128]{3,2,1,0:T(8,128)S(1)}, u32[]{:S(2)}, u32[]{:S(2)}) collective-permute-start(f32[16,2,32,128]{3,2,1,0:T(8,128)} %get-tuple-element.363), channel_id=1, source_target_pairs={{0,1},{1,2},{2,3},{3,4},{4,5},{5,6},{6,7},{7,8},{8,9},{9,10},{10,1... | collective-permute-start | bytes 1572872 | tf_op jit(solution)/shard_map/ppermute | solution.py:612
  286.7 68.8 %collective-permute-start.24 = (f32[16,2,32,128]{3,2,1,0:T(8,128)}, f32[16,2,32,128]{3,2,1,0:T(8,128)}, u32[]{:S(2)}, u32[]{:S(2)}) collective-permute-start(f32[16,2,32,128]{3,2,1,0:T(8,128)} %get-tuple-element.364), channel_id=1, source_target_pairs={{1,0},{2,1},{3,2},{4,3},{5,4},{6,5},{7,6},{8,7},{9,8},{10,9},{11,1... | collective-permute-start | bytes 1572872 | tf_op jit(solution)/shard_map/ppermute | solution.py:613
  356.9 81.4 %all-to-all-start.4 = ((f32[32,2,64,128]{3,2,1,0:T(8,128)}), f32[32,2,64,128]{3,2,1,0:T(8,128)}, u32[]{:S(2)}, u32[]{:S(2)}) async-start(f32[32,2,64,128]{3,2,1,0:T(8,128)} %compress.12), calls=%async_computation.4 | async-start | bytes 4194304 | tf_op jit(solution)/shard_map/all_to_all | solution.py:636
  366.2 50.3 %collective-permute-start.17 = (f32[2,8,64,128]{3,2,1,0:T(8,128)}, f32[2,8,64,128]{3,2,1,0:T(8,128)S(1)}, u32[]{:S(2)}, u32[]{:S(2)}) collective-permute-start(f32[2,8,64,128]{3,2,1,0:T(8,128)} %get-tuple-element.327), channel_id=1, source_target_pairs={{0,24},{8,16},{16,8},{24,0},{1,25},{9,17},{17,9},{25,1},{2,26},{10... | collective-permute-start | bytes 1572872 | tf_op jit(solution)/shard_map/ppermute | solution.py:603
  367.7 70.6 %collective-permute-start.25 = (f32[16,2,32,128]{3,2,1,0:T(8,128)}, f32[16,2,32,128]{3,2,1,0:T(8,128)S(1)}, u32[]{:S(2)}, u32[]{:S(2)}) collective-permute-start(f32[16,2,32,128]{3,2,1,0:T(8,128)} %get-tuple-element.373), channel_id=1, source_target_pairs={{0,1},{1,2},{2,3},{3,4},{4,5},{5,6},{6,7},{7,8},{8,9},{9,10},{10,1... | collective-permute-start | bytes 1572872 | tf_op jit(solution)/shard_map/ppermute | solution.py:612
  369.6 68.7 %collective-permute-start.26 = (f32[16,2,32,128]{3,2,1,0:T(8,128)}, f32[16,2,32,128]{3,2,1,0:T(8,128)S(1)}, u32[]{:S(2)}, u32[]{:S(2)}) collective-permute-start(f32[16,2,32,128]{3,2,1,0:T(8,128)} %get-tuple-element.374), channel_id=1, source_target_pairs={{1,0},{2,1},{3,2},{4,3},{5,4},{6,5},{7,6},{8,7},{9,8},{10,9},{11,1... | collective-permute-start | bytes 1572872 | tf_op jit(solution)/shard_map/ppermute | solution.py:613
  439.4 80.6 %all-to-all-start.5 = ((f32[32,2,64,128]{3,2,1,0:T(8,128)}), f32[32,2,64,128]{3,2,1,0:T(8,128)S(1)}, u32[]{:S(2)}, u32[]{:S(2)}) async-start(f32[32,2,64,128]{3,2,1,0:T(8,128)} %compress.13), calls=%async_computation.5 | async-start | bytes 4194304 | tf_op jit(solution)/shard_map/all_to_all | solution.py:636
  448.7 50.5 %collective-permute-start.22 = (f32[2,8,64,128]{3,2,1,0:T(8,128)}, f32[2,8,64,128]{3,2,1,0:T(8,128)}, u32[]{:S(2)}, u32[]{:S(2)}) collective-permute-start(f32[2,8,64,128]{3,2,1,0:T(8,128)} %get-tuple-element.357), channel_id=1, source_target_pairs={{0,24},{8,16},{16,8},{24,0},{1,25},{9,17},{17,9},{25,1},{2,26},{10... | collective-permute-start | bytes 1572872 | tf_op jit(solution)/shard_map/ppermute | solution.py:603
  450.2 69.8 %collective-permute-start.27 = (f32[16,2,32,128]{3,2,1,0:T(8,128)}, f32[16,2,32,128]{3,2,1,0:T(8,128)S(1)}, u32[]{:S(2)}, u32[]{:S(2)}) collective-permute-start(f32[16,2,32,128]{3,2,1,0:T(8,128)} %get-tuple-element.385), channel_id=1, source_target_pairs={{0,1},{1,2},{2,3},{3,4},{4,5},{5,6},{6,7},{7,8},{8,9},{9,10},{10,1... | collective-permute-start | bytes 1572872 | tf_op jit(solution)/shard_map/ppermute | solution.py:612
  452.1 67.9 %collective-permute-start.28 = (f32[16,2,32,128]{3,2,1,0:T(8,128)}, f32[16,2,32,128]{3,2,1,0:T(8,128)S(1)}, u32[]{:S(2)}, u32[]{:S(2)}) collective-permute-start(f32[16,2,32,128]{3,2,1,0:T(8,128)} %get-tuple-element.386), channel_id=1, source_target_pairs={{1,0},{2,1},{3,2},{4,3},{5,4},{6,5},{7,6},{8,7},{9,8},{10,9},{11,1... | collective-permute-start | bytes 1572872 | tf_op jit(solution)/shard_map/ppermute | solution.py:613
  521.4 73.6 %all-to-all-start.6 = ((f32[32,2,64,128]{3,2,1,0:T(8,128)}), f32[32,2,64,128]{3,2,1,0:T(8,128)S(1)}, u32[]{:S(2)}, u32[]{:S(2)}) async-start(f32[32,2,64,128]{3,2,1,0:T(8,128)} %compress.14), calls=%async_computation.6 | async-start | bytes 4194304 | tf_op jit(solution)/shard_map/all_to_all | solution.py:636
  528.6 31.1 %collective-permute-start.29 = (f32[2,8,64,128]{3,2,1,0:T(8,128)}, f32[2,8,64,128]{3,2,1,0:T(8,128)}, u32[]{:S(2)}, u32[]{:S(2)}) collective-permute-start(f32[2,8,64,128]{3,2,1,0:T(8,128)} %get-tuple-element.389), channel_id=1, source_target_pairs={{0,8},{8,0},{16,24},{24,16},{1,9},{9,1},{17,25},{25,17},{2,10},{10... | collective-permute-start | bytes 1572872 | tf_op jit(solution)/shard_map/ppermute | solution.py:603
  530.7 50.5 %collective-permute-start.31 = (f32[2,8,64,128]{3,2,1,0:T(8,128)}, f32[2,8,64,128]{3,2,1,0:T(8,128)}, u32[]{:S(2)}, u32[]{:S(2)}) collective-permute-start(f32[2,8,64,128]{3,2,1,0:T(8,128)} %get-tuple-element.391), channel_id=1, source_target_pairs={{0,24},{8,16},{16,8},{24,0},{1,25},{9,17},{17,9},{25,1},{2,26},{10... | collective-permute-start | bytes 1572872 | tf_op jit(solution)/shard_map/ppermute | solution.py:603
  532.2 62.0 %collective-permute-start.32 = (f32[16,2,32,128]{3,2,1,0:T(8,128)}, f32[16,2,32,128]{3,2,1,0:T(8,128)S(1)}, u32[]{:S(2)}, u32[]{:S(2)}) collective-permute-start(f32[16,2,32,128]{3,2,1,0:T(8,128)} %get-tuple-element.397), channel_id=1, source_target_pairs={{0,1},{1,2},{2,3},{3,4},{4,5},{5,6},{6,7},{7,8},{8,9},{9,10},{10,1... | collective-permute-start | bytes 1572872 | tf_op jit(solution)/shard_map/ppermute | solution.py:612
  534.1 60.9 %collective-permute-start.33 = (f32[16,2,32,128]{3,2,1,0:T(8,128)}, f32[16,2,32,128]{3,2,1,0:T(8,128)}, u32[]{:S(2)}, u32[]{:S(2)}) collective-permute-start(f32[16,2,32,128]{3,2,1,0:T(8,128)} %get-tuple-element.398), channel_id=1, source_target_pairs={{1,0},{2,1},{3,2},{4,3},{5,4},{6,5},{7,6},{8,7},{9,8},{10,9},{11,1... | collective-permute-start | bytes 1572872 | tf_op jit(solution)/shard_map/ppermute | solution.py:613
  596.3 66.4 %all-to-all-start.7 = ((f32[32,2,64,128]{3,2,1,0:T(8,128)}), f32[32,2,64,128]{3,2,1,0:T(8,128)}, u32[]{:S(2)}, u32[]{:S(2)}) async-start(f32[32,2,64,128]{3,2,1,0:T(8,128)} %compress.15), calls=%async_computation.7 | async-start | bytes 4194304 | tf_op jit(solution)/shard_map/all_to_all | solution.py:636
  610.4 62.3 %collective-permute-start.34 = (f32[16,2,32,128]{3,2,1,0:T(8,128)}, f32[16,2,32,128]{3,2,1,0:T(8,128)S(1)}, u32[]{:S(2)}, u32[]{:S(2)}) collective-permute-start(f32[16,2,32,128]{3,2,1,0:T(8,128)} %get-tuple-element.410), channel_id=1, source_target_pairs={{0,1},{1,2},{2,3},{3,4},{4,5},{5,6},{6,7},{7,8},{8,9},{9,10},{10,1... | collective-permute-start | bytes 1572872 | tf_op jit(solution)/shard_map/ppermute | solution.py:612
  617.6 98.4 %collective-permute-start.37 = (f32[16,2,32,128]{3,2,1,0:T(8,128)S(1)}, f32[16,2,32,128]{3,2,1,0:T(8,128)S(1)}, u32[]{:S(2)}, u32[]{:S(2)}) collective-permute-start(f32[16,2,32,128]{3,2,1,0:T(8,128)S(1)} %copy-done.29), channel_id=1, source_target_pairs={{1,0},{2,1},{3,2},{4,3},{5,4},{6,5},{7,6},{8,7},{9,8},{10,9},{11,1... | collective-permute-start | bytes 1572872 | tf_op jit(solution)/shard_map/ppermute | solution.py:613
  632.6 83.5 %collective-permute-start.35 = (f32[16,2,32,128]{3,2,1,0:T(8,128)}, f32[16,2,32,128]{3,2,1,0:T(8,128)S(1)}, u32[]{:S(2)}, u32[]{:S(2)}) collective-permute-start(f32[16,2,32,128]{3,2,1,0:T(8,128)} %get-tuple-element.411), channel_id=1, source_target_pairs={{0,1},{1,2},{2,3},{3,4},{4,5},{5,6},{6,7},{7,8},{8,9},{9,10},{10,1... | collective-permute-start | bytes 1572872 | tf_op jit(solution)/shard_map/ppermute | solution.py:612
  634.5 81.6 %collective-permute-start.38 = (f32[16,2,32,128]{3,2,1,0:T(8,128)}, f32[16,2,32,128]{3,2,1,0:T(8,128)S(1)}, u32[]{:S(2)}, u32[]{:S(2)}) collective-permute-start(f32[16,2,32,128]{3,2,1,0:T(8,128)} %get-tuple-element.419), channel_id=1, source_target_pairs={{1,0},{2,1},{3,2},{4,3},{5,4},{6,5},{7,6},{8,7},{9,8},{10,9},{11,1... | collective-permute-start | bytes 1572872 | tf_op jit(solution)/shard_map/ppermute | solution.py:613
  670.7 45.4 %collective-permute-start.36 = (f32[16,2,32,128]{3,2,1,0:T(8,128)}, f32[16,2,32,128]{3,2,1,0:T(8,128)S(1)}, u32[]{:S(2)}, u32[]{:S(2)}) collective-permute-start(f32[16,2,32,128]{3,2,1,0:T(8,128)} %get-tuple-element.412), channel_id=1, source_target_pairs={{0,1},{1,2},{2,3},{3,4},{4,5},{5,6},{6,7},{7,8},{8,9},{9,10},{10,1... | collective-permute-start | bytes 1572872 | tf_op jit(solution)/shard_map/ppermute | solution.py:612
  672.7 43.5 %collective-permute-start.39 = (f32[16,2,32,128]{3,2,1,0:T(8,128)}, f32[16,2,32,128]{3,2,1,0:T(8,128)S(1)}, u32[]{:S(2)}, u32[]{:S(2)}) collective-permute-start(f32[16,2,32,128]{3,2,1,0:T(8,128)} %get-tuple-element.420), channel_id=1, source_target_pairs={{1,0},{2,1},{3,2},{4,3},{5,4},{6,5},{7,6},{8,7},{9,8},{10,9},{11,1... | collective-permute-start | bytes 1572872 | tf_op jit(solution)/shard_map/ppermute | solution.py:613
  (63 other events, 1747.7 us)

commit v3 on v2

--- a/solution.py
+++ b/solution.py
@@ -46,8 +46,8 @@
     return split_np(np.block([[c, s], [-s, c]]) * scale)
 
 
-def left_table(sign, scale=1.0):
-    c, s = dft_matrix(sign)
+def left_table(sign, scale=1.0, order=np.arange(LANES)):
+    c, s = (part[:, order] for part in dft_matrix(sign))
     high, low = split_np(np.block([[c, -s], [s, c]]) * scale)
     return np.concatenate([high, high, low], axis=1)
 
@@ -407,54 +407,104 @@
     return 1.0 - twice * s, twice * c
 
 
-def final_kernel(steps, wide, *refs):
-    d_refs, refs = refs[:CHUNKS], refs[CHUNKS:]
-    low_refs, high_refs = (), ()
-    if wide:
-        low_refs, high_refs, refs = refs[:CHUNKS], refs[CHUNKS : 2 * CHUNKS], refs[2 * CHUNKS :]
-    g_ref, rate_ref, inv1_ref, inv2_ref, tw_ref = refs[:5]
-    out_ref, zr_ref, zi_ref, x_ref, s_ref = refs[-5:]
-    own = d_refs[0].shape[2]
-    ext = x_ref.shape[1] // 2
-    bins = rate_ref.shape[0]
+def phase_kernel(part, sets, *refs):
+    k = pl.program_id(0)
+    for rate_ref, out_ref in zip(refs[:sets], refs[sets:]):
+        for half in range(2):
+            k2 = k + PER_CHUNK * (2 * part + half)
+            f = k2 * LANES + lax.broadcasted_iota(jnp.int32, (1, LANES), 1)
+            centred = jnp.where(f >= NAZ // 2, f - NAZ, f).astype(F32) * (1.0 / NAZ)
+            c, s = turn(rate_ref[...] * (centred * centred))
+            out_ref[half, 0, 0] = c
+            out_ref[half, 0, 1] = s
+
+
+def phase_tables(rates, part):
+    shapes = [(2, PER_CHUNK, 2, rate.shape[0], LANES) for rate in rates]
+    points = sum(2 * PER_CHUNK * rate.size for rate in rates)
+    return pl.pallas_call(
+        functools.partial(phase_kernel, part, len(rates)),
+        grid=(PER_CHUNK,),
+        in_specs=[whole_spec(rate) for rate in rates],
+        out_specs=[
+            pl.BlockSpec((2, 1) + shape[2:], lambda i: (0, i, 0, 0, 0)) for shape in shapes
+        ],
+        out_shape=[jax.ShapeDtypeStruct(shape, F32) for shape in shapes],
+        compiler_params=pltpu.CompilerParams(vmem_limit_bytes=VMEM_LIMIT),
+        cost_estimate=pl.CostEstimate(
+            flops=40 * points, bytes_accessed=8 * points, transcendentals=0
+        ),
+        name="phase",
+    )(*rates)
+
+
+def combine(sources, kk, start, put):
+    at = slice(start, start + STEP)
+    values = [(ref[kk, 0, at, :], ref[kk, 1, at, :]) for ref in sources]
+    for q, value in enumerate(dft_list(values, -1.0)):
+        for half, part in enumerate(value):
+            high, low = split(part)
+            put(q, slice(half * LANES, (half + 1) * LANES), high, low)
+
+
+def final_kernel(steps, joins, wide, *refs):
+    refs = list(refs)
+
+    def take(count):
+        taken = refs[:count]
+        del refs[:count]
+        return taken
+
+    sources = take(CHUNKS) if joins else take(1)
+    low_refs, high_refs = (take(CHUNKS), take(CHUNKS)) if wide else ((), ())
+    phase_refs = take(CHUNKS // 2)
+    mover_refs = take(2 if wide else 1)
+    inv1_ref, inv2_ref, tw_ref = take(3)
+    out_ref, own_ref, zr_ref, zi_ref, s_ref, swap_ref = refs[-7:-1] if wide else refs[-6:]
+    halo_ref = refs[-1]
+    if not joins:
+        own_ref = sources[0]
+    own = own_ref.shape[2] // 2
+    rows = phase_refs[0].shape[3]
     step = pl.program_id(0)
 
     @pl.when(step < steps)
     def _():
         def one(kk, buf):
             k = step * KB + kk
-
-            def combine(sources, start, to):
-                at = slice(start, start + STEP)
-                values = [(ref[kk, 0, at, :], ref[kk, 1, at, :]) for ref in sources]
-                for q, (a, b) in enumerate(dft_list(values, -1.0)):
-                    for half, part in enumerate((a, b)):
-                        hi, lo = split(part)
-                        cols = slice(half * LANES, (half + 1) * LANES)
-                        x_ref[buf * CHUNKS + q, to : to + STEP, cols] = hi
-                        x_ref[buf * CHUNKS + q, ext + to : ext + to + STEP, cols] = lo
-
-            for start in range(0, own, STEP):
-                combine(d_refs, start, start)
+            if joins:
+                for start in range(0, own, STEP):
+
+                    def put_own(q, cols, high, low, start=start):
+                        own_ref[q, kk, start : start + STEP, cols] = high
+                        own_ref[q, kk, own + start : own + start + STEP, cols] = low
+
+                    combine(sources, kk, start, put_own)
             if wide:
-                for start in range(0, HALO, STEP):
-                    combine(low_refs, start, own + start)
-                    combine(high_refs, start, own + HALO + start)
+                for side, halo_refs in enumerate((low_refs, high_refs)):
+                    for start in range(0, HALO, STEP):
+
+                        def put_halo(q, cols, high, low, at=side * HALO + start):
+                            halo_ref[buf, q, at : at + STEP, cols] = high
+                            halo_ref[buf, q, 2 * HALO + at : 2 * HALO + at + STEP, cols] = low
+
+                        combine(halo_refs, kk, start, put_halo)
             for q in range(CHUNKS):
                 k2 = k + PER_CHUNK * q
-                moved = dot(g_ref[lax.div(k2, LANES // GROUPS)], x_ref[buf * CHUNKS + q])
-                f = k2 * LANES + lax.broadcasted_iota(jnp.int32, (1, LANES), 1)
-                centred = jnp.where(f >= NAZ // 2, f - NAZ, f).astype(F32) * (1.0 / NAZ)
-                square = centred * centred
-                block = min(bins, 32)
-                for start in range(0, bins, block):
-                    at = slice(start, start + block)
-                    c, s = turn(rate_ref[at, :] * square)
-                    both = moved[at, :] + moved[bins + start : bins + start + block, :]
-                    a, b = both[:, 0:LANES], both[:, LANES : 2 * LANES]
-                    to = pl.ds(pl.multiple_of(k2 * bins + start, block), block)
-                    zr_ref[to, :] = a * c + b * s
-                    zi_ref[to, :] = b * c - a * s
+                band = lax.div(k2, LANES // GROUPS)
+                moved = dot(mover_refs[0][band], own_ref[q, kk])
+                if wide:
+                    moved = moved + dot(mover_refs[1][band], halo_ref[buf, q])
+                both = moved[0:rows, :] + moved[rows : 2 * rows, :]
+                c, s = phase_refs[q // 2][q % 2, kk, 0], phase_refs[q // 2][q % 2, kk, 1]
+                a, b = both[:, 0:LANES], both[:, LANES : 2 * LANES]
+                swap_ref[buf, 0, q] = a * c + b * s
+                swap_ref[buf, 1, q] = b * c - a * s
+            to = pl.ds(pl.multiple_of(k * CHUNKS, CHUNKS), CHUNKS)
+            for start in range(0, rows, BB):
+                at = slice(start, start + BB)
+                zr_ref[at, to, :] = jnp.swapaxes(swap_ref[buf, 0, :, at, :], 0, 1)
+                zi_ref[at, to, :] = jnp.swapaxes(swap_ref[buf, 1, :, at, :], 0, 1)
 
         def first(i, carry):
             one(2 * i, 0)
@@ -470,17 +520,17 @@
         def some(j, carry):
             cols = []
             for t in range(QUAD):
-                at = pl.ds(base + QUAD * j + t, LANES, stride=bins)
-                cols.append(jnp.concatenate([zr_ref[at, :], zi_ref[at, :]], axis=0))
+                at = base + QUAD * j + t
+                cols.append(jnp.concatenate([zr_ref[at], zi_ref[at]], axis=0))
             hi, lo = split(jnp.concatenate(cols, axis=1))
             w = dot(inv1_ref[...], jnp.concatenate([hi, lo, hi], axis=0))
-            rows = []
+            turned = []
             for t in range(QUAD):
                 a = w[0:LANES, t * LANES : (t + 1) * LANES]
                 b = w[LANES : 2 * LANES, t * LANES : (t + 1) * LANES]
                 wr, wi = tw_ref[0], tw_ref[1]
-                rows.append(jnp.concatenate([a * wr - b * wi, a * wi + b * wr], axis=1))
-            hi, lo = split(jnp.concatenate(rows, axis=0))
+                turned.append(jnp.concatenate([a * wr - b * wi, a * wi + b * wr], axis=1))
+            hi, lo = split(jnp.concatenate(turned, axis=0))
             image = lax.dot_general(
                 inv2_ref[...],
                 jnp.concatenate([hi, lo, hi], axis=1),
@@ -489,28 +539,29 @@
             )
             for t in range(QUAD):
                 for ri in range(2):
-                    s_ref[ri, pl.ds(QUAD * j + t, LANES, stride=BB), :] = image[
+                    s_ref[ri, QUAD * j + t] = image[
                         ri * LANES : (ri + 1) * LANES, t * LANES : (t + 1) * LANES
                     ]
             return carry
 
         lax.fori_loop(0, BB // QUAD, some, 0)
         for ri in range(2):
-            for n in range(LANES):
-                out_ref[ri, :, n * LANES : (n + 1) * LANES] = s_ref[ri, n * BB : (n + 1) * BB, :]
-
-
-def final(bins, mains, lows, highs, mover, rate, places, image=None):
-    own, rows = mains[0].shape[2], rate.shape[0]
-    wide = len(lows) > 0
-    ext = own + (2 * HALO if wide else 0)
+            for start in range(0, LANES, 8):
+                lines = jnp.swapaxes(s_ref[ri, :, start : start + 8, :], 0, 1)
+                for n in range(8):
+                    at = (start + n) * LANES
+                    out_ref[ri, :, at : at + LANES] = lines[n]
+
+
+def final(bins, places, sources, lows, highs, phases, movers, image=None):
+    joins, wide = len(sources) > 1, len(lows) > 0
+    rows = len(places) * BB
     steps = PER_CHUNK // KB
     ids = np.arange(LANES)
     tw = jnp.asarray(np.stack(unit(ids[:, None] * ids[None, :], NAZ, 1.0)), F32)
     consts = [
-        mover,
-        rate,
-        jnp.asarray(left_table(1.0)),
+        *movers,
+        jnp.asarray(left_table(1.0, 1.0, ids // CHUNKS + PER_CHUNK * (ids % CHUNKS))),
         jnp.asarray(left_table(1.0, 1.0 / NAZ)),
         tw,
     ]
@@ -524,32 +575,53 @@
     def early(i):
         return (jnp.minimum(i, steps - 1), 0, 0, 0)
 
+    def early_second(i):
+        return (0, jnp.minimum(i, steps - 1), 0, 0)
+
     def late(i):
         at = jnp.maximum(i - steps, 0)
         return (0, start + at + jnp.where(at >= gap_at, gap, 0), 0)
 
-    points = NAZ * rows
-    given = [*mains, *lows, *highs, *consts]
-    specs = [pl.BlockSpec((KB, 2, own, LANES), early)] * CHUNKS
+    joined = (CHUNKS, PER_CHUNK, 2 * bins, 2 * LANES)
+    joined_spec = pl.BlockSpec((CHUNKS, KB, 2 * bins, 2 * LANES), early_second)
+    given = [*sources, *lows, *highs, *phases, *consts]
+    specs = [pl.BlockSpec((KB, 2, bins, LANES), early)] * CHUNKS if joins else [joined_spec]
     specs += [pl.BlockSpec((KB, 2, HALO, LANES), early)] * (2 * CHUNKS if wide else 0)
+    specs += [
+        pl.BlockSpec((2, KB, 2, rows, LANES), lambda i: (0, jnp.minimum(i, steps - 1), 0, 0, 0))
+    ] * len(phases)
     specs += [whole_spec(a) for a in consts]
     aliases = {}
     if image is not None:
         aliases = {len(given): 0}
         given.append(image)
         specs.append(pl.BlockSpec(memory_space=pl.ANY))
+    shapes = [jax.ShapeDtypeStruct((2, bins, NAZ), F32)]
+    out_specs = [pl.BlockSpec((2, BB, NAZ), late)]
+    scratch = []
+    if joins and wide:
+        scratch.append(pltpu.VMEM((CHUNKS, KB, 2 * bins, 2 * LANES), BF16))
+    elif joins:
+        shapes.append(jax.ShapeDtypeStruct(joined, BF16))
+        out_specs.append(joined_spec)
+    else:
+        scratch.append(pltpu.VMEM((16, LANES), BF16))
+    scratch += [
+        pltpu.VMEM((rows, LANES, LANES), F32),
+        pltpu.VMEM((rows, LANES, LANES), F32),
+        pltpu.VMEM((2, BB, LANES, LANES), F32),
+        pltpu.VMEM((2, 2, CHUNKS, rows, LANES), F32),
+    ]
+    if wide:
+        scratch.append(pltpu.VMEM((2, CHUNKS, 4 * HALO, 2 * LANES), BF16))
+    points = NAZ * rows
     return pl.pallas_call(
-        functools.partial(final_kernel, steps, wide),
+        functools.partial(final_kernel, steps, joins, wide),
         grid=(steps + len(places),),
         in_specs=specs,
-        out_specs=pl.BlockSpec((2, BB, NAZ), late),
-        out_shape=jax.ShapeDtypeStruct((2, bins, NAZ), F32),
-        scratch_shapes=[
-            pltpu.VMEM((LANES * rows, LANES), F32),
-            pltpu.VMEM((LANES * rows, LANES), F32),
-            pltpu.VMEM((2 * CHUNKS, 2 * ext, 2 * LANES), BF16),
-            pltpu.VMEM((2, LANES * BB, LANES), F32),
-        ],
+        out_specs=out_specs,
+        out_shape=shapes,
+        scratch_shapes=scratch,
         input_output_aliases=aliases,
         compiler_params=pltpu.CompilerParams(vmem_limit_bytes=VMEM_LIMIT),
         cost_estimate=pl.CostEstimate(
@@ -559,17 +631,12 @@
     )(*given)
 
 
-def mover_table(bins, rows, wide, shift_table, filter_index, tap_table):
-    ext = bins + (2 * HALO if wide else 0)
+def mover_table(rows, columns, shift_table, filter_index, tap_table):
     shift_table, filter_index = shift_table[:, rows], filter_index[:, rows]
     onehot = (filter_index[:, :, None] == jnp.arange(NFILT, dtype=jnp.int32)).astype(F32)
     weights = jnp.einsum("gbf,ft->gbt", onehot, tap_table, precision=lax.Precision.HIGHEST)
     first = rows[None, :].astype(np.int32) + shift_table + (HALO - 4)
-    column = np.arange(ext)
-    natural = np.where(
-        column < bins, column + HALO, np.where(column < bins + HALO, column - bins, column)
-    ).astype(np.int32)
-    offset = natural[None, None, :] - first[:, :, None]
+    offset = columns.astype(np.int32)[None, None, :] - first[:, :, None]
     table = jnp.zeros(offset.shape, F32)
     for t in range(TAPS):
         table = table + jnp.where(offset == t, weights[:, :, t : t + 1], 0.0)
@@ -578,6 +645,24 @@
     top = jnp.concatenate([high, high], axis=2)
     bottom = jnp.concatenate([low, jnp.zeros_like(low)], axis=2)
     return jnp.concatenate([top, bottom], axis=1).astype(BF16)
+
+
+def own_columns(bins):
+    return np.arange(HALO, HALO + bins)
+
+
+def halo_columns(bins):
+    return np.concatenate([np.arange(HALO), np.arange(bins + HALO, bins + 2 * HALO)])
+
+
+def row_sets(bins):
+    blocks = np.arange(bins // BB)
+    inner = (blocks >= HALO // BB) & (blocks < (bins - HALO) // BB)
+    return [blocks[chosen].tolist() for chosen in (inner, ~inner) if chosen.any()]
+
+
+def bins_of(places):
+    return np.concatenate([np.arange(BB) + BB * place for place in places])
 
 
 def neighbours(axes, size, step):
@@ -612,13 +697,17 @@
         lows.append(lax.ppermute(up, axes, neighbours(axes, devices, 1)))
         highs.append(lax.ppermute(down, axes, neighbours(axes, devices, -1)))
 
+    places = row_sets(bins)
+    rates = [rate[bins_of(p)] for p in places]
+    phases = []
     got = [gather(0)]
     packed[1], got[0] = lax.optimization_barrier((packed[1], got[0]))
     got.append(gather(1))
     for c in range(CHUNKS):
         lines = compress(got[c], rank, chirp)
+        if c + 1 < CHUNKS:
+            lines, got[c + 1] = lax.optimization_barrier((lines, got[c + 1]))
         if c + 2 < CHUNKS:
-            packed[c + 2], lines = lax.optimization_barrier((packed[c + 2], lines))
             packed[c + 2], got[c + 1] = lax.optimization_barrier((packed[c + 2], got[c + 1]))
             if c >= 1:
                 held = (packed[c + 2], turned[c - 1])
@@ -627,6 +716,11 @@
         if c >= 2:
             transform(c - 2)
             lines, mains[c - 2] = lax.optimization_barrier((lines, mains[c - 2]))
+            if c - 2 < CHUNKS // 2:
+                rates, turned[c - 2] = lax.optimization_barrier((rates, turned[c - 2]))
+                table = phase_tables(rates, c - 2)
+                lines, table = lax.optimization_barrier((lines, table))
+                phases.append(table)
         if c >= 3:
             held = (lines, lows[c - 3], highs[c - 3])
             lines, lows[c - 3], highs[c - 3] = lax.optimization_barrier(held)
@@ -638,18 +732,20 @@
     transform(CHUNKS - 2)
     transform(CHUNKS - 1)
     tables = (shift_table, filter_index, tap_table)
-    blocks = np.arange(bins // BB)
-    inner = (blocks >= HALO // BB) & (blocks < (bins - HALO) // BB)
-    image = None
-    for chosen, wide in ((inner, False), (~inner, True)):
-        places = blocks[chosen].tolist()
-        if not places:
-            continue
-        ids = np.concatenate([np.arange(BB) + BB * place for place in places])
-        mover = mover_table(bins, ids, wide, *tables)
+    image, sources = None, mains
+    for i, places_of in enumerate(places):
+        ids = bins_of(places_of)
+        wide = i == len(places) - 1
         halos = (lows, highs) if wide else ([], [])
-        image = final(bins, mains, *halos, mover, rate[ids], places, image)
+        columns = [own_columns(bins), halo_columns(bins)] if wide else [own_columns(bins)]
+        movers = [mover_table(ids, cols, *tables) for cols in columns]
+        result = final(
+            bins, places_of, sources, *halos, [table[i] for table in phases], movers, image
+        )
+        image, sources = result[0], result[1:]
     return image
+
+
 def solution(mesh):
     return jax.shard_map(
         functools.partial(local, mesh.shape["rng"], mesh.shape["az"]),

time: 762 us -> 648 us (0.85)
  waiting for transfers between devices: 303 us -> 174 us
  Pallas kernels: 269 us -> 287 us
    ppermute x24, waiting for transfers between devices: 282 us -> 113 us  [gather(): lax.ppermute(packed[c][j], 'rng', [(i, i ^ j) for i in range(nrng)])]
    ppermute x8, waiting for transfers between devices: 0.02 us -> 19.9 us  [transform(): lows.append(lax.ppermute(up, axes, neighbours(axes, devices, 1)))]
    all_to_all x8, waiting for transfers between devices: 21 us -> 40.7 us  [local(): moved = lax.all_to_all(lines, axes, split_axis=0, concat_axis=0, tiled=True)]
    pallas_call x2 -> x6, Pallas kernels: 77.5 us -> 96.1 us  [the longest x2 65.6 us: final(): pl.pallas_call(functools.partial(final_kernel, steps, joins, wide), grid=...]
    unnamed x96 -> x98, local copies, waits for them, and re-layouts: 16.4 us -> 9.16 us
  transfers between devices with their start and end apart: 48 -> 48, of which waited for: 23 -> 19; matrix products, arithmetic and copies ran while one was open for 2% -> 2% of each run, Pallas kernels for 27% -> 38%
where the time goes in v3:
time: 648 us; the launch traced here: 646 us
  Pallas kernels  287 us (44%)
  waiting for transfers between devices  174 us (27%)
  starting transfers between devices  160 us (25%)
  local copies, waits for them, and re-layouts  15.2 us (2%)
  other arithmetic  7.8 us (1%)
    ppermute x24, waiting for transfers between devices, gather(): lax.ppermute(packed[c][j], 'rng', [(i, i ^ j) for i in range(nrng)])  113 us
    pallas_call x8, Pallas kernels, compress(): pl.pallas_call(functools.partial(compress_kernel, parts, block), grid=(ro...  103 us
    pallas_call x2, Pallas kernels, final(): pl.pallas_call(functools.partial(final_kernel, steps, joins, wide), grid=...  65.6 us
    pallas_call x8, Pallas kernels, azimuth(): pl.pallas_call(functools.partial(azimuth_kernel, chunk), grid=(parts,), i...  63.2 us
    all_to_all x8, starting transfers between devices, local(): moved = lax.all_to_all(lines, axes, split_axis=0, concat_axis=0, tiled=True)  58.7 us
    ppermute x8, starting transfers between devices, transform(): highs.append(lax.ppermute(down, axes, neighbours(axes, devices, -1)))  57.6 us
    all_to_all x8, waiting for transfers between devices, local(): moved = lax.all_to_all(lines, axes, split_axis=0, concat_axis=0, tiled=True)  40.7 us
    pallas_call x4, Pallas kernels, phase_tables(): pl.pallas_call(functools.partial(phase_kernel, part, len(rates)), grid=(P...  30.5 us
  transfers between devices with their start and end apart: 48, of which 19 were waited for; matrix products, arithmetic and copies ran while one was open for 2% of the time, Pallas kernels for 38%

profile of v3, /device:TPU:4, one launch (start us, length us, event | category | flops | bytes accessed | tf_op | source)
XLA Modules:
  0.0 645.9 jit_solution(3605534497511277348)
XLA Ops:
  0.0 9.3 %pack.3 = (f32[2,8,64,128]{3,2,1,0:T(8,128)}, f32[2,8,64,128]{3,2,1,0:T(8,128)}, f32[2,8,64,128]{3,2,1,0:T(8,128)}, f32[2,8,64,128]{3,2,1,0:T(8,128)}) custom-call(s32[1]{0:T(128)} %bitcast.rank_ref, f32[2,2048,1024]{2,1,0:T(8,128)} %x_ref.3), custom_call_target="tpu_custom_call" | custom-call | bytes 33554432 | tf_op jit(solution)/shard_map/pack/pallas_call | solution.py:137
  12.8 15.5 %pack.2 = (f32[2,8,64,128]{3,2,1,0:T(8,128)}, f32[2,8,64,128]{3,2,1,0:T(8,128)}, f32[2,8,64,128]{3,2,1,0:T(8,128)}, f32[2,8,64,128]{3,2,1,0:T(8,128)}, f32[2,8,6...) custom-call(s32[1]{0:T(128)} %bitcast.rank_ref, ...), custom_call_target="tpu_custom_call" | custom-call | bytes 33554432 | tf_op jit(solution)/shard_map/pack/pallas_call | solution.py:137
  40.0 12.9 %compress.8 = f32[32,2,64,128]{3,2,1,0:T(8,128)} custom-call(s32[1]{0:T(128)} %bitcast.rank_ref, f32[2,8,64,128]{3,2,1,0:T(8,128)} %get-tuple-element.268.refs_0_, f32[2,8,64,128]{3,2,1,0:T(8,128)} %copy-done.41, f32[2,8,64,128]{3,2,1,0:T(8,128)} %copy-done.42, f32[2,8,64,128]{3,2,1,0:T(8,128)} %copy-done.43, f32[2,32,128]{2,1,0:T(8,128)} %bitcast.68, ...), custom_call_target="tpu_custom_call" | custom-call | flops 1610612736 | bytes 4194304 | tf_op jit(solution)/shard_map/compress/pallas_call | solution.py:276
  69.4 12.9 %compress.9 = f32[32,2,64,128]{3,2,1,0:T(8,128)} custom-call(s32[1]{0:T(128)} %bitcast.rank_ref, f32[2,8,64,128]{3,2,1,0:T(8,128)} %get-tuple-element.280.refs_0_, f32[2,8,64,128]{3,2,1,0:T(8,128)} %copy-done.45, f32[2,8,64,128]{3,2,1,0:T(8,128)} %copy-done.46, f32[2,8,64,128]{3,2,1,0:T(8,128)} %collective-permute-done.5.refs_3_, f32[2,32,128]{2,1,0:T(8,128)} %bitcast.69, ...), custom_call_target="tpu_custom_call" | custom-call | flops 1610612736 | bytes 4194304 | tf_op jit(solution)/shard_map/compress/pallas_call | solution.py:276
  82.3 14.5 %collective-permute-done.6.refs_1_ = f32[2,8,64,128]{3,2,1,0:T(8,128)S(1)} collective-permute-done((f32[2,8,64,128]{3,2,1,0:T(8,128)}, f32[2,8,64,128]{3,2,1,0:T(8,128)S(1)}, u32[]{:S(2)}, u32[]{:S(2)}) %collective-permute-start.6) | collective-permute-done | bytes 524320 | tf_op jit(solution)/shard_map/ppermute | solution.py:688
  97.9 14.8 %collective-permute-done.8.refs_3_ = f32[2,8,64,128]{3,2,1,0:T(8,128)} collective-permute-done((f32[2,8,64,128]{3,2,1,0:T(8,128)}, f32[2,8,64,128]{3,2,1,0:T(8,128)}, u32[]{:S(2)}, u32[]{:S(2)}) %collective-permute-start.8) | collective-permute-done | bytes 524320 | tf_op jit(solution)/shard_map/ppermute | solution.py:688
  127.4 13.0 %compress.10 = f32[32,2,64,128]{3,2,1,0:T(8,128)} custom-call(s32[1]{0:T(128)} %bitcast.rank_ref, f32[2,8,64,128]{3,2,1,0:T(8,128)} %get-tuple-element.292.refs_0_, f32[2,8,64,128]{3,2,1,0:T(8,128)} %copy-done.44, f32[2,8,64,128]{3,2,1,0:T(8,128)} %collective-permute-done.7.refs_2_, f32[2,8,64,128]{3,2,1,0:T(8,128)} %collective-permute-done.8.refs_3_, ...), custom_call_target="tpu_custom_call" | custom-call | flops 1610612736 | bytes 4194304 | tf_op jit(solution)/shard_map/compress/pallas_call | solution.py:276
  155.8 10.0 %collective-permute-done.10.refs_2_ = f32[2,8,64,128]{3,2,1,0:T(8,128)} collective-permute-done((f32[2,8,64,128]{3,2,1,0:T(8,128)}, f32[2,8,64,128]{3,2,1,0:T(8,128)}, u32[]{:S(2)}, u32[]{:S(2)}) %collective-permute-start.10) | collective-permute-done | bytes 524320 | tf_op jit(solution)/shard_map/ppermute | solution.py:688
  197.6 7.9 %azimuth1.1 = (f32[16,2,128,128]{3,2,1,0:T(8,128)}, f32[16,2,32,128]{3,2,1,0:T(8,128)}, f32[16,2,32,128]{3,2,1,0:T(8,128)}) custom-call(f32[4,8,2,4,16,128]{5,4,3,2,1,0:T(8,128)} %bitcast.40, f32[2,128,128]{2,1,0:T(8,128)} %constant.83.clone.tw_ref, bf16[256,256]{1,0:T(8,128)(2,1)} %constant.84.clone.fwd_ref, bf16[256,256]{1,0:T(8,128)(2,1)} %constant.29.clone.refs_7_.fwd_low_ref), custom_call_target="tpu_custom_call" | custom-call | flops 805306368 | bytes 4194304 | tf_op jit(solution)/shard_map/azimuth1/pallas_call | solution.py:358
  205.5 12.9 %compress.11 = f32[32,2,64,128]{3,2,1,0:T(8,128)} custom-call(s32[1]{0:T(128)} %bitcast.rank_ref, f32[2,8,64,128]{3,2,1,0:T(8,128)} %get-tuple-element.324.refs_0_, f32[2,8,64,128]{3,2,1,0:T(8,128)} %collective-permute-done.9.refs_1_, f32[2,8,64,128]{3,2,1,0:T(8,128)} %collective-permute-done.10.refs_2_, f32[2,8,64,128]{3,2,1,0:T(8,128)} %collective-permute-done.11.refs_3_, ...), custom_call_target="tpu_custom_call" | custom-call | flops 1610612736 | bytes 4194304 | tf_op jit(solution)/shard_map/compress/pallas_call | solution.py:276
  218.4 11.4 %collective-permute-done.14.refs_3_ = f32[2,8,64,128]{3,2,1,0:T(8,128)} collective-permute-done((f32[2,8,64,128]{3,2,1,0:T(8,128)}, f32[2,8,64,128]{3,2,1,0:T(8,128)}, u32[]{:S(2)}, u32[]{:S(2)}) %collective-permute-start.14) | collective-permute-done | bytes 524320 | tf_op jit(solution)/shard_map/ppermute | solution.py:688
  233.0 8.6 %all-to-all-start.3 = ((f32[32,2,64,128]{3,2,1,0:T(8,128)}), f32[32,2,64,128]{3,2,1,0:T(8,128)}, u32[]{:S(2)}, u32[]{:S(2)}) async-start(f32[32,2,64,128]{3,2,1,0:T(8,128)} %compress.11), calls=%async_computation.3 | async-start | bytes 4194304 | tf_op jit(solution)/shard_map/all_to_all | solution.py:730
  254.4 12.9 %compress.12 = f32[32,2,64,128]{3,2,1,0:T(8,128)} custom-call(s32[1]{0:T(128)} %bitcast.rank_ref, f32[2,8,64,128]{3,2,1,0:T(8,128)} %get-tuple-element.356.refs_0_, f32[2,8,64,128]{3,2,1,0:T(8,128)} %copy-done.37, f32[2,8,64,128]{3,2,1,0:T(8,128)} %collective-permute-done.13.refs_2_, f32[2,8,64,128]{3,2,1,0:T(8,128)} %collective-permute-done.14.refs_3_, ...), custom_call_target="tpu_custom_call" | custom-call | flops 1610612736 | bytes 4194304 | tf_op jit(solution)/shard_map/compress/pallas_call | solution.py:276
  274.9 7.9 %azimuth2.1 = (f32[16,2,128,128]{3,2,1,0:T(8,128)}, f32[16,2,32,128]{3,2,1,0:T(8,128)}, f32[16,2,32,128]{3,2,1,0:T(8,128)}) custom-call(f32[4,8,2,4,16,128]{5,4,3,2,1,0:T(8,128)} %bitcast.38, f32[2,128,128]{2,1,0:T(8,128)} %constant.83.clone.tw_ref, bf16[256,256]{1,0:T(8,128)(2,1)} %constant.84.clone.fwd_ref, bf16[256,256]{1,0:T(8,128)(2,1)} %constant.29.clone.refs_7_.fwd_low_ref), custom_call_target="tpu_custom_call" | custom-call | flops 805306368 | bytes 4194304 | tf_op jit(solution)/shard_map/azimuth2/pallas_call | solution.py:358
  282.9 11.2 %collective-permute-done.17.refs_3_ = f32[2,8,64,128]{3,2,1,0:T(8,128)S(1)} collective-permute-done((f32[2,8,64,128]{3,2,1,0:T(8,128)}, f32[2,8,64,128]{3,2,1,0:T(8,128)S(1)}, u32[]{:S(2)}, u32[]{:S(2)}) %collective-permute-start.17) | collective-permute-done | bytes 524320 | tf_op jit(solution)/shard_map/ppermute | solution.py:688
  296.2 9.1 %all-to-all-start.4 = ((f32[32,2,64,128]{3,2,1,0:T(8,128)}), f32[32,2,64,128]{3,2,1,0:T(8,128)S(1)}, u32[]{:S(2)}, u32[]{:S(2)}) async-start(f32[32,2,64,128]{3,2,1,0:T(8,128)} %compress.12), calls=%async_computation.4 | async-start | bytes 4194304 | tf_op jit(solution)/shard_map/all_to_all | solution.py:730
  325.7 7.9 %azimuth3.1 = (f32[16,2,128,128]{3,2,1,0:T(8,128)}, f32[16,2,32,128]{3,2,1,0:T(8,128)}, f32[16,2,32,128]{3,2,1,0:T(8,128)}) custom-call(f32[4,8,2,4,16,128]{5,4,3,2,1,0:T(8,128)} %bitcast.5.x_ref, f32[2,128,128]{2,1,0:T(8,128)} %constant.83.clone.tw_ref, bf16[256,256]{1,0:T(8,128)(2,1)} %constant.84.clone.fwd_ref, ...), custom_call_target="tpu_custom_call" | custom-call | flops 805306368 | bytes 4194304 | tf_op jit(solution)/shard_map/azimuth3/pallas_call | solution.py:358
  333.6 12.9 %compress.13 = f32[32,2,64,128]{3,2,1,0:T(8,128)} custom-call(s32[1]{0:T(128)} %bitcast.rank_ref, f32[2,8,64,128]{3,2,1,0:T(8,128)} %get-tuple-element.391.refs_0_, f32[2,8,64,128]{3,2,1,0:T(8,128)} %copy-done.33, f32[2,8,64,128]{3,2,1,0:T(8,128)} %copy-done.34, f32[2,8,64,128]{3,2,1,0:T(8,128)} %copy-done.35, f32[2,32,128]{2,1,0:T(8,128)} %bitcast.73, ...), custom_call_target="tpu_custom_call" | custom-call | flops 1610612736 | bytes 4194304 | tf_op jit(solution)/shard_map/compress/pallas_call | solution.py:276
  346.5 11.4 %collective-permute-done.22.refs_3_ = f32[2,8,64,128]{3,2,1,0:T(8,128)} collective-permute-done((f32[2,8,64,128]{3,2,1,0:T(8,128)}, f32[2,8,64,128]{3,2,1,0:T(8,128)}, u32[]{:S(2)}, u32[]{:S(2)}) %collective-permute-start.22) | collective-permute-done | bytes 524320 | tf_op jit(solution)/shard_map/ppermute | solution.py:688
  361.1 8.6 %all-to-all-start.5 = ((f32[32,2,64,128]{3,2,1,0:T(8,128)}), f32[32,2,64,128]{3,2,1,0:T(8,128)}, u32[]{:S(2)}, u32[]{:S(2)}) async-start(f32[32,2,64,128]{3,2,1,0:T(8,128)} %compress.13), calls=%async_computation.5 | async-start | bytes 4194304 | tf_op jit(solution)/shard_map/all_to_all | solution.py:730
  382.4 12.9 %compress.14 = f32[32,2,64,128]{3,2,1,0:T(8,128)} custom-call(s32[1]{0:T(128)} %bitcast.rank_ref, f32[2,8,64,128]{3,2,1,0:T(8,128)} %get-tuple-element.431.refs_0_, f32[2,8,64,128]{3,2,1,0:T(8,128)} %copy-done.36, f32[2,8,64,128]{3,2,1,0:T(8,128)} %collective-permute-done.21.refs_2_, f32[2,8,64,128]{3,2,1,0:T(8,128)} %collective-permute-done.22.refs_3_, ...), custom_call_target="tpu_custom_call" | custom-call | flops 1610612736 | bytes 4194304 | tf_op jit(solution)/shard_map/compress/pallas_call | solution.py:276
  395.4 7.9 %azimuth4.1 = (f32[16,2,128,128]{3,2,1,0:T(8,128)}, f32[16,2,32,128]{3,2,1,0:T(8,128)}, f32[16,2,32,128]{3,2,1,0:T(8,128)}) custom-call(f32[4,8,2,4,16,128]{5,4,3,2,1,0:T(8,128)} %bitcast.39, f32[2,128,128]{2,1,0:T(8,128)} %constant.83.clone.tw_ref, bf16[256,256]{1,0:T(8,128)(2,1)} %constant.84.clone.fwd_ref, bf16[256,256]{1,0:T(8,128)(2,1)} %constant.29.clone.refs_7_.fwd_low_ref), custom_call_target="tpu_custom_call" | custom-call | flops 805306368 | bytes 4194304 | tf_op jit(solution)/shard_map/azimuth4/pallas_call | solution.py:358
  403.3 18.9 %collective-permute-done.29.refs_3_ = f32[2,8,64,128]{3,2,1,0:T(8,128)S(1)} collective-permute-done((f32[2,8,64,128]{3,2,1,0:T(8,128)}, f32[2,8,64,128]{3,2,1,0:T(8,128)S(1)}, u32[]{:S(2)}, u32[]{:S(2)}) %collective-permute-start.29) | collective-permute-done | bytes 524320 | tf_op jit(solution)/shard_map/ppermute | solution.py:688
  424.3 9.1 %all-to-all-start.6 = ((f32[32,2,64,128]{3,2,1,0:T(8,128)}), f32[32,2,64,128]{3,2,1,0:T(8,128)S(1)}, u32[]{:S(2)}, u32[]{:S(2)}) async-start(f32[32,2,64,128]{3,2,1,0:T(8,128)} %compress.14), calls=%async_computation.6 | async-start | bytes 4194304 | tf_op jit(solution)/shard_map/all_to_all | solution.py:730
  442.6 7.9 %azimuth5.1 = (f32[16,2,128,128]{3,2,1,0:T(8,128)}, f32[16,2,32,128]{3,2,1,0:T(8,128)}, f32[16,2,32,128]{3,2,1,0:T(8,128)}) custom-call(f32[4,8,2,4,16,128]{5,4,3,2,1,0:T(8,128)} %bitcast.7.x_ref, f32[2,128,128]{2,1,0:T(8,128)} %constant.83.clone.tw_ref, bf16[256,256]{1,0:T(8,128)(2,1)} %constant.84.clone.fwd_ref, ...), custom_call_target="tpu_custom_call" | custom-call | flops 805306368 | bytes 4194304 | tf_op jit(solution)/shard_map/azimuth5/pallas_call | solution.py:358
  450.5 12.9 %compress.15 = f32[32,2,64,128]{3,2,1,0:T(8,128)} custom-call(s32[1]{0:T(128)} %bitcast.rank_ref, f32[2,8,64,128]{3,2,1,0:T(8,128)} %get-tuple-element.448.refs_0_, f32[2,8,64,128]{3,2,1,0:T(8,128)} %copy-done.38, f32[2,8,64,128]{3,2,1,0:T(8,128)} %copy-done.39, f32[2,8,64,128]{3,2,1,0:T(8,128)} %copy-done.40, f32[2,32,128]{2,1,0:T(8,128)} %bitcast.75, ...), custom_call_target="tpu_custom_call" | custom-call | flops 1610612736 | bytes 4194304 | tf_op jit(solution)/shard_map/compress/pallas_call | solution.py:276
  463.5 19.9 %collective-permute-done.32.refs_5_ = f32[16,2,32,128]{3,2,1,0:T(8,128)S(1)} collective-permute-done((f32[16,2,32,128]{3,2,1,0:T(8,128)}, f32[16,2,32,128]{3,2,1,0:T(8,128)S(1)}, u32[]{:S(2)}, u32[]{:S(2)}) %collective-permute-start.32) | collective-permute-done | bytes 524320 | tf_op jit(solution)/shard_map/ppermute | solution.py:697
  489.2 8.6 %all-to-all-start.7 = ((f32[32,2,64,128]{3,2,1,0:T(8,128)}), f32[32,2,64,128]{3,2,1,0:T(8,128)}, u32[]{:S(2)}, u32[]{:S(2)}) async-start(f32[32,2,64,128]{3,2,1,0:T(8,128)} %compress.15), calls=%async_computation.7 | async-start | bytes 4194304 | tf_op jit(solution)/shard_map/all_to_all | solution.py:730
  518.2 7.9 %azimuth6.1 = (f32[16,2,128,128]{3,2,1,0:T(8,128)}, f32[16,2,32,128]{3,2,1,0:T(8,128)}, f32[16,2,32,128]{3,2,1,0:T(8,128)}) custom-call(f32[4,8,2,4,16,128]{5,4,3,2,1,0:T(8,128)} %bitcast.37, f32[2,128,128]{2,1,0:T(8,128)} %constant.83.clone.tw_ref, bf16[256,256]{1,0:T(8,128)(2,1)} %constant.84.clone.fwd_ref, bf16[256,256]{1,0:T(8,128)(2,1)} %constant.29.clone.refs_7_.fwd_low_ref), custom_call_target="tpu_custom_call" | custom-call | flops 805306368 | bytes 4194304 | tf_op jit(solution)/shard_map/azimuth6/pallas_call | solution.py:358
  526.1 26.3 %all-to-all-done.7 = f32[32,2,64,128]{3,2,1,0:T(8,128)} async-done(((f32[32,2,64,128]{3,2,1,0:T(8,128)}), f32[32,2,64,128]{3,2,1,0:T(8,128)}, u32[]{:S(2)}, u32[]{:S(2)}) %all-to-all-start.7) | async-done | bytes 2097184 | tf_op jit(solution)/shard_map/all_to_all | solution.py:730
  578.6 34.9 %final_inner.1 = (f32[2,128,16384]{2,1,0:T(8,128)}, bf16[8,16,256,256]{3,2,1,0:T(8,128)(2,1)}) custom-call(f32[16,2,128,128]{3,2,1,0:T(8,128)} %get-tuple-element.319.refs_0_, f32[16,2,128,128]{3,2,1,0:T(8,128)} %get-tuple-element.351.refs_1_, f32[16,2,128,128]{3,2,1,0:T(8,128)} %get-tuple-element.386.refs_2_, ...), custom_call_target="tpu_custom_call" | custom-call | flops 9663676416 | bytes 29360128 | tf_op jit(solution)/shard_map/final_inner/pallas_call | solution.py:618
  615.0 30.7 %final_wide.1 = f32[2,128,16384]{2,1,0:T(8,128)} custom-call(bf16[8,16,256,256]{3,2,1,0:T(8,128)(2,1)} %get-tuple-element.469.refs_0_, f32[16,2,32,128]{3,2,1,0:T(8,128)} %copy-done.7, f32[16,2,32,128]{3,2,1,0:T(8,128)} %copy-done.9, f32[16,2,32,128]{3,2,1,0:T(8,128)} %copy-done.11, f32[16,2,32,128]{3,2,1,0:T(8,128)} %copy-done.13, ...), custom_call_target="tpu_custom_call", output_to_operand_aliasing={{}: (26, {})} | custom-call | flops 9663676416 | bytes 29360128 | tf_op jit(solution)/shard_map/final_wide/pallas_call | solution.py:618
  (213 shorter events, 221.4 us)
Async XLA Ops:
  60.6 54.1 %all-to-all-start = ((f32[32,2,64,128]{3,2,1,0:T(8,128)}), f32[32,2,64,128]{3,2,1,0:T(8,128)S(1)}, u32[]{:S(2)}, u32[]{:S(2)}) async-start(f32[32,2,64,128]{3,2,1,0:T(8,128)} %compress.8), calls=%async_computation | async-start | bytes 4194304 | tf_op jit(solution)/shard_map/all_to_all | solution.py:730
  67.9 44.7 %collective-permute-start.8 = (f32[2,8,64,128]{3,2,1,0:T(8,128)}, f32[2,8,64,128]{3,2,1,0:T(8,128)}, u32[]{:S(2)}, u32[]{:S(2)}) collective-permute-start(f32[2,8,64,128]{3,2,1,0:T(8,128)} %get-tuple-element.287), channel_id=1, source_target_pairs={{0,24},{8,16},{16,8},{24,0},{1,25},{9,17},{17,9},{25,1},{2,26},{10... | collective-permute-start | bytes 1572872 | tf_op jit(solution)/shard_map/ppermute | solution.py:688
  116.1 55.7 %all-to-all-start.1 = ((f32[32,2,64,128]{3,2,1,0:T(8,128)}), f32[32,2,64,128]{3,2,1,0:T(8,128)S(1)}, u32[]{:S(2)}, u32[]{:S(2)}) async-start(f32[32,2,64,128]{3,2,1,0:T(8,128)} %compress.9), calls=%async_computation.1 | async-start | bytes 4194304 | tf_op jit(solution)/shard_map/all_to_all | solution.py:730
  121.4 44.4 %collective-permute-start.10 = (f32[2,8,64,128]{3,2,1,0:T(8,128)}, f32[2,8,64,128]{3,2,1,0:T(8,128)}, u32[]{:S(2)}, u32[]{:S(2)}) collective-permute-start(f32[2,8,64,128]{3,2,1,0:T(8,128)} %get-tuple-element.303), channel_id=1, source_target_pairs={{0,16},{8,24},{16,0},{24,8},{1,17},{9,25},{17,1},{25,9},{2,18},{10... | collective-permute-start | bytes 1572872 | tf_op jit(solution)/shard_map/ppermute | solution.py:688
  121.7 44.1 %collective-permute-start.11 = (f32[2,8,64,128]{3,2,1,0:T(8,128)}, f32[2,8,64,128]{3,2,1,0:T(8,128)}, u32[]{:S(2)}, u32[]{:S(2)}) collective-permute-start(f32[2,8,64,128]{3,2,1,0:T(8,128)} %get-tuple-element.304), channel_id=1, source_target_pairs={{0,24},{8,16},{16,8},{24,0},{1,25},{9,17},{17,9},{25,1},{2,26},{10... | collective-permute-start | bytes 1572872 | tf_op jit(solution)/shard_map/ppermute | solution.py:688
  124.4 47.3 %collective-permute-start.9 = (f32[2,8,64,128]{3,2,1,0:T(8,128)S(1)}, f32[2,8,64,128]{3,2,1,0:T(8,128)}, u32[]{:S(2)}, u32[]{:S(2)}) collective-permute-start(f32[2,8,64,128]{3,2,1,0:T(8,128)S(1)} %copy-done.32), channel_id=1, source_target_pairs={{0,8},{8,0},{16,24},{24,16},{1,9},{9,1},{17,25},{25,17},{2,10},{10... | collective-permute-start | bytes 1572872 | tf_op jit(solution)/shard_map/ppermute | solution.py:688
  173.0 58.7 %all-to-all-start.2 = ((f32[32,2,64,128]{3,2,1,0:T(8,128)}), f32[32,2,64,128]{3,2,1,0:T(8,128)S(1)}, u32[]{:S(2)}, u32[]{:S(2)}) async-start(f32[32,2,64,128]{3,2,1,0:T(8,128)} %compress.10), calls=%async_computation.2 | async-start | bytes 4194304 | tf_op jit(solution)/shard_map/all_to_all | solution.py:730
  179.3 50.5 %collective-permute-start.14 = (f32[2,8,64,128]{3,2,1,0:T(8,128)}, f32[2,8,64,128]{3,2,1,0:T(8,128)}, u32[]{:S(2)}, u32[]{:S(2)}) collective-permute-start(f32[2,8,64,128]{3,2,1,0:T(8,128)} %get-tuple-element.331), channel_id=1, source_target_pairs={{0,24},{8,16},{16,8},{24,0},{1,25},{9,17},{17,9},{25,1},{2,26},{10... | collective-permute-start | bytes 1572872 | tf_op jit(solution)/shard_map/ppermute | solution.py:688
  180.8 49.1 %collective-permute-start.18 = (f32[16,2,32,128]{3,2,1,0:T(8,128)}, f32[16,2,32,128]{3,2,1,0:T(8,128)S(1)}, u32[]{:S(2)}, u32[]{:S(2)}) collective-permute-start(f32[16,2,32,128]{3,2,1,0:T(8,128)} %get-tuple-element.378), channel_id=1, source_target_pairs={{0,1},{1,2},{2,3},{3,4},{4,5},{5,6},{6,7},{7,8},{8,9},{9,10},{10,1... | collective-permute-start | bytes 1572872 | tf_op jit(solution)/shard_map/ppermute | solution.py:697
  182.7 47.2 %collective-permute-start.19 = (f32[16,2,32,128]{3,2,1,0:T(8,128)}, f32[16,2,32,128]{3,2,1,0:T(8,128)S(1)}, u32[]{:S(2)}, u32[]{:S(2)}) collective-permute-start(f32[16,2,32,128]{3,2,1,0:T(8,128)} %get-tuple-element.379), channel_id=1, source_target_pairs={{1,0},{2,1},{3,2},{4,3},{5,4},{6,5},{7,6},{8,7},{9,8},{10,9},{11,1... | collective-permute-start | bytes 1572872 | tf_op jit(solution)/shard_map/ppermute | solution.py:698
  233.0 63.2 %all-to-all-start.3 = ((f32[32,2,64,128]{3,2,1,0:T(8,128)}), f32[32,2,64,128]{3,2,1,0:T(8,128)}, u32[]{:S(2)}, u32[]{:S(2)}) async-start(f32[32,2,64,128]{3,2,1,0:T(8,128)} %compress.11), calls=%async_computation.3 | async-start | bytes 4194304 | tf_op jit(solution)/shard_map/all_to_all | solution.py:730
  243.7 50.3 %collective-permute-start.17 = (f32[2,8,64,128]{3,2,1,0:T(8,128)}, f32[2,8,64,128]{3,2,1,0:T(8,128)S(1)}, u32[]{:S(2)}, u32[]{:S(2)}) collective-permute-start(f32[2,8,64,128]{3,2,1,0:T(8,128)} %get-tuple-element.363), channel_id=1, source_target_pairs={{0,24},{8,16},{16,8},{24,0},{1,25},{9,17},{17,9},{25,1},{2,26},{10... | collective-permute-start | bytes 1572872 | tf_op jit(solution)/shard_map/ppermute | solution.py:688
  245.2 48.9 %collective-permute-start.23 = (f32[16,2,32,128]{3,2,1,0:T(8,128)}, f32[16,2,32,128]{3,2,1,0:T(8,128)S(1)}, u32[]{:S(2)}, u32[]{:S(2)}) collective-permute-start(f32[16,2,32,128]{3,2,1,0:T(8,128)} %get-tuple-element.413), channel_id=1, source_target_pairs={{0,1},{1,2},{2,3},{3,4},{4,5},{5,6},{6,7},{7,8},{8,9},{9,10},{10,1... | collective-permute-start | bytes 1572872 | tf_op jit(solution)/shard_map/ppermute | solution.py:697
  247.1 47.0 %collective-permute-start.24 = (f32[16,2,32,128]{3,2,1,0:T(8,128)}, f32[16,2,32,128]{3,2,1,0:T(8,128)S(1)}, u32[]{:S(2)}, u32[]{:S(2)}) collective-permute-start(f32[16,2,32,128]{3,2,1,0:T(8,128)} %get-tuple-element.414), channel_id=1, source_target_pairs={{1,0},{2,1},{3,2},{4,3},{5,4},{6,5},{7,6},{8,7},{9,8},{10,9},{11,1... | collective-permute-start | bytes 1572872 | tf_op jit(solution)/shard_map/ppermute | solution.py:698
  296.2 63.6 %all-to-all-start.4 = ((f32[32,2,64,128]{3,2,1,0:T(8,128)}), f32[32,2,64,128]{3,2,1,0:T(8,128)S(1)}, u32[]{:S(2)}, u32[]{:S(2)}) async-start(f32[32,2,64,128]{3,2,1,0:T(8,128)} %compress.12), calls=%async_computation.4 | async-start | bytes 4194304 | tf_op jit(solution)/shard_map/all_to_all | solution.py:730
  307.4 50.5 %collective-permute-start.22 = (f32[2,8,64,128]{3,2,1,0:T(8,128)}, f32[2,8,64,128]{3,2,1,0:T(8,128)}, u32[]{:S(2)}, u32[]{:S(2)}) collective-permute-start(f32[2,8,64,128]{3,2,1,0:T(8,128)} %get-tuple-element.398), channel_id=1, source_target_pairs={{0,24},{8,16},{16,8},{24,0},{1,25},{9,17},{17,9},{25,1},{2,26},{10... | collective-permute-start | bytes 1572872 | tf_op jit(solution)/shard_map/ppermute | solution.py:688
  308.8 49.1 %collective-permute-start.25 = (f32[16,2,32,128]{3,2,1,0:T(8,128)}, f32[16,2,32,128]{3,2,1,0:T(8,128)S(1)}, u32[]{:S(2)}, u32[]{:S(2)}) collective-permute-start(f32[16,2,32,128]{3,2,1,0:T(8,128)} %get-tuple-element.428), channel_id=1, source_target_pairs={{0,1},{1,2},{2,3},{3,4},{4,5},{5,6},{6,7},{7,8},{8,9},{9,10},{10,1... | collective-permute-start | bytes 1572872 | tf_op jit(solution)/shard_map/ppermute | solution.py:697
  310.8 47.2 %collective-permute-start.26 = (f32[16,2,32,128]{3,2,1,0:T(8,128)}, f32[16,2,32,128]{3,2,1,0:T(8,128)S(1)}, u32[]{:S(2)}, u32[]{:S(2)}) collective-permute-start(f32[16,2,32,128]{3,2,1,0:T(8,128)} %get-tuple-element.429), channel_id=1, source_target_pairs={{1,0},{2,1},{3,2},{4,3},{5,4},{6,5},{7,6},{8,7},{9,8},{10,9},{11,1... | collective-permute-start | bytes 1572872 | tf_op jit(solution)/shard_map/ppermute | solution.py:698
  361.1 63.2 %all-to-all-start.5 = ((f32[32,2,64,128]{3,2,1,0:T(8,128)}), f32[32,2,64,128]{3,2,1,0:T(8,128)}, u32[]{:S(2)}, u32[]{:S(2)}) async-start(f32[32,2,64,128]{3,2,1,0:T(8,128)} %compress.13), calls=%async_computation.5 | async-start | bytes 4194304 | tf_op jit(solution)/shard_map/all_to_all | solution.py:730
  371.8 50.3 %collective-permute-start.29 = (f32[2,8,64,128]{3,2,1,0:T(8,128)}, f32[2,8,64,128]{3,2,1,0:T(8,128)S(1)}, u32[]{:S(2)}, u32[]{:S(2)}) collective-permute-start(f32[2,8,64,128]{3,2,1,0:T(8,128)} %get-tuple-element.438), channel_id=1, source_target_pairs={{0,24},{8,16},{16,8},{24,0},{1,25},{9,17},{17,9},{25,1},{2,26},{10... | collective-permute-start | bytes 1572872 | tf_op jit(solution)/shard_map/ppermute | solution.py:688
  373.3 48.9 %collective-permute-start.30 = (f32[16,2,32,128]{3,2,1,0:T(8,128)}, f32[16,2,32,128]{3,2,1,0:T(8,128)S(1)}, u32[]{:S(2)}, u32[]{:S(2)}) collective-permute-start(f32[16,2,32,128]{3,2,1,0:T(8,128)} %get-tuple-element.445), channel_id=1, source_target_pairs={{0,1},{1,2},{2,3},{3,4},{4,5},{5,6},{6,7},{7,8},{8,9},{9,10},{10,1... | collective-permute-start | bytes 1572872 | tf_op jit(solution)/shard_map/ppermute | solution.py:697
  375.2 47.0 %collective-permute-start.31 = (f32[16,2,32,128]{3,2,1,0:T(8,128)}, f32[16,2,32,128]{3,2,1,0:T(8,128)S(1)}, u32[]{:S(2)}, u32[]{:S(2)}) collective-permute-start(f32[16,2,32,128]{3,2,1,0:T(8,128)} %get-tuple-element.446), channel_id=1, source_target_pairs={{1,0},{2,1},{3,2},{4,3},{5,4},{6,5},{7,6},{8,7},{9,8},{10,9},{11,1... | collective-permute-start | bytes 1572872 | tf_op jit(solution)/shard_map/ppermute | solution.py:698
  424.3 63.6 %all-to-all-start.6 = ((f32[32,2,64,128]{3,2,1,0:T(8,128)}), f32[32,2,64,128]{3,2,1,0:T(8,128)S(1)}, u32[]{:S(2)}, u32[]{:S(2)}) async-start(f32[32,2,64,128]{3,2,1,0:T(8,128)} %compress.14), calls=%async_computation.6 | async-start | bytes 4194304 | tf_op jit(solution)/shard_map/all_to_all | solution.py:730
  433.4 50.0 %collective-permute-start.32 = (f32[16,2,32,128]{3,2,1,0:T(8,128)}, f32[16,2,32,128]{3,2,1,0:T(8,128)S(1)}, u32[]{:S(2)}, u32[]{:S(2)}) collective-permute-start(f32[16,2,32,128]{3,2,1,0:T(8,128)} %get-tuple-element.457), channel_id=1, source_target_pairs={{0,1},{1,2},{2,3},{3,4},{4,5},{5,6},{6,7},{7,8},{8,9},{9,10},{10,1... | collective-permute-start | bytes 1572872 | tf_op jit(solution)/shard_map/ppermute | solution.py:697
  435.4 47.9 %collective-permute-start.33 = (f32[16,2,32,128]{3,2,1,0:T(8,128)}, f32[16,2,32,128]{3,2,1,0:T(8,128)S(1)}, u32[]{:S(2)}, u32[]{:S(2)}) collective-permute-start(f32[16,2,32,128]{3,2,1,0:T(8,128)} %get-tuple-element.458), channel_id=1, source_target_pairs={{1,0},{2,1},{3,2},{4,3},{5,4},{6,5},{7,6},{8,7},{9,8},{10,9},{11,1... | collective-permute-start | bytes 1572872 | tf_op jit(solution)/shard_map/ppermute | solution.py:698
  489.2 63.2 %all-to-all-start.7 = ((f32[32,2,64,128]{3,2,1,0:T(8,128)}), f32[32,2,64,128]{3,2,1,0:T(8,128)}, u32[]{:S(2)}, u32[]{:S(2)}) async-start(f32[32,2,64,128]{3,2,1,0:T(8,128)} %compress.15), calls=%async_computation.7 | async-start | bytes 4194304 | tf_op jit(solution)/shard_map/all_to_all | solution.py:730
  505.8 65.5 %collective-permute-start.34 = (f32[16,2,32,128]{3,2,1,0:T(8,128)S(1)}, f32[16,2,32,128]{3,2,1,0:T(8,128)S(1)}, u32[]{:S(2)}, u32[]{:S(2)}) collective-permute-start(f32[16,2,32,128]{3,2,1,0:T(8,128)S(1)} %copy-done.31), channel_id=1, source_target_pairs={{0,1},{1,2},{2,3},{3,4},{4,5},{5,6},{6,7},{7,8},{8,9},{9,10},{10,1... | collective-permute-start | bytes 1572872 | tf_op jit(solution)/shard_map/ppermute | solution.py:697
  511.1 102.4 %collective-permute-start.37 = (f32[16,2,32,128]{3,2,1,0:T(8,128)S(1)}, f32[16,2,32,128]{3,2,1,0:T(8,128)S(1)}, u32[]{:S(2)}, u32[]{:S(2)}) collective-permute-start(f32[16,2,32,128]{3,2,1,0:T(8,128)S(1)} %copy-done.30), channel_id=1, source_target_pairs={{1,0},{2,1},{3,2},{4,3},{5,4},{6,5},{7,6},{8,7},{9,8},{10,9},{11,1... | collective-permute-start | bytes 1572872 | tf_op jit(solution)/shard_map/ppermute | solution.py:698
  560.2 53.3 %collective-permute-start.36 = (f32[16,2,32,128]{3,2,1,0:T(8,128)}, f32[16,2,32,128]{3,2,1,0:T(8,128)S(1)}, u32[]{:S(2)}, u32[]{:S(2)}) collective-permute-start(f32[16,2,32,128]{3,2,1,0:T(8,128)} %get-tuple-element.477), channel_id=1, source_target_pairs={{0,1},{1,2},{2,3},{3,4},{4,5},{5,6},{6,7},{7,8},{8,9},{9,10},{10,1... | collective-permute-start | bytes 1572872 | tf_op jit(solution)/shard_map/ppermute | solution.py:697
  562.2 51.4 %collective-permute-start.39 = (f32[16,2,32,128]{3,2,1,0:T(8,128)}, f32[16,2,32,128]{3,2,1,0:T(8,128)S(1)}, u32[]{:S(2)}, u32[]{:S(2)}) collective-permute-start(f32[16,2,32,128]{3,2,1,0:T(8,128)} %get-tuple-element.485), channel_id=1, source_target_pairs={{1,0},{2,1},{3,2},{4,3},{5,4},{6,5},{7,6},{8,7},{9,8},{10,9},{11,1... | collective-permute-start | bytes 1572872 | tf_op jit(solution)/shard_map/ppermute | solution.py:698
  569.4 44.2 %collective-permute-start.35 = (f32[16,2,32,128]{3,2,1,0:T(8,128)}, f32[16,2,32,128]{3,2,1,0:T(8,128)S(1)}, u32[]{:S(2)}, u32[]{:S(2)}) collective-permute-start(f32[16,2,32,128]{3,2,1,0:T(8,128)} %get-tuple-element.476), channel_id=1, source_target_pairs={{0,1},{1,2},{2,3},{3,4},{4,5},{5,6},{6,7},{7,8},{8,9},{9,10},{10,1... | collective-permute-start | bytes 1572872 | tf_op jit(solution)/shard_map/ppermute | solution.py:697
  571.3 42.3 %collective-permute-start.38 = (f32[16,2,32,128]{3,2,1,0:T(8,128)}, f32[16,2,32,128]{3,2,1,0:T(8,128)S(1)}, u32[]{:S(2)}, u32[]{:S(2)}) collective-permute-start(f32[16,2,32,128]{3,2,1,0:T(8,128)} %get-tuple-element.484), channel_id=1, source_target_pairs={{1,0},{2,1},{3,2},{4,3},{5,4},{6,5},{7,6},{8,7},{9,8},{10,9},{11,1... | collective-permute-start | bytes 1572872 | tf_op jit(solution)/shard_map/ppermute | solution.py:698
  (64 other events, 1582.8 us)

commit v4 on v3

--- a/solution.py
+++ b/solution.py
@@ -19,6 +19,7 @@
 RG1 = NRG // LANES
 CHUNKS = 8
 PER_CHUNK = LANES // CHUNKS
+GROUPED = ((0,), (1,), (2, 3), (4, 5), (6,), (7,))
 VMEM_LIMIT = 60 << 20
 BF16 = jnp.bfloat16
 F32 = jnp.float32
@@ -114,40 +115,39 @@
             finish(ka + outer * kb, value)
 
 
-def pack_kernel(chunks, parts, per_part, rows_in, rank_ref, x_ref, *out_refs):
+def pack_kernel(groups, parts, per_part, rows_in, rank_ref, x_ref, *out_refs):
     rank = rank_ref[0]
     for j in range(parts):
         part = jnp.bitwise_xor(rank, j)
-        for at, c in enumerate(chunks):
-            for m in range(per_part):
-                start = CHUNKS * (part * per_part + m) + c
-                for ri in range(2):
-                    out_refs[at * parts + j][ri, 0, m * rows_in : (m + 1) * rows_in, :] = x_ref[
-                        ri, pl.ds(start, rows_in, stride=LANES), :
-                    ]
-
-
-def pack(raw, rank, parts, chunks):
+        for g, chunks in enumerate(groups):
+            for at, c in enumerate(chunks):
+                for m in range(per_part):
+                    start = CHUNKS * (part * per_part + m) + c
+                    to = (at * per_part + m) * rows_in
+                    for ri in range(2):
+                        out_refs[g * parts + j][ri, 0, to : to + rows_in, :] = x_ref[
+                            ri, pl.ds(start, rows_in, stride=LANES), :
+                        ]
+
+
+def pack(raw, rank, parts, groups):
     lines, bins = raw.shape[1], raw.shape[2]
     rows_in, tiles, per_part = lines // LANES, bins // LANES, PER_CHUNK // parts
-    rows = per_part * rows_in
-    count = len(chunks) * parts
-    shape = jax.ShapeDtypeStruct((2, tiles, rows, LANES), F32)
-    spec = pl.BlockSpec((2, 1, rows, LANES), lambda i: (0, i, 0, 0))
+    heights = [len(chunks) * per_part * rows_in for chunks in groups for _ in range(parts)]
     flat = pl.pallas_call(
-        functools.partial(pack_kernel, chunks, parts, per_part, rows_in),
+        functools.partial(pack_kernel, groups, parts, per_part, rows_in),
         grid=(tiles,),
         in_specs=[
             pl.BlockSpec(memory_space=pltpu.SMEM),
             pl.BlockSpec((2, lines, LANES), lambda i: (0, 0, i)),
         ],
-        out_specs=[spec] * count,
-        out_shape=[shape] * count,
+        out_specs=[pl.BlockSpec((2, 1, rows, LANES), lambda i: (0, i, 0, 0)) for rows in heights],
+        out_shape=[jax.ShapeDtypeStruct((2, tiles, rows, LANES), F32) for rows in heights],
         compiler_params=pltpu.CompilerParams(vmem_limit_bytes=VMEM_LIMIT),
         cost_estimate=pl.CostEstimate(flops=0, bytes_accessed=16 * lines * bins, transcendentals=0),
         name="pack",
     )(rank, raw)
-    return [flat[i * parts : (i + 1) * parts] for i in range(len(chunks))]
+    return [flat[i * parts : (i + 1) * parts] for i in range(len(groups))]
 
 
 STEP = 16
@@ -212,7 +212,7 @@
 
     lax.fori_loop(0, rows // STEP, forward, 0)
 
-    group = max(1, LANES // rows)
+    group = max(1, 2 * LANES // rows)
 
     def middle(i, carry):
         at = pl.ds(pl.multiple_of(i * group * rows, group * rows), group * rows)
@@ -259,7 +259,7 @@
 def compress(pieces, rank, chirp):
     parts = len(pieces)
     _, tiles, rows, _ = pieces[0].shape
-    block = min(rows, 32)
+    block = min(rows, 64)
     ids = np.arange(RG1)[:, None] * np.arange(LANES)[None, :]
     tw = jnp.asarray(np.stack(unit(ids, NRG, -1.0)), F32)
     fwd, fwd_low = right_tables(-1.0)
@@ -298,12 +298,12 @@
 
 def azimuth_kernel(chunk, x_ref, tw_ref, fwd_ref, fwd_low_ref, out_ref, up_ref, down_ref, t_ref, mid_ref):
     part = pl.program_id(0)
-    pieces, per_part, bins = x_ref.shape[1], x_ref.shape[3], x_ref.shape[5]
-
-    def stage(m, carry):
+    pieces, per_part, bins = x_ref.shape[1], x_ref.shape[4], x_ref.shape[6]
+
+    def stage(m):
         sides = []
         for ri in range(2):
-            column = jnp.concatenate([x_ref[0, a, ri, m] for a in range(pieces)], axis=0)
+            column = jnp.concatenate([x_ref[0, a, ri, 0, m] for a in range(pieces)], axis=0)
             sides.append(split(jnp.transpose(column)))
         high = jnp.concatenate([sides[0][0], sides[1][0]], axis=1)
         low = jnp.concatenate([sides[0][1], sides[1][1]], axis=1)
@@ -314,9 +314,9 @@
         a, b = y[:, 0:LANES], y[:, LANES : 2 * LANES]
         t_ref[index, 0] = a * wr - b * wi
         t_ref[index, 1] = a * wi + b * wr
-        return carry
-
-    lax.fori_loop(0, per_part, stage, 0)
+
+    for m in range(per_part):
+        stage(m)
 
     @pl.when(part == pl.num_programs(0) - 1)
     def _():
@@ -346,8 +346,8 @@
         lax.fori_loop(0, PER_CHUNK, edges, 0)
 
 
-def azimuth(x, chunk):
-    parts, pieces, _, per_part, rows_in, bins = x.shape
+def azimuth(x, chunk, place):
+    parts, pieces, _, _, per_part, rows_in, bins = x.shape
     ids = np.arange(LANES)
     tw = jnp.asarray(np.stack(unit(ids[:, None] * ids[None, :], NAZ, -1.0)), F32)
     fwd, fwd_low = right_tables(-1.0)
@@ -360,7 +360,8 @@
         grid=(parts,),
         in_specs=[
             pl.BlockSpec(
-                (1, pieces, 2, per_part, rows_in, bins), lambda i: (i, 0, 0, 0, 0, 0)
+                (1, pieces, 2, 1, per_part, rows_in, bins),
+                lambda i: (i, 0, 0, place, 0, 0, 0),
             )
         ]
         + [whole_spec(a) for a in consts],
@@ -460,13 +461,33 @@
     phase_refs = take(CHUNKS // 2)
     mover_refs = take(2 if wide else 1)
     inv1_ref, inv2_ref, tw_ref = take(3)
-    out_ref, own_ref, zr_ref, zi_ref, s_ref, swap_ref = refs[-7:-1] if wide else refs[-6:]
+    out_ref, own_ref, zr_ref, zi_ref, s_ref, swap_ref, half_ref = (
+        refs[-8:-1] if wide else refs[-7:]
+    )
     halo_ref = refs[-1]
     if not joins:
         own_ref = sources[0]
     own = own_ref.shape[2] // 2
     rows = phase_refs[0].shape[3]
     step = pl.program_id(0)
+
+    def first_half(block):
+        base = jnp.minimum(block * BB, rows - BB)
+        for j in range(BB // QUAD):
+            cols = []
+            for t in range(QUAD):
+                at = base + QUAD * j + t
+                cols.append(jnp.concatenate([zr_ref[at], zi_ref[at]], axis=0))
+            hi, lo = split(jnp.concatenate(cols, axis=1))
+            w = dot(inv1_ref[...], jnp.concatenate([hi, lo, hi], axis=0))
+            turned = []
+            for t in range(QUAD):
+                a = w[0:LANES, t * LANES : (t + 1) * LANES]
+                b = w[LANES : 2 * LANES, t * LANES : (t + 1) * LANES]
+                wr, wi = tw_ref[0], tw_ref[1]
+                turned.append(jnp.concatenate([a * wr - b * wi, a * wi + b * wr], axis=1))
+            hi, lo = split(jnp.concatenate(turned, axis=0))
+            half_ref[j] = jnp.concatenate([hi, lo, hi], axis=1)
 
     @pl.when(step < steps)
     def _():
@@ -506,51 +527,31 @@
                 zr_ref[at, to, :] = jnp.swapaxes(swap_ref[buf, 0, :, at, :], 0, 1)
                 zi_ref[at, to, :] = jnp.swapaxes(swap_ref[buf, 1, :, at, :], 0, 1)
 
-        def first(i, carry):
-            one(2 * i, 0)
-            one(2 * i + 1, 1)
-            return carry
-
-        lax.fori_loop(0, KB // 2, first, 0)
-
-    @pl.when(step >= steps)
+        for kk in range(KB):
+            one(kk, kk % 2)
+
+    @pl.when(step > steps)
     def _():
-        base = (step - steps) * BB
-
-        def some(j, carry):
-            cols = []
-            for t in range(QUAD):
-                at = base + QUAD * j + t
-                cols.append(jnp.concatenate([zr_ref[at], zi_ref[at]], axis=0))
-            hi, lo = split(jnp.concatenate(cols, axis=1))
-            w = dot(inv1_ref[...], jnp.concatenate([hi, lo, hi], axis=0))
-            turned = []
-            for t in range(QUAD):
-                a = w[0:LANES, t * LANES : (t + 1) * LANES]
-                b = w[LANES : 2 * LANES, t * LANES : (t + 1) * LANES]
-                wr, wi = tw_ref[0], tw_ref[1]
-                turned.append(jnp.concatenate([a * wr - b * wi, a * wi + b * wr], axis=1))
-            hi, lo = split(jnp.concatenate(turned, axis=0))
+        for j in range(BB // QUAD):
             image = lax.dot_general(
-                inv2_ref[...],
-                jnp.concatenate([hi, lo, hi], axis=1),
-                (((1,), (1,)), ((), ())),
-                preferred_element_type=F32,
+                inv2_ref[...], half_ref[j], (((1,), (1,)), ((), ())), preferred_element_type=F32
             )
             for t in range(QUAD):
                 for ri in range(2):
                     s_ref[ri, QUAD * j + t] = image[
                         ri * LANES : (ri + 1) * LANES, t * LANES : (t + 1) * LANES
                     ]
-            return carry
-
-        lax.fori_loop(0, BB // QUAD, some, 0)
+        first_half(step - steps)
         for ri in range(2):
             for start in range(0, LANES, 8):
                 lines = jnp.swapaxes(s_ref[ri, :, start : start + 8, :], 0, 1)
                 for n in range(8):
                     at = (start + n) * LANES
                     out_ref[ri, :, at : at + LANES] = lines[n]
+
+    @pl.when(step == steps)
+    def _():
+        first_half(0)
 
 
 def final(bins, places, sources, lows, highs, phases, movers, image=None):
@@ -579,7 +580,7 @@
         return (0, jnp.minimum(i, steps - 1), 0, 0)
 
     def late(i):
-        at = jnp.maximum(i - steps, 0)
+        at = jnp.maximum(i - steps - 1, 0)
         return (0, start + at + jnp.where(at >= gap_at, gap, 0), 0)
 
     joined = (CHUNKS, PER_CHUNK, 2 * bins, 2 * LANES)
@@ -611,13 +612,14 @@
         pltpu.VMEM((rows, LANES, LANES), F32),
         pltpu.VMEM((2, BB, LANES, LANES), F32),
         pltpu.VMEM((2, 2, CHUNKS, rows, LANES), F32),
+        pltpu.VMEM((BB // QUAD, QUAD * LANES, 6 * LANES), BF16),
     ]
     if wide:
         scratch.append(pltpu.VMEM((2, CHUNKS, 4 * HALO, 2 * LANES), BF16))
     points = NAZ * rows
     return pl.pallas_call(
         functools.partial(final_kernel, steps, joins, wide),
-        grid=(steps + len(places),),
+        grid=(steps + 1 + len(places),),
         in_specs=specs,
         out_specs=out_specs,
         out_shape=shapes,
@@ -675,27 +677,27 @@
     bins = NRG // devices
     rows_in = raw_echo.shape[1] // LANES
     per_part = PER_CHUNK // nrng
-    rows = per_part * rows_in
     chirp = chirp_spectrum.reshape(2, LANES, RG1).transpose(0, 2, 1)
     rate = jnp.broadcast_to((azimuth_rate * 0.5)[:, None], (bins, LANES))
     rank = lax.axis_index("rng").astype(jnp.int32).reshape(1)
-    packed = pack(raw_echo, rank, nrng, [0]) + pack(raw_echo, rank, nrng, list(range(1, CHUNKS)))
-    mains, lows, highs = [], [], []
+    packed = pack(raw_echo, rank, nrng, GROUPED[:1]) + pack(raw_echo, rank, nrng, GROUPED[1:])
+    mains, lows, highs = [None] * CHUNKS, [None] * CHUNKS, [None] * CHUNKS
     turned = []
 
-    def gather(c):
-        return [packed[c][0]] + [
-            lax.ppermute(packed[c][j], "rng", [(i, i ^ j) for i in range(nrng)])
+    def gather(g):
+        return [packed[g][0]] + [
+            lax.ppermute(packed[g][j], "rng", [(i, i ^ j) for i in range(nrng)])
             for j in range(1, nrng)
         ]
 
-    def transform(c):
-        if c > 0:
-            turned[c], mains[c - 1] = lax.optimization_barrier((turned[c], mains[c - 1]))
-        main, up, down = azimuth(turned[c], c)
-        mains.append(main)
-        lows.append(lax.ppermute(up, axes, neighbours(axes, devices, 1)))
-        highs.append(lax.ppermute(down, axes, neighbours(axes, devices, -1)))
+    def transform(g):
+        for place, c in enumerate(GROUPED[g]):
+            if c > 0:
+                turned[g], mains[c - 1] = lax.optimization_barrier((turned[g], mains[c - 1]))
+            main, up, down = azimuth(turned[g], c, place)
+            mains[c] = main
+            lows[c] = lax.ppermute(up, axes, neighbours(axes, devices, 1))
+            highs[c] = lax.ppermute(down, axes, neighbours(axes, devices, -1))
 
     places = row_sets(bins)
     rates = [rate[bins_of(p)] for p in places]
@@ -703,34 +705,37 @@
     got = [gather(0)]
     packed[1], got[0] = lax.optimization_barrier((packed[1], got[0]))
     got.append(gather(1))
-    for c in range(CHUNKS):
-        lines = compress(got[c], rank, chirp)
-        if c + 1 < CHUNKS:
-            lines, got[c + 1] = lax.optimization_barrier((lines, got[c + 1]))
-        if c + 2 < CHUNKS:
-            packed[c + 2], got[c + 1] = lax.optimization_barrier((packed[c + 2], got[c + 1]))
-            if c >= 1:
-                held = (packed[c + 2], turned[c - 1])
-                packed[c + 2], turned[c - 1] = lax.optimization_barrier(held)
-            got.append(gather(c + 2))
-        if c >= 2:
-            transform(c - 2)
-            lines, mains[c - 2] = lax.optimization_barrier((lines, mains[c - 2]))
-            if c - 2 < CHUNKS // 2:
-                rates, turned[c - 2] = lax.optimization_barrier((rates, turned[c - 2]))
-                table = phase_tables(rates, c - 2)
+    count = len(GROUPED)
+    for g, chunks in enumerate(GROUPED):
+        lines = compress(got[g], rank, chirp)
+        if g + 1 < count:
+            lines, got[g + 1] = lax.optimization_barrier((lines, got[g + 1]))
+        if g + 2 < count:
+            packed[g + 2], got[g + 1] = lax.optimization_barrier((packed[g + 2], got[g + 1]))
+            if g >= 1:
+                held = (packed[g + 2], turned[g - 1])
+                packed[g + 2], turned[g - 1] = lax.optimization_barrier(held)
+            got.append(gather(g + 2))
+        if g >= 2:
+            transform(g - 2)
+            for c in GROUPED[g - 2]:
+                lines, mains[c] = lax.optimization_barrier((lines, mains[c]))
+        if g >= 3:
+            for c in GROUPED[g - 3]:
+                held = (lines, lows[c], highs[c])
+                lines, lows[c], highs[c] = lax.optimization_barrier(held)
+            for _ in range(2 if len(phases) < CHUNKS // 2 else 0):
+                rates, turned[g - 2] = lax.optimization_barrier((rates, turned[g - 2]))
+                table = phase_tables(rates, len(phases))
                 lines, table = lax.optimization_barrier((lines, table))
                 phases.append(table)
-        if c >= 3:
-            held = (lines, lows[c - 3], highs[c - 3])
-            lines, lows[c - 3], highs[c - 3] = lax.optimization_barrier(held)
         if bins < LANES:
-            cut = lines.reshape(RG1, 2, rows, LANES // bins, bins)
-            lines = cut.transpose(0, 3, 1, 2, 4).reshape(devices, 2, rows, bins)
+            cut = lines.reshape(RG1, 2, -1, LANES // bins, bins)
+            lines = cut.transpose(0, 3, 1, 2, 4).reshape(devices, 2, -1, bins)
         moved = lax.all_to_all(lines, axes, split_axis=0, concat_axis=0, tiled=True)
-        turned.append(moved.reshape(nrng, naz, 2, per_part, rows_in, bins))
-    transform(CHUNKS - 2)
-    transform(CHUNKS - 1)
+        turned.append(moved.reshape(nrng, naz, 2, len(chunks), per_part, rows_in, bins))
+    transform(count - 2)
+    transform(count - 1)
     tables = (shift_table, filter_index, tap_table)
     image, sources = None, mains
     for i, places_of in enumerate(places):

time: 648 us -> 661 us (1.020)
  waiting for transfers between devices: 174 us -> 253 us
  Pallas kernels: 287 us -> 244 us
  starting transfers between devices: 160 us -> 140 us
    ppermute x40 -> x34, waiting for transfers between devices: 133 us -> 199 us  [the longest x18 145 us: gather(): lax.ppermute(packed[g][j], 'rng', [(i, i ^ j) for i in range(nrng)])]
    pallas_call x8 -> x6, Pallas kernels: 103 us -> 81.5 us  [compress(): pl.pallas_call(functools.partial(compress_kernel, parts, block), grid=(ro...]
    pallas_call x8, Pallas kernels: 63.2 us -> 48.7 us  [azimuth(): pl.pallas_call(functools.partial(azimuth_kernel, chunk), grid=(parts,), i...]
    all_to_all x8 -> x6, waiting for transfers between devices: 40.7 us -> 54.1 us  [local(): moved = lax.all_to_all(lines, axes, split_axis=0, concat_axis=0, tiled=True)]
    all_to_all x8 -> x6, starting transfers between devices: 58.7 us -> 45.6 us  [local(): moved = lax.all_to_all(lines, axes, split_axis=0, concat_axis=0, tiled=True)]
    ppermute x40 -> x34, starting transfers between devices: 102 us -> 94.7 us  [the longest x8 57.5 us: transform(): highs[c] = lax.ppermute(down, axes, neighbours(axes, devices, -1))]
    pallas_call x2, Pallas kernels: 65.6 us -> 58.8 us  [final(): pl.pallas_call(functools.partial(final_kernel, steps, joins, wide), grid=...]
  transfers between devices with their start and end apart: 48 -> 40, of which waited for: 19 -> 15; matrix products, arithmetic and copies ran while one was open for 2% -> 2% of each run, Pallas kernels for 38% -> 31%
where the time goes in v4:
time: 661 us; the launch traced here: 659 us
  waiting for transfers between devices  253 us (38%)
  Pallas kernels  244 us (37%)
  starting transfers between devices  140 us (21%)
  local copies, waits for them, and re-layouts  13.1 us (2%)
  other arithmetic  7.78 us (1%)
    ppermute x18, waiting for transfers between devices, gather(): lax.ppermute(packed[g][j], 'rng', [(i, i ^ j) for i in range(nrng)])  145 us
    pallas_call x6, Pallas kernels, compress(): pl.pallas_call(functools.partial(compress_kernel, parts, block), grid=(ro...  81.5 us
    pallas_call x2, Pallas kernels, final(): pl.pallas_call(functools.partial(final_kernel, steps, joins, wide), grid=...  58.8 us
    ppermute x8, starting transfers between devices, transform(): highs[c] = lax.ppermute(down, axes, neighbours(axes, devices, -1))  57.5 us
    all_to_all x6, waiting for transfers between devices, local(): moved = lax.all_to_all(lines, axes, split_axis=0, concat_axis=0, tiled=True)  54.1 us
    ppermute x8, waiting for transfers between devices, transform(): lows[c] = lax.ppermute(up, axes, neighbours(axes, devices, 1))  53.6 us
    pallas_call x8, Pallas kernels, azimuth(): pl.pallas_call(functools.partial(azimuth_kernel, chunk), grid=(parts,), i...  48.7 us
    all_to_all x6, starting transfers between devices, local(): moved = lax.all_to_all(lines, axes, split_axis=0, concat_axis=0, tiled=True)  45.6 us
  transfers between devices with their start and end apart: 40, of which 15 were waited for; matrix products, arithmetic and copies ran while one was open for 2% of the time, Pallas kernels for 31%

profile of v4, /device:TPU:4, one launch (start us, length us, event | category | flops | bytes accessed | tf_op | source)
XLA Modules:
  0.0 659.2 jit_solution(9796312958767198373)
XLA Ops:
  0.0 9.2 %pack.3 = (f32[2,8,64,128]{3,2,1,0:T(8,128)}, f32[2,8,64,128]{3,2,1,0:T(8,128)}, f32[2,8,64,128]{3,2,1,0:T(8,128)}, f32[2,8,64,128]{3,2,1,0:T(8,128)}) custom-call(s32[1]{0:T(128)} %bitcast.rank_ref, f32[2,2048,1024]{2,1,0:T(8,128)} %x_ref.3), custom_call_target="tpu_custom_call" | custom-call | bytes 33554432 | tf_op jit(solution)/shard_map/pack/pallas_call | solution.py:137
  12.7 15.6 %pack.2 = (f32[2,8,64,128]{3,2,1,0:T(8,128)}, f32[2,8,64,128]{3,2,1,0:T(8,128)}, f32[2,8,64,128]{3,2,1,0:T(8,128)}, f32[2,8,64,128]{3,2,1,0:T(8,128)}, f32[2,8,1...) custom-call(s32[1]{0:T(128)} %bitcast.rank_ref, ...), custom_call_target="tpu_custom_call" | custom-call | bytes 33554432 | tf_op jit(solution)/shard_map/pack/pallas_call | solution.py:137
  39.9 11.2 %compress.6 = f32[32,2,64,128]{3,2,1,0:T(8,128)} custom-call(s32[1]{0:T(128)} %bitcast.rank_ref, f32[2,8,64,128]{3,2,1,0:T(8,128)} %get-tuple-element.225.refs_0_, f32[2,8,64,128]{3,2,1,0:T(8,128)} %copy-done.37, f32[2,8,64,128]{3,2,1,0:T(8,128)} %copy-done.38, f32[2,8,64,128]{3,2,1,0:T(8,128)} %copy-done.39, f32[2,32,128]{2,1,0:T(8,128)} %bitcast.64, ...), custom_call_target="tpu_custom_call" | custom-call | flops 1610612736 | bytes 4194304 | tf_op jit(solution)/shard_map/compress/pallas_call | solution.py:276
  51.1 8.7 %collective-permute-done.4.refs_2_ = f32[2,8,64,128]{3,2,1,0:T(8,128)S(1)} collective-permute-done((f32[2,8,64,128]{3,2,1,0:T(8,128)}, f32[2,8,64,128]{3,2,1,0:T(8,128)S(1)}, u32[]{:S(2)}, u32[]{:S(2)}) %collective-permute-start.4) | collective-permute-done | bytes 524320 | tf_op jit(solution)/shard_map/ppermute | solution.py:689
  69.4 11.2 %compress.7 = f32[32,2,64,128]{3,2,1,0:T(8,128)} custom-call(s32[1]{0:T(128)} %bitcast.rank_ref, f32[2,8,64,128]{3,2,1,0:T(8,128)} %get-tuple-element.237.refs_0_, f32[2,8,64,128]{3,2,1,0:T(8,128)} %copy-done.40, f32[2,8,64,128]{3,2,1,0:T(8,128)} %copy-done.41, f32[2,8,64,128]{3,2,1,0:T(8,128)} %collective-permute-done.5.refs_3_, f32[2,32,128]{2,1,0:T(8,128)} %bitcast.65, ...), custom_call_target="tpu_custom_call" | custom-call | flops 1610612736 | bytes 4194304 | tf_op jit(solution)/shard_map/compress/pallas_call | solution.py:276
  80.6 32.3 %collective-permute-done.6.refs_1_ = f32[2,8,128,128]{3,2,1,0:T(8,128)} collective-permute-done((f32[2,8,128,128]{3,2,1,0:T(8,128)}, f32[2,8,128,128]{3,2,1,0:T(8,128)}, u32[]{:S(2)}, u32[]{:S(2)}) %collective-permute-start.6) | collective-permute-done | bytes 1048608 | tf_op jit(solution)/shard_map/ppermute | solution.py:689
  112.9 23.6 %collective-permute-done.8.refs_3_ = f32[2,8,128,128]{3,2,1,0:T(8,128)} collective-permute-done((f32[2,8,128,128]{3,2,1,0:T(8,128)}, f32[2,8,128,128]{3,2,1,0:T(8,128)}, u32[]{:S(2)}, u32[]{:S(2)}) %collective-permute-start.8) | collective-permute-done | bytes 1048608 | tf_op jit(solution)/shard_map/ppermute | solution.py:689
  145.9 18.4 %compress.8 = f32[32,2,128,128]{3,2,1,0:T(8,128)} custom-call(s32[1]{0:T(128)} %bitcast.rank_ref, f32[2,8,128,128]{3,2,1,0:T(8,128)} %get-tuple-element.249.refs_0_, f32[2,8,128,128]{3,2,1,0:T(8,128)} %collective-permute-done.6.refs_1_, f32[2,8,128,128]{3,2,1,0:T(8,128)} %collective-permute-done.7.refs_2_, ...), custom_call_target="tpu_custom_call" | custom-call | flops 3221225472 | bytes 8388608 | tf_op jit(solution)/shard_map/compress/pallas_call | solution.py:276
  170.2 41.1 %collective-permute-done.10.refs_2_ = f32[2,8,128,128]{3,2,1,0:T(8,128)} collective-permute-done((f32[2,8,128,128]{3,2,1,0:T(8,128)}, f32[2,8,128,128]{3,2,1,0:T(8,128)}, u32[]{:S(2)}, u32[]{:S(2)}) %collective-permute-start.10) | collective-permute-done | bytes 1048608 | tf_op jit(solution)/shard_map/ppermute | solution.py:689
  237.0 7.6 %phase.4 = (f32[2,16,2,64,128]{4,3,2,1,0:T(8,128)}, f32[2,16,2,64,128]{4,3,2,1,0:T(8,128)}) custom-call(f32[64,128]{1,0:T(8,128)} %gather_fusion, f32[64,128]{1,0:T(8,128)} %gather_fusion.1), custom_call_target="tpu_custom_call" | custom-call | flops 20971520 | bytes 4194304 | tf_op jit(solution)/shard_map/phase/pallas_call | solution.py:426
  244.6 7.5 %phase.5 = (f32[2,16,2,64,128]{4,3,2,1,0:T(8,128)}, f32[2,16,2,64,128]{4,3,2,1,0:T(8,128)}) custom-call(f32[64,128]{1,0:T(8,128)} %gather_fusion, f32[64,128]{1,0:T(8,128)} %gather_fusion.1), custom_call_target="tpu_custom_call" | custom-call | flops 20971520 | bytes 4194304 | tf_op jit(solution)/shard_map/phase/pallas_call | solution.py:426
  258.2 18.4 %compress.9 = f32[32,2,128,128]{3,2,1,0:T(8,128)} custom-call(s32[1]{0:T(128)} %bitcast.rank_ref, f32[2,8,128,128]{3,2,1,0:T(8,128)} %get-tuple-element.281.refs_0_, f32[2,8,128,128]{3,2,1,0:T(8,128)} %collective-permute-done.9.refs_1_, f32[2,8,128,128]{3,2,1,0:T(8,128)} %collective-permute-done.10.refs_2_, ...), custom_call_target="tpu_custom_call" | custom-call | flops 3221225472 | bytes 8388608 | tf_op jit(solution)/shard_map/compress/pallas_call | solution.py:276
  276.6 12.2 %collective-permute-done.14.refs_3_ = f32[2,8,64,128]{3,2,1,0:T(8,128)S(1)} collective-permute-done((f32[2,8,64,128]{3,2,1,0:T(8,128)}, f32[2,8,64,128]{3,2,1,0:T(8,128)S(1)}, u32[]{:S(2)}, u32[]{:S(2)}) %collective-permute-start.14) | collective-permute-done | bytes 524320 | tf_op jit(solution)/shard_map/ppermute | solution.py:689
  288.8 17.3 %collective-permute-done.18.refs_1_ = f32[16,2,32,128]{3,2,1,0:T(8,128)S(1)} collective-permute-done((f32[16,2,32,128]{3,2,1,0:T(8,128)}, f32[16,2,32,128]{3,2,1,0:T(8,128)S(1)}, u32[]{:S(2)}, u32[]{:S(2)}) %collective-permute-start.18) | collective-permute-done | bytes 524320 | tf_op jit(solution)/shard_map/ppermute | solution.py:699
  306.1 15.2 %all-to-all-done.2 = f32[32,2,128,128]{3,2,1,0:T(8,128)} async-done(((f32[32,2,128,128]{3,2,1,0:T(8,128)}), f32[32,2,128,128]{3,2,1,0:T(8,128)}, u32[]{:S(2)}, u32[]{:S(2)}) %all-to-all-start.2) | async-done | bytes 4194336 | tf_op jit(solution)/shard_map/all_to_all | solution.py:735
  321.4 9.1 %all-to-all-start.3 = ((f32[32,2,128,128]{3,2,1,0:T(8,128)}), f32[32,2,128,128]{3,2,1,0:T(8,128)}, u32[]{:S(2)}, u32[]{:S(2)}) async-start(f32[32,2,128,128]{3,2,1,0:T(8,128)} %compress.9), calls=%async_computation.3 | async-start | bytes 8388608 | tf_op jit(solution)/shard_map/all_to_all | solution.py:735
  343.2 11.2 %compress.10 = f32[32,2,64,128]{3,2,1,0:T(8,128)} custom-call(s32[1]{0:T(128)} %bitcast.rank_ref, f32[2,8,64,128]{3,2,1,0:T(8,128)} %get-tuple-element.304.refs_0_, f32[2,8,64,128]{3,2,1,0:T(8,128)} %copy-done.34, f32[2,8,64,128]{3,2,1,0:T(8,128)} %copy-done.35, f32[2,8,64,128]{3,2,1,0:T(8,128)} %copy-done.36, f32[2,32,128]{2,1,0:T(8,128)} %bitcast.68, ...), custom_call_target="tpu_custom_call" | custom-call | flops 1610612736 | bytes 4194304 | tf_op jit(solution)/shard_map/compress/pallas_call | solution.py:276
  360.5 7.5 %phase.6 = (f32[2,16,2,64,128]{4,3,2,1,0:T(8,128)}, f32[2,16,2,64,128]{4,3,2,1,0:T(8,128)}) custom-call(f32[64,128]{1,0:T(8,128)} %gather_fusion, f32[64,128]{1,0:T(8,128)} %gather_fusion.1), custom_call_target="tpu_custom_call" | custom-call | flops 20971520 | bytes 4194304 | tf_op jit(solution)/shard_map/phase/pallas_call | solution.py:426
  368.0 7.5 %phase.7 = (f32[2,16,2,64,128]{4,3,2,1,0:T(8,128)}, f32[2,16,2,64,128]{4,3,2,1,0:T(8,128)}) custom-call(f32[64,128]{1,0:T(8,128)} %gather_fusion, f32[64,128]{1,0:T(8,128)} %gather_fusion.1), custom_call_target="tpu_custom_call" | custom-call | flops 20971520 | bytes 4194304 | tf_op jit(solution)/shard_map/phase/pallas_call | solution.py:426
  381.6 16.0 %collective-permute-done.17.refs_3_ = f32[2,8,64,128]{3,2,1,0:T(8,128)} collective-permute-done((f32[2,8,64,128]{3,2,1,0:T(8,128)S(1)}, f32[2,8,64,128]{3,2,1,0:T(8,128)}, u32[]{:S(2)}, u32[]{:S(2)}) %collective-permute-start.17) | collective-permute-done | bytes 524320 | tf_op jit(solution)/shard_map/ppermute | solution.py:689
  397.5 17.2 %collective-permute-done.20.refs_2_ = f32[16,2,32,128]{3,2,1,0:T(8,128)S(1)} collective-permute-done((f32[16,2,32,128]{3,2,1,0:T(8,128)}, f32[16,2,32,128]{3,2,1,0:T(8,128)S(1)}, u32[]{:S(2)}, u32[]{:S(2)}) %collective-permute-start.20) | collective-permute-done | bytes 524320 | tf_op jit(solution)/shard_map/ppermute | solution.py:699
  414.7 15.3 %all-to-all-done.3 = f32[32,2,128,128]{3,2,1,0:T(8,128)} async-done(((f32[32,2,128,128]{3,2,1,0:T(8,128)}), f32[32,2,128,128]{3,2,1,0:T(8,128)}, u32[]{:S(2)}, u32[]{:S(2)}) %all-to-all-start.3) | async-done | bytes 4194336 | tf_op jit(solution)/shard_map/all_to_all | solution.py:735
  430.0 9.1 %all-to-all-start.4 = ((f32[32,2,64,128]{3,2,1,0:T(8,128)}), f32[32,2,64,128]{3,2,1,0:T(8,128)S(1)}, u32[]{:S(2)}, u32[]{:S(2)}) async-start(f32[32,2,64,128]{3,2,1,0:T(8,128)} %compress.10), calls=%async_computation.4 | async-start | bytes 4194304 | tf_op jit(solution)/shard_map/all_to_all | solution.py:735
  450.4 7.2 %collective-permute-start.25 = (f32[16,2,32,128]{3,2,1,0:T(8,128)}, f32[16,2,32,128]{3,2,1,0:T(8,128)}, u32[]{:S(2)}, u32[]{:S(2)}) collective-permute-start(f32[16,2,32,128]{3,2,1,0:T(8,128)} %get-tuple-element.368), channel_id=1, source_target_pairs={{1,0},{2,1},{3,2},{4,3},{5,4},{6,5},{7,6},{8,7},{9,8},{10,9},{11,1... | collective-permute-start | bytes 1572872 | tf_op jit(solution)/shard_map/ppermute | solution.py:700
  463.7 11.2 %compress.11 = f32[32,2,64,128]{3,2,1,0:T(8,128)} custom-call(s32[1]{0:T(128)} %bitcast.rank_ref, f32[2,8,64,128]{3,2,1,0:T(8,128)} %get-tuple-element.336.refs_0_, f32[2,8,64,128]{3,2,1,0:T(8,128)} %copy-done.32, f32[2,8,64,128]{3,2,1,0:T(8,128)} %copy-done.33, f32[2,8,64,128]{3,2,1,0:T(8,128)} %collective-permute-done.17.refs_3_, f32[2,32,128]{2,1,0:T(8,128)} %bitcast.69, ...), custom_call_target="tpu_custom_call" | custom-call | flops 1610612736 | bytes 4194304 | tf_op jit(solution)/shard_map/compress/pallas_call | solution.py:276
  481.1 7.9 %collective-permute-done.22.refs_3_ = f32[16,2,32,128]{3,2,1,0:T(8,128)S(1)} collective-permute-done((f32[16,2,32,128]{3,2,1,0:T(8,128)}, f32[16,2,32,128]{3,2,1,0:T(8,128)S(1)}, u32[]{:S(2)}, u32[]{:S(2)}) %collective-permute-start.22) | collective-permute-done | bytes 524320 | tf_op jit(solution)/shard_map/ppermute | solution.py:699
  489.0 11.2 %collective-permute-done.24.refs_4_ = f32[16,2,32,128]{3,2,1,0:T(8,128)S(1)} collective-permute-done((f32[16,2,32,128]{3,2,1,0:T(8,128)}, f32[16,2,32,128]{3,2,1,0:T(8,128)S(1)}, u32[]{:S(2)}, u32[]{:S(2)}) %collective-permute-start.24) | collective-permute-done | bytes 524320 | tf_op jit(solution)/shard_map/ppermute | solution.py:699
  502.4 12.8 %all-to-all-start.5 = ((f32[32,2,64,128]{3,2,1,0:T(8,128)}), f32[32,2,64,128]{3,2,1,0:T(8,128)}, u32[]{:S(2)}, u32[]{:S(2)}) async-start(f32[32,2,64,128]{3,2,1,0:T(8,128)} %compress.11), calls=%async_computation.5 | async-start | bytes 4194304 | tf_op jit(solution)/shard_map/all_to_all | solution.py:735
  550.8 23.6 %all-to-all-done.5 = f32[32,2,64,128]{3,2,1,0:T(8,128)} async-done(((f32[32,2,64,128]{3,2,1,0:T(8,128)}), f32[32,2,64,128]{3,2,1,0:T(8,128)}, u32[]{:S(2)}, u32[]{:S(2)}) %all-to-all-start.5) | async-done | bytes 2097184 | tf_op jit(solution)/shard_map/all_to_all | solution.py:735
  591.6 7.2 %collective-permute-start.32 = (f32[16,2,32,128]{3,2,1,0:T(8,128)}, f32[16,2,32,128]{3,2,1,0:T(8,128)}, u32[]{:S(2)}, u32[]{:S(2)}) collective-permute-start(f32[16,2,32,128]{3,2,1,0:T(8,128)} %get-tuple-element.394), channel_id=1, source_target_pairs={{1,0},{2,1},{3,2},{4,3},{5,4},{6,5},{7,6},{8,7},{9,8},{10,9},{11,1... | collective-permute-start | bytes 1572872 | tf_op jit(solution)/shard_map/ppermute | solution.py:700
  598.8 31.4 %final_inner.1 = (f32[2,128,16384]{2,1,0:T(8,128)}, bf16[8,16,256,256]{3,2,1,0:T(8,128)(2,1)}) custom-call(f32[16,2,128,128]{3,2,1,0:T(8,128)} %get-tuple-element.276.refs_0_, f32[16,2,128,128]{3,2,1,0:T(8,128)} %get-tuple-element.303.refs_1_, f32[16,2,128,128]{3,2,1,0:T(8,128)} %get-tuple-element.316.refs_2_, ...), custom_call_target="tpu_custom_call" | custom-call | flops 9663676416 | bytes 29360128 | tf_op jit(solution)/shard_map/final_inner/pallas_call | solution.py:620
  631.6 27.4 %final_wide.1 = f32[2,128,16384]{2,1,0:T(8,128)} custom-call(bf16[8,16,256,256]{3,2,1,0:T(8,128)(2,1)} %get-tuple-element.379.refs_0_, f32[16,2,32,128]{3,2,1,0:T(8,128)} %copy-done.5, f32[16,2,32,128]{3,2,1,0:T(8,128)} %copy-done.7, f32[16,2,32,128]{3,2,1,0:T(8,128)} %copy-done.9, f32[16,2,32,128]{3,2,1,0:T(8,128)} %copy-done.11, ...), custom_call_target="tpu_custom_call", output_to_operand_aliasing={{}: (26, {})} | custom-call | flops 9663676416 | bytes 29360128 | tf_op jit(solution)/shard_map/final_wide/pallas_call | solution.py:620
  (185 shorter events, 176.2 us)
Async XLA Ops:
  60.6 75.9 %all-to-all-start = ((f32[32,2,64,128]{3,2,1,0:T(8,128)}), f32[32,2,64,128]{3,2,1,0:T(8,128)S(1)}, u32[]{:S(2)}, u32[]{:S(2)}) async-start(f32[32,2,64,128]{3,2,1,0:T(8,128)} %compress.6), calls=%async_computation | async-start | bytes 4194304 | tf_op jit(solution)/shard_map/all_to_all | solution.py:735
  65.8 47.1 %collective-permute-start.6 = (f32[2,8,128,128]{3,2,1,0:T(8,128)}, f32[2,8,128,128]{3,2,1,0:T(8,128)}, u32[]{:S(2)}, u32[]{:S(2)}) collective-permute-start(f32[2,8,128,128]{3,2,1,0:T(8,128)} %get-tuple-element.242), channel_id=1, source_target_pairs={{0,8},{8,0},{16,24},{24,16},{1,9},{9,1},{17,25},{25,17},{2,10},{10... | collective-permute-start | bytes 3145736 | tf_op jit(solution)/shard_map/ppermute | solution.py:689
  67.4 45.5 %collective-permute-start.7 = (f32[2,8,128,128]{3,2,1,0:T(8,128)}, f32[2,8,128,128]{3,2,1,0:T(8,128)}, u32[]{:S(2)}, u32[]{:S(2)}) collective-permute-start(f32[2,8,128,128]{3,2,1,0:T(8,128)} %get-tuple-element.243), channel_id=1, source_target_pairs={{0,16},{8,24},{16,0},{24,8},{1,17},{9,25},{17,1},{25,9},{2,18},{10... | collective-permute-start | bytes 3145736 | tf_op jit(solution)/shard_map/ppermute | solution.py:689
  67.9 68.6 %collective-permute-start.8 = (f32[2,8,128,128]{3,2,1,0:T(8,128)}, f32[2,8,128,128]{3,2,1,0:T(8,128)}, u32[]{:S(2)}, u32[]{:S(2)}) collective-permute-start(f32[2,8,128,128]{3,2,1,0:T(8,128)} %get-tuple-element.244), channel_id=1, source_target_pairs={{0,24},{8,16},{16,8},{24,0},{1,25},{9,17},{17,9},{25,1},{2,26},{10... | collective-permute-start | bytes 3145736 | tf_op jit(solution)/shard_map/ppermute | solution.py:689
  137.8 77.8 %all-to-all-start.1 = ((f32[32,2,64,128]{3,2,1,0:T(8,128)}), f32[32,2,64,128]{3,2,1,0:T(8,128)S(1)}, u32[]{:S(2)}, u32[]{:S(2)}) async-start(f32[32,2,64,128]{3,2,1,0:T(8,128)} %compress.7), calls=%async_computation.1 | async-start | bytes 4194304 | tf_op jit(solution)/shard_map/all_to_all | solution.py:735
  142.4 69.0 %collective-permute-start.10 = (f32[2,8,128,128]{3,2,1,0:T(8,128)}, f32[2,8,128,128]{3,2,1,0:T(8,128)}, u32[]{:S(2)}, u32[]{:S(2)}) collective-permute-start(f32[2,8,128,128]{3,2,1,0:T(8,128)} %get-tuple-element.260), channel_id=1, source_target_pairs={{0,16},{8,24},{16,0},{24,8},{1,17},{9,25},{17,1},{25,9},{2,18},{10... | collective-permute-start | bytes 3145736 | tf_op jit(solution)/shard_map/ppermute | solution.py:689
  142.7 68.7 %collective-permute-start.11 = (f32[2,8,128,128]{3,2,1,0:T(8,128)}, f32[2,8,128,128]{3,2,1,0:T(8,128)}, u32[]{:S(2)}, u32[]{:S(2)}) collective-permute-start(f32[2,8,128,128]{3,2,1,0:T(8,128)} %get-tuple-element.261), channel_id=1, source_target_pairs={{0,24},{8,16},{16,8},{24,0},{1,25},{9,17},{17,9},{25,1},{2,26},{10... | collective-permute-start | bytes 3145736 | tf_op jit(solution)/shard_map/ppermute | solution.py:689
  145.4 70.3 %collective-permute-start.9 = (f32[2,8,128,128]{3,2,1,0:T(8,128)S(1)}, f32[2,8,128,128]{3,2,1,0:T(8,128)}, u32[]{:S(2)}, u32[]{:S(2)}) collective-permute-start(f32[2,8,128,128]{3,2,1,0:T(8,128)S(1)} %copy-done.26), channel_id=1, source_target_pairs={{0,8},{8,0},{16,24},{24,16},{1,9},{9,1},{17,25},{25,17},{2,10},{10... | collective-permute-start | bytes 3145736 | tf_op jit(solution)/shard_map/ppermute | solution.py:689
  217.0 104.4 %all-to-all-start.2 = ((f32[32,2,128,128]{3,2,1,0:T(8,128)}), f32[32,2,128,128]{3,2,1,0:T(8,128)}, u32[]{:S(2)}, u32[]{:S(2)}) async-start(f32[32,2,128,128]{3,2,1,0:T(8,128)} %compress.8), calls=%async_computation.2 | async-start | bytes 8388608 | tf_op jit(solution)/shard_map/all_to_all | solution.py:735
  221.9 84.2 %collective-permute-start.18 = (f32[16,2,32,128]{3,2,1,0:T(8,128)}, f32[16,2,32,128]{3,2,1,0:T(8,128)S(1)}, u32[]{:S(2)}, u32[]{:S(2)}) collective-permute-start(f32[16,2,32,128]{3,2,1,0:T(8,128)} %get-tuple-element.318), channel_id=1, source_target_pairs={{0,1},{1,2},{2,3},{3,4},{4,5},{5,6},{6,7},{7,8},{8,9},{9,10},{10,1... | collective-permute-start | bytes 1572872 | tf_op jit(solution)/shard_map/ppermute | solution.py:699
  223.9 82.1 %collective-permute-start.19 = (f32[16,2,32,128]{3,2,1,0:T(8,128)}, f32[16,2,32,128]{3,2,1,0:T(8,128)S(1)}, u32[]{:S(2)}, u32[]{:S(2)}) collective-permute-start(f32[16,2,32,128]{3,2,1,0:T(8,128)} %get-tuple-element.319), channel_id=1, source_target_pairs={{1,0},{2,1},{3,2},{4,3},{5,4},{6,5},{7,6},{8,7},{9,8},{10,9},{11,1... | collective-permute-start | bytes 1572872 | tf_op jit(solution)/shard_map/ppermute | solution.py:700
  231.0 45.6 %collective-permute-start.12 = (f32[2,8,64,128]{3,2,1,0:T(8,128)}, f32[2,8,64,128]{3,2,1,0:T(8,128)S(1)}, u32[]{:S(2)}, u32[]{:S(2)}) collective-permute-start(f32[2,8,64,128]{3,2,1,0:T(8,128)} %get-tuple-element.286), channel_id=1, source_target_pairs={{0,8},{8,0},{16,24},{24,16},{1,9},{9,1},{17,25},{25,17},{2,10},{10... | collective-permute-start | bytes 1572872 | tf_op jit(solution)/shard_map/ppermute | solution.py:689
  231.7 44.9 %collective-permute-start.13 = (f32[2,8,64,128]{3,2,1,0:T(8,128)}, f32[2,8,64,128]{3,2,1,0:T(8,128)S(1)}, u32[]{:S(2)}, u32[]{:S(2)}) collective-permute-start(f32[2,8,64,128]{3,2,1,0:T(8,128)} %get-tuple-element.287), channel_id=1, source_target_pairs={{0,16},{8,24},{16,0},{24,8},{1,17},{9,25},{17,1},{25,9},{2,18},{10... | collective-permute-start | bytes 1572872 | tf_op jit(solution)/shard_map/ppermute | solution.py:689
  232.2 56.6 %collective-permute-start.14 = (f32[2,8,64,128]{3,2,1,0:T(8,128)}, f32[2,8,64,128]{3,2,1,0:T(8,128)S(1)}, u32[]{:S(2)}, u32[]{:S(2)}) collective-permute-start(f32[2,8,64,128]{3,2,1,0:T(8,128)} %get-tuple-element.288), channel_id=1, source_target_pairs={{0,24},{8,16},{16,8},{24,0},{1,25},{9,17},{17,9},{25,1},{2,26},{10... | collective-permute-start | bytes 1572872 | tf_op jit(solution)/shard_map/ppermute | solution.py:689
  321.4 108.6 %all-to-all-start.3 = ((f32[32,2,128,128]{3,2,1,0:T(8,128)}), f32[32,2,128,128]{3,2,1,0:T(8,128)}, u32[]{:S(2)}, u32[]{:S(2)}) async-start(f32[32,2,128,128]{3,2,1,0:T(8,128)} %compress.9), calls=%async_computation.3 | async-start | bytes 8388608 | tf_op jit(solution)/shard_map/all_to_all | solution.py:735
  330.5 51.1 %collective-permute-start.15 = (f32[2,8,64,128]{3,2,1,0:T(8,128)S(1)}, f32[2,8,64,128]{3,2,1,0:T(8,128)S(1)}, u32[]{:S(2)}, u32[]{:S(2)}) collective-permute-start(f32[2,8,64,128]{3,2,1,0:T(8,128)S(1)} %copy-done.29), channel_id=1, source_target_pairs={{0,8},{8,0},{16,24},{24,16},{1,9},{9,1},{17,25},{25,17},{2,10},{10... | collective-permute-start | bytes 1572872 | tf_op jit(solution)/shard_map/ppermute | solution.py:689
  332.0 49.5 %collective-permute-start.16 = (f32[2,8,64,128]{3,2,1,0:T(8,128)S(1)}, f32[2,8,64,128]{3,2,1,0:T(8,128)S(1)}, u32[]{:S(2)}, u32[]{:S(2)}) collective-permute-start(f32[2,8,64,128]{3,2,1,0:T(8,128)S(1)} %copy-done.28), channel_id=1, source_target_pairs={{0,16},{8,24},{16,0},{24,8},{1,17},{9,25},{17,1},{25,9},{2,18},{10... | collective-permute-start | bytes 1572872 | tf_op jit(solution)/shard_map/ppermute | solution.py:689
  332.6 64.9 %collective-permute-start.17 = (f32[2,8,64,128]{3,2,1,0:T(8,128)S(1)}, f32[2,8,64,128]{3,2,1,0:T(8,128)}, u32[]{:S(2)}, u32[]{:S(2)}) collective-permute-start(f32[2,8,64,128]{3,2,1,0:T(8,128)S(1)} %copy-done.27), channel_id=1, source_target_pairs={{0,24},{8,16},{16,8},{24,0},{1,25},{9,17},{17,9},{25,1},{2,26},{10... | collective-permute-start | bytes 1572872 | tf_op jit(solution)/shard_map/ppermute | solution.py:689
  334.1 80.7 %collective-permute-start.20 = (f32[16,2,32,128]{3,2,1,0:T(8,128)}, f32[16,2,32,128]{3,2,1,0:T(8,128)S(1)}, u32[]{:S(2)}, u32[]{:S(2)}) collective-permute-start(f32[16,2,32,128]{3,2,1,0:T(8,128)} %get-tuple-element.345), channel_id=1, source_target_pairs={{0,1},{1,2},{2,3},{3,4},{4,5},{5,6},{6,7},{7,8},{8,9},{9,10},{10,1... | collective-permute-start | bytes 1572872 | tf_op jit(solution)/shard_map/ppermute | solution.py:699
  336.0 78.7 %collective-permute-start.21 = (f32[16,2,32,128]{3,2,1,0:T(8,128)}, f32[16,2,32,128]{3,2,1,0:T(8,128)S(1)}, u32[]{:S(2)}, u32[]{:S(2)}) collective-permute-start(f32[16,2,32,128]{3,2,1,0:T(8,128)} %get-tuple-element.346), channel_id=1, source_target_pairs={{1,0},{2,1},{3,2},{4,3},{5,4},{6,5},{7,6},{8,7},{9,8},{10,9},{11,1... | collective-permute-start | bytes 1572872 | tf_op jit(solution)/shard_map/ppermute | solution.py:700
  430.0 71.1 %all-to-all-start.4 = ((f32[32,2,64,128]{3,2,1,0:T(8,128)}), f32[32,2,64,128]{3,2,1,0:T(8,128)S(1)}, u32[]{:S(2)}, u32[]{:S(2)}) async-start(f32[32,2,64,128]{3,2,1,0:T(8,128)} %compress.10), calls=%async_computation.4 | async-start | bytes 4194304 | tf_op jit(solution)/shard_map/all_to_all | solution.py:735
  439.1 50.0 %collective-permute-start.22 = (f32[16,2,32,128]{3,2,1,0:T(8,128)}, f32[16,2,32,128]{3,2,1,0:T(8,128)S(1)}, u32[]{:S(2)}, u32[]{:S(2)}) collective-permute-start(f32[16,2,32,128]{3,2,1,0:T(8,128)} %get-tuple-element.364), channel_id=1, source_target_pairs={{0,1},{1,2},{2,3},{3,4},{4,5},{5,6},{6,7},{7,8},{8,9},{9,10},{10,1... | collective-permute-start | bytes 1572872 | tf_op jit(solution)/shard_map/ppermute | solution.py:699
  441.1 47.9 %collective-permute-start.23 = (f32[16,2,32,128]{3,2,1,0:T(8,128)}, f32[16,2,32,128]{3,2,1,0:T(8,128)S(1)}, u32[]{:S(2)}, u32[]{:S(2)}) collective-permute-start(f32[16,2,32,128]{3,2,1,0:T(8,128)} %get-tuple-element.365), channel_id=1, source_target_pairs={{1,0},{2,1},{3,2},{4,3},{5,4},{6,5},{7,6},{8,7},{9,8},{10,9},{11,1... | collective-permute-start | bytes 1572872 | tf_op jit(solution)/shard_map/ppermute | solution.py:700
  448.2 52.0 %collective-permute-start.24 = (f32[16,2,32,128]{3,2,1,0:T(8,128)}, f32[16,2,32,128]{3,2,1,0:T(8,128)S(1)}, u32[]{:S(2)}, u32[]{:S(2)}) collective-permute-start(f32[16,2,32,128]{3,2,1,0:T(8,128)} %get-tuple-element.367), channel_id=1, source_target_pairs={{0,1},{1,2},{2,3},{3,4},{4,5},{5,6},{6,7},{7,8},{8,9},{9,10},{10,1... | collective-permute-start | bytes 1572872 | tf_op jit(solution)/shard_map/ppermute | solution.py:699
  450.4 50.7 %collective-permute-start.25 = (f32[16,2,32,128]{3,2,1,0:T(8,128)}, f32[16,2,32,128]{3,2,1,0:T(8,128)}, u32[]{:S(2)}, u32[]{:S(2)}) collective-permute-start(f32[16,2,32,128]{3,2,1,0:T(8,128)} %get-tuple-element.368), channel_id=1, source_target_pairs={{1,0},{2,1},{3,2},{4,3},{5,4},{6,5},{7,6},{8,7},{9,8},{10,9},{11,1... | collective-permute-start | bytes 1572872 | tf_op jit(solution)/shard_map/ppermute | solution.py:700
  502.4 72.0 %all-to-all-start.5 = ((f32[32,2,64,128]{3,2,1,0:T(8,128)}), f32[32,2,64,128]{3,2,1,0:T(8,128)}, u32[]{:S(2)}, u32[]{:S(2)}) async-start(f32[32,2,64,128]{3,2,1,0:T(8,128)} %compress.11), calls=%async_computation.5 | async-start | bytes 4194304 | tf_op jit(solution)/shard_map/all_to_all | solution.py:735
  523.2 59.1 %collective-permute-start.27 = (f32[16,2,32,128]{3,2,1,0:T(8,128)S(1)}, f32[16,2,32,128]{3,2,1,0:T(8,128)S(1)}, u32[]{:S(2)}, u32[]{:S(2)}) collective-permute-start(f32[16,2,32,128]{3,2,1,0:T(8,128)S(1)} %copy-done.31), channel_id=1, source_target_pairs={{0,1},{1,2},{2,3},{3,4},{4,5},{5,6},{6,7},{7,8},{8,9},{9,10},{10,1... | collective-permute-start | bytes 1572872 | tf_op jit(solution)/shard_map/ppermute | solution.py:699
  525.3 64.3 %collective-permute-start.31 = (f32[16,2,32,128]{3,2,1,0:T(8,128)S(1)}, f32[16,2,32,128]{3,2,1,0:T(8,128)S(1)}, u32[]{:S(2)}, u32[]{:S(2)}) collective-permute-start(f32[16,2,32,128]{3,2,1,0:T(8,128)S(1)} %copy-done.30), channel_id=1, source_target_pairs={{1,0},{2,1},{3,2},{4,3},{5,4},{6,5},{7,6},{8,7},{9,8},{10,9},{11,1... | collective-permute-start | bytes 1572872 | tf_op jit(solution)/shard_map/ppermute | solution.py:700
  532.4 59.2 %collective-permute-start.26 = (f32[16,2,32,128]{3,2,1,0:T(8,128)}, f32[16,2,32,128]{3,2,1,0:T(8,128)S(1)}, u32[]{:S(2)}, u32[]{:S(2)}) collective-permute-start(f32[16,2,32,128]{3,2,1,0:T(8,128)} %get-tuple-element.384), channel_id=1, source_target_pairs={{0,1},{1,2},{2,3},{3,4},{4,5},{5,6},{6,7},{7,8},{8,9},{9,10},{10,1... | collective-permute-start | bytes 1572872 | tf_op jit(solution)/shard_map/ppermute | solution.py:699
  537.5 92.8 %collective-permute-start.30 = (f32[16,2,32,128]{3,2,1,0:T(8,128)}, f32[16,2,32,128]{3,2,1,0:T(8,128)S(1)}, u32[]{:S(2)}, u32[]{:S(2)}) collective-permute-start(f32[16,2,32,128]{3,2,1,0:T(8,128)} %get-tuple-element.392), channel_id=1, source_target_pairs={{1,0},{2,1},{3,2},{4,3},{5,4},{6,5},{7,6},{8,7},{9,8},{10,9},{11,1... | collective-permute-start | bytes 1572872 | tf_op jit(solution)/shard_map/ppermute | solution.py:700
  580.4 49.9 %collective-permute-start.29 = (f32[16,2,32,128]{3,2,1,0:T(8,128)}, f32[16,2,32,128]{3,2,1,0:T(8,128)S(1)}, u32[]{:S(2)}, u32[]{:S(2)}) collective-permute-start(f32[16,2,32,128]{3,2,1,0:T(8,128)} %get-tuple-element.387), channel_id=1, source_target_pairs={{0,1},{1,2},{2,3},{3,4},{4,5},{5,6},{6,7},{7,8},{8,9},{9,10},{10,1... | collective-permute-start | bytes 1572872 | tf_op jit(solution)/shard_map/ppermute | solution.py:699
  582.4 48.0 %collective-permute-start.33 = (f32[16,2,32,128]{3,2,1,0:T(8,128)}, f32[16,2,32,128]{3,2,1,0:T(8,128)S(1)}, u32[]{:S(2)}, u32[]{:S(2)}) collective-permute-start(f32[16,2,32,128]{3,2,1,0:T(8,128)} %get-tuple-element.395), channel_id=1, source_target_pairs={{1,0},{2,1},{3,2},{4,3},{5,4},{6,5},{7,6},{8,7},{9,8},{10,9},{11,1... | collective-permute-start | bytes 1572872 | tf_op jit(solution)/shard_map/ppermute | solution.py:700
  (51 other events, 1543.7 us)

commit v5 on v4

--- a/solution.py
+++ b/solution.py
@@ -19,7 +19,7 @@
 RG1 = NRG // LANES
 CHUNKS = 8
 PER_CHUNK = LANES // CHUNKS
-GROUPED = ((0,), (1,), (2, 3), (4, 5), (6,), (7,))
+GROUPED = tuple((c,) for c in range(CHUNKS))
 VMEM_LIMIT = 60 << 20
 BF16 = jnp.bfloat16
 F32 = jnp.float32
@@ -399,6 +399,12 @@
     return total
 
 
+def square_of(k2):
+    f = k2 * LANES + lax.broadcasted_iota(jnp.int32, (1, LANES), 1)
+    centred = jnp.where(f >= NAZ // 2, f - NAZ, f).astype(F32) * (1.0 / NAZ)
+    return centred * centred
+
+
 def turn(t):
     z = t - jnp.round(t)
     z2 = z * z
@@ -408,35 +414,29 @@
     return 1.0 - twice * s, twice * c
 
 
-def phase_kernel(part, sets, *refs):
+def phase_kernel(part, rate_ref, out_ref):
     k = pl.program_id(0)
-    for rate_ref, out_ref in zip(refs[:sets], refs[sets:]):
-        for half in range(2):
-            k2 = k + PER_CHUNK * (2 * part + half)
-            f = k2 * LANES + lax.broadcasted_iota(jnp.int32, (1, LANES), 1)
-            centred = jnp.where(f >= NAZ // 2, f - NAZ, f).astype(F32) * (1.0 / NAZ)
-            c, s = turn(rate_ref[...] * (centred * centred))
-            out_ref[half, 0, 0] = c
-            out_ref[half, 0, 1] = s
-
-
-def phase_tables(rates, part):
-    shapes = [(2, PER_CHUNK, 2, rate.shape[0], LANES) for rate in rates]
-    points = sum(2 * PER_CHUNK * rate.size for rate in rates)
+    for half in range(2):
+        c, s = turn(rate_ref[...] * square_of(k + PER_CHUNK * (2 * part + half)))
+        out_ref[half, 0, 0] = c
+        out_ref[half, 0, 1] = s
+
+
+def phase_table(rate, part):
+    shape = (2, PER_CHUNK, 2, rate.shape[0], LANES)
+    points = 2 * PER_CHUNK * rate.size
     return pl.pallas_call(
-        functools.partial(phase_kernel, part, len(rates)),
+        functools.partial(phase_kernel, part),
         grid=(PER_CHUNK,),
-        in_specs=[whole_spec(rate) for rate in rates],
-        out_specs=[
-            pl.BlockSpec((2, 1) + shape[2:], lambda i: (0, i, 0, 0, 0)) for shape in shapes
-        ],
-        out_shape=[jax.ShapeDtypeStruct(shape, F32) for shape in shapes],
+        in_specs=[whole_spec(rate)],
+        out_specs=pl.BlockSpec((2, 1) + shape[2:], lambda i: (0, i, 0, 0, 0)),
+        out_shape=jax.ShapeDtypeStruct(shape, F32),
         compiler_params=pltpu.CompilerParams(vmem_limit_bytes=VMEM_LIMIT),
         cost_estimate=pl.CostEstimate(
             flops=40 * points, bytes_accessed=8 * points, transcendentals=0
         ),
         name="phase",
-    )(*rates)
+    )(rate)
 
 
 def combine(sources, kk, start, put):
@@ -458,18 +458,28 @@
 
     sources = take(CHUNKS) if joins else take(1)
     low_refs, high_refs = (take(CHUNKS), take(CHUNKS)) if wide else ((), ())
-    phase_refs = take(CHUNKS // 2)
+    phase_refs = take(1 if wide else CHUNKS // 2)
     mover_refs = take(2 if wide else 1)
     inv1_ref, inv2_ref, tw_ref = take(3)
-    out_ref, own_ref, zr_ref, zi_ref, s_ref, swap_ref, half_ref = (
-        refs[-8:-1] if wide else refs[-7:]
-    )
-    halo_ref = refs[-1]
-    if not joins:
-        own_ref = sources[0]
+    if not joins or wide:
+        out_ref, own_ref, zr_ref, zi_ref, s_ref, swap_ref, half_ref, halo_ref = refs[-8:]
+        if not joins:
+            own_ref = sources[0]
+    else:
+        out_ref, joined_ref, own_ref, zr_ref, zi_ref, s_ref, swap_ref, half_ref, sems = refs[-9:]
+    step = pl.program_id(0)
     own = own_ref.shape[2] // 2
-    rows = phase_refs[0].shape[3]
-    step = pl.program_id(0)
+    rows = zr_ref.shape[0]
+    keeps = joins and not wide
+    copies = []
+    if keeps:
+        copies = [
+            pltpu.make_async_copy(own_ref.at[q], joined_ref.at[q], sems.at[q])
+            for q in range(CHUNKS)
+        ]
+
+    def own_at(kk):
+        return step * KB + kk if keeps else kk
 
     def first_half(block):
         base = jnp.minimum(block * BB, rows - BB)
@@ -497,8 +507,8 @@
                 for start in range(0, own, STEP):
 
                     def put_own(q, cols, high, low, start=start):
-                        own_ref[q, kk, start : start + STEP, cols] = high
-                        own_ref[q, kk, own + start : own + start + STEP, cols] = low
+                        own_ref[q, own_at(kk), start : start + STEP, cols] = high
+                        own_ref[q, own_at(kk), own + start : own + start + STEP, cols] = low
 
                     combine(sources, kk, start, put_own)
             if wide:
@@ -513,11 +523,14 @@
             for q in range(CHUNKS):
                 k2 = k + PER_CHUNK * q
                 band = lax.div(k2, LANES // GROUPS)
-                moved = dot(mover_refs[0][band], own_ref[q, kk])
+                moved = dot(mover_refs[0][band], own_ref[q, own_at(kk)])
                 if wide:
                     moved = moved + dot(mover_refs[1][band], halo_ref[buf, q])
                 both = moved[0:rows, :] + moved[rows : 2 * rows, :]
-                c, s = phase_refs[q // 2][q % 2, kk, 0], phase_refs[q // 2][q % 2, kk, 1]
+                if wide:
+                    c, s = turn(phase_refs[0][...] * square_of(k2))
+                else:
+                    c, s = phase_refs[q // 2][q % 2, kk, 0], phase_refs[q // 2][q % 2, kk, 1]
                 a, b = both[:, 0:LANES], both[:, LANES : 2 * LANES]
                 swap_ref[buf, 0, q] = a * c + b * s
                 swap_ref[buf, 1, q] = b * c - a * s
@@ -551,7 +564,14 @@
 
     @pl.when(step == steps)
     def _():
+        for copy in copies:
+            copy.start()
         first_half(0)
+
+    @pl.when(step == pl.num_programs(0) - 1)
+    def _():
+        for copy in copies:
+            copy.wait()
 
 
 def final(bins, places, sources, lows, highs, phases, movers, image=None):
@@ -588,9 +608,12 @@
     given = [*sources, *lows, *highs, *phases, *consts]
     specs = [pl.BlockSpec((KB, 2, bins, LANES), early)] * CHUNKS if joins else [joined_spec]
     specs += [pl.BlockSpec((KB, 2, HALO, LANES), early)] * (2 * CHUNKS if wide else 0)
-    specs += [
-        pl.BlockSpec((2, KB, 2, rows, LANES), lambda i: (0, jnp.minimum(i, steps - 1), 0, 0, 0))
-    ] * len(phases)
+    if wide:
+        specs += [whole_spec(a) for a in phases]
+    else:
+        specs += [
+            pl.BlockSpec((2, KB, 2, rows, LANES), lambda i: (0, jnp.minimum(i, steps - 1), 0, 0, 0))
+        ] * len(phases)
     specs += [whole_spec(a) for a in consts]
     aliases = {}
     if image is not None:
@@ -604,7 +627,8 @@
         scratch.append(pltpu.VMEM((CHUNKS, KB, 2 * bins, 2 * LANES), BF16))
     elif joins:
         shapes.append(jax.ShapeDtypeStruct(joined, BF16))
-        out_specs.append(joined_spec)
+        out_specs.append(pl.BlockSpec(memory_space=pl.ANY))
+        scratch.append(pltpu.VMEM(joined, BF16))
     else:
         scratch.append(pltpu.VMEM((16, LANES), BF16))
     scratch += [
@@ -616,6 +640,8 @@
     ]
     if wide:
         scratch.append(pltpu.VMEM((2, CHUNKS, 4 * HALO, 2 * LANES), BF16))
+    else:
+        scratch.append(pltpu.SemaphoreType.DMA((CHUNKS,)))
     points = NAZ * rows
     return pl.pallas_call(
         functools.partial(final_kernel, steps, joins, wide),
@@ -701,6 +727,7 @@
 
     places = row_sets(bins)
     rates = [rate[bins_of(p)] for p in places]
+    inner_rate = rates[0]
     phases = []
     got = [gather(0)]
     packed[1], got[0] = lax.optimization_barrier((packed[1], got[0]))
@@ -709,7 +736,9 @@
     for g, chunks in enumerate(GROUPED):
         lines = compress(got[g], rank, chirp)
         if g + 1 < count:
-            lines, got[g + 1] = lax.optimization_barrier((lines, got[g + 1]))
+            held = got[g + 1][1 : (3 if g < 2 else nrng)]
+            lines, held = lax.optimization_barrier((lines, held))
+            got[g + 1][1 : 1 + len(held)] = held
         if g + 2 < count:
             packed[g + 2], got[g + 1] = lax.optimization_barrier((packed[g + 2], got[g + 1]))
             if g >= 1:
@@ -724,11 +753,11 @@
             for c in GROUPED[g - 3]:
                 held = (lines, lows[c], highs[c])
                 lines, lows[c], highs[c] = lax.optimization_barrier(held)
-            for _ in range(2 if len(phases) < CHUNKS // 2 else 0):
-                rates, turned[g - 2] = lax.optimization_barrier((rates, turned[g - 2]))
-                table = phase_tables(rates, len(phases))
-                lines, table = lax.optimization_barrier((lines, table))
-                phases.append(table)
+        if 2 <= g and len(places) > 1 and len(phases) < CHUNKS // 2:
+            inner_rate, turned[g - 2] = lax.optimization_barrier((inner_rate, turned[g - 2]))
+            table = phase_table(inner_rate, len(phases))
+            lines, table = lax.optimization_barrier((lines, table))
+            phases.append(table)
         if bins < LANES:
             cut = lines.reshape(RG1, 2, -1, LANES // bins, bins)
             lines = cut.transpose(0, 3, 1, 2, 4).reshape(devices, 2, -1, bins)
@@ -745,7 +774,7 @@
         columns = [own_columns(bins), halo_columns(bins)] if wide else [own_columns(bins)]
         movers = [mover_table(ids, cols, *tables) for cols in columns]
         result = final(
-            bins, places_of, sources, *halos, [table[i] for table in phases], movers, image
+            bins, places_of, sources, *halos, [rates[i]] if wide else phases, movers, image
         )
         image, sources = result[0], result[1:]
     return image

time: 661 us -> 647 us (0.979)
  waiting for transfers between devices: 253 us -> 213 us
  starting transfers between devices: 140 us -> 159 us
    ppermute x8, waiting for transfers between devices: 53.6 us -> 23.4 us  [transform(): lows[c] = lax.ppermute(up, axes, neighbours(axes, devices, 1))]
    all_to_all x6 -> x8, waiting for transfers between devices: 54.1 us -> 39.3 us  [local(): moved = lax.all_to_all(lines, axes, split_axis=0, concat_axis=0, tiled=True)]
    all_to_all x6 -> x8, starting transfers between devices: 45.6 us -> 57.7 us  [local(): moved = lax.all_to_all(lines, axes, split_axis=0, concat_axis=0, tiled=True)]
    pallas_call x6 -> x8, Pallas kernels: 81.5 us -> 89.5 us  [compress(): pl.pallas_call(functools.partial(compress_kernel, parts, block), grid=(ro...]
    ppermute x18 -> x24, starting transfers between devices: 21.2 us -> 27.4 us  [gather(): lax.ppermute(packed[g][j], 'rng', [(i, i ^ j) for i in range(nrng)])]
    ppermute x18 -> x24, waiting for transfers between devices: 145 us -> 151 us  [gather(): lax.ppermute(packed[g][j], 'rng', [(i, i ^ j) for i in range(nrng)])]
  transfers between devices with their start and end apart: 40 -> 48, of which waited for: 15 -> 18; matrix products, arithmetic and copies ran while one was open for 2% -> 2% of each run, Pallas kernels for 31% -> 33%
where the time goes in v5:
time: 647 us; the launch traced here: 645 us
  Pallas kernels  248 us (38%)
  waiting for transfers between devices  213 us (33%)
  starting transfers between devices  159 us (25%)
  local copies, waits for them, and re-layouts  15.9 us (2%)
  other arithmetic  7.75 us (1%)
    ppermute x24, waiting for transfers between devices, gather(): lax.ppermute(packed[g][j], 'rng', [(i, i ^ j) for i in range(nrng)])  151 us
    pallas_call x8, Pallas kernels, compress(): pl.pallas_call(functools.partial(compress_kernel, parts, block), grid=(ro...  89.5 us
    pallas_call x2, Pallas kernels, final(): pl.pallas_call(functools.partial(final_kernel, steps, joins, wide), grid=...  58.5 us
    ppermute x8, starting transfers between devices, transform(): highs[c] = lax.ppermute(down, axes, neighbours(axes, devices, -1))  58 us
    all_to_all x8, starting transfers between devices, local(): moved = lax.all_to_all(lines, axes, split_axis=0, concat_axis=0, tiled=True)  57.7 us
    pallas_call x8, Pallas kernels, azimuth(): pl.pallas_call(functools.partial(azimuth_kernel, chunk), grid=(parts,), i...  48.7 us
    all_to_all x8, waiting for transfers between devices, local(): moved = lax.all_to_all(lines, axes, split_axis=0, concat_axis=0, tiled=True)  39.3 us
    ppermute x24, starting transfers between devices, gather(): lax.ppermute(packed[g][j], 'rng', [(i, i ^ j) for i in range(nrng)])  27.4 us
  transfers between devices with their start and end apart: 48, of which 18 were waited for; matrix products, arithmetic and copies ran while one was open for 2% of the time, Pallas kernels for 33%

profile of v5, /device:TPU:4, one launch (start us, length us, event | category | flops | bytes accessed | tf_op | source)
XLA Modules:
  0.0 644.8 jit_solution(15567940976599713483)
XLA Ops:
  0.0 9.2 %pack.3 = (f32[2,8,64,128]{3,2,1,0:T(8,128)}, f32[2,8,64,128]{3,2,1,0:T(8,128)}, f32[2,8,64,128]{3,2,1,0:T(8,128)}, f32[2,8,64,128]{3,2,1,0:T(8,128)}) custom-call(s32[1]{0:T(128)} %bitcast.rank_ref, f32[2,2048,1024]{2,1,0:T(8,128)} %x_ref.3), custom_call_target="tpu_custom_call" | custom-call | bytes 33554432 | tf_op jit(solution)/shard_map/pack/pallas_call | solution.py:137
  12.7 15.5 %pack.2 = (f32[2,8,64,128]{3,2,1,0:T(8,128)}, f32[2,8,64,128]{3,2,1,0:T(8,128)}, f32[2,8,64,128]{3,2,1,0:T(8,128)}, f32[2,8,64,128]{3,2,1,0:T(8,128)}, f32[2,8,6...) custom-call(s32[1]{0:T(128)} %bitcast.rank_ref, ...), custom_call_target="tpu_custom_call" | custom-call | bytes 33554432 | tf_op jit(solution)/shard_map/pack/pallas_call | solution.py:137
  28.3 7.3 %collective-permute-done.1.refs_2_ = f32[2,8,64,128]{3,2,1,0:T(8,128)S(1)} collective-permute-done((f32[2,8,64,128]{3,2,1,0:T(8,128)}, f32[2,8,64,128]{3,2,1,0:T(8,128)S(1)}, u32[]{:S(2)}, u32[]{:S(2)}) %collective-permute-start.1) | collective-permute-done | bytes 524320 | tf_op jit(solution)/shard_map/ppermute | solution.py:715
  38.1 11.2 %compress.8 = f32[32,2,64,128]{3,2,1,0:T(8,128)} custom-call(s32[1]{0:T(128)} %bitcast.rank_ref, f32[2,8,64,128]{3,2,1,0:T(8,128)} %get-tuple-element.244.refs_0_, f32[2,8,64,128]{3,2,1,0:T(8,128)} %copy-done.43, f32[2,8,64,128]{3,2,1,0:T(8,128)} %copy-done.44, f32[2,8,64,128]{3,2,1,0:T(8,128)} %copy-done.45, f32[2,32,128]{2,1,0:T(8,128)} %bitcast.68, ...), custom_call_target="tpu_custom_call" | custom-call | flops 1610612736 | bytes 4194304 | tf_op jit(solution)/shard_map/compress/pallas_call | solution.py:276
  57.2 33.2 %collective-permute-done.5.refs_3_ = f32[2,8,64,128]{3,2,1,0:T(8,128)S(1)} collective-permute-done((f32[2,8,64,128]{3,2,1,0:T(8,128)S(1)}, f32[2,8,64,128]{3,2,1,0:T(8,128)S(1)}, u32[]{:S(2)}, u32[]{:S(2)}) %collective-permute-start.5) | collective-permute-done | bytes 524320 | tf_op jit(solution)/shard_map/ppermute | solution.py:715
  91.8 11.2 %compress.9 = f32[32,2,64,128]{3,2,1,0:T(8,128)} custom-call(s32[1]{0:T(128)} %bitcast.rank_ref, f32[2,8,64,128]{3,2,1,0:T(8,128)} %get-tuple-element.254.refs_0_, f32[2,8,64,128]{3,2,1,0:T(8,128)} %copy-done.47, f32[2,8,64,128]{3,2,1,0:T(8,128)} %collective-permute-done.4.refs_2_, f32[2,8,64,128]{3,2,1,0:T(8,128)} %copy-done.49, f32[2,32,128]{2,1,0:T(8,128)} %bitcast.69, ...), custom_call_target="tpu_custom_call" | custom-call | flops 1610612736 | bytes 4194304 | tf_op jit(solution)/shard_map/compress/pallas_call | solution.py:276
  115.7 33.2 %collective-permute-done.8.refs_3_ = f32[2,8,64,128]{3,2,1,0:T(8,128)S(1)} collective-permute-done((f32[2,8,64,128]{3,2,1,0:T(8,128)}, f32[2,8,64,128]{3,2,1,0:T(8,128)S(1)}, u32[]{:S(2)}, u32[]{:S(2)}) %collective-permute-start.8) | collective-permute-done | bytes 524320 | tf_op jit(solution)/shard_map/ppermute | solution.py:715
  153.7 11.2 %compress.10 = f32[32,2,64,128]{3,2,1,0:T(8,128)} custom-call(s32[1]{0:T(128)} %bitcast.rank_ref, f32[2,8,64,128]{3,2,1,0:T(8,128)} %get-tuple-element.269.refs_0_, f32[2,8,64,128]{3,2,1,0:T(8,128)} %copy-done.46, f32[2,8,64,128]{3,2,1,0:T(8,128)} %collective-permute-done.7.refs_2_, f32[2,8,64,128]{3,2,1,0:T(8,128)} %copy-done.48, f32[2,32,128]{2,1,0:T(8,128)} %bitcast.70, ...), custom_call_target="tpu_custom_call" | custom-call | flops 1610612736 | bytes 4194304 | tf_op jit(solution)/shard_map/compress/pallas_call | solution.py:276
  190.1 7.2 %collective-permute-start.19 = (f32[16,2,32,128]{3,2,1,0:T(8,128)}, f32[16,2,32,128]{3,2,1,0:T(8,128)S(1)}, u32[]{:S(2)}, u32[]{:S(2)}) collective-permute-start(f32[16,2,32,128]{3,2,1,0:T(8,128)} %get-tuple-element.339), channel_id=1, source_target_pairs={{1,0},{2,1},{3,2},{4,3},{5,4},{6,5},{7,6},{8,7},{9,8},{10,9},{11,1... | collective-permute-start | bytes 1572872 | tf_op jit(solution)/shard_map/ppermute | solution.py:726
  210.1 11.2 %compress.11 = f32[32,2,64,128]{3,2,1,0:T(8,128)} custom-call(s32[1]{0:T(128)} %bitcast.rank_ref, f32[2,8,64,128]{3,2,1,0:T(8,128)} %get-tuple-element.295.refs_0_, f32[2,8,64,128]{3,2,1,0:T(8,128)} %collective-permute-done.9.refs_1_, f32[2,8,64,128]{3,2,1,0:T(8,128)} %collective-permute-done.10.refs_2_, f32[2,8,64,128]{3,2,1,0:T(8,128)} %collective-permute-done.11.refs_3_, ...), custom_call_target="tpu_custom_call" | custom-call | flops 1610612736 | bytes 4194304 | tf_op jit(solution)/shard_map/compress/pallas_call | solution.py:276
  221.4 15.9 %collective-permute-done.14.refs_3_ = f32[2,8,64,128]{3,2,1,0:T(8,128)} collective-permute-done((f32[2,8,64,128]{3,2,1,0:T(8,128)}, f32[2,8,64,128]{3,2,1,0:T(8,128)}, u32[]{:S(2)}, u32[]{:S(2)}) %collective-permute-start.14) | collective-permute-done | bytes 524320 | tf_op jit(solution)/shard_map/ppermute | solution.py:715
  240.5 8.6 %all-to-all-start.3 = ((f32[32,2,64,128]{3,2,1,0:T(8,128)}), f32[32,2,64,128]{3,2,1,0:T(8,128)}, u32[]{:S(2)}, u32[]{:S(2)}) async-start(f32[32,2,64,128]{3,2,1,0:T(8,128)} %compress.11), calls=%async_computation.3 | async-start | bytes 4194304 | tf_op jit(solution)/shard_map/all_to_all | solution.py:764
  254.6 7.2 %collective-permute-start.24 = (f32[16,2,32,128]{3,2,1,0:T(8,128)}, f32[16,2,32,128]{3,2,1,0:T(8,128)S(1)}, u32[]{:S(2)}, u32[]{:S(2)}) collective-permute-start(f32[16,2,32,128]{3,2,1,0:T(8,128)} %get-tuple-element.370), channel_id=1, source_target_pairs={{1,0},{2,1},{3,2},{4,3},{5,4},{6,5},{7,6},{8,7},{9,8},{10,9},{11,1... | collective-permute-start | bytes 1572872 | tf_op jit(solution)/shard_map/ppermute | solution.py:726
  261.8 11.2 %compress.12 = f32[32,2,64,128]{3,2,1,0:T(8,128)} custom-call(s32[1]{0:T(128)} %bitcast.rank_ref, f32[2,8,64,128]{3,2,1,0:T(8,128)} %get-tuple-element.323.refs_0_, f32[2,8,64,128]{3,2,1,0:T(8,128)} %copy-done.38, f32[2,8,64,128]{3,2,1,0:T(8,128)} %collective-permute-done.13.refs_2_, f32[2,8,64,128]{3,2,1,0:T(8,128)} %collective-permute-done.14.refs_3_, ...), custom_call_target="tpu_custom_call" | custom-call | flops 1610612736 | bytes 4194304 | tf_op jit(solution)/shard_map/compress/pallas_call | solution.py:276
  285.7 15.8 %collective-permute-done.17.refs_3_ = f32[2,8,64,128]{3,2,1,0:T(8,128)S(1)} collective-permute-done((f32[2,8,64,128]{3,2,1,0:T(8,128)}, f32[2,8,64,128]{3,2,1,0:T(8,128)S(1)}, u32[]{:S(2)}, u32[]{:S(2)}) %collective-permute-start.17) | collective-permute-done | bytes 524320 | tf_op jit(solution)/shard_map/ppermute | solution.py:715
  303.7 9.1 %all-to-all-start.4 = ((f32[32,2,64,128]{3,2,1,0:T(8,128)}), f32[32,2,64,128]{3,2,1,0:T(8,128)S(1)}, u32[]{:S(2)}, u32[]{:S(2)}) async-start(f32[32,2,64,128]{3,2,1,0:T(8,128)} %compress.12), calls=%async_computation.4 | async-start | bytes 4194304 | tf_op jit(solution)/shard_map/all_to_all | solution.py:764
  318.3 7.4 %collective-permute-start.26 = (f32[16,2,32,128]{3,2,1,0:T(8,128)}, f32[16,2,32,128]{3,2,1,0:T(8,128)S(1)}, u32[]{:S(2)}, u32[]{:S(2)}) collective-permute-start(f32[16,2,32,128]{3,2,1,0:T(8,128)} %get-tuple-element.382), channel_id=1, source_target_pairs={{1,0},{2,1},{3,2},{4,3},{5,4},{6,5},{7,6},{8,7},{9,8},{10,9},{11,1... | collective-permute-start | bytes 1572872 | tf_op jit(solution)/shard_map/ppermute | solution.py:726
  338.4 11.2 %compress.13 = f32[32,2,64,128]{3,2,1,0:T(8,128)} custom-call(s32[1]{0:T(128)} %bitcast.rank_ref, f32[2,8,64,128]{3,2,1,0:T(8,128)} %get-tuple-element.354.refs_0_, f32[2,8,64,128]{3,2,1,0:T(8,128)} %copy-done.34, f32[2,8,64,128]{3,2,1,0:T(8,128)} %copy-done.35, f32[2,8,64,128]{3,2,1,0:T(8,128)} %copy-done.37, f32[2,32,128]{2,1,0:T(8,128)} %bitcast.73, ...), custom_call_target="tpu_custom_call" | custom-call | flops 1610612736 | bytes 4194304 | tf_op jit(solution)/shard_map/compress/pallas_call | solution.py:276
  349.6 15.8 %collective-permute-done.22.refs_3_ = f32[2,8,64,128]{3,2,1,0:T(8,128)} collective-permute-done((f32[2,8,64,128]{3,2,1,0:T(8,128)}, f32[2,8,64,128]{3,2,1,0:T(8,128)}, u32[]{:S(2)}, u32[]{:S(2)}) %collective-permute-start.22) | collective-permute-done | bytes 524320 | tf_op jit(solution)/shard_map/ppermute | solution.py:715
  368.6 8.6 %all-to-all-start.5 = ((f32[32,2,64,128]{3,2,1,0:T(8,128)}), f32[32,2,64,128]{3,2,1,0:T(8,128)}, u32[]{:S(2)}, u32[]{:S(2)}) async-start(f32[32,2,64,128]{3,2,1,0:T(8,128)} %compress.13), calls=%async_computation.5 | async-start | bytes 4194304 | tf_op jit(solution)/shard_map/all_to_all | solution.py:764
  382.7 7.2 %collective-permute-start.31 = (f32[16,2,32,128]{3,2,1,0:T(8,128)}, f32[16,2,32,128]{3,2,1,0:T(8,128)S(1)}, u32[]{:S(2)}, u32[]{:S(2)}) collective-permute-start(f32[16,2,32,128]{3,2,1,0:T(8,128)} %get-tuple-element.400), channel_id=1, source_target_pairs={{1,0},{2,1},{3,2},{4,3},{5,4},{6,5},{7,6},{8,7},{9,8},{10,9},{11,1... | collective-permute-start | bytes 1572872 | tf_op jit(solution)/shard_map/ppermute | solution.py:726
  390.0 11.2 %compress.14 = f32[32,2,64,128]{3,2,1,0:T(8,128)} custom-call(s32[1]{0:T(128)} %bitcast.rank_ref, f32[2,8,64,128]{3,2,1,0:T(8,128)} %get-tuple-element.386.refs_0_, f32[2,8,64,128]{3,2,1,0:T(8,128)} %copy-done.36, f32[2,8,64,128]{3,2,1,0:T(8,128)} %collective-permute-done.21.refs_2_, f32[2,8,64,128]{3,2,1,0:T(8,128)} %collective-permute-done.22.refs_3_, ...), custom_call_target="tpu_custom_call" | custom-call | flops 1610612736 | bytes 4194304 | tf_op jit(solution)/shard_map/compress/pallas_call | solution.py:276
  409.2 20.5 %collective-permute-done.29.refs_3_ = f32[2,8,64,128]{3,2,1,0:T(8,128)S(1)} collective-permute-done((f32[2,8,64,128]{3,2,1,0:T(8,128)}, f32[2,8,64,128]{3,2,1,0:T(8,128)S(1)}, u32[]{:S(2)}, u32[]{:S(2)}) %collective-permute-start.29) | collective-permute-done | bytes 524320 | tf_op jit(solution)/shard_map/ppermute | solution.py:715
  431.8 9.1 %all-to-all-start.6 = ((f32[32,2,64,128]{3,2,1,0:T(8,128)}), f32[32,2,64,128]{3,2,1,0:T(8,128)S(1)}, u32[]{:S(2)}, u32[]{:S(2)}) async-start(f32[32,2,64,128]{3,2,1,0:T(8,128)} %compress.14), calls=%async_computation.6 | async-start | bytes 4194304 | tf_op jit(solution)/shard_map/all_to_all | solution.py:764
  456.2 11.2 %compress.15 = f32[32,2,64,128]{3,2,1,0:T(8,128)} custom-call(s32[1]{0:T(128)} %bitcast.rank_ref, f32[2,8,64,128]{3,2,1,0:T(8,128)} %get-tuple-element.402.refs_0_, f32[2,8,64,128]{3,2,1,0:T(8,128)} %copy-done.39, f32[2,8,64,128]{3,2,1,0:T(8,128)} %copy-done.40, f32[2,8,64,128]{3,2,1,0:T(8,128)} %copy-done.41, f32[2,32,128]{2,1,0:T(8,128)} %bitcast.75, ...), custom_call_target="tpu_custom_call" | custom-call | flops 1610612736 | bytes 4194304 | tf_op jit(solution)/shard_map/compress/pallas_call | solution.py:276
  467.4 23.4 %collective-permute-done.32.refs_5_ = f32[16,2,32,128]{3,2,1,0:T(8,128)S(1)} collective-permute-done((f32[16,2,32,128]{3,2,1,0:T(8,128)}, f32[16,2,32,128]{3,2,1,0:T(8,128)S(1)}, u32[]{:S(2)}, u32[]{:S(2)}) %collective-permute-start.32) | collective-permute-done | bytes 524320 | tf_op jit(solution)/shard_map/ppermute | solution.py:725
  496.7 8.6 %all-to-all-start.7 = ((f32[32,2,64,128]{3,2,1,0:T(8,128)}), f32[32,2,64,128]{3,2,1,0:T(8,128)}, u32[]{:S(2)}, u32[]{:S(2)}) async-start(f32[32,2,64,128]{3,2,1,0:T(8,128)} %compress.15), calls=%async_computation.7 | async-start | bytes 4194304 | tf_op jit(solution)/shard_map/all_to_all | solution.py:764
  533.0 26.9 %all-to-all-done.7 = f32[32,2,64,128]{3,2,1,0:T(8,128)} async-done(((f32[32,2,64,128]{3,2,1,0:T(8,128)}), f32[32,2,64,128]{3,2,1,0:T(8,128)}, u32[]{:S(2)}, u32[]{:S(2)}) %all-to-all-start.7) | async-done | bytes 2097184 | tf_op jit(solution)/shard_map/all_to_all | solution.py:764
  567.9 7.2 %collective-permute-start.39 = (f32[16,2,32,128]{3,2,1,0:T(8,128)}, f32[16,2,32,128]{3,2,1,0:T(8,128)S(1)}, u32[]{:S(2)}, u32[]{:S(2)}) collective-permute-start(f32[16,2,32,128]{3,2,1,0:T(8,128)} %get-tuple-element.439), channel_id=1, source_target_pairs={{1,0},{2,1},{3,2},{4,3},{5,4},{6,5},{7,6},{8,7},{9,8},{10,9},{11,1... | collective-permute-start | bytes 1572872 | tf_op jit(solution)/shard_map/ppermute | solution.py:726
  577.1 7.5 %collective-permute-start.38 = (f32[16,2,32,128]{3,2,1,0:T(8,128)}, f32[16,2,32,128]{3,2,1,0:T(8,128)S(1)}, u32[]{:S(2)}, u32[]{:S(2)}) collective-permute-start(f32[16,2,32,128]{3,2,1,0:T(8,128)} %get-tuple-element.438), channel_id=1, source_target_pairs={{1,0},{2,1},{3,2},{4,3},{5,4},{6,5},{7,6},{8,7},{9,8},{10,9},{11,1... | collective-permute-start | bytes 1572872 | tf_op jit(solution)/shard_map/ppermute | solution.py:726
  584.6 30.8 %final_inner.1 = (f32[2,128,16384]{2,1,0:T(8,128)}, bf16[8,16,256,256]{3,2,1,0:T(8,128)(2,1)}) custom-call(f32[16,2,128,128]{3,2,1,0:T(8,128)} %get-tuple-element.289.refs_0_, f32[16,2,128,128]{3,2,1,0:T(8,128)} %get-tuple-element.317.refs_1_, f32[16,2,128,128]{3,2,1,0:T(8,128)} %get-tuple-element.348.refs_2_, ...), custom_call_target="tpu_custom_call" | custom-call | flops 9663676416 | bytes 29360128 | tf_op jit(solution)/shard_map/final_inner/pallas_call | solution.py:646
  616.9 27.7 %final_wide.1 = f32[2,128,16384]{2,1,0:T(8,128)} custom-call(bf16[8,16,256,256]{3,2,1,0:T(8,128)(2,1)} %get-tuple-element.423.refs_0_, f32[16,2,32,128]{3,2,1,0:T(8,128)} %copy-done.7, f32[16,2,32,128]{3,2,1,0:T(8,128)} %copy-done.9, f32[16,2,32,128]{3,2,1,0:T(8,128)} %copy-done.11, f32[16,2,32,128]{3,2,1,0:T(8,128)} %copy-done.13, ...), custom_call_target="tpu_custom_call", output_to_operand_aliasing={{}: (23, {})} | custom-call | flops 9663676416 | bytes 29360128 | tf_op jit(solution)/shard_map/final_wide/pallas_call | solution.py:646
  (219 shorter events, 191.0 us)
Async XLA Ops:
  50.1 58.7 %all-to-all-start = ((f32[32,2,64,128]{3,2,1,0:T(8,128)}), f32[32,2,64,128]{3,2,1,0:T(8,128)S(1)}, u32[]{:S(2)}, u32[]{:S(2)}) async-start(f32[32,2,64,128]{3,2,1,0:T(8,128)} %compress.8), calls=%async_computation | async-start | bytes 4194304 | tf_op jit(solution)/shard_map/all_to_all | solution.py:764
  110.2 69.2 %all-to-all-start.1 = ((f32[32,2,64,128]{3,2,1,0:T(8,128)}), f32[32,2,64,128]{3,2,1,0:T(8,128)S(1)}, u32[]{:S(2)}, u32[]{:S(2)}) async-start(f32[32,2,64,128]{3,2,1,0:T(8,128)} %compress.9), calls=%async_computation.1 | async-start | bytes 4194304 | tf_op jit(solution)/shard_map/all_to_all | solution.py:764
  180.7 58.5 %all-to-all-start.2 = ((f32[32,2,64,128]{3,2,1,0:T(8,128)}), f32[32,2,64,128]{3,2,1,0:T(8,128)S(1)}, u32[]{:S(2)}, u32[]{:S(2)}) async-start(f32[32,2,64,128]{3,2,1,0:T(8,128)} %compress.10), calls=%async_computation.2 | async-start | bytes 4194304 | tf_op jit(solution)/shard_map/all_to_all | solution.py:764
  184.7 36.6 %collective-permute-start.12 = (f32[2,8,64,128]{3,2,1,0:T(8,128)}, f32[2,8,64,128]{3,2,1,0:T(8,128)S(1)}, u32[]{:S(2)}, u32[]{:S(2)}) collective-permute-start(f32[2,8,64,128]{3,2,1,0:T(8,128)} %get-tuple-element.299), channel_id=1, source_target_pairs={{0,8},{8,0},{16,24},{24,16},{1,9},{9,1},{17,25},{25,17},{2,10},{10... | collective-permute-start | bytes 1572872 | tf_op jit(solution)/shard_map/ppermute | solution.py:715
  186.8 50.5 %collective-permute-start.14 = (f32[2,8,64,128]{3,2,1,0:T(8,128)}, f32[2,8,64,128]{3,2,1,0:T(8,128)}, u32[]{:S(2)}, u32[]{:S(2)}) collective-permute-start(f32[2,8,64,128]{3,2,1,0:T(8,128)} %get-tuple-element.301), channel_id=1, source_target_pairs={{0,24},{8,16},{16,8},{24,0},{1,25},{9,17},{17,9},{25,1},{2,26},{10... | collective-permute-start | bytes 1572872 | tf_op jit(solution)/shard_map/ppermute | solution.py:715
  188.2 49.1 %collective-permute-start.18 = (f32[16,2,32,128]{3,2,1,0:T(8,128)}, f32[16,2,32,128]{3,2,1,0:T(8,128)S(1)}, u32[]{:S(2)}, u32[]{:S(2)}) collective-permute-start(f32[16,2,32,128]{3,2,1,0:T(8,128)} %get-tuple-element.338), channel_id=1, source_target_pairs={{0,1},{1,2},{2,3},{3,4},{4,5},{5,6},{6,7},{7,8},{8,9},{9,10},{10,1... | collective-permute-start | bytes 1572872 | tf_op jit(solution)/shard_map/ppermute | solution.py:725
  190.1 47.2 %collective-permute-start.19 = (f32[16,2,32,128]{3,2,1,0:T(8,128)}, f32[16,2,32,128]{3,2,1,0:T(8,128)S(1)}, u32[]{:S(2)}, u32[]{:S(2)}) collective-permute-start(f32[16,2,32,128]{3,2,1,0:T(8,128)} %get-tuple-element.339), channel_id=1, source_target_pairs={{1,0},{2,1},{3,2},{4,3},{5,4},{6,5},{7,6},{8,7},{9,8},{10,9},{11,1... | collective-permute-start | bytes 1572872 | tf_op jit(solution)/shard_map/ppermute | solution.py:726
  240.5 63.2 %all-to-all-start.3 = ((f32[32,2,64,128]{3,2,1,0:T(8,128)}), f32[32,2,64,128]{3,2,1,0:T(8,128)}, u32[]{:S(2)}, u32[]{:S(2)}) async-start(f32[32,2,64,128]{3,2,1,0:T(8,128)} %compress.11), calls=%async_computation.3 | async-start | bytes 4194304 | tf_op jit(solution)/shard_map/all_to_all | solution.py:764
  249.1 36.6 %collective-permute-start.15 = (f32[2,8,64,128]{3,2,1,0:T(8,128)}, f32[2,8,64,128]{3,2,1,0:T(8,128)S(1)}, u32[]{:S(2)}, u32[]{:S(2)}) collective-permute-start(f32[2,8,64,128]{3,2,1,0:T(8,128)} %get-tuple-element.327), channel_id=1, source_target_pairs={{0,8},{8,0},{16,24},{24,16},{1,9},{9,1},{17,25},{25,17},{2,10},{10... | collective-permute-start | bytes 1572872 | tf_op jit(solution)/shard_map/ppermute | solution.py:715
  251.2 50.3 %collective-permute-start.17 = (f32[2,8,64,128]{3,2,1,0:T(8,128)}, f32[2,8,64,128]{3,2,1,0:T(8,128)S(1)}, u32[]{:S(2)}, u32[]{:S(2)}) collective-permute-start(f32[2,8,64,128]{3,2,1,0:T(8,128)} %get-tuple-element.329), channel_id=1, source_target_pairs={{0,24},{8,16},{16,8},{24,0},{1,25},{9,17},{17,9},{25,1},{2,26},{10... | collective-permute-start | bytes 1572872 | tf_op jit(solution)/shard_map/ppermute | solution.py:715
  252.7 48.9 %collective-permute-start.23 = (f32[16,2,32,128]{3,2,1,0:T(8,128)}, f32[16,2,32,128]{3,2,1,0:T(8,128)S(1)}, u32[]{:S(2)}, u32[]{:S(2)}) collective-permute-start(f32[16,2,32,128]{3,2,1,0:T(8,128)} %get-tuple-element.369), channel_id=1, source_target_pairs={{0,1},{1,2},{2,3},{3,4},{4,5},{5,6},{6,7},{7,8},{8,9},{9,10},{10,1... | collective-permute-start | bytes 1572872 | tf_op jit(solution)/shard_map/ppermute | solution.py:725
  254.6 47.0 %collective-permute-start.24 = (f32[16,2,32,128]{3,2,1,0:T(8,128)}, f32[16,2,32,128]{3,2,1,0:T(8,128)S(1)}, u32[]{:S(2)}, u32[]{:S(2)}) collective-permute-start(f32[16,2,32,128]{3,2,1,0:T(8,128)} %get-tuple-element.370), channel_id=1, source_target_pairs={{1,0},{2,1},{3,2},{4,3},{5,4},{6,5},{7,6},{8,7},{9,8},{10,9},{11,1... | collective-permute-start | bytes 1572872 | tf_op jit(solution)/shard_map/ppermute | solution.py:726
  303.7 63.6 %all-to-all-start.4 = ((f32[32,2,64,128]{3,2,1,0:T(8,128)}), f32[32,2,64,128]{3,2,1,0:T(8,128)S(1)}, u32[]{:S(2)}, u32[]{:S(2)}) async-start(f32[32,2,64,128]{3,2,1,0:T(8,128)} %compress.12), calls=%async_computation.4 | async-start | bytes 4194304 | tf_op jit(solution)/shard_map/all_to_all | solution.py:764
  312.8 36.8 %collective-permute-start.20 = (f32[2,8,64,128]{3,2,1,0:T(8,128)}, f32[2,8,64,128]{3,2,1,0:T(8,128)S(1)}, u32[]{:S(2)}, u32[]{:S(2)}) collective-permute-start(f32[2,8,64,128]{3,2,1,0:T(8,128)} %get-tuple-element.358), channel_id=1, source_target_pairs={{0,8},{8,0},{16,24},{24,16},{1,9},{9,1},{17,25},{25,17},{2,10},{10... | collective-permute-start | bytes 1572872 | tf_op jit(solution)/shard_map/ppermute | solution.py:715
  314.3 35.3 %collective-permute-start.21 = (f32[2,8,64,128]{3,2,1,0:T(8,128)}, f32[2,8,64,128]{3,2,1,0:T(8,128)}, u32[]{:S(2)}, u32[]{:S(2)}) collective-permute-start(f32[2,8,64,128]{3,2,1,0:T(8,128)} %get-tuple-element.359), channel_id=1, source_target_pairs={{0,16},{8,24},{16,0},{24,8},{1,17},{9,25},{17,1},{25,9},{2,18},{10... | collective-permute-start | bytes 1572872 | tf_op jit(solution)/shard_map/ppermute | solution.py:715
  314.9 50.5 %collective-permute-start.22 = (f32[2,8,64,128]{3,2,1,0:T(8,128)}, f32[2,8,64,128]{3,2,1,0:T(8,128)}, u32[]{:S(2)}, u32[]{:S(2)}) collective-permute-start(f32[2,8,64,128]{3,2,1,0:T(8,128)} %get-tuple-element.360), channel_id=1, source_target_pairs={{0,24},{8,16},{16,8},{24,0},{1,25},{9,17},{17,9},{25,1},{2,26},{10... | collective-permute-start | bytes 1572872 | tf_op jit(solution)/shard_map/ppermute | solution.py:715
  316.4 49.1 %collective-permute-start.25 = (f32[16,2,32,128]{3,2,1,0:T(8,128)}, f32[16,2,32,128]{3,2,1,0:T(8,128)S(1)}, u32[]{:S(2)}, u32[]{:S(2)}) collective-permute-start(f32[16,2,32,128]{3,2,1,0:T(8,128)} %get-tuple-element.381), channel_id=1, source_target_pairs={{0,1},{1,2},{2,3},{3,4},{4,5},{5,6},{6,7},{7,8},{8,9},{9,10},{10,1... | collective-permute-start | bytes 1572872 | tf_op jit(solution)/shard_map/ppermute | solution.py:725
  318.3 47.2 %collective-permute-start.26 = (f32[16,2,32,128]{3,2,1,0:T(8,128)}, f32[16,2,32,128]{3,2,1,0:T(8,128)S(1)}, u32[]{:S(2)}, u32[]{:S(2)}) collective-permute-start(f32[16,2,32,128]{3,2,1,0:T(8,128)} %get-tuple-element.382), channel_id=1, source_target_pairs={{1,0},{2,1},{3,2},{4,3},{5,4},{6,5},{7,6},{8,7},{9,8},{10,9},{11,1... | collective-permute-start | bytes 1572872 | tf_op jit(solution)/shard_map/ppermute | solution.py:726
  368.6 63.2 %all-to-all-start.5 = ((f32[32,2,64,128]{3,2,1,0:T(8,128)}), f32[32,2,64,128]{3,2,1,0:T(8,128)}, u32[]{:S(2)}, u32[]{:S(2)}) async-start(f32[32,2,64,128]{3,2,1,0:T(8,128)} %compress.13), calls=%async_computation.5 | async-start | bytes 4194304 | tf_op jit(solution)/shard_map/all_to_all | solution.py:764
  379.3 50.3 %collective-permute-start.29 = (f32[2,8,64,128]{3,2,1,0:T(8,128)}, f32[2,8,64,128]{3,2,1,0:T(8,128)S(1)}, u32[]{:S(2)}, u32[]{:S(2)}) collective-permute-start(f32[2,8,64,128]{3,2,1,0:T(8,128)} %get-tuple-element.392), channel_id=1, source_target_pairs={{0,24},{8,16},{16,8},{24,0},{1,25},{9,17},{17,9},{25,1},{2,26},{10... | collective-permute-start | bytes 1572872 | tf_op jit(solution)/shard_map/ppermute | solution.py:715
  380.8 48.9 %collective-permute-start.30 = (f32[16,2,32,128]{3,2,1,0:T(8,128)}, f32[16,2,32,128]{3,2,1,0:T(8,128)S(1)}, u32[]{:S(2)}, u32[]{:S(2)}) collective-permute-start(f32[16,2,32,128]{3,2,1,0:T(8,128)} %get-tuple-element.399), channel_id=1, source_target_pairs={{0,1},{1,2},{2,3},{3,4},{4,5},{5,6},{6,7},{7,8},{8,9},{9,10},{10,1... | collective-permute-start | bytes 1572872 | tf_op jit(solution)/shard_map/ppermute | solution.py:725
  382.7 47.0 %collective-permute-start.31 = (f32[16,2,32,128]{3,2,1,0:T(8,128)}, f32[16,2,32,128]{3,2,1,0:T(8,128)S(1)}, u32[]{:S(2)}, u32[]{:S(2)}) collective-permute-start(f32[16,2,32,128]{3,2,1,0:T(8,128)} %get-tuple-element.400), channel_id=1, source_target_pairs={{1,0},{2,1},{3,2},{4,3},{5,4},{6,5},{7,6},{8,7},{9,8},{10,9},{11,1... | collective-permute-start | bytes 1572872 | tf_op jit(solution)/shard_map/ppermute | solution.py:726
  431.8 63.6 %all-to-all-start.6 = ((f32[32,2,64,128]{3,2,1,0:T(8,128)}), f32[32,2,64,128]{3,2,1,0:T(8,128)S(1)}, u32[]{:S(2)}, u32[]{:S(2)}) async-start(f32[32,2,64,128]{3,2,1,0:T(8,128)} %compress.14), calls=%async_computation.6 | async-start | bytes 4194304 | tf_op jit(solution)/shard_map/all_to_all | solution.py:764
  440.9 50.0 %collective-permute-start.32 = (f32[16,2,32,128]{3,2,1,0:T(8,128)}, f32[16,2,32,128]{3,2,1,0:T(8,128)S(1)}, u32[]{:S(2)}, u32[]{:S(2)}) collective-permute-start(f32[16,2,32,128]{3,2,1,0:T(8,128)} %get-tuple-element.411), channel_id=1, source_target_pairs={{0,1},{1,2},{2,3},{3,4},{4,5},{5,6},{6,7},{7,8},{8,9},{9,10},{10,1... | collective-permute-start | bytes 1572872 | tf_op jit(solution)/shard_map/ppermute | solution.py:725
  443.0 47.9 %collective-permute-start.33 = (f32[16,2,32,128]{3,2,1,0:T(8,128)}, f32[16,2,32,128]{3,2,1,0:T(8,128)S(1)}, u32[]{:S(2)}, u32[]{:S(2)}) collective-permute-start(f32[16,2,32,128]{3,2,1,0:T(8,128)} %get-tuple-element.412), channel_id=1, source_target_pairs={{1,0},{2,1},{3,2},{4,3},{5,4},{6,5},{7,6},{8,7},{9,8},{10,9},{11,1... | collective-permute-start | bytes 1572872 | tf_op jit(solution)/shard_map/ppermute | solution.py:726
  496.7 63.2 %all-to-all-start.7 = ((f32[32,2,64,128]{3,2,1,0:T(8,128)}), f32[32,2,64,128]{3,2,1,0:T(8,128)}, u32[]{:S(2)}, u32[]{:S(2)}) async-start(f32[32,2,64,128]{3,2,1,0:T(8,128)} %compress.15), calls=%async_computation.7 | async-start | bytes 4194304 | tf_op jit(solution)/shard_map/all_to_all | solution.py:764
  514.5 62.6 %collective-permute-start.34 = (f32[16,2,32,128]{3,2,1,0:T(8,128)S(1)}, f32[16,2,32,128]{3,2,1,0:T(8,128)S(1)}, u32[]{:S(2)}, u32[]{:S(2)}) collective-permute-start(f32[16,2,32,128]{3,2,1,0:T(8,128)S(1)} %copy-done.31), channel_id=1, source_target_pairs={{0,1},{1,2},{2,3},{3,4},{4,5},{5,6},{6,7},{7,8},{8,9},{9,10},{10,1... | collective-permute-start | bytes 1572872 | tf_op jit(solution)/shard_map/ppermute | solution.py:725
  519.8 95.7 %collective-permute-start.37 = (f32[16,2,32,128]{3,2,1,0:T(8,128)S(1)}, f32[16,2,32,128]{3,2,1,0:T(8,128)S(1)}, u32[]{:S(2)}, u32[]{:S(2)}) collective-permute-start(f32[16,2,32,128]{3,2,1,0:T(8,128)S(1)} %copy-done.30), channel_id=1, source_target_pairs={{1,0},{2,1},{3,2},{4,3},{5,4},{6,5},{7,6},{8,7},{9,8},{10,9},{11,1... | collective-permute-start | bytes 1572872 | tf_op jit(solution)/shard_map/ppermute | solution.py:726
  566.0 49.4 %collective-permute-start.36 = (f32[16,2,32,128]{3,2,1,0:T(8,128)}, f32[16,2,32,128]{3,2,1,0:T(8,128)S(1)}, u32[]{:S(2)}, u32[]{:S(2)}) collective-permute-start(f32[16,2,32,128]{3,2,1,0:T(8,128)} %get-tuple-element.431), channel_id=1, source_target_pairs={{0,1},{1,2},{2,3},{3,4},{4,5},{5,6},{6,7},{7,8},{8,9},{9,10},{10,1... | collective-permute-start | bytes 1572872 | tf_op jit(solution)/shard_map/ppermute | solution.py:725
  567.9 47.5 %collective-permute-start.39 = (f32[16,2,32,128]{3,2,1,0:T(8,128)}, f32[16,2,32,128]{3,2,1,0:T(8,128)S(1)}, u32[]{:S(2)}, u32[]{:S(2)}) collective-permute-start(f32[16,2,32,128]{3,2,1,0:T(8,128)} %get-tuple-element.439), channel_id=1, source_target_pairs={{1,0},{2,1},{3,2},{4,3},{5,4},{6,5},{7,6},{8,7},{9,8},{10,9},{11,1... | collective-permute-start | bytes 1572872 | tf_op jit(solution)/shard_map/ppermute | solution.py:726
  575.2 40.3 %collective-permute-start.35 = (f32[16,2,32,128]{3,2,1,0:T(8,128)}, f32[16,2,32,128]{3,2,1,0:T(8,128)S(1)}, u32[]{:S(2)}, u32[]{:S(2)}) collective-permute-start(f32[16,2,32,128]{3,2,1,0:T(8,128)} %get-tuple-element.430), channel_id=1, source_target_pairs={{0,1},{1,2},{2,3},{3,4},{4,5},{5,6},{6,7},{7,8},{8,9},{9,10},{10,1... | collective-permute-start | bytes 1572872 | tf_op jit(solution)/shard_map/ppermute | solution.py:725
  577.1 38.4 %collective-permute-start.38 = (f32[16,2,32,128]{3,2,1,0:T(8,128)}, f32[16,2,32,128]{3,2,1,0:T(8,128)S(1)}, u32[]{:S(2)}, u32[]{:S(2)}) collective-permute-start(f32[16,2,32,128]{3,2,1,0:T(8,128)} %get-tuple-element.438), channel_id=1, source_target_pairs={{1,0},{2,1},{3,2},{4,3},{5,4},{6,5},{7,6},{8,7},{9,8},{10,9},{11,1... | collective-permute-start | bytes 1572872 | tf_op jit(solution)/shard_map/ppermute | solution.py:726
  (67 other events, 1565.7 us)

commit v6 on v5

--- a/solution.py
+++ b/solution.py
@@ -720,6 +720,9 @@
         for place, c in enumerate(GROUPED[g]):
             if c > 0:
                 turned[g], mains[c - 1] = lax.optimization_barrier((turned[g], mains[c - 1]))
+            if 0 < c < CHUNKS - 1:
+                held = (turned[g], lows[c - 1], highs[c - 1])
+                turned[g], lows[c - 1], highs[c - 1] = lax.optimization_barrier(held)
             main, up, down = azimuth(turned[g], c, place)
             mains[c] = main
             lows[c] = lax.ppermute(up, axes, neighbours(axes, devices, 1))
@@ -734,25 +737,19 @@
     got.append(gather(1))
     count = len(GROUPED)
     for g, chunks in enumerate(GROUPED):
+        if g >= 2:
+            transform(g - 2)
+            for c in GROUPED[g - 2]:
+                got[g], mains[c] = lax.optimization_barrier((got[g], mains[c]))
         lines = compress(got[g], rank, chirp)
         if g + 1 < count:
-            held = got[g + 1][1 : (3 if g < 2 else nrng)]
-            lines, held = lax.optimization_barrier((lines, held))
-            got[g + 1][1 : 1 + len(held)] = held
+            lines, got[g + 1] = lax.optimization_barrier((lines, got[g + 1]))
         if g + 2 < count:
             packed[g + 2], got[g + 1] = lax.optimization_barrier((packed[g + 2], got[g + 1]))
             if g >= 1:
                 held = (packed[g + 2], turned[g - 1])
                 packed[g + 2], turned[g - 1] = lax.optimization_barrier(held)
             got.append(gather(g + 2))
-        if g >= 2:
-            transform(g - 2)
-            for c in GROUPED[g - 2]:
-                lines, mains[c] = lax.optimization_barrier((lines, mains[c]))
-        if g >= 3:
-            for c in GROUPED[g - 3]:
-                held = (lines, lows[c], highs[c])
-                lines, lows[c], highs[c] = lax.optimization_barrier(held)
         if 2 <= g and len(places) > 1 and len(phases) < CHUNKS // 2:
             inner_rate, turned[g - 2] = lax.optimization_barrier((inner_rate, turned[g - 2]))
             table = phase_table(inner_rate, len(phases))

time: 647 us -> 751 us (1.16)
  waiting for transfers between devices: 213 us -> 289 us
  starting transfers between devices: 159 us -> 181 us
    ppermute x8, waiting for transfers between devices: 23.4 us -> 218 us  [transform(): lows[c] = lax.ppermute(up, axes, neighbours(axes, devices, 1))]
    ppermute x24, waiting for transfers between devices: 151 us -> 69.7 us  [gather(): lax.ppermute(packed[g][j], 'rng', [(i, i ^ j) for i in range(nrng)])]
    all_to_all x8, waiting for transfers between devices: 39.3 us -> 2.12 us  [local(): moved = lax.all_to_all(lines, axes, split_axis=0, concat_axis=0, tiled=True)]
    all_to_all x8, starting transfers between devices: 57.7 us -> 78.7 us  [local(): moved = lax.all_to_all(lines, axes, split_axis=0, concat_axis=0, tiled=True)]
  transfers between devices with their start and end apart: 48 -> 48, of which waited for: 18 -> 14; matrix products, arithmetic and copies ran while one was open for 2% -> 2% of each run, Pallas kernels for 33% -> 28%
where the time goes in v6:
time: 751 us; the launch traced here: 748 us
  waiting for transfers between devices  289 us (38%)
  Pallas kernels  250 us (33%)
  starting transfers between devices  181 us (24%)
  local copies, waits for them, and re-layouts  18.4 us (2%)
  other arithmetic  7.79 us (1%)
    ppermute x8, waiting for transfers between devices, transform(): lows[c] = lax.ppermute(up, axes, neighbours(axes, devices, 1))  218 us
    pallas_call x8, Pallas kernels, compress(): pl.pallas_call(functools.partial(compress_kernel, parts, block), grid=(ro...  89.5 us
    all_to_all x8, starting transfers between devices, local(): moved = lax.all_to_all(lines, axes, split_axis=0, concat_axis=0, tiled=True)  78.7 us
    ppermute x24, waiting for transfers between devices, gather(): lax.ppermute(packed[g][j], 'rng', [(i, i ^ j) for i in range(nrng)])  69.7 us
    pallas_call x2, Pallas kernels, final(): pl.pallas_call(functools.partial(final_kernel, steps, joins, wide), grid=...  58.5 us
    ppermute x8, starting transfers between devices, transform(): highs[c] = lax.ppermute(down, axes, neighbours(axes, devices, -1))  57.5 us
    pallas_call x8, Pallas kernels, azimuth(): pl.pallas_call(functools.partial(azimuth_kernel, chunk), grid=(parts,), i...  50.8 us
    ppermute x24, starting transfers between devices, gather(): lax.ppermute(packed[g][j], 'rng', [(i, i ^ j) for i in range(nrng)])  28.4 us
  transfers between devices with their start and end apart: 48, of which 14 were waited for; matrix products, arithmetic and copies ran while one was open for 2% of the time, Pallas kernels for 28%

profile of v6, /device:TPU:4, one launch (start us, length us, event | category | flops | bytes accessed | tf_op | source)
XLA Modules:
  0.0 748.0 jit_solution(7960550206711262422)
XLA Ops:
  0.0 9.3 %pack.3 = (f32[2,8,64,128]{3,2,1,0:T(8,128)}, f32[2,8,64,128]{3,2,1,0:T(8,128)}, f32[2,8,64,128]{3,2,1,0:T(8,128)}, f32[2,8,64,128]{3,2,1,0:T(8,128)}) custom-call(s32[1]{0:T(128)} %bitcast.rank_ref, f32[2,2048,1024]{2,1,0:T(8,128)} %x_ref.3), custom_call_target="tpu_custom_call" | custom-call | bytes 33554432 | tf_op jit(solution)/shard_map/pack/pallas_call | solution.py:137
  12.8 15.6 %pack.2 = (f32[2,8,64,128]{3,2,1,0:T(8,128)}, f32[2,8,64,128]{3,2,1,0:T(8,128)}, f32[2,8,64,128]{3,2,1,0:T(8,128)}, f32[2,8,64,128]{3,2,1,0:T(8,128)}, f32[2,8,6...) custom-call(s32[1]{0:T(128)} %bitcast.rank_ref, ...), custom_call_target="tpu_custom_call" | custom-call | bytes 33554432 | tf_op jit(solution)/shard_map/pack/pallas_call | solution.py:137
  28.4 7.2 collective-permute-done.1.refs_2_
  40.0 11.2 %compress.8 = f32[32,2,64,128]{3,2,1,0:T(8,128)} custom-call(s32[1]{0:T(128)} %bitcast.rank_ref, f32[2,8,64,128]{3,2,1,0:T(8,128)} %get-tuple-element.273.refs_0_, f32[2,8,64,128]{3,2,1,0:T(8,128)} %copy-done.39, f32[2,8,64,128]{3,2,1,0:T(8,128)} %copy-done.40, f32[2,8,64,128]{3,2,1,0:T(8,128)} %copy-done.41, f32[2,32,128]{2,1,0:T(8,128)} %bitcast.68, ...), custom_call_target="tpu_custom_call" | custom-call | flops 1610612736 | bytes 4194304 | tf_op jit(solution)/shard_map/compress/pallas_call | solution.py:276
  51.2 8.6 %collective-permute-done.4.refs_2_ = f32[2,8,64,128]{3,2,1,0:T(8,128)S(1)} collective-permute-done((f32[2,8,64,128]{3,2,1,0:T(8,128)}, f32[2,8,64,128]{3,2,1,0:T(8,128)S(1)}, u32[]{:S(2)}, u32[]{:S(2)}) %collective-permute-start.4) | collective-permute-done | bytes 524320 | tf_op jit(solution)/shard_map/ppermute | solution.py:715
  69.4 11.2 %compress.9 = f32[32,2,64,128]{3,2,1,0:T(8,128)} custom-call(s32[1]{0:T(128)} %bitcast.rank_ref, f32[2,8,64,128]{3,2,1,0:T(8,128)} %get-tuple-element.285.refs_0_, f32[2,8,64,128]{3,2,1,0:T(8,128)} %copy-done.45, f32[2,8,64,128]{3,2,1,0:T(8,128)} %copy-done.46, f32[2,8,64,128]{3,2,1,0:T(8,128)} %collective-permute-done.5.refs_3_, f32[2,32,128]{2,1,0:T(8,128)} %bitcast.69, ...), custom_call_target="tpu_custom_call" | custom-call | flops 1610612736 | bytes 4194304 | tf_op jit(solution)/shard_map/compress/pallas_call | solution.py:276
  80.7 16.2 %collective-permute-done.6.refs_1_ = f32[2,8,64,128]{3,2,1,0:T(8,128)S(1)} collective-permute-done((f32[2,8,64,128]{3,2,1,0:T(8,128)}, f32[2,8,64,128]{3,2,1,0:T(8,128)S(1)}, u32[]{:S(2)}, u32[]{:S(2)}) %collective-permute-start.6) | collective-permute-done | bytes 524320 | tf_op jit(solution)/shard_map/ppermute | solution.py:715
  97.9 14.8 %collective-permute-done.8.refs_3_ = f32[2,8,64,128]{3,2,1,0:T(8,128)} collective-permute-done((f32[2,8,64,128]{3,2,1,0:T(8,128)}, f32[2,8,64,128]{3,2,1,0:T(8,128)}, u32[]{:S(2)}, u32[]{:S(2)}) %collective-permute-start.8) | collective-permute-done | bytes 524320 | tf_op jit(solution)/shard_map/ppermute | solution.py:715
  138.8 11.2 %compress.10 = f32[32,2,64,128]{3,2,1,0:T(8,128)} custom-call(s32[1]{0:T(128)} %bitcast.rank_ref, f32[2,8,64,128]{3,2,1,0:T(8,128)} %get-tuple-element.308.refs_0_, f32[2,8,64,128]{3,2,1,0:T(8,128)} %copy-done.42, f32[2,8,64,128]{3,2,1,0:T(8,128)} %collective-permute-done.7.refs_2_, f32[2,8,64,128]{3,2,1,0:T(8,128)} %collective-permute-done.8.refs_3_, ...), custom_call_target="tpu_custom_call" | custom-call | flops 1610612736 | bytes 4194304 | tf_op jit(solution)/shard_map/compress/pallas_call | solution.py:276
  149.9 15.9 %collective-permute-done.10.refs_2_ = f32[2,8,64,128]{3,2,1,0:T(8,128)} collective-permute-done((f32[2,8,64,128]{3,2,1,0:T(8,128)}, f32[2,8,64,128]{3,2,1,0:T(8,128)}, u32[]{:S(2)}, u32[]{:S(2)}) %collective-permute-start.10) | collective-permute-done | bytes 524320 | tf_op jit(solution)/shard_map/ppermute | solution.py:715
  189.9 37.2 %collective-permute-done.12.refs_1_ = f32[16,2,32,128]{3,2,1,0:T(8,128)S(1)} collective-permute-done((f32[16,2,32,128]{3,2,1,0:T(8,128)}, f32[16,2,32,128]{3,2,1,0:T(8,128)S(1)}, u32[]{:S(2)}, u32[]{:S(2)}) %collective-permute-start.12) | collective-permute-done | bytes 524320 | tf_op jit(solution)/shard_map/ppermute | solution.py:728
  240.3 11.2 %compress.11 = f32[32,2,64,128]{3,2,1,0:T(8,128)} custom-call(s32[1]{0:T(128)} %bitcast.rank_ref, f32[2,8,64,128]{3,2,1,0:T(8,128)} %get-tuple-element.341.refs_0_, f32[2,8,64,128]{3,2,1,0:T(8,128)} %collective-permute-done.9.refs_1_, f32[2,8,64,128]{3,2,1,0:T(8,128)} %collective-permute-done.10.refs_2_, f32[2,8,64,128]{3,2,1,0:T(8,128)} %collective-permute-done.11.refs_3_, ...), custom_call_target="tpu_custom_call" | custom-call | flops 1610612736 | bytes 4194304 | tf_op jit(solution)/shard_map/compress/pallas_call | solution.py:276
  253.7 12.8 %all-to-all-start.3 = ((f32[32,2,64,128]{3,2,1,0:T(8,128)}), f32[32,2,64,128]{3,2,1,0:T(8,128)}, u32[]{:S(2)}, u32[]{:S(2)}) async-start(f32[32,2,64,128]{3,2,1,0:T(8,128)} %compress.11), calls=%async_computation.3 | async-start | bytes 4194304 | tf_op jit(solution)/shard_map/all_to_all | solution.py:761
  279.2 37.2 %collective-permute-done.17.refs_2_ = f32[16,2,32,128]{3,2,1,0:T(8,128)S(1)} collective-permute-done((f32[16,2,32,128]{3,2,1,0:T(8,128)}, f32[16,2,32,128]{3,2,1,0:T(8,128)S(1)}, u32[]{:S(2)}, u32[]{:S(2)}) %collective-permute-start.17) | collective-permute-done | bytes 524320 | tf_op jit(solution)/shard_map/ppermute | solution.py:728
  329.6 11.2 %compress.12 = f32[32,2,64,128]{3,2,1,0:T(8,128)} custom-call(s32[1]{0:T(128)} %bitcast.rank_ref, f32[2,8,64,128]{3,2,1,0:T(8,128)} %get-tuple-element.376.refs_0_, f32[2,8,64,128]{3,2,1,0:T(8,128)} %copy-done.35, f32[2,8,64,128]{3,2,1,0:T(8,128)} %collective-permute-done.15.refs_2_, f32[2,8,64,128]{3,2,1,0:T(8,128)} %collective-permute-done.16.refs_3_, ...), custom_call_target="tpu_custom_call" | custom-call | flops 1610612736 | bytes 4194304 | tf_op jit(solution)/shard_map/compress/pallas_call | solution.py:276
  340.8 12.8 %all-to-all-start.4 = ((f32[32,2,64,128]{3,2,1,0:T(8,128)}), f32[32,2,64,128]{3,2,1,0:T(8,128)S(1)}, u32[]{:S(2)}, u32[]{:S(2)}) async-start(f32[32,2,64,128]{3,2,1,0:T(8,128)} %compress.12), calls=%async_computation.4 | async-start | bytes 4194304 | tf_op jit(solution)/shard_map/all_to_all | solution.py:761
  355.6 7.3 collective-permute-start.23
  366.5 37.0 %collective-permute-done.22.refs_3_ = f32[16,2,32,128]{3,2,1,0:T(8,128)S(1)} collective-permute-done((f32[16,2,32,128]{3,2,1,0:T(8,128)}, f32[16,2,32,128]{3,2,1,0:T(8,128)S(1)}, u32[]{:S(2)}, u32[]{:S(2)}) %collective-permute-start.22) | collective-permute-done | bytes 524320 | tf_op jit(solution)/shard_map/ppermute | solution.py:728
  416.7 11.2 %compress.13 = f32[32,2,64,128]{3,2,1,0:T(8,128)} custom-call(s32[1]{0:T(128)} %bitcast.rank_ref, f32[2,8,64,128]{3,2,1,0:T(8,128)} %get-tuple-element.411.refs_0_, f32[2,8,64,128]{3,2,1,0:T(8,128)} %collective-permute-done.19.refs_1_, f32[2,8,64,128]{3,2,1,0:T(8,128)} %collective-permute-done.20.refs_2_, f32[2,8,64,128]{3,2,1,0:T(8,128)} %collective-permute-done.21.refs_3_, ...), custom_call_target="tpu_custom_call" | custom-call | flops 1610612736 | bytes 4194304 | tf_op jit(solution)/shard_map/compress/pallas_call | solution.py:276
  430.0 12.8 %all-to-all-start.5 = ((f32[32,2,64,128]{3,2,1,0:T(8,128)}), f32[32,2,64,128]{3,2,1,0:T(8,128)}, u32[]{:S(2)}, u32[]{:S(2)}) async-start(f32[32,2,64,128]{3,2,1,0:T(8,128)} %compress.13), calls=%async_computation.5 | async-start | bytes 4194304 | tf_op jit(solution)/shard_map/all_to_all | solution.py:761
  455.5 37.2 %collective-permute-done.27.refs_4_ = f32[16,2,32,128]{3,2,1,0:T(8,128)S(1)} collective-permute-done((f32[16,2,32,128]{3,2,1,0:T(8,128)}, f32[16,2,32,128]{3,2,1,0:T(8,128)S(1)}, u32[]{:S(2)}, u32[]{:S(2)}) %collective-permute-start.27) | collective-permute-done | bytes 524320 | tf_op jit(solution)/shard_map/ppermute | solution.py:728
  499.2 11.2 %compress.14 = f32[32,2,64,128]{3,2,1,0:T(8,128)} custom-call(s32[1]{0:T(128)} %bitcast.rank_ref, f32[2,8,64,128]{3,2,1,0:T(8,128)} %get-tuple-element.447.refs_0_, f32[2,8,64,128]{3,2,1,0:T(8,128)} %copy-done.34, f32[2,8,64,128]{3,2,1,0:T(8,128)} %collective-permute-done.25.refs_2_, f32[2,8,64,128]{3,2,1,0:T(8,128)} %collective-permute-done.26.refs_3_, ...), custom_call_target="tpu_custom_call" | custom-call | flops 1610612736 | bytes 4194304 | tf_op jit(solution)/shard_map/compress/pallas_call | solution.py:276
  512.2 12.8 %all-to-all-start.6 = ((f32[32,2,64,128]{3,2,1,0:T(8,128)}), f32[32,2,64,128]{3,2,1,0:T(8,128)S(1)}, u32[]{:S(2)}, u32[]{:S(2)}) async-start(f32[32,2,64,128]{3,2,1,0:T(8,128)} %compress.14), calls=%async_computation.6 | async-start | bytes 4194304 | tf_op jit(solution)/shard_map/all_to_all | solution.py:761
  534.1 40.8 %collective-permute-done.32.refs_5_ = f32[16,2,32,128]{3,2,1,0:T(8,128)S(1)} collective-permute-done((f32[16,2,32,128]{3,2,1,0:T(8,128)}, f32[16,2,32,128]{3,2,1,0:T(8,128)S(1)}, u32[]{:S(2)}, u32[]{:S(2)}) %collective-permute-start.32) | collective-permute-done | bytes 524320 | tf_op jit(solution)/shard_map/ppermute | solution.py:728
  581.4 11.2 %compress.15 = f32[32,2,64,128]{3,2,1,0:T(8,128)} custom-call(s32[1]{0:T(128)} %bitcast.rank_ref, f32[2,8,64,128]{3,2,1,0:T(8,128)} %get-tuple-element.467.refs_0_, f32[2,8,64,128]{3,2,1,0:T(8,128)} %copy-done.36, f32[2,8,64,128]{3,2,1,0:T(8,128)} %copy-done.37, f32[2,8,64,128]{3,2,1,0:T(8,128)} %copy-done.38, f32[2,32,128]{2,1,0:T(8,128)} %bitcast.75, ...), custom_call_target="tpu_custom_call" | custom-call | flops 1610612736 | bytes 4194304 | tf_op jit(solution)/shard_map/compress/pallas_call | solution.py:276
  594.0 12.8 %all-to-all-start.7 = ((f32[32,2,64,128]{3,2,1,0:T(8,128)}), f32[32,2,64,128]{3,2,1,0:T(8,128)}, u32[]{:S(2)}, u32[]{:S(2)}) async-start(f32[32,2,64,128]{3,2,1,0:T(8,128)} %compress.15), calls=%async_computation.7 | async-start | bytes 4194304 | tf_op jit(solution)/shard_map/all_to_all | solution.py:761
  616.3 7.1 collective-permute-start.35
  628.4 28.3 %collective-permute-done.34.refs_6_ = f32[16,2,32,128]{3,2,1,0:T(8,128)S(1)} collective-permute-done((f32[16,2,32,128]{3,2,1,0:T(8,128)S(1)}, f32[16,2,32,128]{3,2,1,0:T(8,128)S(1)}, u32[]{:S(2)}, u32[]{:S(2)}) %collective-permute-start.34) | collective-permute-done | bytes 524320 | tf_op jit(solution)/shard_map/ppermute | solution.py:728
  671.3 7.2 collective-permute-start.39
  680.5 7.5 collective-permute-start.38
  688.0 30.8 %final_inner.1 = (f32[2,128,16384]{2,1,0:T(8,128)}, bf16[8,16,256,256]{3,2,1,0:T(8,128)(2,1)}) custom-call(f32[16,2,128,128]{3,2,1,0:T(8,128)} %get-tuple-element.327.refs_0_, f32[16,2,128,128]{3,2,1,0:T(8,128)} %get-tuple-element.362.refs_1_, f32[16,2,128,128]{3,2,1,0:T(8,128)} %get-tuple-element.397.refs_2_, ...), custom_call_target="tpu_custom_call" | custom-call | flops 9663676416 | bytes 29360128 | tf_op jit(solution)/shard_map/final_inner/pallas_call | solution.py:646
  720.1 27.7 %final_wide.1 = f32[2,128,16384]{2,1,0:T(8,128)} custom-call(bf16[8,16,256,256]{3,2,1,0:T(8,128)(2,1)} %get-tuple-element.483.refs_0_, f32[16,2,32,128]{3,2,1,0:T(8,128)} %copy-done.7, f32[16,2,32,128]{3,2,1,0:T(8,128)} %copy-done.9, f32[16,2,32,128]{3,2,1,0:T(8,128)} %copy-done.11, f32[16,2,32,128]{3,2,1,0:T(8,128)} %copy-done.13, ...), custom_call_target="tpu_custom_call", output_to_operand_aliasing={{}: (23, {})} | custom-call | flops 9663676416 | bytes 29360128 | tf_op jit(solution)/shard_map/final_wide/pallas_call | solution.py:646
  (213 shorter events, 200.6 us)
Async XLA Ops:
  60.7 54.1 %all-to-all-start = ((f32[32,2,64,128]{3,2,1,0:T(8,128)}), f32[32,2,64,128]{3,2,1,0:T(8,128)S(1)}, u32[]{:S(2)}, u32[]{:S(2)}) async-start(f32[32,2,64,128]{3,2,1,0:T(8,128)} %compress.8), calls=%async_computation | async-start | bytes 4194304 | tf_op jit(solution)/shard_map/all_to_all | solution.py:761
  116.1 55.7 %all-to-all-start.1 = ((f32[32,2,64,128]{3,2,1,0:T(8,128)}), f32[32,2,64,128]{3,2,1,0:T(8,128)S(1)}, u32[]{:S(2)}, u32[]{:S(2)}) async-start(f32[32,2,64,128]{3,2,1,0:T(8,128)} %compress.9), calls=%async_computation.1 | async-start | bytes 4194304 | tf_op jit(solution)/shard_map/all_to_all | solution.py:761
  173.0 79.3 %all-to-all-start.2 = ((f32[32,2,64,128]{3,2,1,0:T(8,128)}), f32[32,2,64,128]{3,2,1,0:T(8,128)S(1)}, u32[]{:S(2)}, u32[]{:S(2)}) async-start(f32[32,2,64,128]{3,2,1,0:T(8,128)} %compress.10), calls=%async_computation.2 | async-start | bytes 4194304 | tf_op jit(solution)/shard_map/all_to_all | solution.py:761
  177.2 50.0 %collective-permute-start.12 = (f32[16,2,32,128]{3,2,1,0:T(8,128)}, f32[16,2,32,128]{3,2,1,0:T(8,128)S(1)}, u32[]{:S(2)}, u32[]{:S(2)}) collective-permute-start(f32[16,2,32,128]{3,2,1,0:T(8,128)} %get-tuple-element.337), channel_id=1, source_target_pairs={{0,1},{1,2},{2,3},{3,4},{4,5},{5,6},{6,7},{7,8},{8,9},{9,10},{10,1... | collective-permute-start | bytes 1572872 | tf_op jit(solution)/shard_map/ppermute | solution.py:728
  179.3 47.9 %collective-permute-start.13 = (f32[16,2,32,128]{3,2,1,0:T(8,128)}, f32[16,2,32,128]{3,2,1,0:T(8,128)S(1)}, u32[]{:S(2)}, u32[]{:S(2)}) collective-permute-start(f32[16,2,32,128]{3,2,1,0:T(8,128)} %get-tuple-element.338), channel_id=1, source_target_pairs={{1,0},{2,1},{3,2},{4,3},{5,4},{6,5},{7,6},{8,7},{9,8},{10,9},{11,1... | collective-permute-start | bytes 1572872 | tf_op jit(solution)/shard_map/ppermute | solution.py:729
  186.4 65.1 %collective-permute-start.14 = (f32[2,8,64,128]{3,2,1,0:T(8,128)}, f32[2,8,64,128]{3,2,1,0:T(8,128)S(1)}, u32[]{:S(2)}, u32[]{:S(2)}) collective-permute-start(f32[2,8,64,128]{3,2,1,0:T(8,128)} %get-tuple-element.346), channel_id=1, source_target_pairs={{0,8},{8,0},{16,24},{24,16},{1,9},{9,1},{17,25},{25,17},{2,10},{10... | collective-permute-start | bytes 1572872 | tf_op jit(solution)/shard_map/ppermute | solution.py:715
  187.0 64.5 %collective-permute-start.15 = (f32[2,8,64,128]{3,2,1,0:T(8,128)}, f32[2,8,64,128]{3,2,1,0:T(8,128)}, u32[]{:S(2)}, u32[]{:S(2)}) collective-permute-start(f32[2,8,64,128]{3,2,1,0:T(8,128)} %get-tuple-element.347), channel_id=1, source_target_pairs={{0,16},{8,24},{16,0},{24,8},{1,17},{9,25},{17,1},{25,9},{2,18},{10... | collective-permute-start | bytes 1572872 | tf_op jit(solution)/shard_map/ppermute | solution.py:715
  187.6 64.8 %collective-permute-start.16 = (f32[2,8,64,128]{3,2,1,0:T(8,128)}, f32[2,8,64,128]{3,2,1,0:T(8,128)}, u32[]{:S(2)}, u32[]{:S(2)}) collective-permute-start(f32[2,8,64,128]{3,2,1,0:T(8,128)} %get-tuple-element.348), channel_id=1, source_target_pairs={{0,24},{8,16},{16,8},{24,0},{1,25},{9,17},{17,9},{25,1},{2,26},{10... | collective-permute-start | bytes 1572872 | tf_op jit(solution)/shard_map/ppermute | solution.py:715
  253.7 87.1 %all-to-all-start.3 = ((f32[32,2,64,128]{3,2,1,0:T(8,128)}), f32[32,2,64,128]{3,2,1,0:T(8,128)}, u32[]{:S(2)}, u32[]{:S(2)}) async-start(f32[32,2,64,128]{3,2,1,0:T(8,128)} %compress.11), calls=%async_computation.3 | async-start | bytes 4194304 | tf_op jit(solution)/shard_map/all_to_all | solution.py:761
  266.5 49.9 %collective-permute-start.17 = (f32[16,2,32,128]{3,2,1,0:T(8,128)}, f32[16,2,32,128]{3,2,1,0:T(8,128)S(1)}, u32[]{:S(2)}, u32[]{:S(2)}) collective-permute-start(f32[16,2,32,128]{3,2,1,0:T(8,128)} %get-tuple-element.372), channel_id=1, source_target_pairs={{0,1},{1,2},{2,3},{3,4},{4,5},{5,6},{6,7},{7,8},{8,9},{9,10},{10,1... | collective-permute-start | bytes 1572872 | tf_op jit(solution)/shard_map/ppermute | solution.py:728
  268.6 47.8 %collective-permute-start.18 = (f32[16,2,32,128]{3,2,1,0:T(8,128)}, f32[16,2,32,128]{3,2,1,0:T(8,128)S(1)}, u32[]{:S(2)}, u32[]{:S(2)}) collective-permute-start(f32[16,2,32,128]{3,2,1,0:T(8,128)} %get-tuple-element.373), channel_id=1, source_target_pairs={{1,0},{2,1},{3,2},{4,3},{5,4},{6,5},{7,6},{8,7},{9,8},{10,9},{11,1... | collective-permute-start | bytes 1572872 | tf_op jit(solution)/shard_map/ppermute | solution.py:729
  275.7 65.1 %collective-permute-start.19 = (f32[2,8,64,128]{3,2,1,0:T(8,128)}, f32[2,8,64,128]{3,2,1,0:T(8,128)}, u32[]{:S(2)}, u32[]{:S(2)}) collective-permute-start(f32[2,8,64,128]{3,2,1,0:T(8,128)} %get-tuple-element.381), channel_id=1, source_target_pairs={{0,8},{8,0},{16,24},{24,16},{1,9},{9,1},{17,25},{25,17},{2,10},{10... | collective-permute-start | bytes 1572872 | tf_op jit(solution)/shard_map/ppermute | solution.py:715
  276.3 64.4 %collective-permute-start.20 = (f32[2,8,64,128]{3,2,1,0:T(8,128)}, f32[2,8,64,128]{3,2,1,0:T(8,128)}, u32[]{:S(2)}, u32[]{:S(2)}) collective-permute-start(f32[2,8,64,128]{3,2,1,0:T(8,128)} %get-tuple-element.382), channel_id=1, source_target_pairs={{0,16},{8,24},{16,0},{24,8},{1,17},{9,25},{17,1},{25,9},{2,18},{10... | collective-permute-start | bytes 1572872 | tf_op jit(solution)/shard_map/ppermute | solution.py:715
  276.9 63.9 %collective-permute-start.21 = (f32[2,8,64,128]{3,2,1,0:T(8,128)}, f32[2,8,64,128]{3,2,1,0:T(8,128)}, u32[]{:S(2)}, u32[]{:S(2)}) collective-permute-start(f32[2,8,64,128]{3,2,1,0:T(8,128)} %get-tuple-element.383), channel_id=1, source_target_pairs={{0,24},{8,16},{16,8},{24,0},{1,25},{9,17},{17,9},{25,1},{2,26},{10... | collective-permute-start | bytes 1572872 | tf_op jit(solution)/shard_map/ppermute | solution.py:715
  340.8 87.9 %all-to-all-start.4 = ((f32[32,2,64,128]{3,2,1,0:T(8,128)}), f32[32,2,64,128]{3,2,1,0:T(8,128)S(1)}, u32[]{:S(2)}, u32[]{:S(2)}) async-start(f32[32,2,64,128]{3,2,1,0:T(8,128)} %compress.12), calls=%async_computation.4 | async-start | bytes 4194304 | tf_op jit(solution)/shard_map/all_to_all | solution.py:761
  353.6 50.0 %collective-permute-start.22 = (f32[16,2,32,128]{3,2,1,0:T(8,128)}, f32[16,2,32,128]{3,2,1,0:T(8,128)S(1)}, u32[]{:S(2)}, u32[]{:S(2)}) collective-permute-start(f32[16,2,32,128]{3,2,1,0:T(8,128)} %get-tuple-element.407), channel_id=1, source_target_pairs={{0,1},{1,2},{2,3},{3,4},{4,5},{5,6},{6,7},{7,8},{8,9},{9,10},{10,1... | collective-permute-start | bytes 1572872 | tf_op jit(solution)/shard_map/ppermute | solution.py:728
  355.6 47.9 %collective-permute-start.23 = (f32[16,2,32,128]{3,2,1,0:T(8,128)}, f32[16,2,32,128]{3,2,1,0:T(8,128)S(1)}, u32[]{:S(2)}, u32[]{:S(2)}) collective-permute-start(f32[16,2,32,128]{3,2,1,0:T(8,128)} %get-tuple-element.408), channel_id=1, source_target_pairs={{1,0},{2,1},{3,2},{4,3},{5,4},{6,5},{7,6},{8,7},{9,8},{10,9},{11,1... | collective-permute-start | bytes 1572872 | tf_op jit(solution)/shard_map/ppermute | solution.py:729
  362.9 64.9 %collective-permute-start.24 = (f32[2,8,64,128]{3,2,1,0:T(8,128)}, f32[2,8,64,128]{3,2,1,0:T(8,128)S(1)}, u32[]{:S(2)}, u32[]{:S(2)}) collective-permute-start(f32[2,8,64,128]{3,2,1,0:T(8,128)} %get-tuple-element.416), channel_id=1, source_target_pairs={{0,8},{8,0},{16,24},{24,16},{1,9},{9,1},{17,25},{25,17},{2,10},{10... | collective-permute-start | bytes 1572872 | tf_op jit(solution)/shard_map/ppermute | solution.py:715
  363.6 64.3 %collective-permute-start.25 = (f32[2,8,64,128]{3,2,1,0:T(8,128)}, f32[2,8,64,128]{3,2,1,0:T(8,128)}, u32[]{:S(2)}, u32[]{:S(2)}) collective-permute-start(f32[2,8,64,128]{3,2,1,0:T(8,128)} %get-tuple-element.417), channel_id=1, source_target_pairs={{0,16},{8,24},{16,0},{24,8},{1,17},{9,25},{17,1},{25,9},{2,18},{10... | collective-permute-start | bytes 1572872 | tf_op jit(solution)/shard_map/ppermute | solution.py:715
  364.1 64.5 %collective-permute-start.26 = (f32[2,8,64,128]{3,2,1,0:T(8,128)}, f32[2,8,64,128]{3,2,1,0:T(8,128)}, u32[]{:S(2)}, u32[]{:S(2)}) collective-permute-start(f32[2,8,64,128]{3,2,1,0:T(8,128)} %get-tuple-element.418), channel_id=1, source_target_pairs={{0,24},{8,16},{16,8},{24,0},{1,25},{9,17},{17,9},{25,1},{2,26},{10... | collective-permute-start | bytes 1572872 | tf_op jit(solution)/shard_map/ppermute | solution.py:715
  430.0 81.2 %all-to-all-start.5 = ((f32[32,2,64,128]{3,2,1,0:T(8,128)}), f32[32,2,64,128]{3,2,1,0:T(8,128)}, u32[]{:S(2)}, u32[]{:S(2)}) async-start(f32[32,2,64,128]{3,2,1,0:T(8,128)} %compress.13), calls=%async_computation.5 | async-start | bytes 4194304 | tf_op jit(solution)/shard_map/all_to_all | solution.py:761
  442.8 49.9 %collective-permute-start.27 = (f32[16,2,32,128]{3,2,1,0:T(8,128)}, f32[16,2,32,128]{3,2,1,0:T(8,128)S(1)}, u32[]{:S(2)}, u32[]{:S(2)}) collective-permute-start(f32[16,2,32,128]{3,2,1,0:T(8,128)} %get-tuple-element.441), channel_id=1, source_target_pairs={{0,1},{1,2},{2,3},{3,4},{4,5},{5,6},{6,7},{7,8},{8,9},{9,10},{10,1... | collective-permute-start | bytes 1572872 | tf_op jit(solution)/shard_map/ppermute | solution.py:728
  444.9 47.8 %collective-permute-start.28 = (f32[16,2,32,128]{3,2,1,0:T(8,128)}, f32[16,2,32,128]{3,2,1,0:T(8,128)S(1)}, u32[]{:S(2)}, u32[]{:S(2)}) collective-permute-start(f32[16,2,32,128]{3,2,1,0:T(8,128)} %get-tuple-element.442), channel_id=1, source_target_pairs={{1,0},{2,1},{3,2},{4,3},{5,4},{6,5},{7,6},{8,7},{9,8},{10,9},{11,1... | collective-permute-start | bytes 1572872 | tf_op jit(solution)/shard_map/ppermute | solution.py:729
  452.0 58.4 %collective-permute-start.29 = (f32[2,8,64,128]{3,2,1,0:T(8,128)}, f32[2,8,64,128]{3,2,1,0:T(8,128)S(1)}, u32[]{:S(2)}, u32[]{:S(2)}) collective-permute-start(f32[2,8,64,128]{3,2,1,0:T(8,128)} %get-tuple-element.452), channel_id=1, source_target_pairs={{0,8},{8,0},{16,24},{24,16},{1,9},{9,1},{17,25},{25,17},{2,10},{10... | collective-permute-start | bytes 1572872 | tf_op jit(solution)/shard_map/ppermute | solution.py:715
  452.6 58.6 %collective-permute-start.30 = (f32[2,8,64,128]{3,2,1,0:T(8,128)}, f32[2,8,64,128]{3,2,1,0:T(8,128)S(1)}, u32[]{:S(2)}, u32[]{:S(2)}) collective-permute-start(f32[2,8,64,128]{3,2,1,0:T(8,128)} %get-tuple-element.453), channel_id=1, source_target_pairs={{0,16},{8,24},{16,0},{24,8},{1,17},{9,25},{17,1},{25,9},{2,18},{10... | collective-permute-start | bytes 1572872 | tf_op jit(solution)/shard_map/ppermute | solution.py:715
  453.2 58.0 %collective-permute-start.31 = (f32[2,8,64,128]{3,2,1,0:T(8,128)}, f32[2,8,64,128]{3,2,1,0:T(8,128)S(1)}, u32[]{:S(2)}, u32[]{:S(2)}) collective-permute-start(f32[2,8,64,128]{3,2,1,0:T(8,128)} %get-tuple-element.454), channel_id=1, source_target_pairs={{0,24},{8,16},{16,8},{24,0},{1,25},{9,17},{17,9},{25,1},{2,26},{10... | collective-permute-start | bytes 1572872 | tf_op jit(solution)/shard_map/ppermute | solution.py:715
  512.2 80.5 %all-to-all-start.6 = ((f32[32,2,64,128]{3,2,1,0:T(8,128)}), f32[32,2,64,128]{3,2,1,0:T(8,128)S(1)}, u32[]{:S(2)}, u32[]{:S(2)}) async-start(f32[32,2,64,128]{3,2,1,0:T(8,128)} %compress.14), calls=%async_computation.6 | async-start | bytes 4194304 | tf_op jit(solution)/shard_map/all_to_all | solution.py:761
  525.0 50.0 %collective-permute-start.32 = (f32[16,2,32,128]{3,2,1,0:T(8,128)}, f32[16,2,32,128]{3,2,1,0:T(8,128)S(1)}, u32[]{:S(2)}, u32[]{:S(2)}) collective-permute-start(f32[16,2,32,128]{3,2,1,0:T(8,128)} %get-tuple-element.461), channel_id=1, source_target_pairs={{0,1},{1,2},{2,3},{3,4},{4,5},{5,6},{6,7},{7,8},{8,9},{9,10},{10,1... | collective-permute-start | bytes 1572872 | tf_op jit(solution)/shard_map/ppermute | solution.py:728
  527.0 47.9 %collective-permute-start.33 = (f32[16,2,32,128]{3,2,1,0:T(8,128)}, f32[16,2,32,128]{3,2,1,0:T(8,128)S(1)}, u32[]{:S(2)}, u32[]{:S(2)}) collective-permute-start(f32[16,2,32,128]{3,2,1,0:T(8,128)} %get-tuple-element.462), channel_id=1, source_target_pairs={{1,0},{2,1},{3,2},{4,3},{5,4},{6,5},{7,6},{8,7},{9,8},{10,9},{11,1... | collective-permute-start | bytes 1572872 | tf_op jit(solution)/shard_map/ppermute | solution.py:729
  594.0 69.2 %all-to-all-start.7 = ((f32[32,2,64,128]{3,2,1,0:T(8,128)}), f32[32,2,64,128]{3,2,1,0:T(8,128)}, u32[]{:S(2)}, u32[]{:S(2)}) async-start(f32[32,2,64,128]{3,2,1,0:T(8,128)} %compress.15), calls=%async_computation.7 | async-start | bytes 4194304 | tf_op jit(solution)/shard_map/all_to_all | solution.py:761
  669.4 49.4 %collective-permute-start.37 = (f32[16,2,32,128]{3,2,1,0:T(8,128)}, f32[16,2,32,128]{3,2,1,0:T(8,128)S(1)}, u32[]{:S(2)}, u32[]{:S(2)}) collective-permute-start(f32[16,2,32,128]{3,2,1,0:T(8,128)} %get-tuple-element.491), channel_id=1, source_target_pairs={{0,1},{1,2},{2,3},{3,4},{4,5},{5,6},{6,7},{7,8},{8,9},{9,10},{10,1... | collective-permute-start | bytes 1572872 | tf_op jit(solution)/shard_map/ppermute | solution.py:728
  671.3 47.5 %collective-permute-start.39 = (f32[16,2,32,128]{3,2,1,0:T(8,128)}, f32[16,2,32,128]{3,2,1,0:T(8,128)S(1)}, u32[]{:S(2)}, u32[]{:S(2)}) collective-permute-start(f32[16,2,32,128]{3,2,1,0:T(8,128)} %get-tuple-element.499), channel_id=1, source_target_pairs={{1,0},{2,1},{3,2},{4,3},{5,4},{6,5},{7,6},{8,7},{9,8},{10,9},{11,1... | collective-permute-start | bytes 1572872 | tf_op jit(solution)/shard_map/ppermute | solution.py:729
  (64 other events, 1723.9 us)

commit v7 on v5

--- a/solution.py
+++ b/solution.py
@@ -50,7 +50,7 @@
 def left_table(sign, scale=1.0, order=np.arange(LANES)):
     c, s = (part[:, order] for part in dft_matrix(sign))
     high, low = split_np(np.block([[c, -s], [s, c]]) * scale)
-    return np.concatenate([high, high, low], axis=1)
+    return np.concatenate([high, low], axis=0)
 
 
 def split(x):
@@ -61,6 +61,10 @@
 
 def dot(a, b):
     return jnp.dot(a, b, preferred_element_type=F32)
+
+
+def dot_nt(a, b):
+    return lax.dot_general(a, b, (((1,), (1,)), ((), ())), preferred_element_type=F32)
 
 
 def scale_by(value, re, im):
@@ -296,7 +300,9 @@
     )(rank, *pieces, *consts)
 
 
-def azimuth_kernel(chunk, x_ref, tw_ref, fwd_ref, fwd_low_ref, out_ref, up_ref, down_ref, t_ref, mid_ref):
+def azimuth_kernel(chunk, joined, x_ref, *refs):
+    edges_before, refs = refs[: 2 * joined], refs[2 * joined :]
+    tw_ref, fwd_ref, fwd_low_ref, out_ref, up_ref, down_ref, t_ref, mid_ref = refs
     part = pl.program_id(0)
     pieces, per_part, bins = x_ref.shape[1], x_ref.shape[4], x_ref.shape[6]
 
@@ -339,14 +345,17 @@
 
         def edges(k, carry):
             for ri in range(2):
-                up_ref[k, ri] = out_ref[k, ri, bins - HALO : bins, :]
-                down_ref[k, ri] = out_ref[k, ri, 0:HALO, :]
+                at = joined * PER_CHUNK + k
+                up_ref[at, ri] = out_ref[k, ri, bins - HALO : bins, :]
+                down_ref[at, ri] = out_ref[k, ri, 0:HALO, :]
+                for before_ref, edge_ref in zip(edges_before, (up_ref, down_ref)):
+                    edge_ref[k, ri] = before_ref[k, ri]
             return carry
 
         lax.fori_loop(0, PER_CHUNK, edges, 0)
 
 
-def azimuth(x, chunk, place):
+def azimuth(x, chunk, place, before=()):
     parts, pieces, _, _, per_part, rows_in, bins = x.shape
     ids = np.arange(LANES)
     tw = jnp.asarray(np.stack(unit(ids[:, None] * ids[None, :], NAZ, -1.0)), F32)
@@ -354,9 +363,10 @@
     consts = [tw, jnp.asarray(fwd), jnp.asarray(fwd_low)]
     points = PER_CHUNK * LANES * bins
     shape = (PER_CHUNK, 2, bins, LANES)
-    edge = (PER_CHUNK, 2, HALO, LANES)
+    joined = len(before) // 2
+    edge = ((1 + joined) * PER_CHUNK, 2, HALO, LANES)
     return pl.pallas_call(
-        functools.partial(azimuth_kernel, chunk),
+        functools.partial(azimuth_kernel, chunk, joined),
         grid=(parts,),
         in_specs=[
             pl.BlockSpec(
@@ -364,7 +374,7 @@
                 lambda i: (i, 0, 0, place, 0, 0, 0),
             )
         ]
-        + [whole_spec(a) for a in consts],
+        + [whole_spec(a) for a in (*before, *consts)],
         out_specs=[pl.BlockSpec(s, lambda i: (0, 0, 0, 0)) for s in (shape, edge, edge)],
         out_shape=[jax.ShapeDtypeStruct(s, F32) for s in (shape, edge, edge)],
         scratch_shapes=[pltpu.VMEM(shape, F32), pltpu.VMEM((PER_CHUNK, 2, STEP, LANES), F32)],
@@ -373,7 +383,7 @@
             flops=points * 8 * LANES * 3, bytes_accessed=16 * points, transcendentals=0
         ),
         name=f"azimuth{chunk}",
-    )(x, *consts)
+    )(x, *before, *consts)
 
 
 KB = 4
@@ -489,7 +499,8 @@
                 at = base + QUAD * j + t
                 cols.append(jnp.concatenate([zr_ref[at], zi_ref[at]], axis=0))
             hi, lo = split(jnp.concatenate(cols, axis=1))
-            w = dot(inv1_ref[...], jnp.concatenate([hi, lo, hi], axis=0))
+            w = dot(inv1_ref[...], hi)
+            w = w[0 : 2 * LANES] + w[2 * LANES :] + dot(inv1_ref[0 : 2 * LANES, :], lo)
             turned = []
             for t in range(QUAD):
                 a = w[0:LANES, t * LANES : (t + 1) * LANES]
@@ -497,7 +508,8 @@
                 wr, wi = tw_ref[0], tw_ref[1]
                 turned.append(jnp.concatenate([a * wr - b * wi, a * wi + b * wr], axis=1))
             hi, lo = split(jnp.concatenate(turned, axis=0))
-            half_ref[j] = jnp.concatenate([hi, lo, hi], axis=1)
+            half_ref[j, 0] = hi
+            half_ref[j, 1] = lo
 
     @pl.when(step < steps)
     def _():
@@ -546,9 +558,9 @@
     @pl.when(step > steps)
     def _():
         for j in range(BB // QUAD):
-            image = lax.dot_general(
-                inv2_ref[...], half_ref[j], (((1,), (1,)), ((), ())), preferred_element_type=F32
-            )
+            image = dot_nt(inv2_ref[...], half_ref[j, 0])
+            image = image[0 : 2 * LANES] + image[2 * LANES :]
+            image = image + dot_nt(inv2_ref[0 : 2 * LANES, :], half_ref[j, 1])
             for t in range(QUAD):
                 for ri in range(2):
                     s_ref[ri, QUAD * j + t] = image[
@@ -603,11 +615,18 @@
         at = jnp.maximum(i - steps - 1, 0)
         return (0, start + at + jnp.where(at >= gap_at, gap, 0), 0)
 
+    def halo_spec(chunk, held):
+        first = (chunk - CHUNKS + held) * steps if held > 1 else 0
+        return pl.BlockSpec(
+            (KB, 2, HALO, LANES), lambda i: (first + jnp.minimum(i, steps - 1), 0, 0, 0)
+        )
+
     joined = (CHUNKS, PER_CHUNK, 2 * bins, 2 * LANES)
     joined_spec = pl.BlockSpec((CHUNKS, KB, 2 * bins, 2 * LANES), early_second)
     given = [*sources, *lows, *highs, *phases, *consts]
     specs = [pl.BlockSpec((KB, 2, bins, LANES), early)] * CHUNKS if joins else [joined_spec]
-    specs += [pl.BlockSpec((KB, 2, HALO, LANES), early)] * (2 * CHUNKS if wide else 0)
+    for halos in (lows, highs):
+        specs += [halo_spec(i, halo.shape[0] // PER_CHUNK) for i, halo in enumerate(halos)]
     if wide:
         specs += [whole_spec(a) for a in phases]
     else:
@@ -636,7 +655,7 @@
         pltpu.VMEM((rows, LANES, LANES), F32),
         pltpu.VMEM((2, BB, LANES, LANES), F32),
         pltpu.VMEM((2, 2, CHUNKS, rows, LANES), F32),
-        pltpu.VMEM((BB // QUAD, QUAD * LANES, 6 * LANES), BF16),
+        pltpu.VMEM((BB // QUAD, 2, QUAD * LANES, 2 * LANES), BF16),
     ]
     if wide:
         scratch.append(pltpu.VMEM((2, CHUNKS, 4 * HALO, 2 * LANES), BF16))
@@ -708,7 +727,7 @@
     rank = lax.axis_index("rng").astype(jnp.int32).reshape(1)
     packed = pack(raw_echo, rank, nrng, GROUPED[:1]) + pack(raw_echo, rank, nrng, GROUPED[1:])
     mains, lows, highs = [None] * CHUNKS, [None] * CHUNKS, [None] * CHUNKS
-    turned = []
+    turned, edges = [], []
 
     def gather(g):
         return [packed[g][0]] + [
@@ -720,8 +739,10 @@
         for place, c in enumerate(GROUPED[g]):
             if c > 0:
                 turned[g], mains[c - 1] = lax.optimization_barrier((turned[g], mains[c - 1]))
-            main, up, down = azimuth(turned[g], c, place)
-            mains[c] = main
+            mains[c], up, down = azimuth(turned[g], c, place, edges if c == CHUNKS - 1 else ())
+            if c == CHUNKS - 2:
+                edges.extend([up, down])
+                continue
             lows[c] = lax.ppermute(up, axes, neighbours(axes, devices, 1))
             highs[c] = lax.ppermute(down, axes, neighbours(axes, devices, -1))
 
@@ -736,9 +757,7 @@
     for g, chunks in enumerate(GROUPED):
         lines = compress(got[g], rank, chirp)
         if g + 1 < count:
-            held = got[g + 1][1 : (3 if g < 2 else nrng)]
-            lines, held = lax.optimization_barrier((lines, held))
-            got[g + 1][1 : 1 + len(held)] = held
+            lines, got[g + 1] = lax.optimization_barrier((lines, got[g + 1]))
         if g + 2 < count:
             packed[g + 2], got[g + 1] = lax.optimization_barrier((packed[g + 2], got[g + 1]))
             if g >= 1:
@@ -765,6 +784,7 @@
         turned.append(moved.reshape(nrng, naz, 2, len(chunks), per_part, rows_in, bins))
     transform(count - 2)
     transform(count - 1)
+    lows[-2], highs[-2] = lows[-1], highs[-1]
     tables = (shift_table, filter_index, tap_table)
     image, sources = None, mains
     for i, places_of in enumerate(places):

time: 647 us -> 640 us (0.989)
  starting transfers between devices: 159 us -> 152 us
    ppermute x24, waiting for transfers between devices: 151 us -> 140 us  [gather(): lax.ppermute(packed[g][j], 'rng', [(i, i ^ j) for i in range(nrng)])]
    ppermute x8 -> x7, starting transfers between devices: 58 us -> 50.6 us  [transform(): highs[c] = lax.ppermute(down, axes, neighbours(axes, devices, -1))]
    ppermute x8 -> x7, starting transfers between devices: 15.6 us -> 13.8 us  [transform(): lows[c] = lax.ppermute(up, axes, neighbours(axes, devices, 1))]
    ppermute x8 -> x7, waiting for transfers between devices: 23.4 us -> 23.4 us  [transform(): lows[c] = lax.ppermute(up, axes, neighbours(axes, devices, 1))]
  transfers between devices with their start and end apart: 48 -> 46, of which waited for: 18 -> 21; matrix products, arithmetic and copies ran while one was open for 2% -> 2% of each run, Pallas kernels for 33% -> 32%
where the time goes in v7:
time: 640 us; the launch traced here: 638 us
  Pallas kernels  249 us (39%)
  waiting for transfers between devices  209 us (33%)
  starting transfers between devices  152 us (24%)
  local copies, waits for them, and re-layouts  18.2 us (3%)
  other arithmetic  7.79 us (1%)
    ppermute x24, waiting for transfers between devices, gather(): lax.ppermute(packed[g][j], 'rng', [(i, i ^ j) for i in range(nrng)])  140 us
    pallas_call x8, Pallas kernels, compress(): pl.pallas_call(functools.partial(compress_kernel, parts, block), grid=(ro...  89.6 us
    all_to_all x8, starting transfers between devices, local(): moved = lax.all_to_all(lines, axes, split_axis=0, concat_axis=0, tiled=True)  59.5 us
    pallas_call x2, Pallas kernels, final(): pl.pallas_call(functools.partial(final_kernel, steps, joins, wide), grid=...  59.5 us
    ppermute x7, starting transfers between devices, transform(): highs[c] = lax.ppermute(down, axes, neighbours(axes, devices, -1))  50.6 us
    pallas_call x8, Pallas kernels, azimuth(): pl.pallas_call(functools.partial(azimuth_kernel, chunk, joined), grid=(pa...  49.3 us
    all_to_all x8, waiting for transfers between devices, local(): moved = lax.all_to_all(lines, axes, split_axis=0, concat_axis=0, tiled=True)  45.7 us
    ppermute x24, starting transfers between devices, gather(): lax.ppermute(packed[g][j], 'rng', [(i, i ^ j) for i in range(nrng)])  28.4 us
  transfers between devices with their start and end apart: 46, of which 21 were waited for; matrix products, arithmetic and copies ran while one was open for 2% of the time, Pallas kernels for 32%

profile of v7, /device:TPU:4, one launch (start us, length us, event | category | flops | bytes accessed | tf_op | source)
XLA Modules:
  0.0 637.9 jit_solution(572123780983263952)
XLA Ops:
  0.0 9.2 %pack.3 = (f32[2,8,64,128]{3,2,1,0:T(8,128)}, f32[2,8,64,128]{3,2,1,0:T(8,128)}, f32[2,8,64,128]{3,2,1,0:T(8,128)}, f32[2,8,64,128]{3,2,1,0:T(8,128)}) custom-call(s32[1]{0:T(128)} %bitcast.rank_ref, f32[2,2048,1024]{2,1,0:T(8,128)} %x_ref.3), custom_call_target="tpu_custom_call" | custom-call | bytes 33554432 | tf_op jit(solution)/shard_map/pack/pallas_call | solution.py:141
  12.7 15.5 %pack.2 = (f32[2,8,64,128]{3,2,1,0:T(8,128)}, f32[2,8,64,128]{3,2,1,0:T(8,128)}, f32[2,8,64,128]{3,2,1,0:T(8,128)}, f32[2,8,64,128]{3,2,1,0:T(8,128)}, f32[2,8,6...) custom-call(s32[1]{0:T(128)} %bitcast.rank_ref, ...), custom_call_target="tpu_custom_call" | custom-call | bytes 33554432 | tf_op jit(solution)/shard_map/pack/pallas_call | solution.py:141
  28.3 7.3 %collective-permute-done.1.refs_2_ = f32[2,8,64,128]{3,2,1,0:T(8,128)S(1)} collective-permute-done((f32[2,8,64,128]{3,2,1,0:T(8,128)}, f32[2,8,64,128]{3,2,1,0:T(8,128)S(1)}, u32[]{:S(2)}, u32[]{:S(2)}) %collective-permute-start.1) | collective-permute-done | bytes 524320 | tf_op jit(solution)/shard_map/ppermute | solution.py:734
  39.9 11.2 %compress.8 = f32[32,2,64,128]{3,2,1,0:T(8,128)} custom-call(s32[1]{0:T(128)} %bitcast.rank_ref, f32[2,8,64,128]{3,2,1,0:T(8,128)} %get-tuple-element.252.refs_0_, f32[2,8,64,128]{3,2,1,0:T(8,128)} %copy-done.27, f32[2,8,64,128]{3,2,1,0:T(8,128)} %copy-done.28, f32[2,8,64,128]{3,2,1,0:T(8,128)} %copy-done.29, f32[2,32,128]{2,1,0:T(8,128)} %bitcast.69, ...), custom_call_target="tpu_custom_call" | custom-call | flops 1610612736 | bytes 4194304 | tf_op jit(solution)/shard_map/compress/pallas_call | solution.py:280
  51.2 8.7 %collective-permute-done.4.refs_2_ = f32[2,8,64,128]{3,2,1,0:T(8,128)} collective-permute-done((f32[2,8,64,128]{3,2,1,0:T(8,128)}, f32[2,8,64,128]{3,2,1,0:T(8,128)}, u32[]{:S(2)}, u32[]{:S(2)}) %collective-permute-start.4) | collective-permute-done | bytes 524320 | tf_op jit(solution)/shard_map/ppermute | solution.py:734
  69.3 11.2 %compress.9 = f32[32,2,64,128]{3,2,1,0:T(8,128)} custom-call(s32[1]{0:T(128)} %bitcast.rank_ref, f32[2,8,64,128]{3,2,1,0:T(8,128)} %get-tuple-element.264.refs_0_, f32[2,8,64,128]{3,2,1,0:T(8,128)} %copy-done.31, f32[2,8,64,128]{3,2,1,0:T(8,128)} %collective-permute-done.4.refs_2_, f32[2,8,64,128]{3,2,1,0:T(8,128)} %collective-permute-done.5.refs_3_, ...), custom_call_target="tpu_custom_call" | custom-call | flops 1610612736 | bytes 4194304 | tf_op jit(solution)/shard_map/compress/pallas_call | solution.py:280
  80.5 16.2 %collective-permute-done.6.refs_1_ = f32[2,8,64,128]{3,2,1,0:T(8,128)S(1)} collective-permute-done((f32[2,8,64,128]{3,2,1,0:T(8,128)}, f32[2,8,64,128]{3,2,1,0:T(8,128)S(1)}, u32[]{:S(2)}, u32[]{:S(2)}) %collective-permute-start.6) | collective-permute-done | bytes 524320 | tf_op jit(solution)/shard_map/ppermute | solution.py:734
  97.8 14.8 %collective-permute-done.8.refs_3_ = f32[2,8,64,128]{3,2,1,0:T(8,128)} collective-permute-done((f32[2,8,64,128]{3,2,1,0:T(8,128)S(1)}, f32[2,8,64,128]{3,2,1,0:T(8,128)}, u32[]{:S(2)}, u32[]{:S(2)}) %collective-permute-start.8) | collective-permute-done | bytes 524320 | tf_op jit(solution)/shard_map/ppermute | solution.py:734
  126.1 11.2 %compress.10 = f32[32,2,64,128]{3,2,1,0:T(8,128)} custom-call(s32[1]{0:T(128)} %bitcast.rank_ref, f32[2,8,64,128]{3,2,1,0:T(8,128)} %get-tuple-element.276.refs_0_, f32[2,8,64,128]{3,2,1,0:T(8,128)} %copy-done.30, f32[2,8,64,128]{3,2,1,0:T(8,128)} %collective-permute-done.7.refs_2_, f32[2,8,64,128]{3,2,1,0:T(8,128)} %collective-permute-done.8.refs_3_, ...), custom_call_target="tpu_custom_call" | custom-call | flops 1610612736 | bytes 4194304 | tf_op jit(solution)/shard_map/compress/pallas_call | solution.py:280
  149.8 15.9 %collective-permute-done.10.refs_2_ = f32[2,8,64,128]{3,2,1,0:T(8,128)} collective-permute-done((f32[2,8,64,128]{3,2,1,0:T(8,128)}, f32[2,8,64,128]{3,2,1,0:T(8,128)}, u32[]{:S(2)}, u32[]{:S(2)}) %collective-permute-start.10) | collective-permute-done | bytes 524320 | tf_op jit(solution)/shard_map/ppermute | solution.py:734
  202.5 11.2 %compress.11 = f32[32,2,64,128]{3,2,1,0:T(8,128)} custom-call(s32[1]{0:T(128)} %bitcast.rank_ref, f32[2,8,64,128]{3,2,1,0:T(8,128)} %get-tuple-element.308.refs_0_, f32[2,8,64,128]{3,2,1,0:T(8,128)} %collective-permute-done.9.refs_1_, f32[2,8,64,128]{3,2,1,0:T(8,128)} %collective-permute-done.10.refs_2_, f32[2,8,64,128]{3,2,1,0:T(8,128)} %collective-permute-done.11.refs_3_, ...), custom_call_target="tpu_custom_call" | custom-call | flops 1610612736 | bytes 4194304 | tf_op jit(solution)/shard_map/compress/pallas_call | solution.py:280
  213.8 15.9 %collective-permute-done.14.refs_3_ = f32[2,8,64,128]{3,2,1,0:T(8,128)} collective-permute-done((f32[2,8,64,128]{3,2,1,0:T(8,128)}, f32[2,8,64,128]{3,2,1,0:T(8,128)}, u32[]{:S(2)}, u32[]{:S(2)}) %collective-permute-start.14) | collective-permute-done | bytes 524320 | tf_op jit(solution)/shard_map/ppermute | solution.py:734
  232.9 9.3 %all-to-all-start.3 = ((f32[32,2,64,128]{3,2,1,0:T(8,128)}), f32[32,2,64,128]{3,2,1,0:T(8,128)}, u32[]{:S(2)}, u32[]{:S(2)}) async-start(f32[32,2,64,128]{3,2,1,0:T(8,128)} %compress.11), calls=%async_computation.3 | async-start | bytes 4194304 | tf_op jit(solution)/shard_map/all_to_all | solution.py:783
  247.6 7.2 %collective-permute-start.24 = (f32[16,2,32,128]{3,2,1,0:T(8,128)}, f32[16,2,32,128]{3,2,1,0:T(8,128)}, u32[]{:S(2)}, u32[]{:S(2)}) collective-permute-start(f32[16,2,32,128]{3,2,1,0:T(8,128)} %get-tuple-element.387), channel_id=1, source_target_pairs={{1,0},{2,1},{3,2},{4,3},{5,4},{6,5},{7,6},{8,7},{9,8},{10,9},{11,1... | collective-permute-start | bytes 1572872 | tf_op jit(solution)/shard_map/ppermute | solution.py:747
  254.9 11.2 %compress.12 = f32[32,2,64,128]{3,2,1,0:T(8,128)} custom-call(s32[1]{0:T(128)} %bitcast.rank_ref, f32[2,8,64,128]{3,2,1,0:T(8,128)} %get-tuple-element.337.refs_0_, f32[2,8,64,128]{3,2,1,0:T(8,128)} %collective-permute-done.12.refs_1_, f32[2,8,64,128]{3,2,1,0:T(8,128)} %collective-permute-done.13.refs_2_, f32[2,8,64,128]{3,2,1,0:T(8,128)} %collective-permute-done.14.refs_3_, ...), custom_call_target="tpu_custom_call" | custom-call | flops 1610612736 | bytes 4194304 | tf_op jit(solution)/shard_map/compress/pallas_call | solution.py:280
  278.8 15.9 %collective-permute-done.17.refs_3_ = f32[2,8,64,128]{3,2,1,0:T(8,128)} collective-permute-done((f32[2,8,64,128]{3,2,1,0:T(8,128)}, f32[2,8,64,128]{3,2,1,0:T(8,128)}, u32[]{:S(2)}, u32[]{:S(2)}) %collective-permute-start.17) | collective-permute-done | bytes 524320 | tf_op jit(solution)/shard_map/ppermute | solution.py:734
  296.7 8.2 %all-to-all-start.4 = ((f32[32,2,64,128]{3,2,1,0:T(8,128)}), f32[32,2,64,128]{3,2,1,0:T(8,128)S(1)}, u32[]{:S(2)}, u32[]{:S(2)}) async-start(f32[32,2,64,128]{3,2,1,0:T(8,128)} %compress.12), calls=%async_computation.4 | async-start | bytes 4194304 | tf_op jit(solution)/shard_map/all_to_all | solution.py:783
  310.4 7.4 %collective-permute-start.26 = (f32[16,2,32,128]{3,2,1,0:T(8,128)}, f32[16,2,32,128]{3,2,1,0:T(8,128)S(1)}, u32[]{:S(2)}, u32[]{:S(2)}) collective-permute-start(f32[16,2,32,128]{3,2,1,0:T(8,128)} %get-tuple-element.399), channel_id=1, source_target_pairs={{1,0},{2,1},{3,2},{4,3},{5,4},{6,5},{7,6},{8,7},{9,8},{10,9},{11,1... | collective-permute-start | bytes 1572872 | tf_op jit(solution)/shard_map/ppermute | solution.py:747
  330.5 11.2 %compress.13 = f32[32,2,64,128]{3,2,1,0:T(8,128)} custom-call(s32[1]{0:T(128)} %bitcast.rank_ref, f32[2,8,64,128]{3,2,1,0:T(8,128)} %get-tuple-element.369.refs_0_, f32[2,8,64,128]{3,2,1,0:T(8,128)} %collective-permute-done.15.refs_1_, f32[2,8,64,128]{3,2,1,0:T(8,128)} %collective-permute-done.16.refs_2_, f32[2,8,64,128]{3,2,1,0:T(8,128)} %collective-permute-done.17.refs_3_, ...), custom_call_target="tpu_custom_call" | custom-call | flops 1610612736 | bytes 4194304 | tf_op jit(solution)/shard_map/compress/pallas_call | solution.py:280
  341.8 15.8 %collective-permute-done.22.refs_3_ = f32[2,8,64,128]{3,2,1,0:T(8,128)} collective-permute-done((f32[2,8,64,128]{3,2,1,0:T(8,128)}, f32[2,8,64,128]{3,2,1,0:T(8,128)}, u32[]{:S(2)}, u32[]{:S(2)}) %collective-permute-start.22) | collective-permute-done | bytes 524320 | tf_op jit(solution)/shard_map/ppermute | solution.py:734
  360.7 9.2 %all-to-all-start.5 = ((f32[32,2,64,128]{3,2,1,0:T(8,128)}), f32[32,2,64,128]{3,2,1,0:T(8,128)}, u32[]{:S(2)}, u32[]{:S(2)}) async-start(f32[32,2,64,128]{3,2,1,0:T(8,128)} %compress.13), calls=%async_computation.5 | async-start | bytes 4194304 | tf_op jit(solution)/shard_map/all_to_all | solution.py:783
  375.5 7.2 %collective-permute-start.31 = (f32[16,2,32,128]{3,2,1,0:T(8,128)}, f32[16,2,32,128]{3,2,1,0:T(8,128)}, u32[]{:S(2)}, u32[]{:S(2)}) collective-permute-start(f32[16,2,32,128]{3,2,1,0:T(8,128)} %get-tuple-element.418), channel_id=1, source_target_pairs={{1,0},{2,1},{3,2},{4,3},{5,4},{6,5},{7,6},{8,7},{9,8},{10,9},{11,1... | collective-permute-start | bytes 1572872 | tf_op jit(solution)/shard_map/ppermute | solution.py:747
  382.7 11.2 %compress.14 = f32[32,2,64,128]{3,2,1,0:T(8,128)} custom-call(s32[1]{0:T(128)} %bitcast.rank_ref, f32[2,8,64,128]{3,2,1,0:T(8,128)} %get-tuple-element.403.refs_0_, f32[2,8,64,128]{3,2,1,0:T(8,128)} %collective-permute-done.20.refs_1_, f32[2,8,64,128]{3,2,1,0:T(8,128)} %collective-permute-done.21.refs_2_, f32[2,8,64,128]{3,2,1,0:T(8,128)} %collective-permute-done.22.refs_3_, ...), custom_call_target="tpu_custom_call" | custom-call | flops 1610612736 | bytes 4194304 | tf_op jit(solution)/shard_map/compress/pallas_call | solution.py:280
  402.0 20.5 %collective-permute-done.29.refs_3_ = f32[2,8,64,128]{3,2,1,0:T(8,128)} collective-permute-done((f32[2,8,64,128]{3,2,1,0:T(8,128)}, f32[2,8,64,128]{3,2,1,0:T(8,128)}, u32[]{:S(2)}, u32[]{:S(2)}) %collective-permute-start.29) | collective-permute-done | bytes 524320 | tf_op jit(solution)/shard_map/ppermute | solution.py:734
  424.5 8.2 %all-to-all-start.6 = ((f32[32,2,64,128]{3,2,1,0:T(8,128)}), f32[32,2,64,128]{3,2,1,0:T(8,128)S(1)}, u32[]{:S(2)}, u32[]{:S(2)}) async-start(f32[32,2,64,128]{3,2,1,0:T(8,128)} %compress.14), calls=%async_computation.6 | async-start | bytes 4194304 | tf_op jit(solution)/shard_map/all_to_all | solution.py:783
  448.0 11.2 %compress.15 = f32[32,2,64,128]{3,2,1,0:T(8,128)} custom-call(s32[1]{0:T(128)} %bitcast.rank_ref, f32[2,8,64,128]{3,2,1,0:T(8,128)} %get-tuple-element.420.refs_0_, f32[2,8,64,128]{3,2,1,0:T(8,128)} %collective-permute-done.27.refs_1_, f32[2,8,64,128]{3,2,1,0:T(8,128)} %collective-permute-done.28.refs_2_, f32[2,8,64,128]{3,2,1,0:T(8,128)} %collective-permute-done.29.refs_3_, ...), custom_call_target="tpu_custom_call" | custom-call | flops 1610612736 | bytes 4194304 | tf_op jit(solution)/shard_map/compress/pallas_call | solution.py:280
  459.3 23.4 %collective-permute-done.32.refs_5_ = f32[16,2,32,128]{3,2,1,0:T(8,128)S(1)} collective-permute-done((f32[16,2,32,128]{3,2,1,0:T(8,128)}, f32[16,2,32,128]{3,2,1,0:T(8,128)S(1)}, u32[]{:S(2)}, u32[]{:S(2)}) %collective-permute-start.32) | collective-permute-done | bytes 524320 | tf_op jit(solution)/shard_map/ppermute | solution.py:746
  488.6 9.2 %all-to-all-start.7 = ((f32[32,2,64,128]{3,2,1,0:T(8,128)}), f32[32,2,64,128]{3,2,1,0:T(8,128)S(1)}, u32[]{:S(2)}, u32[]{:S(2)}) async-start(f32[32,2,64,128]{3,2,1,0:T(8,128)} %compress.15), calls=%async_computation.7 | async-start | bytes 4194304 | tf_op jit(solution)/shard_map/all_to_all | solution.py:783
  513.0 33.7 %all-to-all-done.7 = f32[32,2,64,128]{3,2,1,0:T(8,128)S(1)} async-done(((f32[32,2,64,128]{3,2,1,0:T(8,128)}), f32[32,2,64,128]{3,2,1,0:T(8,128)S(1)}, u32[]{:S(2)}, u32[]{:S(2)}) %all-to-all-start.7) | async-done | bytes 2097184 | tf_op jit(solution)/shard_map/all_to_all | solution.py:783
  569.1 7.5 %collective-permute-start.36 = (f32[16,2,32,128]{3,2,1,0:T(8,128)}, f32[16,2,32,128]{3,2,1,0:T(8,128)S(1)}, u32[]{:S(2)}, u32[]{:S(2)}) collective-permute-start(f32[16,2,32,128]{3,2,1,0:T(8,128)} %get-tuple-element.456), channel_id=1, source_target_pairs={{1,0},{2,1},{3,2},{4,3},{5,4},{6,5},{7,6},{8,7},{9,8},{10,9},{11,1... | collective-permute-start | bytes 1572872 | tf_op jit(solution)/shard_map/ppermute | solution.py:747
  576.6 31.1 %final_inner.1 = (f32[2,128,16384]{2,1,0:T(8,128)}, bf16[8,16,256,256]{3,2,1,0:T(8,128)(2,1)}) custom-call(f32[16,2,128,128]{3,2,1,0:T(8,128)} %get-tuple-element.303.refs_0_, f32[16,2,128,128]{3,2,1,0:T(8,128)} %get-tuple-element.332.refs_1_, f32[16,2,128,128]{3,2,1,0:T(8,128)} %get-tuple-element.364.refs_2_, ...), custom_call_target="tpu_custom_call" | custom-call | flops 9663676416 | bytes 29360128 | tf_op jit(solution)/shard_map/final_inner/pallas_call | solution.py:665
  609.4 28.4 %final_wide.1 = f32[2,128,16384]{2,1,0:T(8,128)} custom-call(bf16[8,16,256,256]{3,2,1,0:T(8,128)(2,1)} %get-tuple-element.443.refs_0_, f32[16,2,32,128]{3,2,1,0:T(8,128)} %copy-done.10, f32[16,2,32,128]{3,2,1,0:T(8,128)} %collective-permute-done.23.refs_2_, f32[16,2,32,128]{3,2,1,0:T(8,128)} %copy-done.12, ...), custom_call_target="tpu_custom_call", output_to_operand_aliasing={{}: (23, {})} | custom-call | flops 9663676416 | bytes 29360128 | tf_op jit(solution)/shard_map/final_wide/pallas_call | solution.py:665
  (179 shorter events, 201.6 us)
Async XLA Ops:
  59.9 54.7 %all-to-all-start = ((f32[32,2,64,128]{3,2,1,0:T(8,128)}), f32[32,2,64,128]{3,2,1,0:T(8,128)S(1)}, u32[]{:S(2)}, u32[]{:S(2)}) async-start(f32[32,2,64,128]{3,2,1,0:T(8,128)} %compress.8), calls=%async_computation | async-start | bytes 4194304 | tf_op jit(solution)/shard_map/all_to_all | solution.py:783
  67.8 44.7 %collective-permute-start.8 = (f32[2,8,64,128]{3,2,1,0:T(8,128)S(1)}, f32[2,8,64,128]{3,2,1,0:T(8,128)}, u32[]{:S(2)}, u32[]{:S(2)}) collective-permute-start(f32[2,8,64,128]{3,2,1,0:T(8,128)S(1)} %copy-done.26), channel_id=1, source_target_pairs={{0,24},{8,16},{16,8},{24,0},{1,25},{9,17},{17,9},{25,1},{2,26},{10... | collective-permute-start | bytes 1572872 | tf_op jit(solution)/shard_map/ppermute | solution.py:734
  115.9 55.7 %all-to-all-start.1 = ((f32[32,2,64,128]{3,2,1,0:T(8,128)}), f32[32,2,64,128]{3,2,1,0:T(8,128)S(1)}, u32[]{:S(2)}, u32[]{:S(2)}) async-start(f32[32,2,64,128]{3,2,1,0:T(8,128)} %compress.9), calls=%async_computation.1 | async-start | bytes 4194304 | tf_op jit(solution)/shard_map/all_to_all | solution.py:783
  121.2 44.5 %collective-permute-start.10 = (f32[2,8,64,128]{3,2,1,0:T(8,128)}, f32[2,8,64,128]{3,2,1,0:T(8,128)}, u32[]{:S(2)}, u32[]{:S(2)}) collective-permute-start(f32[2,8,64,128]{3,2,1,0:T(8,128)} %get-tuple-element.287), channel_id=1, source_target_pairs={{0,16},{8,24},{16,0},{24,8},{1,17},{9,25},{17,1},{25,9},{2,18},{10... | collective-permute-start | bytes 1572872 | tf_op jit(solution)/shard_map/ppermute | solution.py:734
  121.6 44.1 %collective-permute-start.11 = (f32[2,8,64,128]{3,2,1,0:T(8,128)}, f32[2,8,64,128]{3,2,1,0:T(8,128)}, u32[]{:S(2)}, u32[]{:S(2)}) collective-permute-start(f32[2,8,64,128]{3,2,1,0:T(8,128)} %get-tuple-element.288), channel_id=1, source_target_pairs={{0,24},{8,16},{16,8},{24,0},{1,25},{9,17},{17,9},{25,1},{2,26},{10... | collective-permute-start | bytes 1572872 | tf_op jit(solution)/shard_map/ppermute | solution.py:734
  124.2 47.3 %collective-permute-start.9 = (f32[2,8,64,128]{3,2,1,0:T(8,128)S(1)}, f32[2,8,64,128]{3,2,1,0:T(8,128)}, u32[]{:S(2)}, u32[]{:S(2)}) collective-permute-start(f32[2,8,64,128]{3,2,1,0:T(8,128)S(1)} %copy-done.25), channel_id=1, source_target_pairs={{0,8},{8,0},{16,24},{24,16},{1,9},{9,1},{17,25},{25,17},{2,10},{10... | collective-permute-start | bytes 1572872 | tf_op jit(solution)/shard_map/ppermute | solution.py:734
  172.9 58.7 %all-to-all-start.2 = ((f32[32,2,64,128]{3,2,1,0:T(8,128)}), f32[32,2,64,128]{3,2,1,0:T(8,128)S(1)}, u32[]{:S(2)}, u32[]{:S(2)}) async-start(f32[32,2,64,128]{3,2,1,0:T(8,128)} %compress.10), calls=%async_computation.2 | async-start | bytes 4194304 | tf_op jit(solution)/shard_map/all_to_all | solution.py:783
  177.1 36.7 %collective-permute-start.12 = (f32[2,8,64,128]{3,2,1,0:T(8,128)}, f32[2,8,64,128]{3,2,1,0:T(8,128)}, u32[]{:S(2)}, u32[]{:S(2)}) collective-permute-start(f32[2,8,64,128]{3,2,1,0:T(8,128)} %get-tuple-element.313), channel_id=1, source_target_pairs={{0,8},{8,0},{16,24},{24,16},{1,9},{9,1},{17,25},{25,17},{2,10},{10... | collective-permute-start | bytes 1572872 | tf_op jit(solution)/shard_map/ppermute | solution.py:734
  179.2 50.5 %collective-permute-start.14 = (f32[2,8,64,128]{3,2,1,0:T(8,128)}, f32[2,8,64,128]{3,2,1,0:T(8,128)}, u32[]{:S(2)}, u32[]{:S(2)}) collective-permute-start(f32[2,8,64,128]{3,2,1,0:T(8,128)} %get-tuple-element.315), channel_id=1, source_target_pairs={{0,24},{8,16},{16,8},{24,0},{1,25},{9,17},{17,9},{25,1},{2,26},{10... | collective-permute-start | bytes 1572872 | tf_op jit(solution)/shard_map/ppermute | solution.py:734
  180.6 49.1 %collective-permute-start.18 = (f32[16,2,32,128]{3,2,1,0:T(8,128)}, f32[16,2,32,128]{3,2,1,0:T(8,128)S(1)}, u32[]{:S(2)}, u32[]{:S(2)}) collective-permute-start(f32[16,2,32,128]{3,2,1,0:T(8,128)} %get-tuple-element.354), channel_id=1, source_target_pairs={{0,1},{1,2},{2,3},{3,4},{4,5},{5,6},{6,7},{7,8},{8,9},{9,10},{10,1... | collective-permute-start | bytes 1572872 | tf_op jit(solution)/shard_map/ppermute | solution.py:746
  182.6 47.9 %collective-permute-start.19 = (f32[16,2,32,128]{3,2,1,0:T(8,128)}, f32[16,2,32,128]{3,2,1,0:T(8,128)S(1)}, u32[]{:S(2)}, u32[]{:S(2)}) collective-permute-start(f32[16,2,32,128]{3,2,1,0:T(8,128)} %get-tuple-element.355), channel_id=1, source_target_pairs={{1,0},{2,1},{3,2},{4,3},{5,4},{6,5},{7,6},{8,7},{9,8},{10,9},{11,1... | collective-permute-start | bytes 1572872 | tf_op jit(solution)/shard_map/ppermute | solution.py:747
  232.9 63.8 %all-to-all-start.3 = ((f32[32,2,64,128]{3,2,1,0:T(8,128)}), f32[32,2,64,128]{3,2,1,0:T(8,128)}, u32[]{:S(2)}, u32[]{:S(2)}) async-start(f32[32,2,64,128]{3,2,1,0:T(8,128)} %compress.11), calls=%async_computation.3 | async-start | bytes 4194304 | tf_op jit(solution)/shard_map/all_to_all | solution.py:783
  244.2 50.5 %collective-permute-start.17 = (f32[2,8,64,128]{3,2,1,0:T(8,128)}, f32[2,8,64,128]{3,2,1,0:T(8,128)}, u32[]{:S(2)}, u32[]{:S(2)}) collective-permute-start(f32[2,8,64,128]{3,2,1,0:T(8,128)} %get-tuple-element.344), channel_id=1, source_target_pairs={{0,24},{8,16},{16,8},{24,0},{1,25},{9,17},{17,9},{25,1},{2,26},{10... | collective-permute-start | bytes 1572872 | tf_op jit(solution)/shard_map/ppermute | solution.py:734
  245.7 49.0 %collective-permute-start.23 = (f32[16,2,32,128]{3,2,1,0:T(8,128)}, f32[16,2,32,128]{3,2,1,0:T(8,128)}, u32[]{:S(2)}, u32[]{:S(2)}) collective-permute-start(f32[16,2,32,128]{3,2,1,0:T(8,128)} %get-tuple-element.386), channel_id=1, source_target_pairs={{0,1},{1,2},{2,3},{3,4},{4,5},{5,6},{6,7},{7,8},{8,9},{9,10},{10,1... | collective-permute-start | bytes 1572872 | tf_op jit(solution)/shard_map/ppermute | solution.py:746
  247.6 47.1 %collective-permute-start.24 = (f32[16,2,32,128]{3,2,1,0:T(8,128)}, f32[16,2,32,128]{3,2,1,0:T(8,128)}, u32[]{:S(2)}, u32[]{:S(2)}) collective-permute-start(f32[16,2,32,128]{3,2,1,0:T(8,128)} %get-tuple-element.387), channel_id=1, source_target_pairs={{1,0},{2,1},{3,2},{4,3},{5,4},{6,5},{7,6},{8,7},{9,8},{10,9},{11,1... | collective-permute-start | bytes 1572872 | tf_op jit(solution)/shard_map/ppermute | solution.py:747
  296.7 62.7 %all-to-all-start.4 = ((f32[32,2,64,128]{3,2,1,0:T(8,128)}), f32[32,2,64,128]{3,2,1,0:T(8,128)S(1)}, u32[]{:S(2)}, u32[]{:S(2)}) async-start(f32[32,2,64,128]{3,2,1,0:T(8,128)} %compress.12), calls=%async_computation.4 | async-start | bytes 4194304 | tf_op jit(solution)/shard_map/all_to_all | solution.py:783
  304.9 36.8 %collective-permute-start.20 = (f32[2,8,64,128]{3,2,1,0:T(8,128)}, f32[2,8,64,128]{3,2,1,0:T(8,128)}, u32[]{:S(2)}, u32[]{:S(2)}) collective-permute-start(f32[2,8,64,128]{3,2,1,0:T(8,128)} %get-tuple-element.374), channel_id=1, source_target_pairs={{0,8},{8,0},{16,24},{24,16},{1,9},{9,1},{17,25},{25,17},{2,10},{10... | collective-permute-start | bytes 1572872 | tf_op jit(solution)/shard_map/ppermute | solution.py:734
  307.0 50.5 %collective-permute-start.22 = (f32[2,8,64,128]{3,2,1,0:T(8,128)}, f32[2,8,64,128]{3,2,1,0:T(8,128)}, u32[]{:S(2)}, u32[]{:S(2)}) collective-permute-start(f32[2,8,64,128]{3,2,1,0:T(8,128)} %get-tuple-element.376), channel_id=1, source_target_pairs={{0,24},{8,16},{16,8},{24,0},{1,25},{9,17},{17,9},{25,1},{2,26},{10... | collective-permute-start | bytes 1572872 | tf_op jit(solution)/shard_map/ppermute | solution.py:734
  308.5 49.1 %collective-permute-start.25 = (f32[16,2,32,128]{3,2,1,0:T(8,128)}, f32[16,2,32,128]{3,2,1,0:T(8,128)S(1)}, u32[]{:S(2)}, u32[]{:S(2)}) collective-permute-start(f32[16,2,32,128]{3,2,1,0:T(8,128)} %get-tuple-element.398), channel_id=1, source_target_pairs={{0,1},{1,2},{2,3},{3,4},{4,5},{5,6},{6,7},{7,8},{8,9},{9,10},{10,1... | collective-permute-start | bytes 1572872 | tf_op jit(solution)/shard_map/ppermute | solution.py:746
  310.4 47.9 %collective-permute-start.26 = (f32[16,2,32,128]{3,2,1,0:T(8,128)}, f32[16,2,32,128]{3,2,1,0:T(8,128)S(1)}, u32[]{:S(2)}, u32[]{:S(2)}) collective-permute-start(f32[16,2,32,128]{3,2,1,0:T(8,128)} %get-tuple-element.399), channel_id=1, source_target_pairs={{1,0},{2,1},{3,2},{4,3},{5,4},{6,5},{7,6},{8,7},{9,8},{10,9},{11,1... | collective-permute-start | bytes 1572872 | tf_op jit(solution)/shard_map/ppermute | solution.py:747
  360.7 63.8 %all-to-all-start.5 = ((f32[32,2,64,128]{3,2,1,0:T(8,128)}), f32[32,2,64,128]{3,2,1,0:T(8,128)}, u32[]{:S(2)}, u32[]{:S(2)}) async-start(f32[32,2,64,128]{3,2,1,0:T(8,128)} %compress.13), calls=%async_computation.5 | async-start | bytes 4194304 | tf_op jit(solution)/shard_map/all_to_all | solution.py:783
  372.1 50.5 %collective-permute-start.29 = (f32[2,8,64,128]{3,2,1,0:T(8,128)}, f32[2,8,64,128]{3,2,1,0:T(8,128)}, u32[]{:S(2)}, u32[]{:S(2)}) collective-permute-start(f32[2,8,64,128]{3,2,1,0:T(8,128)} %get-tuple-element.410), channel_id=1, source_target_pairs={{0,24},{8,16},{16,8},{24,0},{1,25},{9,17},{17,9},{25,1},{2,26},{10... | collective-permute-start | bytes 1572872 | tf_op jit(solution)/shard_map/ppermute | solution.py:734
  373.6 49.0 %collective-permute-start.30 = (f32[16,2,32,128]{3,2,1,0:T(8,128)}, f32[16,2,32,128]{3,2,1,0:T(8,128)}, u32[]{:S(2)}, u32[]{:S(2)}) collective-permute-start(f32[16,2,32,128]{3,2,1,0:T(8,128)} %get-tuple-element.417), channel_id=1, source_target_pairs={{0,1},{1,2},{2,3},{3,4},{4,5},{5,6},{6,7},{7,8},{8,9},{9,10},{10,1... | collective-permute-start | bytes 1572872 | tf_op jit(solution)/shard_map/ppermute | solution.py:746
  375.5 47.1 %collective-permute-start.31 = (f32[16,2,32,128]{3,2,1,0:T(8,128)}, f32[16,2,32,128]{3,2,1,0:T(8,128)}, u32[]{:S(2)}, u32[]{:S(2)}) collective-permute-start(f32[16,2,32,128]{3,2,1,0:T(8,128)} %get-tuple-element.418), channel_id=1, source_target_pairs={{1,0},{2,1},{3,2},{4,3},{5,4},{6,5},{7,6},{8,7},{9,8},{10,9},{11,1... | collective-permute-start | bytes 1572872 | tf_op jit(solution)/shard_map/ppermute | solution.py:747
  424.5 62.7 %all-to-all-start.6 = ((f32[32,2,64,128]{3,2,1,0:T(8,128)}), f32[32,2,64,128]{3,2,1,0:T(8,128)S(1)}, u32[]{:S(2)}, u32[]{:S(2)}) async-start(f32[32,2,64,128]{3,2,1,0:T(8,128)} %compress.14), calls=%async_computation.6 | async-start | bytes 4194304 | tf_op jit(solution)/shard_map/all_to_all | solution.py:783
  432.8 50.0 %collective-permute-start.32 = (f32[16,2,32,128]{3,2,1,0:T(8,128)}, f32[16,2,32,128]{3,2,1,0:T(8,128)S(1)}, u32[]{:S(2)}, u32[]{:S(2)}) collective-permute-start(f32[16,2,32,128]{3,2,1,0:T(8,128)} %get-tuple-element.429), channel_id=1, source_target_pairs={{0,1},{1,2},{2,3},{3,4},{4,5},{5,6},{6,7},{7,8},{8,9},{9,10},{10,1... | collective-permute-start | bytes 1572872 | tf_op jit(solution)/shard_map/ppermute | solution.py:746
  434.8 48.7 %collective-permute-start.33 = (f32[16,2,32,128]{3,2,1,0:T(8,128)}, f32[16,2,32,128]{3,2,1,0:T(8,128)S(1)}, u32[]{:S(2)}, u32[]{:S(2)}) collective-permute-start(f32[16,2,32,128]{3,2,1,0:T(8,128)} %get-tuple-element.430), channel_id=1, source_target_pairs={{1,0},{2,1},{3,2},{4,3},{5,4},{6,5},{7,6},{8,7},{9,8},{10,9},{11,1... | collective-permute-start | bytes 1572872 | tf_op jit(solution)/shard_map/ppermute | solution.py:747
  488.6 58.1 %all-to-all-start.7 = ((f32[32,2,64,128]{3,2,1,0:T(8,128)}), f32[32,2,64,128]{3,2,1,0:T(8,128)S(1)}, u32[]{:S(2)}, u32[]{:S(2)}) async-start(f32[32,2,64,128]{3,2,1,0:T(8,128)} %compress.15), calls=%async_computation.7 | async-start | bytes 4194304 | tf_op jit(solution)/shard_map/all_to_all | solution.py:783
  554.8 53.0 %collective-permute-start.35 = (f32[32,2,32,128]{3,2,1,0:T(8,128)}, f32[32,2,32,128]{3,2,1,0:T(8,128)S(1)}, u32[]{:S(2)}, u32[]{:S(2)}) collective-permute-start(f32[32,2,32,128]{3,2,1,0:T(8,128)} %get-tuple-element.450), channel_id=1, source_target_pairs={{0,1},{1,2},{2,3},{3,4},{4,5},{5,6},{6,7},{7,8},{8,9},{9,10},{10,1... | collective-permute-start | bytes 3145736 | tf_op jit(solution)/shard_map/ppermute | solution.py:746
  557.0 50.8 %collective-permute-start.37 = (f32[32,2,32,128]{3,2,1,0:T(8,128)}, f32[32,2,32,128]{3,2,1,0:T(8,128)S(1)}, u32[]{:S(2)}, u32[]{:S(2)}) collective-permute-start(f32[32,2,32,128]{3,2,1,0:T(8,128)} %get-tuple-element.457), channel_id=1, source_target_pairs={{1,0},{2,1},{3,2},{4,3},{5,4},{6,5},{7,6},{8,7},{9,8},{10,9},{11,1... | collective-permute-start | bytes 3145736 | tf_op jit(solution)/shard_map/ppermute | solution.py:747
  567.2 40.5 %collective-permute-start.34 = (f32[16,2,32,128]{3,2,1,0:T(8,128)}, f32[16,2,32,128]{3,2,1,0:T(8,128)S(1)}, u32[]{:S(2)}, u32[]{:S(2)}) collective-permute-start(f32[16,2,32,128]{3,2,1,0:T(8,128)} %get-tuple-element.449), channel_id=1, source_target_pairs={{0,1},{1,2},{2,3},{3,4},{4,5},{5,6},{6,7},{7,8},{8,9},{9,10},{10,1... | collective-permute-start | bytes 1572872 | tf_op jit(solution)/shard_map/ppermute | solution.py:746
  569.1 38.6 %collective-permute-start.36 = (f32[16,2,32,128]{3,2,1,0:T(8,128)}, f32[16,2,32,128]{3,2,1,0:T(8,128)S(1)}, u32[]{:S(2)}, u32[]{:S(2)}) collective-permute-start(f32[16,2,32,128]{3,2,1,0:T(8,128)} %get-tuple-element.456), channel_id=1, source_target_pairs={{1,0},{2,1},{3,2},{4,3},{5,4},{6,5},{7,6},{8,7},{9,8},{10,9},{11,1... | collective-permute-start | bytes 1572872 | tf_op jit(solution)/shard_map/ppermute | solution.py:747
  (47 other events, 1321.2 us)

commit v8 on v7

--- a/solution.py
+++ b/solution.py
@@ -348,8 +348,9 @@
                 at = joined * PER_CHUNK + k
                 up_ref[at, ri] = out_ref[k, ri, bins - HALO : bins, :]
                 down_ref[at, ri] = out_ref[k, ri, 0:HALO, :]
-                for before_ref, edge_ref in zip(edges_before, (up_ref, down_ref)):
-                    edge_ref[k, ri] = before_ref[k, ri]
+                for i in range(joined):
+                    up_ref[i * PER_CHUNK + k, ri] = edges_before[2 * i][k, ri]
+                    down_ref[i * PER_CHUNK + k, ri] = edges_before[2 * i + 1][k, ri]
             return carry
 
         lax.fori_loop(0, PER_CHUNK, edges, 0)
@@ -387,7 +388,7 @@
 
 
 KB = 4
-BB = 8
+BB = 16
 QUAD = 4
 
 
@@ -492,7 +493,7 @@
         return step * KB + kk if keeps else kk
 
     def first_half(block):
-        base = jnp.minimum(block * BB, rows - BB)
+        base = block * BB
         for j in range(BB // QUAD):
             cols = []
             for t in range(QUAD):
@@ -555,8 +556,7 @@
         for kk in range(KB):
             one(kk, kk % 2)
 
-    @pl.when(step > steps)
-    def _():
+    def second_half():
         for j in range(BB // QUAD):
             image = dot_nt(inv2_ref[...], half_ref[j, 0])
             image = image[0 : 2 * LANES] + image[2 * LANES :]
@@ -566,13 +566,27 @@
                     s_ref[ri, QUAD * j + t] = image[
                         ri * LANES : (ri + 1) * LANES, t * LANES : (t + 1) * LANES
                     ]
-        first_half(step - steps)
+
+    def write():
         for ri in range(2):
             for start in range(0, LANES, 8):
                 lines = jnp.swapaxes(s_ref[ri, :, start : start + 8, :], 0, 1)
                 for n in range(8):
                     at = (start + n) * LANES
                     out_ref[ri, :, at : at + LANES] = lines[n]
+
+    last = pl.num_programs(0) - 1
+
+    @pl.when((step > steps) & (step < last))
+    def _():
+        second_half()
+        first_half(step - steps)
+        write()
+
+    @pl.when(step == last)
+    def _():
+        second_half()
+        write()
 
     @pl.when(step == steps)
     def _():
@@ -740,7 +754,7 @@
             if c > 0:
                 turned[g], mains[c - 1] = lax.optimization_barrier((turned[g], mains[c - 1]))
             mains[c], up, down = azimuth(turned[g], c, place, edges if c == CHUNKS - 1 else ())
-            if c == CHUNKS - 2:
+            if CHUNKS - 3 <= c < CHUNKS - 1:
                 edges.extend([up, down])
                 continue
             lows[c] = lax.ppermute(up, axes, neighbours(axes, devices, 1))
@@ -784,7 +798,7 @@
         turned.append(moved.reshape(nrng, naz, 2, len(chunks), per_part, rows_in, bins))
     transform(count - 2)
     transform(count - 1)
-    lows[-2], highs[-2] = lows[-1], highs[-1]
+    lows[-3:], highs[-3:] = lows[-1:] * 3, highs[-1:] * 3
     tables = (shift_table, filter_index, tap_table)
     image, sources = None, mains
     for i, places_of in enumerate(places):

time: 640 us -> 632 us (0.988)
  starting transfers between devices: 152 us -> 143 us
    ppermute x7 -> x6, starting transfers between devices: 50.6 us -> 43.4 us  [transform(): highs[c] = lax.ppermute(down, axes, neighbours(axes, devices, -1))]
    ppermute x7 -> x6, starting transfers between devices: 13.8 us -> 11.9 us  [transform(): lows[c] = lax.ppermute(up, axes, neighbours(axes, devices, 1))]
    unnamed x68 -> x96, local copies, waits for them, and re-layouts: 12.2 us -> 13.1 us
    ppermute x7 -> x6, waiting for transfers between devices: 23.4 us -> 23.4 us  [transform(): lows[c] = lax.ppermute(up, axes, neighbours(axes, devices, 1))]
  transfers between devices with their start and end apart: 46 -> 44, of which waited for: 21 -> 21; matrix products, arithmetic and copies ran while one was open for 2% -> 3% of each run, Pallas kernels for 32% -> 32%
where the time goes in v8:
time: 632 us; the launch traced here: 630 us
  Pallas kernels  245 us (39%)
  waiting for transfers between devices  211 us (33%)
  starting transfers between devices  143 us (23%)
  local copies, waits for them, and re-layouts  19.7 us (3%)
  other arithmetic  9.7 us (2%)
    ppermute x24, waiting for transfers between devices, gather(): lax.ppermute(packed[g][j], 'rng', [(i, i ^ j) for i in range(nrng)])  140 us
    pallas_call x8, Pallas kernels, compress(): pl.pallas_call(functools.partial(compress_kernel, parts, block), grid=(ro...  89.6 us
    all_to_all x8, starting transfers between devices, local(): moved = lax.all_to_all(lines, axes, split_axis=0, concat_axis=0, tiled=True)  58.9 us
    pallas_call x2, Pallas kernels, final(): pl.pallas_call(functools.partial(final_kernel, steps, joins, wide), grid=...  54.2 us
    pallas_call x8, Pallas kernels, azimuth(): pl.pallas_call(functools.partial(azimuth_kernel, chunk, joined), grid=(pa...  50.1 us
    all_to_all x8, waiting for transfers between devices, local(): moved = lax.all_to_all(lines, axes, split_axis=0, concat_axis=0, tiled=True)  48.4 us
    ppermute x6, starting transfers between devices, transform(): highs[c] = lax.ppermute(down, axes, neighbours(axes, devices, -1))  43.4 us
    ppermute x24, starting transfers between devices, gather(): lax.ppermute(packed[g][j], 'rng', [(i, i ^ j) for i in range(nrng)])  28.4 us
  transfers between devices with their start and end apart: 44, of which 21 were waited for; matrix products, arithmetic and copies ran while one was open for 3% of the time, Pallas kernels for 32%

profile of v8, /device:TPU:4, one launch (start us, length us, event | category | flops | bytes accessed | tf_op | source)
XLA Modules:
  0.0 629.5 jit_solution(3354795626715337624)
XLA Ops:
  0.0 9.2 %pack.3 = (f32[2,8,64,128]{3,2,1,0:T(8,128)}, f32[2,8,64,128]{3,2,1,0:T(8,128)}, f32[2,8,64,128]{3,2,1,0:T(8,128)}, f32[2,8,64,128]{3,2,1,0:T(8,128)}) custom-call(s32[1]{0:T(128)} %bitcast.rank_ref, f32[2,2048,1024]{2,1,0:T(8,128)} %x_ref.3), custom_call_target="tpu_custom_call" | custom-call | bytes 33554432 | tf_op jit(solution)/shard_map/pack/pallas_call | solution.py:141
  12.7 15.5 %pack.2 = (f32[2,8,64,128]{3,2,1,0:T(8,128)}, f32[2,8,64,128]{3,2,1,0:T(8,128)}, f32[2,8,64,128]{3,2,1,0:T(8,128)}, f32[2,8,64,128]{3,2,1,0:T(8,128)}, f32[2,8,6...) custom-call(s32[1]{0:T(128)} %bitcast.rank_ref, ...), custom_call_target="tpu_custom_call" | custom-call | bytes 33554432 | tf_op jit(solution)/shard_map/pack/pallas_call | solution.py:141
  28.3 7.3 %collective-permute-done.1.refs_2_ = f32[2,8,64,128]{3,2,1,0:T(8,128)S(1)} collective-permute-done((f32[2,8,64,128]{3,2,1,0:T(8,128)}, f32[2,8,64,128]{3,2,1,0:T(8,128)S(1)}, u32[]{:S(2)}, u32[]{:S(2)}) %collective-permute-start.1) | collective-permute-done | bytes 524320 | tf_op jit(solution)/shard_map/ppermute | solution.py:748
  39.9 11.2 %compress.8 = f32[32,2,64,128]{3,2,1,0:T(8,128)} custom-call(s32[1]{0:T(128)} %bitcast.rank_ref, f32[2,8,64,128]{3,2,1,0:T(8,128)} %get-tuple-element.252.refs_0_, f32[2,8,64,128]{3,2,1,0:T(8,128)} %copy-done.39, f32[2,8,64,128]{3,2,1,0:T(8,128)} %copy-done.40, f32[2,8,64,128]{3,2,1,0:T(8,128)} %copy-done.41, f32[2,32,128]{2,1,0:T(8,128)} %bitcast.69, ...), custom_call_target="tpu_custom_call" | custom-call | flops 1610612736 | bytes 4194304 | tf_op jit(solution)/shard_map/compress/pallas_call | solution.py:280
  51.1 8.6 %collective-permute-done.4.refs_2_ = f32[2,8,64,128]{3,2,1,0:T(8,128)S(1)} collective-permute-done((f32[2,8,64,128]{3,2,1,0:T(8,128)}, f32[2,8,64,128]{3,2,1,0:T(8,128)S(1)}, u32[]{:S(2)}, u32[]{:S(2)}) %collective-permute-start.4) | collective-permute-done | bytes 524320 | tf_op jit(solution)/shard_map/ppermute | solution.py:748
  69.4 11.2 %compress.9 = f32[32,2,64,128]{3,2,1,0:T(8,128)} custom-call(s32[1]{0:T(128)} %bitcast.rank_ref, f32[2,8,64,128]{3,2,1,0:T(8,128)} %get-tuple-element.264.refs_0_, f32[2,8,64,128]{3,2,1,0:T(8,128)} %copy-done.44, f32[2,8,64,128]{3,2,1,0:T(8,128)} %copy-done.45, f32[2,8,64,128]{3,2,1,0:T(8,128)} %collective-permute-done.5.refs_3_, f32[2,32,128]{2,1,0:T(8,128)} %bitcast.70, ...), custom_call_target="tpu_custom_call" | custom-call | flops 1610612736 | bytes 4194304 | tf_op jit(solution)/shard_map/compress/pallas_call | solution.py:280
  80.7 16.2 %collective-permute-done.6.refs_1_ = f32[2,8,64,128]{3,2,1,0:T(8,128)S(1)} collective-permute-done((f32[2,8,64,128]{3,2,1,0:T(8,128)}, f32[2,8,64,128]{3,2,1,0:T(8,128)S(1)}, u32[]{:S(2)}, u32[]{:S(2)}) %collective-permute-start.6) | collective-permute-done | bytes 524320 | tf_op jit(solution)/shard_map/ppermute | solution.py:748
  97.9 14.8 %collective-permute-done.8.refs_3_ = f32[2,8,64,128]{3,2,1,0:T(8,128)} collective-permute-done((f32[2,8,64,128]{3,2,1,0:T(8,128)}, f32[2,8,64,128]{3,2,1,0:T(8,128)}, u32[]{:S(2)}, u32[]{:S(2)}) %collective-permute-start.8) | collective-permute-done | bytes 524320 | tf_op jit(solution)/shard_map/ppermute | solution.py:748
  126.2 11.2 %compress.10 = f32[32,2,64,128]{3,2,1,0:T(8,128)} custom-call(s32[1]{0:T(128)} %bitcast.rank_ref, f32[2,8,64,128]{3,2,1,0:T(8,128)} %get-tuple-element.276.refs_0_, f32[2,8,64,128]{3,2,1,0:T(8,128)} %copy-done.43, f32[2,8,64,128]{3,2,1,0:T(8,128)} %collective-permute-done.7.refs_2_, f32[2,8,64,128]{3,2,1,0:T(8,128)} %collective-permute-done.8.refs_3_, ...), custom_call_target="tpu_custom_call" | custom-call | flops 1610612736 | bytes 4194304 | tf_op jit(solution)/shard_map/compress/pallas_call | solution.py:280
  149.9 15.9 %collective-permute-done.10.refs_2_ = f32[2,8,64,128]{3,2,1,0:T(8,128)} collective-permute-done((f32[2,8,64,128]{3,2,1,0:T(8,128)}, f32[2,8,64,128]{3,2,1,0:T(8,128)}, u32[]{:S(2)}, u32[]{:S(2)}) %collective-permute-start.10) | collective-permute-done | bytes 524320 | tf_op jit(solution)/shard_map/ppermute | solution.py:748
  202.7 11.2 %compress.11 = f32[32,2,64,128]{3,2,1,0:T(8,128)} custom-call(s32[1]{0:T(128)} %bitcast.rank_ref, f32[2,8,64,128]{3,2,1,0:T(8,128)} %get-tuple-element.308.refs_0_, f32[2,8,64,128]{3,2,1,0:T(8,128)} %collective-permute-done.9.refs_1_, f32[2,8,64,128]{3,2,1,0:T(8,128)} %collective-permute-done.10.refs_2_, f32[2,8,64,128]{3,2,1,0:T(8,128)} %collective-permute-done.11.refs_3_, ...), custom_call_target="tpu_custom_call" | custom-call | flops 1610612736 | bytes 4194304 | tf_op jit(solution)/shard_map/compress/pallas_call | solution.py:280
  213.9 15.9 %collective-permute-done.14.refs_3_ = f32[2,8,64,128]{3,2,1,0:T(8,128)} collective-permute-done((f32[2,8,64,128]{3,2,1,0:T(8,128)S(1)}, f32[2,8,64,128]{3,2,1,0:T(8,128)}, u32[]{:S(2)}, u32[]{:S(2)}) %collective-permute-start.14) | collective-permute-done | bytes 524320 | tf_op jit(solution)/shard_map/ppermute | solution.py:748
  233.0 9.3 %all-to-all-start.3 = ((f32[32,2,64,128]{3,2,1,0:T(8,128)}), f32[32,2,64,128]{3,2,1,0:T(8,128)}, u32[]{:S(2)}, u32[]{:S(2)}) async-start(f32[32,2,64,128]{3,2,1,0:T(8,128)} %compress.11), calls=%async_computation.3 | async-start | bytes 4194304 | tf_op jit(solution)/shard_map/all_to_all | solution.py:797
  247.8 7.2 %collective-permute-start.24 = (f32[16,2,32,128]{3,2,1,0:T(8,128)}, f32[16,2,32,128]{3,2,1,0:T(8,128)}, u32[]{:S(2)}, u32[]{:S(2)}) collective-permute-start(f32[16,2,32,128]{3,2,1,0:T(8,128)} %get-tuple-element.387), channel_id=1, source_target_pairs={{1,0},{2,1},{3,2},{4,3},{5,4},{6,5},{7,6},{8,7},{9,8},{10,9},{11,1... | collective-permute-start | bytes 1572872 | tf_op jit(solution)/shard_map/ppermute | solution.py:761
  255.0 11.2 %compress.12 = f32[32,2,64,128]{3,2,1,0:T(8,128)} custom-call(s32[1]{0:T(128)} %bitcast.rank_ref, f32[2,8,64,128]{3,2,1,0:T(8,128)} %get-tuple-element.337.refs_0_, f32[2,8,64,128]{3,2,1,0:T(8,128)} %collective-permute-done.12.refs_1_, f32[2,8,64,128]{3,2,1,0:T(8,128)} %collective-permute-done.13.refs_2_, f32[2,8,64,128]{3,2,1,0:T(8,128)} %collective-permute-done.14.refs_3_, ...), custom_call_target="tpu_custom_call" | custom-call | flops 1610612736 | bytes 4194304 | tf_op jit(solution)/shard_map/compress/pallas_call | solution.py:280
  279.0 15.7 %collective-permute-done.17.refs_3_ = f32[2,8,64,128]{3,2,1,0:T(8,128)S(1)} collective-permute-done((f32[2,8,64,128]{3,2,1,0:T(8,128)S(1)}, f32[2,8,64,128]{3,2,1,0:T(8,128)S(1)}, u32[]{:S(2)}, u32[]{:S(2)}) %collective-permute-start.17) | collective-permute-done | bytes 524320 | tf_op jit(solution)/shard_map/ppermute | solution.py:748
  296.8 8.2 %all-to-all-start.4 = ((f32[32,2,64,128]{3,2,1,0:T(8,128)}), f32[32,2,64,128]{3,2,1,0:T(8,128)S(1)}, u32[]{:S(2)}, u32[]{:S(2)}) async-start(f32[32,2,64,128]{3,2,1,0:T(8,128)} %compress.12), calls=%async_computation.4 | async-start | bytes 4194304 | tf_op jit(solution)/shard_map/all_to_all | solution.py:797
  310.6 7.4 %collective-permute-start.26 = (f32[16,2,32,128]{3,2,1,0:T(8,128)}, f32[16,2,32,128]{3,2,1,0:T(8,128)S(1)}, u32[]{:S(2)}, u32[]{:S(2)}) collective-permute-start(f32[16,2,32,128]{3,2,1,0:T(8,128)} %get-tuple-element.399), channel_id=1, source_target_pairs={{1,0},{2,1},{3,2},{4,3},{5,4},{6,5},{7,6},{8,7},{9,8},{10,9},{11,1... | collective-permute-start | bytes 1572872 | tf_op jit(solution)/shard_map/ppermute | solution.py:761
  330.6 11.2 %compress.13 = f32[32,2,64,128]{3,2,1,0:T(8,128)} custom-call(s32[1]{0:T(128)} %bitcast.rank_ref, f32[2,8,64,128]{3,2,1,0:T(8,128)} %get-tuple-element.369.refs_0_, f32[2,8,64,128]{3,2,1,0:T(8,128)} %copy-done.33, f32[2,8,64,128]{3,2,1,0:T(8,128)} %copy-done.34, f32[2,8,64,128]{3,2,1,0:T(8,128)} %copy-done.35, f32[2,32,128]{2,1,0:T(8,128)} %bitcast.74, ...), custom_call_target="tpu_custom_call" | custom-call | flops 1610612736 | bytes 4194304 | tf_op jit(solution)/shard_map/compress/pallas_call | solution.py:280
  341.8 15.8 %collective-permute-done.22.refs_3_ = f32[2,8,64,128]{3,2,1,0:T(8,128)} collective-permute-done((f32[2,8,64,128]{3,2,1,0:T(8,128)S(1)}, f32[2,8,64,128]{3,2,1,0:T(8,128)}, u32[]{:S(2)}, u32[]{:S(2)}) %collective-permute-start.22) | collective-permute-done | bytes 524320 | tf_op jit(solution)/shard_map/ppermute | solution.py:748
  360.9 9.3 %all-to-all-start.5 = ((f32[32,2,64,128]{3,2,1,0:T(8,128)}), f32[32,2,64,128]{3,2,1,0:T(8,128)}, u32[]{:S(2)}, u32[]{:S(2)}) async-start(f32[32,2,64,128]{3,2,1,0:T(8,128)} %compress.13), calls=%async_computation.5 | async-start | bytes 4194304 | tf_op jit(solution)/shard_map/all_to_all | solution.py:797
  375.6 7.2 %collective-permute-start.31 = (f32[16,2,32,128]{3,2,1,0:T(8,128)}, f32[16,2,32,128]{3,2,1,0:T(8,128)}, u32[]{:S(2)}, u32[]{:S(2)}) collective-permute-start(f32[16,2,32,128]{3,2,1,0:T(8,128)} %get-tuple-element.418), channel_id=1, source_target_pairs={{1,0},{2,1},{3,2},{4,3},{5,4},{6,5},{7,6},{8,7},{9,8},{10,9},{11,1... | collective-permute-start | bytes 1572872 | tf_op jit(solution)/shard_map/ppermute | solution.py:761
  382.9 11.2 %compress.14 = f32[32,2,64,128]{3,2,1,0:T(8,128)} custom-call(s32[1]{0:T(128)} %bitcast.rank_ref, f32[2,8,64,128]{3,2,1,0:T(8,128)} %get-tuple-element.403.refs_0_, f32[2,8,64,128]{3,2,1,0:T(8,128)} %collective-permute-done.20.refs_1_, f32[2,8,64,128]{3,2,1,0:T(8,128)} %collective-permute-done.21.refs_2_, f32[2,8,64,128]{3,2,1,0:T(8,128)} %collective-permute-done.22.refs_3_, ...), custom_call_target="tpu_custom_call" | custom-call | flops 1610612736 | bytes 4194304 | tf_op jit(solution)/shard_map/compress/pallas_call | solution.py:280
  402.1 20.5 %collective-permute-done.29.refs_3_ = f32[2,8,64,128]{3,2,1,0:T(8,128)S(1)} collective-permute-done((f32[2,8,64,128]{3,2,1,0:T(8,128)S(1)}, f32[2,8,64,128]{3,2,1,0:T(8,128)S(1)}, u32[]{:S(2)}, u32[]{:S(2)}) %collective-permute-start.29) | collective-permute-done | bytes 524320 | tf_op jit(solution)/shard_map/ppermute | solution.py:748
  424.7 8.2 %all-to-all-start.6 = ((f32[32,2,64,128]{3,2,1,0:T(8,128)}), f32[32,2,64,128]{3,2,1,0:T(8,128)S(1)}, u32[]{:S(2)}, u32[]{:S(2)}) async-start(f32[32,2,64,128]{3,2,1,0:T(8,128)} %compress.14), calls=%async_computation.6 | async-start | bytes 4194304 | tf_op jit(solution)/shard_map/all_to_all | solution.py:797
  448.2 11.2 %compress.15 = f32[32,2,64,128]{3,2,1,0:T(8,128)} custom-call(s32[1]{0:T(128)} %bitcast.rank_ref, f32[2,8,64,128]{3,2,1,0:T(8,128)} %get-tuple-element.420.refs_0_, f32[2,8,64,128]{3,2,1,0:T(8,128)} %copy-done.36, f32[2,8,64,128]{3,2,1,0:T(8,128)} %copy-done.37, f32[2,8,64,128]{3,2,1,0:T(8,128)} %copy-done.38, f32[2,32,128]{2,1,0:T(8,128)} %bitcast.76, ...), custom_call_target="tpu_custom_call" | custom-call | flops 1610612736 | bytes 4194304 | tf_op jit(solution)/shard_map/compress/pallas_call | solution.py:280
  459.5 23.4 %collective-permute-done.32.refs_5_ = f32[16,2,32,128]{3,2,1,0:T(8,128)S(1)} collective-permute-done((f32[16,2,32,128]{3,2,1,0:T(8,128)}, f32[16,2,32,128]{3,2,1,0:T(8,128)S(1)}, u32[]{:S(2)}, u32[]{:S(2)}) %collective-permute-start.32) | collective-permute-done | bytes 524320 | tf_op jit(solution)/shard_map/ppermute | solution.py:760
  488.8 9.2 %all-to-all-start.7 = ((f32[32,2,64,128]{3,2,1,0:T(8,128)}), f32[32,2,64,128]{3,2,1,0:T(8,128)S(1)}, u32[]{:S(2)}, u32[]{:S(2)}) async-start(f32[32,2,64,128]{3,2,1,0:T(8,128)} %compress.15), calls=%async_computation.7 | async-start | bytes 4194304 | tf_op jit(solution)/shard_map/all_to_all | solution.py:797
  510.5 36.3 %all-to-all-done.7 = f32[32,2,64,128]{3,2,1,0:T(8,128)S(1)} async-done(((f32[32,2,64,128]{3,2,1,0:T(8,128)}), f32[32,2,64,128]{3,2,1,0:T(8,128)S(1)}, u32[]{:S(2)}, u32[]{:S(2)}) %all-to-all-start.7) | async-done | bytes 2097184 | tf_op jit(solution)/shard_map/all_to_all | solution.py:797
  548.1 7.5 %azimuth7.1 = (f32[16,2,128,128]{3,2,1,0:T(8,128)}, f32[48,2,32,128]{3,2,1,0:T(8,128)}, f32[48,2,32,128]{3,2,1,0:T(8,128)}) custom-call(f32[4,8,2,1,4,16,128]{6,5,4,3,2,1,0:T(8,128)} %bitcast.37, f32[16,2,32,128]{3,2,1,0:T(8,128)} %get-tuple-element.436.refs_0_, f32[16,2,32,128]{3,2,1,0:T(8,128)} %get-tuple-element.437.refs_1_, ...), custom_call_target="tpu_custom_call" | custom-call | flops 805306368 | bytes 4194304 | tf_op jit(solution)/shard_map/azimuth7/pallas_call | solution.py:369
  573.5 27.1 %final_inner.1 = (f32[2,128,16384]{2,1,0:T(8,128)}, bf16[8,16,256,256]{3,2,1,0:T(8,128)(2,1)}) custom-call(f32[16,2,128,128]{3,2,1,0:T(8,128)} %get-tuple-element.303.refs_0_, f32[16,2,128,128]{3,2,1,0:T(8,128)} %get-tuple-element.332.refs_1_, f32[16,2,128,128]{3,2,1,0:T(8,128)} %get-tuple-element.364.refs_2_, ...), custom_call_target="tpu_custom_call" | custom-call | flops 9663676416 | bytes 29360128 | tf_op jit(solution)/shard_map/final_inner/pallas_call | solution.py:679
  602.3 27.0 %final_wide.1 = f32[2,128,16384]{2,1,0:T(8,128)} custom-call(bf16[8,16,256,256]{3,2,1,0:T(8,128)(2,1)} %get-tuple-element.445.refs_0_, f32[16,2,32,128]{3,2,1,0:T(8,128)} %copy-done.11, f32[16,2,32,128]{3,2,1,0:T(8,128)} %collective-permute-done.23.refs_2_, f32[16,2,32,128]{3,2,1,0:T(8,128)} %copy-done.13, ...), custom_call_target="tpu_custom_call", output_to_operand_aliasing={{}: (23, {})} | custom-call | flops 9663676416 | bytes 29360128 | tf_op jit(solution)/shard_map/final_wide/pallas_call | solution.py:679
  (203 shorter events, 196.0 us)
Async XLA Ops:
  60.6 54.1 %all-to-all-start = ((f32[32,2,64,128]{3,2,1,0:T(8,128)}), f32[32,2,64,128]{3,2,1,0:T(8,128)S(1)}, u32[]{:S(2)}, u32[]{:S(2)}) async-start(f32[32,2,64,128]{3,2,1,0:T(8,128)} %compress.8), calls=%async_computation | async-start | bytes 4194304 | tf_op jit(solution)/shard_map/all_to_all | solution.py:797
  67.9 44.7 %collective-permute-start.8 = (f32[2,8,64,128]{3,2,1,0:T(8,128)}, f32[2,8,64,128]{3,2,1,0:T(8,128)}, u32[]{:S(2)}, u32[]{:S(2)}) collective-permute-start(f32[2,8,64,128]{3,2,1,0:T(8,128)} %get-tuple-element.271), channel_id=1, source_target_pairs={{0,24},{8,16},{16,8},{24,0},{1,25},{9,17},{17,9},{25,1},{2,26},{10... | collective-permute-start | bytes 1572872 | tf_op jit(solution)/shard_map/ppermute | solution.py:748
  116.1 55.7 %all-to-all-start.1 = ((f32[32,2,64,128]{3,2,1,0:T(8,128)}), f32[32,2,64,128]{3,2,1,0:T(8,128)S(1)}, u32[]{:S(2)}, u32[]{:S(2)}) async-start(f32[32,2,64,128]{3,2,1,0:T(8,128)} %compress.9), calls=%async_computation.1 | async-start | bytes 4194304 | tf_op jit(solution)/shard_map/all_to_all | solution.py:797
  121.4 44.5 %collective-permute-start.10 = (f32[2,8,64,128]{3,2,1,0:T(8,128)}, f32[2,8,64,128]{3,2,1,0:T(8,128)}, u32[]{:S(2)}, u32[]{:S(2)}) collective-permute-start(f32[2,8,64,128]{3,2,1,0:T(8,128)} %get-tuple-element.287), channel_id=1, source_target_pairs={{0,16},{8,24},{16,0},{24,8},{1,17},{9,25},{17,1},{25,9},{2,18},{10... | collective-permute-start | bytes 1572872 | tf_op jit(solution)/shard_map/ppermute | solution.py:748
  121.7 44.1 %collective-permute-start.11 = (f32[2,8,64,128]{3,2,1,0:T(8,128)S(1)}, f32[2,8,64,128]{3,2,1,0:T(8,128)}, u32[]{:S(2)}, u32[]{:S(2)}) collective-permute-start(f32[2,8,64,128]{3,2,1,0:T(8,128)S(1)} %copy-done.32), channel_id=1, source_target_pairs={{0,24},{8,16},{16,8},{24,0},{1,25},{9,17},{17,9},{25,1},{2,26},{10... | collective-permute-start | bytes 1572872 | tf_op jit(solution)/shard_map/ppermute | solution.py:748
  124.4 47.3 %collective-permute-start.9 = (f32[2,8,64,128]{3,2,1,0:T(8,128)S(1)}, f32[2,8,64,128]{3,2,1,0:T(8,128)}, u32[]{:S(2)}, u32[]{:S(2)}) collective-permute-start(f32[2,8,64,128]{3,2,1,0:T(8,128)S(1)} %copy-done.31), channel_id=1, source_target_pairs={{0,8},{8,0},{16,24},{24,16},{1,9},{9,1},{17,25},{25,17},{2,10},{10... | collective-permute-start | bytes 1572872 | tf_op jit(solution)/shard_map/ppermute | solution.py:748
  173.0 58.7 %all-to-all-start.2 = ((f32[32,2,64,128]{3,2,1,0:T(8,128)}), f32[32,2,64,128]{3,2,1,0:T(8,128)S(1)}, u32[]{:S(2)}, u32[]{:S(2)}) async-start(f32[32,2,64,128]{3,2,1,0:T(8,128)} %compress.10), calls=%async_computation.2 | async-start | bytes 4194304 | tf_op jit(solution)/shard_map/all_to_all | solution.py:797
  177.2 36.7 %collective-permute-start.12 = (f32[2,8,64,128]{3,2,1,0:T(8,128)}, f32[2,8,64,128]{3,2,1,0:T(8,128)}, u32[]{:S(2)}, u32[]{:S(2)}) collective-permute-start(f32[2,8,64,128]{3,2,1,0:T(8,128)} %get-tuple-element.313), channel_id=1, source_target_pairs={{0,8},{8,0},{16,24},{24,16},{1,9},{9,1},{17,25},{25,17},{2,10},{10... | collective-permute-start | bytes 1572872 | tf_op jit(solution)/shard_map/ppermute | solution.py:748
  179.3 50.5 %collective-permute-start.14 = (f32[2,8,64,128]{3,2,1,0:T(8,128)S(1)}, f32[2,8,64,128]{3,2,1,0:T(8,128)}, u32[]{:S(2)}, u32[]{:S(2)}) collective-permute-start(f32[2,8,64,128]{3,2,1,0:T(8,128)S(1)} %copy-done.30), channel_id=1, source_target_pairs={{0,24},{8,16},{16,8},{24,0},{1,25},{9,17},{17,9},{25,1},{2,26},{10... | collective-permute-start | bytes 1572872 | tf_op jit(solution)/shard_map/ppermute | solution.py:748
  180.8 49.1 %collective-permute-start.18 = (f32[16,2,32,128]{3,2,1,0:T(8,128)}, f32[16,2,32,128]{3,2,1,0:T(8,128)S(1)}, u32[]{:S(2)}, u32[]{:S(2)}) collective-permute-start(f32[16,2,32,128]{3,2,1,0:T(8,128)} %get-tuple-element.354), channel_id=1, source_target_pairs={{0,1},{1,2},{2,3},{3,4},{4,5},{5,6},{6,7},{7,8},{8,9},{9,10},{10,1... | collective-permute-start | bytes 1572872 | tf_op jit(solution)/shard_map/ppermute | solution.py:760
  182.7 47.9 %collective-permute-start.19 = (f32[16,2,32,128]{3,2,1,0:T(8,128)}, f32[16,2,32,128]{3,2,1,0:T(8,128)S(1)}, u32[]{:S(2)}, u32[]{:S(2)}) collective-permute-start(f32[16,2,32,128]{3,2,1,0:T(8,128)} %get-tuple-element.355), channel_id=1, source_target_pairs={{1,0},{2,1},{3,2},{4,3},{5,4},{6,5},{7,6},{8,7},{9,8},{10,9},{11,1... | collective-permute-start | bytes 1572872 | tf_op jit(solution)/shard_map/ppermute | solution.py:761
  233.0 63.8 %all-to-all-start.3 = ((f32[32,2,64,128]{3,2,1,0:T(8,128)}), f32[32,2,64,128]{3,2,1,0:T(8,128)}, u32[]{:S(2)}, u32[]{:S(2)}) async-start(f32[32,2,64,128]{3,2,1,0:T(8,128)} %compress.11), calls=%async_computation.3 | async-start | bytes 4194304 | tf_op jit(solution)/shard_map/all_to_all | solution.py:797
  242.3 36.7 %collective-permute-start.15 = (f32[2,8,64,128]{3,2,1,0:T(8,128)}, f32[2,8,64,128]{3,2,1,0:T(8,128)S(1)}, u32[]{:S(2)}, u32[]{:S(2)}) collective-permute-start(f32[2,8,64,128]{3,2,1,0:T(8,128)} %get-tuple-element.342), channel_id=1, source_target_pairs={{0,8},{8,0},{16,24},{24,16},{1,9},{9,1},{17,25},{25,17},{2,10},{10... | collective-permute-start | bytes 1572872 | tf_op jit(solution)/shard_map/ppermute | solution.py:748
  244.4 50.3 %collective-permute-start.17 = (f32[2,8,64,128]{3,2,1,0:T(8,128)S(1)}, f32[2,8,64,128]{3,2,1,0:T(8,128)S(1)}, u32[]{:S(2)}, u32[]{:S(2)}) collective-permute-start(f32[2,8,64,128]{3,2,1,0:T(8,128)S(1)} %copy-done.29), channel_id=1, source_target_pairs={{0,24},{8,16},{16,8},{24,0},{1,25},{9,17},{17,9},{25,1},{2,26},{10... | collective-permute-start | bytes 1572872 | tf_op jit(solution)/shard_map/ppermute | solution.py:748
  245.8 48.9 %collective-permute-start.23 = (f32[16,2,32,128]{3,2,1,0:T(8,128)}, f32[16,2,32,128]{3,2,1,0:T(8,128)}, u32[]{:S(2)}, u32[]{:S(2)}) collective-permute-start(f32[16,2,32,128]{3,2,1,0:T(8,128)} %get-tuple-element.386), channel_id=1, source_target_pairs={{0,1},{1,2},{2,3},{3,4},{4,5},{5,6},{6,7},{7,8},{8,9},{9,10},{10,1... | collective-permute-start | bytes 1572872 | tf_op jit(solution)/shard_map/ppermute | solution.py:760
  247.8 47.0 %collective-permute-start.24 = (f32[16,2,32,128]{3,2,1,0:T(8,128)}, f32[16,2,32,128]{3,2,1,0:T(8,128)}, u32[]{:S(2)}, u32[]{:S(2)}) collective-permute-start(f32[16,2,32,128]{3,2,1,0:T(8,128)} %get-tuple-element.387), channel_id=1, source_target_pairs={{1,0},{2,1},{3,2},{4,3},{5,4},{6,5},{7,6},{8,7},{9,8},{10,9},{11,1... | collective-permute-start | bytes 1572872 | tf_op jit(solution)/shard_map/ppermute | solution.py:761
  296.8 62.7 %all-to-all-start.4 = ((f32[32,2,64,128]{3,2,1,0:T(8,128)}), f32[32,2,64,128]{3,2,1,0:T(8,128)S(1)}, u32[]{:S(2)}, u32[]{:S(2)}) async-start(f32[32,2,64,128]{3,2,1,0:T(8,128)} %compress.12), calls=%async_computation.4 | async-start | bytes 4194304 | tf_op jit(solution)/shard_map/all_to_all | solution.py:797
  305.1 36.7 %collective-permute-start.20 = (f32[2,8,64,128]{3,2,1,0:T(8,128)}, f32[2,8,64,128]{3,2,1,0:T(8,128)}, u32[]{:S(2)}, u32[]{:S(2)}) collective-permute-start(f32[2,8,64,128]{3,2,1,0:T(8,128)} %get-tuple-element.374), channel_id=1, source_target_pairs={{0,8},{8,0},{16,24},{24,16},{1,9},{9,1},{17,25},{25,17},{2,10},{10... | collective-permute-start | bytes 1572872 | tf_op jit(solution)/shard_map/ppermute | solution.py:748
  306.6 35.2 %collective-permute-start.21 = (f32[2,8,64,128]{3,2,1,0:T(8,128)}, f32[2,8,64,128]{3,2,1,0:T(8,128)}, u32[]{:S(2)}, u32[]{:S(2)}) collective-permute-start(f32[2,8,64,128]{3,2,1,0:T(8,128)} %get-tuple-element.375), channel_id=1, source_target_pairs={{0,16},{8,24},{16,0},{24,8},{1,17},{9,25},{17,1},{25,9},{2,18},{10... | collective-permute-start | bytes 1572872 | tf_op jit(solution)/shard_map/ppermute | solution.py:748
  307.2 50.5 %collective-permute-start.22 = (f32[2,8,64,128]{3,2,1,0:T(8,128)S(1)}, f32[2,8,64,128]{3,2,1,0:T(8,128)}, u32[]{:S(2)}, u32[]{:S(2)}) collective-permute-start(f32[2,8,64,128]{3,2,1,0:T(8,128)S(1)} %copy-done.28), channel_id=1, source_target_pairs={{0,24},{8,16},{16,8},{24,0},{1,25},{9,17},{17,9},{25,1},{2,26},{10... | collective-permute-start | bytes 1572872 | tf_op jit(solution)/shard_map/ppermute | solution.py:748
  308.6 49.1 %collective-permute-start.25 = (f32[16,2,32,128]{3,2,1,0:T(8,128)}, f32[16,2,32,128]{3,2,1,0:T(8,128)S(1)}, u32[]{:S(2)}, u32[]{:S(2)}) collective-permute-start(f32[16,2,32,128]{3,2,1,0:T(8,128)} %get-tuple-element.398), channel_id=1, source_target_pairs={{0,1},{1,2},{2,3},{3,4},{4,5},{5,6},{6,7},{7,8},{8,9},{9,10},{10,1... | collective-permute-start | bytes 1572872 | tf_op jit(solution)/shard_map/ppermute | solution.py:760
  310.6 48.0 %collective-permute-start.26 = (f32[16,2,32,128]{3,2,1,0:T(8,128)}, f32[16,2,32,128]{3,2,1,0:T(8,128)S(1)}, u32[]{:S(2)}, u32[]{:S(2)}) collective-permute-start(f32[16,2,32,128]{3,2,1,0:T(8,128)} %get-tuple-element.399), channel_id=1, source_target_pairs={{1,0},{2,1},{3,2},{4,3},{5,4},{6,5},{7,6},{8,7},{9,8},{10,9},{11,1... | collective-permute-start | bytes 1572872 | tf_op jit(solution)/shard_map/ppermute | solution.py:761
  360.9 63.8 %all-to-all-start.5 = ((f32[32,2,64,128]{3,2,1,0:T(8,128)}), f32[32,2,64,128]{3,2,1,0:T(8,128)}, u32[]{:S(2)}, u32[]{:S(2)}) async-start(f32[32,2,64,128]{3,2,1,0:T(8,128)} %compress.13), calls=%async_computation.5 | async-start | bytes 4194304 | tf_op jit(solution)/shard_map/all_to_all | solution.py:797
  372.3 50.3 %collective-permute-start.29 = (f32[2,8,64,128]{3,2,1,0:T(8,128)S(1)}, f32[2,8,64,128]{3,2,1,0:T(8,128)S(1)}, u32[]{:S(2)}, u32[]{:S(2)}) collective-permute-start(f32[2,8,64,128]{3,2,1,0:T(8,128)S(1)} %copy-done.27), channel_id=1, source_target_pairs={{0,24},{8,16},{16,8},{24,0},{1,25},{9,17},{17,9},{25,1},{2,26},{10... | collective-permute-start | bytes 1572872 | tf_op jit(solution)/shard_map/ppermute | solution.py:748
  373.7 48.9 %collective-permute-start.30 = (f32[16,2,32,128]{3,2,1,0:T(8,128)}, f32[16,2,32,128]{3,2,1,0:T(8,128)}, u32[]{:S(2)}, u32[]{:S(2)}) collective-permute-start(f32[16,2,32,128]{3,2,1,0:T(8,128)} %get-tuple-element.417), channel_id=1, source_target_pairs={{0,1},{1,2},{2,3},{3,4},{4,5},{5,6},{6,7},{7,8},{8,9},{9,10},{10,1... | collective-permute-start | bytes 1572872 | tf_op jit(solution)/shard_map/ppermute | solution.py:760
  375.6 47.0 %collective-permute-start.31 = (f32[16,2,32,128]{3,2,1,0:T(8,128)}, f32[16,2,32,128]{3,2,1,0:T(8,128)}, u32[]{:S(2)}, u32[]{:S(2)}) collective-permute-start(f32[16,2,32,128]{3,2,1,0:T(8,128)} %get-tuple-element.418), channel_id=1, source_target_pairs={{1,0},{2,1},{3,2},{4,3},{5,4},{6,5},{7,6},{8,7},{9,8},{10,9},{11,1... | collective-permute-start | bytes 1572872 | tf_op jit(solution)/shard_map/ppermute | solution.py:761
  424.7 62.7 %all-to-all-start.6 = ((f32[32,2,64,128]{3,2,1,0:T(8,128)}), f32[32,2,64,128]{3,2,1,0:T(8,128)S(1)}, u32[]{:S(2)}, u32[]{:S(2)}) async-start(f32[32,2,64,128]{3,2,1,0:T(8,128)} %compress.14), calls=%async_computation.6 | async-start | bytes 4194304 | tf_op jit(solution)/shard_map/all_to_all | solution.py:797
  433.0 50.0 %collective-permute-start.32 = (f32[16,2,32,128]{3,2,1,0:T(8,128)}, f32[16,2,32,128]{3,2,1,0:T(8,128)S(1)}, u32[]{:S(2)}, u32[]{:S(2)}) collective-permute-start(f32[16,2,32,128]{3,2,1,0:T(8,128)} %get-tuple-element.429), channel_id=1, source_target_pairs={{0,1},{1,2},{2,3},{3,4},{4,5},{5,6},{6,7},{7,8},{8,9},{9,10},{10,1... | collective-permute-start | bytes 1572872 | tf_op jit(solution)/shard_map/ppermute | solution.py:760
  435.0 48.7 %collective-permute-start.33 = (f32[16,2,32,128]{3,2,1,0:T(8,128)S(1)}, f32[16,2,32,128]{3,2,1,0:T(8,128)S(1)}, u32[]{:S(2)}, u32[]{:S(2)}) collective-permute-start(f32[16,2,32,128]{3,2,1,0:T(8,128)S(1)} %copy-done.42), channel_id=1, source_target_pairs={{1,0},{2,1},{3,2},{4,3},{5,4},{6,5},{7,6},{8,7},{9,8},{10,9},{11,1... | collective-permute-start | bytes 1572872 | tf_op jit(solution)/shard_map/ppermute | solution.py:761
  488.8 58.0 %all-to-all-start.7 = ((f32[32,2,64,128]{3,2,1,0:T(8,128)}), f32[32,2,64,128]{3,2,1,0:T(8,128)S(1)}, u32[]{:S(2)}, u32[]{:S(2)}) async-start(f32[32,2,64,128]{3,2,1,0:T(8,128)} %compress.15), calls=%async_computation.7 | async-start | bytes 4194304 | tf_op jit(solution)/shard_map/all_to_all | solution.py:797
  555.7 44.9 %collective-permute-start.34 = (f32[48,2,32,128]{3,2,1,0:T(8,128)}, f32[48,2,32,128]{3,2,1,0:T(8,128)S(1)}, u32[]{:S(2)}, u32[]{:S(2)}) collective-permute-start(f32[48,2,32,128]{3,2,1,0:T(8,128)} %get-tuple-element.451), channel_id=1, source_target_pairs={{0,1},{1,2},{2,3},{3,4},{4,5},{5,6},{6,7},{7,8},{8,9},{9,10},{10,1... | collective-permute-start | bytes 4718600 | tf_op jit(solution)/shard_map/ppermute | solution.py:760
  557.9 42.7 %collective-permute-start.35 = (f32[48,2,32,128]{3,2,1,0:T(8,128)}, f32[48,2,32,128]{3,2,1,0:T(8,128)S(1)}, u32[]{:S(2)}, u32[]{:S(2)}) collective-permute-start(f32[48,2,32,128]{3,2,1,0:T(8,128)} %get-tuple-element.457), channel_id=1, source_target_pairs={{1,0},{2,1},{3,2},{4,3},{5,4},{6,5},{7,6},{8,7},{9,8},{10,9},{11,1... | collective-permute-start | bytes 4718600 | tf_op jit(solution)/shard_map/ppermute | solution.py:761
  (59 other events, 1637.2 us)
